TPU v7x, 32 devices: a whole 2x2x4 slice. The times are simulated.
32 devices in a mesh: section: 2 (over core), dp: 16 (over z, y, x).
Axes of the slice: x: 2, y: 2, z: 4, core: 2. Of those that a mesh axis runs over, the one named last changes fastest.
Arguments:
- images: bfloat16 [256, 2, 147, 128], P('dp'), may hold values from -6 to 6
- proprio: bfloat16 [256, 2, 16, 64], P('dp'), may hold values from -6 to 6
- view_mask: int32 [256, 3], P('dp'), may hold values from 0 to 1, as said below
- embodiment: int32 [256], P('dp'), may hold values from 0 to 3
- ctx_steps: int32 [256], P('dp'), may hold values from 1 to 2
- queries: bfloat16 [4, 16, 128], replicated, may hold values from -5 to 5
- key_weight: bfloat16 [4, 128, 128], replicated, may hold values from -0.5 to 0.5
- value_weight: bfloat16 [4, 128, 128], replicated, may hold values from -0.5 to 0.5
- stem_proj: bfloat16 [128, 128], replicated, may hold values from -1.5 to 1.5
- prop_lift: bfloat16 [4, 64, 128], replicated, may hold values from -0.75 to 0.75
- prop_mix: bfloat16 [4, 128, 128], replicated, may hold values from -0.5 to 0.5
- attn_gain: bfloat16 [128], replicated, may hold values from 0.5 to 1.5
- attn_bias: bfloat16 [128], replicated, may hold values from -2 to 2
- query_key_value_weight: bfloat16 [128, 384], replicated, may hold values from -0.5 to 0.5
- attention_output_weight: bfloat16 [128, 128], replicated, may hold values from -1.5 to 1.5
- mlp_gain: bfloat16 [128], replicated, may hold values from 0.5 to 1.5
- mlp_bias: bfloat16 [128], replicated, may hold values from -2 to 2
- up_weight: bfloat16 [128, 512], replicated, may hold values from -0.5 to 0.5
- up_bias: bfloat16 [512], replicated, may hold values from -2 to 2
- down_weight: bfloat16 [512, 128], replicated, may hold values from -0.25 to 0.25
- down_bias: bfloat16 [128], replicated, may hold values from -2 to 2
- out_grad: bfloat16 [256, 64, 128], P('dp'), may hold values from -6 to 6
Outputs:
- block_out: bfloat16 [256, 64, 128], P('dp', 'section')
- image_grad: bfloat16 [256, 2, 147, 128], P('dp', 'section')
- proprio_grad: bfloat16 [256, 2, 16, 64], P('dp', 'section')
- queries_grad: float32 [4, 16, 128], replicated
- keyw_grad: float32 [4, 128, 128], replicated
- valuew_grad: float32 [4, 128, 128], replicated
- stem_grad: float32 [128, 128], replicated
- lift_grad: float32 [4, 64, 128], replicated
- mixer_grad: float32 [4, 128, 128], replicated
- again_grad: float32 [128], replicated
- abias_grad: float32 [128], replicated
- qkvw_grad: float32 [128, 384], replicated
- aproj_grad: float32 [128, 128], replicated
- mgain_grad: float32 [128], replicated
- mbias_grad: float32 [128], replicated
- upw_grad: float32 [128, 512], replicated
- upb_grad: float32 [512], replicated
- downw_grad: float32 [512, 128], replicated
- downb_grad: float32 [128], replicated
Inputs may be any that keep to these rules, and one draw needn't show every extreme that they name: `view_mask`: every sample has one to 3 of its views present.
All inputs are finite; a program needn't handle non-finite values.
Results may differ from a plain program's by a relative error of at most 0.02.
Values may be sent and summed in bfloat16 or wider, within the bound.
No kernel may reach another device: no remote copies, remote signals or barrier semaphores. Data moves between devices by JAX's collectives and lax.ppermute only.
A program may use at most 128 MiB of HBM per device.

v0:
```python
import math

import jax
import jax.numpy as jnp
from jax import lax
from jax.sharding import PartitionSpec as P

HEADS = 8
STEPS = 2
MICRO = 4


def shifted(block, axis, distance):
    devices = range(lax.axis_size(axis))
    route = [(i - distance, i) for i in devices if i - distance in devices]
    return lax.ppermute(block, axis, route)


def partner(value, axis, distance):
    mask = 2**distance
    pairs = [(source, source ^ mask) for source in range(lax.axis_size(axis))]
    return lax.ppermute(value, axis, pairs)


def layer_norm(values, gain_row, bias_row):
    center = values - jnp.mean(values, axis=-1, keepdims=True)
    spread = jnp.mean(center * center, axis=-1, keepdims=True)
    return center * lax.rsqrt(spread + 1e-05) * gain_row + bias_row


def head_table(width):
    column_head = jnp.arange(width) // (width // HEADS)
    return (column_head[None, :] == jnp.arange(HEADS)[:, None]).astype(jnp.bfloat16)


def spread_heads(rows, table):
    spread = rows[..., None, :, :] * table[:, None, :]
    return spread.reshape(rows.shape[:-2] + (HEADS * rows.shape[-2], rows.shape[-1]))


def fold_heads(rows, table):
    grouped = rows.reshape(rows.shape[:-2] + (HEADS, rows.shape[-2] // HEADS, rows.shape[-1]))
    return jnp.sum(grouped * table.astype(jnp.float32)[:, None, :], axis=-3)


def masked_softmax(scores, keep):
    grouped = scores.reshape(scores.shape[:-1] + (HEADS, scores.shape[-1] // HEADS))
    grouped = jnp.where(keep[..., None, :], grouped, -1e30)
    highest = jnp.max(grouped, axis=-1, keepdims=True)
    expo = jnp.exp(grouped - highest)
    probs = expo / jnp.sum(expo, axis=-1, keepdims=True)
    return probs.reshape(scores.shape)


def gelu_exact(values):
    return jax.nn.gelu(values, approximate=False)


def softmax_grad(probs, grad_low, scale):
    grouped_shape = probs.shape[:-1] + (HEADS, probs.shape[-1] // HEADS)
    prob_groups = probs.reshape(grouped_shape)
    grad_groups = grad_low.astype(jnp.float32).reshape(grouped_shape)
    inner = jnp.sum(prob_groups * grad_groups, axis=-1, keepdims=True)
    return (prob_groups * (grad_groups - inner) * scale).astype(jnp.bfloat16).reshape(probs.shape)


def per_embodiment(terms, embod_mb, count):
    table = (embod_mb[:, None] == jnp.arange(count)[None, :]).astype(jnp.float32)
    return jnp.einsum("se,s...->e...", table, terms)


def stem_forward(images_mb, proprio_mb, mask_mb, embod_mb, stem_weights):
    queries, kv_weight, stem_proj, prop_lift, prop_mix = stem_weights
    samples, steps_n, keys_n, width = images_mb.shape
    scale = 1.0 / math.sqrt(width // HEADS)
    table = head_table(width)
    kv_rows = jnp.take(kv_weight, embod_mb, axis=0)
    key_value = jnp.einsum(
        "stkd,sde->stke", images_mb, kv_rows, preferred_element_type=jnp.float32
    ).astype(jnp.bfloat16)
    key_spread = spread_heads(key_value[..., :width], table)
    value_spread = spread_heads(key_value[..., width:], table)
    query_rows = jnp.take(queries, embod_mb, axis=0)
    raw_scores = jnp.einsum(
        "sqd,stjd->stqj", query_rows, key_spread, preferred_element_type=jnp.float32
    )
    view_keep = (jnp.repeat(mask_mb, keys_n // mask_mb.shape[1], axis=1) > 0)[:, None, None, :]
    stem_prob = masked_softmax(raw_scores * scale, view_keep)
    attention_mixed = jnp.einsum(
        "stqj,stjd->stqd",
        stem_prob.astype(jnp.bfloat16),
        value_spread,
        preferred_element_type=jnp.float32,
    ).astype(jnp.bfloat16)
    image_tok = jnp.einsum(
        "stqd,de->stqe", attention_mixed, stem_proj, preferred_element_type=jnp.float32
    )
    lift_rows = jnp.take(prop_lift, embod_mb, axis=0)
    mix_rows = jnp.take(prop_mix, embod_mb, axis=0)
    lifted = jnp.einsum("stjp,spd->stjd", proprio_mb, lift_rows, preferred_element_type=jnp.float32)
    mixed_in = gelu_exact(lifted).astype(jnp.bfloat16)
    prop_tok = jnp.einsum("stjd,sde->stje", mixed_in, mix_rows, preferred_element_type=jnp.float32)
    token_rows = (
        jnp.concatenate([image_tok, prop_tok], axis=2)
        .astype(jnp.bfloat16)
        .reshape(samples, -1, width)
    )
    return (token_rows, (key_value, stem_prob, attention_mixed, lifted, mixed_in))


def blank_forward(images_mb, proprio_mb, query_count):
    samples, steps_n, keys_n, width = images_mb.shape
    prop_count = proprio_mb.shape[2]
    token_rows = jnp.zeros((samples, steps_n * (query_count + prop_count), width), jnp.bfloat16)
    kept = (
        jnp.zeros((samples, steps_n, keys_n, 2 * width), jnp.bfloat16),
        jnp.zeros((samples, steps_n, query_count, HEADS * keys_n), jnp.float32),
        jnp.zeros((samples, steps_n, query_count, width), jnp.bfloat16),
        jnp.zeros((samples, steps_n, prop_count, width), jnp.float32),
        jnp.zeros((samples, steps_n, prop_count, width), jnp.bfloat16),
    )
    return (token_rows, kept)


def stem_backward(back_tokens, images_mb, proprio_mb, embod_mb, stem_weights, kept, totals):
    queries, kv_weight, stem_proj, prop_lift, prop_mix = stem_weights
    key_value, stem_prob, attention_mixed, lifted, mixed_in = kept
    samples, steps_n, keys_n, width = images_mb.shape
    scale = 1.0 / math.sqrt(width // HEADS)
    table = head_table(width)
    emb_count, query_count = (queries.shape[0], queries.shape[1])
    grad_tok = back_tokens.reshape(samples, steps_n, -1, width)
    grad_image = grad_tok[:, :, :query_count]
    grad_prop = grad_tok[:, :, query_count:]
    kv_rows = jnp.take(kv_weight, embod_mb, axis=0)
    lift_rows = jnp.take(prop_lift, embod_mb, axis=0)
    mix_rows = jnp.take(prop_mix, embod_mb, axis=0)
    mix_terms = jnp.einsum(
        "stjd,stje->sde", mixed_in, grad_prop, preferred_element_type=jnp.float32
    )
    grad_mixed = jnp.einsum(
        "stje,sde->stjd", grad_prop, mix_rows, preferred_element_type=jnp.float32
    ).astype(jnp.bfloat16)
    grad_lift = jax.vjp(gelu_exact, lifted)[1](grad_mixed.astype(jnp.float32))[0].astype(
        jnp.bfloat16
    )
    lift_terms = jnp.einsum(
        "stjp,stjd->spd", proprio_mb, grad_lift, preferred_element_type=jnp.float32
    )
    proprio_grad = jnp.einsum(
        "stjd,spd->stjp", grad_lift, lift_rows, preferred_element_type=jnp.float32
    ).astype(jnp.bfloat16)
    proj_terms = jnp.einsum(
        "stqd,stqe->de", attention_mixed, grad_image, preferred_element_type=jnp.float32
    )
    grad_att = jnp.einsum(
        "stqe,de->stqd", grad_image, stem_proj, preferred_element_type=jnp.float32
    ).astype(jnp.bfloat16)
    key_spread = spread_heads(key_value[..., :width], table)
    value_spread = spread_heads(key_value[..., width:], table)
    query_rows = jnp.take(queries, embod_mb, axis=0)
    grad_prob = jnp.einsum(
        "stqd,stjd->stqj", grad_att, value_spread, preferred_element_type=jnp.float32
    ).astype(jnp.bfloat16)
    grad_values = fold_heads(
        jnp.einsum(
            "stqj,stqd->stjd",
            stem_prob.astype(jnp.bfloat16),
            grad_att,
            preferred_element_type=jnp.float32,
        ),
        table,
    )
    grad_raw = softmax_grad(stem_prob, grad_prob, scale)
    query_terms = jnp.einsum(
        "stqj,stjd->sqd", grad_raw, key_spread, preferred_element_type=jnp.float32
    )
    grad_keys = fold_heads(
        jnp.einsum("stqj,sqd->stjd", grad_raw, query_rows, preferred_element_type=jnp.float32),
        table,
    )
    grad_kv = jnp.concatenate([grad_keys, grad_values], axis=-1).astype(jnp.bfloat16)
    kv_terms = jnp.einsum("stkd,stke->sde", images_mb, grad_kv, preferred_element_type=jnp.float32)
    image_grad = jnp.einsum(
        "stke,sde->stkd", grad_kv, kv_rows, preferred_element_type=jnp.float32
    ).astype(jnp.bfloat16)
    terms = (
        per_embodiment(query_terms, embod_mb, emb_count),
        per_embodiment(kv_terms, embod_mb, emb_count),
        proj_terms,
        per_embodiment(lift_terms, embod_mb, emb_count),
        per_embodiment(mix_terms, embod_mb, emb_count),
    )
    return (image_grad, proprio_grad, jax.tree.map(jnp.add, totals, terms))


def trunk_step(tokens_in, grad_mb, steps_mb, trunk_weights, totals):
    (
        attn_gain,
        attn_bias,
        query_key_value_weight,
        attention_output_weight,
        mlp_gain,
        mlp_bias,
        up_weight,
        up_bias,
        down_weight,
        down_bias,
    ) = trunk_weights
    samples, ctx_n, width = tokens_in.shape
    scale = 1.0 / math.sqrt(width // HEADS)
    table = head_table(width)
    resid = tokens_in.astype(jnp.float32)
    live = jnp.arange(ctx_n)[None, :] // (ctx_n // STEPS) < steps_mb[:, None]
    normalized_tokens, norm_back = jax.vjp(layer_norm, resid, attn_gain, attn_bias)
    normalized_reduced = normalized_tokens.astype(jnp.bfloat16)
    query_key_value_full = jnp.einsum(
        "zqj,jt->zqt",
        normalized_reduced,
        query_key_value_weight,
        preferred_element_type=jnp.float32,
    ).astype(jnp.bfloat16)
    query_rows = query_key_value_full[..., :width]
    key_spread = spread_heads(query_key_value_full[..., width : 2 * width], table)
    value_spread = spread_heads(query_key_value_full[..., 2 * width :], table)
    raw_scores = jnp.einsum(
        "sqd,sjd->sqj", query_rows, key_spread, preferred_element_type=jnp.float32
    )
    trunk_prob = masked_softmax(raw_scores * scale, live[:, None, :])
    prob_low = trunk_prob.astype(jnp.bfloat16)
    attention_mixed = jnp.einsum(
        "sqj,sjd->sqd", prob_low, value_spread, preferred_element_type=jnp.float32
    ).astype(jnp.bfloat16)
    middle_activation = resid + jnp.einsum(
        "zqj,jt->zqt", attention_mixed, attention_output_weight, preferred_element_type=jnp.float32
    )
    normed2, norm2_back = jax.vjp(layer_norm, middle_activation, mlp_gain, mlp_bias)
    normed2_low = normed2.astype(jnp.bfloat16)
    up_pre = (
        jnp.einsum("snd,df->snf", normed2_low, up_weight, preferred_element_type=jnp.float32)
        + up_bias
    )
    up_act, gelu_back = jax.vjp(gelu_exact, up_pre)
    up_low = up_act.astype(jnp.bfloat16)
    result = (
        middle_activation
        + jnp.einsum("snf,fd->snd", up_low, down_weight, preferred_element_type=jnp.float32)
        + down_bias
    )
    live_col = live[..., None]
    block_mb = jnp.where(live_col, result, 0.0).astype(jnp.bfloat16)
    grad_low = jnp.where(live_col, grad_mb, jnp.zeros_like(grad_mb))
    grad_full = grad_low.astype(jnp.float32)
    down_bias_term = jnp.sum(grad_full, axis=(0, 1))
    down_term = jnp.einsum("snf,snd->fd", up_low, grad_low, preferred_element_type=jnp.float32)
    grad_up = jnp.einsum(
        "snd,fd->snf", grad_low, down_weight, preferred_element_type=jnp.float32
    ).astype(jnp.bfloat16)
    grad_pre = gelu_back(grad_up.astype(jnp.float32))[0].astype(jnp.bfloat16)
    up_bias_term = jnp.sum(grad_pre.astype(jnp.float32), axis=(0, 1))
    up_term = jnp.einsum("snd,snf->df", normed2_low, grad_pre, preferred_element_type=jnp.float32)
    grad_norm2 = jnp.einsum(
        "snf,df->snd", grad_pre, up_weight, preferred_element_type=jnp.float32
    ).astype(jnp.bfloat16)
    grad_mid, mgain_term, mbias_term = norm2_back(grad_norm2.astype(jnp.float32))
    grad_mid = grad_mid + grad_full
    middle_gradient_reduced = grad_mid.astype(jnp.bfloat16)
    proj_term = jnp.einsum(
        "ocq,ocb->qb", attention_mixed, middle_gradient_reduced, preferred_element_type=jnp.float32
    )
    grad_att = jnp.einsum(
        "rwo,fo->rwf",
        middle_gradient_reduced,
        attention_output_weight,
        preferred_element_type=jnp.float32,
    ).astype(jnp.bfloat16)
    grad_prob = jnp.einsum(
        "sqd,sjd->sqj", grad_att, value_spread, preferred_element_type=jnp.float32
    ).astype(jnp.bfloat16)
    grad_values = fold_heads(
        jnp.einsum("sqj,sqd->sjd", prob_low, grad_att, preferred_element_type=jnp.float32), table
    )
    grad_raw = softmax_grad(trunk_prob, grad_prob, scale)
    grad_query = jnp.einsum(
        "sqj,sjd->sqd", grad_raw, key_spread, preferred_element_type=jnp.float32
    )
    grad_keys = fold_heads(
        jnp.einsum("sqj,sqd->sjd", grad_raw, query_rows, preferred_element_type=jnp.float32), table
    )
    query_key_value_gradient = jnp.concatenate(
        [grad_query, grad_keys, grad_values], axis=-1
    ).astype(jnp.bfloat16)
    query_key_value_partial = jnp.einsum(
        "ocq,ocb->qb",
        normalized_reduced,
        query_key_value_gradient,
        preferred_element_type=jnp.float32,
    )
    grad_norm = jnp.einsum(
        "rwo,fo->rwf",
        query_key_value_gradient,
        query_key_value_weight,
        preferred_element_type=jnp.float32,
    ).astype(jnp.bfloat16)
    grad_resid, again_term, abias_term = norm_back(grad_norm.astype(jnp.float32))
    grad_tokens = (grad_resid + grad_mid).astype(jnp.bfloat16)
    terms = (
        again_term,
        abias_term,
        query_key_value_partial,
        proj_term,
        mgain_term,
        mbias_term,
        up_term,
        up_bias_term,
        down_term,
        down_bias_term,
    )
    return (block_mb, grad_tokens, jax.tree.map(jnp.add, totals, terms))


def gather_grads(stem_totals, trunk_totals, width):
    kv_total = stem_totals[1]
    return (
        stem_totals[0],
        kv_total[:, :, :width],
        kv_total[:, :, width:],
        stem_totals[2],
        stem_totals[3],
        stem_totals[4],
    ) + tuple(trunk_totals)


def per_device(
    images,
    proprio,
    view_mask,
    embodiment,
    ctx_steps,
    queries,
    key_weight,
    value_weight,
    stem_proj,
    prop_lift,
    prop_mix,
    attn_gain,
    attn_bias,
    query_key_value_weight,
    attention_output_weight,
    mlp_gain,
    mlp_bias,
    up_weight,
    up_bias,
    down_weight,
    down_bias,
    out_grad,
):
    width = key_weight.shape[1]
    query_count = queries.shape[1]
    stem_weights = (
        queries,
        jnp.concatenate([key_weight, value_weight], axis=2),
        stem_proj,
        prop_lift,
        prop_mix,
    )
    trunk_weights = (
        attn_gain.astype(jnp.float32),
        attn_bias.astype(jnp.float32),
        query_key_value_weight,
        attention_output_weight,
        mlp_gain.astype(jnp.float32),
        mlp_bias.astype(jnp.float32),
        up_weight,
        up_bias.astype(jnp.float32),
        down_weight,
        down_bias.astype(jnp.float32),
    )
    stem_totals = tuple((jnp.zeros(weight_arr.shape, jnp.float32) for weight_arr in stem_weights))
    trunk_totals = tuple((jnp.zeros(weight_arr.shape, jnp.float32) for weight_arr in trunk_weights))
    arrays = (images, proprio, view_mask, embodiment, ctx_steps, out_grad)
    per_batch = images.shape[0] // MICRO
    is_stem = lax.axis_index("section") == 0
    block_parts, image_parts, prop_parts = ([], [], [])
    for micro_index in range(MICRO):
        first = micro_index * per_batch
        images_mb, proprio_mb, mask_mb, embod_mb, steps_mb, grad_mb = tuple(
            (array[first : first + per_batch] for array in arrays)
        )

        def run_forward():
            return stem_forward(images_mb, proprio_mb, mask_mb, embod_mb, stem_weights)

        def skip_forward():
            return blank_forward(images_mb, proprio_mb, query_count)

        token_rows, kept = lax.cond(is_stem, run_forward, skip_forward)
        arrived = shifted(token_rows, "section", 1)

        def run_trunk():
            return trunk_step(arrived, grad_mb, steps_mb, trunk_weights, trunk_totals)

        def skip_trunk():
            return (jnp.zeros_like(arrived), jnp.zeros_like(arrived), trunk_totals)

        block_mb, grad_tokens, trunk_totals = lax.cond(is_stem, skip_trunk, run_trunk)
        returned = shifted(grad_tokens, "section", -1)

        def run_backward():
            return stem_backward(
                returned, images_mb, proprio_mb, embod_mb, stem_weights, kept, stem_totals
            )

        def skip_backward():
            return (jnp.zeros_like(images_mb), jnp.zeros_like(proprio_mb), stem_totals)

        image_mb_grad, prop_mb_grad, stem_totals = lax.cond(is_stem, run_backward, skip_backward)
        block_parts.append(block_mb)
        image_parts.append(image_mb_grad)
        prop_parts.append(prop_mb_grad)
    block_all = jnp.concatenate(block_parts, axis=0)
    image_all = jnp.concatenate(image_parts, axis=0)
    prop_all = jnp.concatenate(prop_parts, axis=0)
    ctx_half = block_all.shape[1] // 2
    steps_half = image_all.shape[1] // 2
    other_block, other_image, other_prop = partner(
        (block_all[:, :ctx_half], image_all[:, steps_half:], prop_all[:, steps_half:]), "section", 0
    )
    block_out = jnp.where(is_stem, other_block, block_all[:, ctx_half:])
    image_grad = jnp.where(is_stem, image_all[:, :steps_half], other_image)
    proprio_grad = jnp.where(is_stem, prop_all[:, :steps_half], other_prop)
    grads = gather_grads(stem_totals, trunk_totals, width)
    summed = lax.psum(
        (
            grads[0],
            grads[1],
            grads[2],
            grads[3],
            grads[4],
            grads[5],
            grads[6],
            grads[7],
            grads[8],
            grads[9],
            grads[10],
            grads[11],
            grads[12],
            grads[13],
            grads[14],
            grads[15],
        ),
        ("section", "dp"),
    )
    return (block_out, image_grad, proprio_grad) + tuple(summed)


def solution(mesh):
    placed = (
        P("dp", None, None, None),
        P("dp", None, None, None),
        P("dp", None),
        P("dp"),
        P("dp"),
        P(),
        P(),
        P(),
        P(),
        P(),
        P(),
        P(),
        P(),
        P(),
        P(),
        P(),
        P(),
        P(),
        P(),
        P(),
        P(),
        P("dp", None, None),
    )
    return jax.shard_map(
        per_device,
        mesh=mesh,
        in_specs=placed,
        out_specs=(
            P("dp", "section", None),
            P("dp", "section", None, None),
            P("dp", "section", None, None),
            P(),
            P(),
            P(),
            P(),
            P(),
            P(),
            P(),
            P(),
            P(),
            P(),
            P(),
            P(),
            P(),
            P(),
            P(),
            P(),
        ),
        check_vma=False,
    )
```

profile of v0, /device:TPU:0, one launch (start us, length us, event | category | flops | bytes accessed | tf_op | source)
XLA Modules:
  0.0 567.4 jit_solution(18314326496273688582)
XLA Ops:
  14.9 25.0 %conditional.12 = (bf16[4,64,128]{2,1,0:T(8,128)(2,1)}, bf16[4,2,147,256]{3,2,1,0:T(8,128)(2,1)S(1)}, f32[4,2,16,1176]{3,2,1,0:T(8,128)}, bf16[4,2,16,128]{3,2,1...) conditional(s32[]{:T(128)} %convert_element_type.800, () %tuple.108, ...), branch_computations={%region_0.0_spmd, %region_1.8_spmd} | conditional | flops 170326064 | bytes 43616280 | solution.py:397
  43.5 27.4 %conditional.14 = (bf16[4,64,128]{2,1,0:T(8,128)(2,1)}, bf16[4,2,147,256]{3,2,1,0:T(8,128)(2,1)S(1)}, f32[4,2,16,1176]{3,2,1,0:T(8,128)}, bf16[4,2,16,128]{3,2,1...) conditional(s32[]{:T(128)} %convert_element_type.800, () %tuple.112, ...), branch_computations={%region_25.30_spmd, %region_26.33_spmd} | conditional | flops 170326064 | bytes 43597436 | solution.py:397
  74.6 27.6 %conditional.16 = (bf16[4,64,128]{2,1,0:T(8,128)(2,1)}, bf16[4,2,147,256]{3,2,1,0:T(8,128)(2,1)S(1)}, f32[4,2,16,1176]{3,2,1,0:T(8,128)}, bf16[4,2,16,128]{3,2,1...) conditional(s32[]{:T(128)} %convert_element_type.800, () %tuple.116, ...), branch_computations={%region_50.55_spmd, %region_51.58_spmd} | conditional | flops 170326064 | bytes 43597436 | solution.py:397
  105.2 27.0 %conditional.18 = (bf16[4,64,128]{2,1,0:T(8,128)(2,1)}, bf16[4,2,147,256]{3,2,1,0:T(8,128)(2,1)S(1)}, f32[4,2,16,1176]{3,2,1,0:T(8,128)}, bf16[4,2,16,128]{3,2,1...) conditional(s32[]{:T(128)} %convert_element_type.800, () %tuple.120, ...), branch_computations={%region_75.80_spmd, %region_76.83_spmd} | conditional | flops 170326064 | bytes 43878480 | solution.py:397
  139.6 6.2 %conditional.13 = (bf16[4,64,128]{2,1,0:T(8,128)(2,1)}, bf16[4,64,128]{2,1,0:T(8,128)(2,1)}, f32[128]{0:T(128)}, f32[128]{0:T(128)}, f32[128,384]{1,0:T(8,128)},...) conditional(s32[]{:T(128)} %convert_element_type.800, ...), branch_computations={%region_4.28_spmd, %region_24.29_spmd} | conditional | flops 525407424 | bytes 51061604 | solution.py:406
  150.8 6.9 %conditional.17 = (bf16[4,64,128]{2,1,0:T(8,128)(2,1)}, bf16[4,64,128]{2,1,0:T(8,128)(2,1)}, f32[128]{0:T(128)}, f32[128]{0:T(128)}, f32[128,384]{1,0:T(8,128)},...) conditional(s32[]{:T(128)} %convert_element_type.800, ...), branch_computations={%region_54.78_spmd, %region_74.79_spmd} | conditional | flops 525605184 | bytes 50313800 | solution.py:406
  160.5 5.7 %conditional.19 = (bf16[4,64,128]{2,1,0:T(8,128)(2,1)}, bf16[4,64,128]{2,1,0:T(8,128)(2,1)}, f32[128]{0:T(128)}, f32[128]{0:T(128)}, f32[128,384]{1,0:T(8,128)},...) conditional(s32[]{:T(128)} %convert_element_type.800, ...), branch_computations={%region_79.103_spmd, %region_99.104_spmd} | conditional | flops 525605184 | bytes 50300404 | solution.py:406
  170.4 57.5 %conditional.20 = (bf16[4,2,16,64]{3,2,1,0:T(8,128)(2,1)S(1)}, f32[4,16,128]{2,0,1:T(4,128)S(1)}, f32[4,128,256]{2,0,1:T(4,128)S(1)}, f32[128,128]{1,0:T(8,128)}...) conditional(s32[]{:T(128)} %convert_element_type.800, ...), branch_computations={%region_100.105_spmd, %region_101.109_spmd} | conditional | flops 343321856 | bytes 94492536 | solution.py:417
  207.0 5.2 reshape.1552
  215.4 5.2 reshape.1551
  220.6 4.8 multiply_reduce_fusion.1
  228.6 58.3 %conditional.21 = (bf16[4,2,16,64]{3,2,1,0:T(8,128)(2,1)S(1)}, f32[4,16,128]{2,0,1:T(4,128)S(1)}, f32[4,128,256]{2,0,1:T(4,128)S(1)}, f32[128,128]{1,0:T(8,128)}...) conditional(s32[]{:T(128)} %convert_element_type.800, ...), branch_computations={%region_105.110_spmd, %region_106.114_spmd} | conditional | flops 343575808 | bytes 98523096 | solution.py:417
  265.7 5.2 reshape.1555
  274.1 5.2 reshape.1554
  279.4 4.8 multiply_reduce_fusion.3
  287.6 58.4 %conditional.22 = (bf16[4,2,16,64]{3,2,1,0:T(8,128)(2,1)S(1)}, f32[4,16,128]{2,0,1:T(4,128)S(1)}, f32[4,128,256]{2,0,1:T(4,128)S(1)}, f32[128,128]{1,0:T(8,128)}...) conditional(s32[]{:T(128)} %convert_element_type.800, ...), branch_computations={%region_110.115_spmd, %region_111.119_spmd} | conditional | flops 343575808 | bytes 98523096 | solution.py:417
  324.8 5.2 reshape.1558
  333.2 5.2 reshape.1557
  338.5 4.8 multiply_reduce_fusion.5
  347.5 56.5 %conditional.23 = (bf16[4,2,16,64]{3,2,1,0:T(8,128)(2,1)S(1)}, f32[4,16,128]{2,0,1:T(4,128)S(1)}, f32[4,128,256]{2,0,1:T(4,128)S(1)}, f32[128,128]{1,0:T(8,128)}...) conditional(s32[]{:T(128)} %convert_element_type.800, ...), branch_computations={%region_115.120_spmd, %region_116.124_spmd} | conditional | flops 343575808 | bytes 96426008 | solution.py:417
  382.7 5.1 reshape.1561
  391.1 5.2 reshape.1560
  409.3 43.4 %all-reduce = (f32[4,16,128]{2,1,0:T(8,128)}, f32[128]{0:T(128)}, f32[128]{0:T(128)}, f32[128]{0:T(128)}, f32[128]{0:T(128)}, /*index=5*/f32[512]{0:T(512)}, f32[128]{0:T(128)}) all-reduce(f32[4,16,128]{2,1,0:T(8,128)S(1)} %copy.70, f32[128]{0:T(128)} %get-tuple-element.927, ...), channel_id=1, replica_groups=mesh['section'=2,'dp'=16] {'section','dp'}, use_global_device_ids=true, to_apply=%region_120.125 | all-reduce | flops 9344 | bytes 74752 | tf_op jit(solution)/shard_map/psum | solution.py:433
  454.9 93.4 %all-reduce.4.cloned.1.call-done = (f32[4,128,128]{2,1,0:T(8,128)}, f32[4,128,128]{2,1,0:T(8,128)}, f32[128,128]{1,0:T(8,128)}, f32[4,64,128]{2,1,0:T(8,128)}, f...) async-done(((f32[4,128,128]{2,1,0:T(8,128)}, f32[4,128,128]{2,1,0:T(8,128)}, ...) | async-done | bytes 1769488 | tf_op jit(solution)/shard_map/psum | solution.py:433
  (668 shorter events, 345.9 us)
Async XLA Ops:
  7.3 541.0 %all-reduce.4.cloned.1.call-start = ((), (), s32[]{:S(2)}) async-start(), calls=%async_computation | async-start | bytes 3538944 | tf_op jit(solution)/shard_map/psum | solution.py:433
  39.9 99.7 %collective-permute-start = (bf16[4,64,128]{2,1,0:T(8,128)(2,1)}, bf16[4,64,128]{2,1,0:T(8,128)(2,1)}, u32[]{:S(2)}, u32[]{:S(2)}) collective-permute-start(bf16[4,64,128]{2,1,0:T(8,128)(2,1)} %get-tuple-element.837), channel_id=1, source_target_pairs={{0,16},{1,17},{2,18},{3,19},{4,20},{5,21},{6,22},{7,23},{8,24},{9,... | collective-permute-start | bytes 196616 | tf_op jit(solution)/shard_map/ppermute | solution.py:16
  70.9 76.1 %collective-permute-start.1 = (bf16[4,64,128]{2,1,0:T(8,128)(2,1)}, bf16[4,64,128]{2,1,0:T(8,128)(2,1)}, u32[]{:S(2)}, u32[]{:S(2)}) collective-permute-start(bf16[4,64,128]{2,1,0:T(8,128)(2,1)} %get-tuple-element.839), channel_id=1, source_target_pairs={{0,16},{1,17},{2,18},{3,19},{4,20},{5,21},{6,22},{7,23},{8,24},{9,... | collective-permute-start | bytes 196616 | tf_op jit(solution)/shard_map/ppermute | solution.py:16
  102.2 48.6 %collective-permute-start.2 = (bf16[4,64,128]{2,1,0:T(8,128)(2,1)}, bf16[4,64,128]{2,1,0:T(8,128)(2,1)S(1)}, u32[]{:S(2)}, u32[]{:S(2)}) collective-permute-start(bf16[4,64,128]{2,1,0:T(8,128)(2,1)} %get-tuple-element.851), channel_id=1, source_target_pairs={{0,16},{1,17},{2,18},{3,19},{4,20},{5,21},{6,22},{7,23},{8,24},{9,... | collective-permute-start | bytes 196616 | tf_op jit(solution)/shard_map/ppermute | solution.py:16
  132.2 28.3 %collective-permute-start.3 = (bf16[4,64,128]{2,1,0:T(8,128)(2,1)}, bf16[4,64,128]{2,1,0:T(8,128)(2,1)S(1)}, u32[]{:S(2)}, u32[]{:S(2)}) collective-permute-start(bf16[4,64,128]{2,1,0:T(8,128)(2,1)} %get-tuple-element.863), channel_id=1, source_target_pairs={{0,16},{1,17},{2,18},{3,19},{4,20},{5,21},{6,22},{7,23},{8,24},{9,... | collective-permute-start | bytes 196616 | tf_op jit(solution)/shard_map/ppermute | solution.py:16
  134.1 16.6 %copy-start.166 = (f32[128]{0:T(128)}, f32[128]{0:T(128)S(1)}, u32[]{:S(2)}) copy-start(f32[128]{0:T(128)S(1)} %convert_element_type.801) | copy-start | bytes 1540
  136.0 14.8 %copy-start.168 = (f32[128]{0:T(128)}, f32[128]{0:T(128)S(1)}, u32[]{:S(2)}) copy-start(f32[128]{0:T(128)S(1)} %convert_element_type.803) | copy-start | bytes 1540
  145.7 24.7 %collective-permute-start.5 = (bf16[4,64,128]{2,1,0:T(8,128)(2,1)}, bf16[4,64,128]{2,1,0:T(8,128)(2,1)}, u32[]{:S(2)}, u32[]{:S(2)}) collective-permute-start(bf16[4,64,128]{2,1,0:T(8,128)(2,1)} %get-tuple-element.875), channel_id=1, source_target_pairs={{16,0},{17,1},{18,2},{19,3},{20,4},{21,5},{22,6},{23,7},{24,8},{25... | collective-permute-start | bytes 196616 | tf_op jit(solution)/shard_map/ppermute | solution.py:16
  149.5 78.4 %collective-permute-start.6 = (bf16[4,64,128]{2,1,0:T(8,128)(2,1)}, bf16[4,64,128]{2,1,0:T(8,128)(2,1)}, u32[]{:S(2)}, u32[]{:S(2)}) collective-permute-start(bf16[4,64,128]{2,1,0:T(8,128)(2,1)} %get-tuple-element.887), channel_id=1, source_target_pairs={{16,0},{17,1},{18,2},{19,3},{20,4},{21,5},{22,6},{23,7},{24,8},{25... | collective-permute-start | bytes 196616 | tf_op jit(solution)/shard_map/ppermute | solution.py:16
  157.7 129.2 %collective-permute-start.7 = (bf16[4,64,128]{2,1,0:T(8,128)(2,1)}, bf16[4,64,128]{2,1,0:T(8,128)(2,1)}, u32[]{:S(2)}, u32[]{:S(2)}) collective-permute-start(bf16[4,64,128]{2,1,0:T(8,128)(2,1)} %get-tuple-element.899), channel_id=1, source_target_pairs={{16,0},{17,1},{18,2},{19,3},{20,4},{21,5},{22,6},{23,7},{24,8},{25... | collective-permute-start | bytes 196616 | tf_op jit(solution)/shard_map/ppermute | solution.py:16
  166.2 181.3 %collective-permute-start.8 = (bf16[4,64,128]{2,1,0:T(8,128)(2,1)}, bf16[4,64,128]{2,1,0:T(8,128)(2,1)}, u32[]{:S(2)}, u32[]{:S(2)}) collective-permute-start(bf16[4,64,128]{2,1,0:T(8,128)(2,1)} %get-tuple-element.911), channel_id=1, source_target_pairs={{16,0},{17,1},{18,2},{19,3},{20,4},{21,5},{22,6},{23,7},{24,8},{25... | collective-permute-start | bytes 196616 | tf_op jit(solution)/shard_map/ppermute | solution.py:16
  172.7 11.8 %copy-start.264 = (pred[4]{0:T(512)(128)(4,1)}, pred[4]{0:T(512)(128)(4,1)S(1)}, u32[]{:S(2)}) copy-start(pred[4]{0:T(512)(128)(4,1)S(1)} %compare_and_fusion.4) | copy-start | bytes 16 | tf_op jit(solution)/shard_map/cond
  177.3 14.3 %copy-start.140 = (bf16[4,2,16,128]{3,2,1,0:T(8,128)(2,1)}, bf16[4,2,16,128]{3,2,1,0:T(8,128)(2,1)S(1)}, u32[]{:S(2)}) copy-start(bf16[4,2,16,128]{3,2,1,0:T(8,128)(2,1)S(1)} %convolution_convert_fusion.15) | copy-start | bytes 98308 | tf_op jit(solution)/shard_map/cond
  228.8 13.1 %copy-start.163 = (bf16[4,2,16,64]{3,2,1,0:T(8,128)(2,1)S(1)}, bf16[4,2,16,64]{3,2,1,0:T(8,128)(2,1)}, u32[]{:S(2)}) copy-start(bf16[4,2,16,64]{3,2,1,0:T(8,128)(2,1)} %get-tuple-element.667) | copy-start | bytes 49156 | tf_op jit(solution)/shard_map/cond
  228.8 13.3 %copy-start.223 = (s32[4]{0:T(128)S(1)}, s32[4]{0:T(128)}, u32[]{:S(2)}) copy-start(s32[4]{0:T(128)} %get-tuple-element.656) | copy-start | bytes 52 | tf_op jit(solution)/shard_map/cond
  231.1 12.1 %copy-start.258 = (pred[4]{0:T(512)(128)(4,1)}, pred[4]{0:T(512)(128)(4,1)S(1)}, u32[]{:S(2)}) copy-start(pred[4]{0:T(512)(128)(4,1)S(1)} %compare_and_fusion.5) | copy-start | bytes 16 | tf_op jit(solution)/shard_map/cond
  287.8 13.1 %copy-start.162 = (bf16[4,2,16,64]{3,2,1,0:T(8,128)(2,1)S(1)}, bf16[4,2,16,64]{3,2,1,0:T(8,128)(2,1)}, u32[]{:S(2)}) copy-start(bf16[4,2,16,64]{3,2,1,0:T(8,128)(2,1)} %get-tuple-element.691) | copy-start | bytes 49156 | tf_op jit(solution)/shard_map/cond
  287.8 13.3 %copy-start.221 = (s32[4]{0:T(128)S(1)}, s32[4]{0:T(128)}, u32[]{:S(2)}) copy-start(s32[4]{0:T(128)} %get-tuple-element.680) | copy-start | bytes 52 | tf_op jit(solution)/shard_map/cond
  290.2 12.1 %copy-start.260 = (pred[4]{0:T(512)(128)(4,1)}, pred[4]{0:T(512)(128)(4,1)S(1)}, u32[]{:S(2)}) copy-start(pred[4]{0:T(512)(128)(4,1)S(1)} %compare_and_fusion.6) | copy-start | bytes 16 | tf_op jit(solution)/shard_map/cond
  347.7 11.9 %copy-start.129 = (f32[4,16,128]{2,0,1:T(4,128)}, f32[4,16,128]{2,0,1:T(4,128)S(1)}, u32[]{:S(2)}) copy-start(f32[4,16,128]{2,0,1:T(4,128)S(1)} %get-tuple-element.709) | copy-start | bytes 98308 | tf_op jit(solution)/shard_map/cond
  347.8 11.5 %copy-start.218 = (s32[4]{0:T(128)S(1)}, s32[4]{0:T(128)}, u32[]{:S(2)}) copy-start(s32[4]{0:T(128)} %get-tuple-element.704) | copy-start | bytes 52 | tf_op jit(solution)/shard_map/cond
  408.4 45.6 %collective-permute-start.9 = (bf16[16,1,147,128]{3,0,2,1:T(8,128)(2,1)S(1)}, bf16[16,1,147,128]{3,0,2,1:T(8,128)(2,1)S(1)}, u32[]{:S(2)}, u32[]{:S(2)}) collective-permute-start(bf16[16,1,147,128]{3,0,2,1:T(8,128)(2,1)S(1)} %slice.335), channel_id=1, source_target_pairs={{0,16},{16,0},{1,17},{17,1},{2,18},{18,2},{3,19},{19,3},{4,20},{20... | collective-permute-start | bytes 1806344 | tf_op jit(solution)/shard_map/ppermute | solution.py:22
  408.6 44.1 %collective-permute-start.10 = (bf16[16,1,16,64]{3,2,1,0:T(8,128)(2,1)S(1)}, bf16[16,1,16,64]{3,2,1,0:T(8,128)(2,1)S(1)}, u32[]{:S(2)}, u32[]{:S(2)}) collective-permute-start(bf16[16,1,16,64]{3,2,1,0:T(8,128)(2,1)S(1)} %slice.337), channel_id=1, source_target_pairs={{0,16},{16,0},{1,17},{17,1},{2,18},{18,2},{3,19},{19,3},{4,20},{20... | collective-permute-start | bytes 98312 | tf_op jit(solution)/shard_map/ppermute | solution.py:22
  409.2 44.2 %collective-permute-start.4 = (bf16[16,32,128]{2,1,0:T(8,128)(2,1)S(1)}, bf16[16,32,128]{2,1,0:T(8,128)(2,1)S(1)}, u32[]{:S(2)}, u32[]{:S(2)}) collective-permute-start(bf16[16,32,128]{2,1,0:T(8,128)(2,1)S(1)} %slice.332), channel_id=1, source_target_pairs={{0,16},{16,0},{1,17},{17,1},{2,18},{18,2},{3,19},{19,3},{4,20},{20... | collective-permute-start | bytes 393224 | tf_op jit(solution)/shard_map/ppermute | solution.py:22
  (128 other events, 514.9 us)
Sparse Core Ops, SparseCore 0:
  408.7 139.5 all-reduce.3
where the time goes:
time: 578 us; the launch traced here: 567 us
  local copies, waits for them, and re-layouts  195 us (34%)
  matrix products  131 us (23%)
  waiting for transfers between devices  93.4 us (16%)
  other arithmetic  61.1 us (11%)
  blocking collectives  43.4 us (8%)
  loops' own time  16.2 us (3%)
  between operations  15.1 us (3%)
  starting transfers between devices  12.3 us (2%)
    psum x1, waiting for transfers between devices, per_device(): lax.psum((grads[0], grads[1], grads[2], grads[3], grads[4], grads[5], gra...  93.4 us
    mul x48, local copies, waits for them, and re-layouts, spread_heads(): spread = rows[..., None, :, :] * table[:, None, :]  52.4 us
    psum x1, blocking collectives, per_device(): lax.psum((grads[0], grads[1], grads[2], grads[3], grads[4], grads[5], gra...  43.4 us
    reshape x8, local copies, waits for them, and re-layouts, fold_heads(): rows.reshape(rows.shape[:-2] + (HEADS, rows.shape[-2] // HEADS, rows.shap...  41.5 us
    unnamed x98, local copies, waits for them, and re-layouts  26 us
    reduce_sum x4, other arithmetic, fold_heads(): return jnp.sum(grouped * table.astype(jnp.float32)[:, None, :], axis=-3)  19.2 us
    dot_general x4, matrix products, stem_backward(): jnp.einsum('stqj,stqd->stjd', stem_prob.astype(jnp.bfloat16), grad_att, p...  19.1 us
    dot_general x4, matrix products, stem_backward(): jnp.einsum('stqd,stjd->stqj', grad_att, value_spread, preferred_element_t...  14.4 us
  transfers between devices with their start and end apart: 12, of which 1 were waited for; matrix products, arithmetic and copies ran while one was open for 49% of the time, Pallas kernels for 0%

commit v1 on v0

v1 whole, which is shorter than its diff:
```python
import functools
import math

import jax
import jax.numpy as jnp
from jax import lax
from jax.experimental import pallas as pl
from jax.experimental.pallas import tpu as pltpu
from jax.sharding import PartitionSpec as P

HEADS = 8
F32 = jnp.float32
BF16 = jnp.bfloat16
CORES = 2
PIECES = 4
EPS = 1e-05
INV_SQRT2 = 1.0 / math.sqrt(2.0)
INV_SQRT2PI = 1.0 / math.sqrt(2.0 * math.pi)
ANY = pl.BlockSpec(memory_space=pl.ANY)
VMEM = pl.BlockSpec(memory_space=pltpu.VMEM)
SMEM = pl.BlockSpec(memory_space=pltpu.SMEM)


def mm(left, right):
    return lax.dot_general(left, right, (((1,), (0,)), ((), ())), preferred_element_type=F32)


def mm_bt(left, right):
    return lax.dot_general(left, right, (((1,), (1,)), ((), ())), preferred_element_type=F32)


def mm_at(left, right):
    return lax.dot_general(left, right, (((0,), (0,)), ((), ())), preferred_element_type=F32)


def layout(width, ffw, emb, queries, feats):
    counts = (
        ("keyw", emb * width),
        ("valuew", emb * width),
        ("mixer", emb * width),
        ("stem", width),
        ("lift", emb * feats),
        ("queries", emb * queries),
        ("qkv", 3 * width),
        ("aproj", width),
        ("up", ffw),
        ("down", ffw),
        ("vectors", 16),
    )
    table, first = {}, 0
    for name, rows in counts:
        table[name] = (first, rows)
        first += rows
    step = CORES * PIECES * 16
    return table, (first + step - 1) // step * step


def cuts(first, rows, piece):
    done = 0
    while done < rows:
        at = first + done
        count = min(rows - done, piece - at % piece)
        yield at // piece, at % piece, done, count
        done += count


def head_mask(rows, per_head, width):
    row = lax.broadcasted_iota(jnp.int32, (rows, width), 0) // per_head
    col = lax.broadcasted_iota(jnp.int32, (rows, width), 1) // (width // HEADS)
    return (row == col).astype(F32)


def spread(rows, mask):
    return jnp.concatenate([rows] * HEADS, axis=0) * mask


def fold(full, mask):
    per = full.shape[0] // HEADS
    return jnp.sum((full * mask).reshape(HEADS, per, full.shape[1]), axis=0)


def gelu_parts(values):
    cdf = 0.5 * (1.0 + lax.erf(values * INV_SQRT2))
    pdf = INV_SQRT2PI * jnp.exp(-0.5 * values * values)
    return values * cdf, cdf + values * pdf


def softmax_rows(scores, bias):
    scores = scores + bias
    expo = jnp.exp(scores - jnp.max(scores, axis=0, keepdims=True))
    return expo / jnp.sum(expo, axis=0, keepdims=True)


def softmax_rows_grad(probs, grad):
    terms = probs * grad
    return terms - probs * jnp.sum(terms, axis=0, keepdims=True)


def norm_parts(values):
    center = values - jnp.mean(values, axis=-1, keepdims=True)
    rstd = lax.rsqrt(jnp.mean(center * center, axis=-1, keepdims=True) + EPS)
    return center * rstd, rstd


def norm_grad(grad, gain, hat, rstd):
    scaled = grad * gain
    first = jnp.mean(scaled, axis=-1, keepdims=True)
    second = jnp.mean(scaled * hat, axis=-1, keepdims=True)
    return rstd * (scaled - first - hat * second)


def compute_kernel(
    dims,
    emb_ref,
    steps_ref,
    views_ref,
    images,
    proprio,
    out_grad,
    queries,
    key_w,
    value_w,
    stem_proj,
    lift_w,
    mix_w,
    again,
    abias,
    qkv_w,
    aproj,
    mgain,
    mbias,
    up_w,
    up_b,
    down_w,
    down_b,
    keep,
    send,
    block_out,
    block_send,
    image_out,
    image_send,
    prop_out,
    prop_send,
    x_s,
    p_s,
    g_s,
    qs_s,
    a_s,
    tok_s,
    xt_s,
    prob_s,
    probb_s,
    ut_s,
    satt_s,
    act_s,
    dact_s,
    hat1_s,
    rstd1_s,
    norm1_s,
    qkv_s,
    tprob_s,
    att_s,
    hat2_s,
    rstd2_s,
    norm2_s,
    up_s,
    dup_s,
    glow_s,
    gpre_s,
    gn2_s,
    gmid_s,
    gatt_s,
    gqkv_s,
    gn1_s,
    gtok_s,
    gsatt_s,
    blk_s,
    img_s,
    prp_s,
    macc_s,
    vacc_s,
    mixacc_s,
    liftacc_s,
    pack_s,
    in_sem,
    out_sem,
):
    n, steps, keys, width, qry, ptok, emb, ffw, table, views = dims
    half_tok = qry + ptok
    ctx = steps * half_tok
    rows = n * ctx
    scale = 1.0 / math.sqrt(width // HEADS)
    piece = pack_s.shape[2]
    sec = lax.axis_index("section")
    base = sec * n

    def put(name, row, value):
        first = table[name][0] + row
        for at, lo, done, count in cuts(first, value.shape[0], piece):
            pack_s[at // PIECES, at % PIECES, lo : lo + count] = value[done : done + count].astype(BF16)

    loads = [pltpu.make_async_copy(proprio.at[pl.ds(base, n)], p_s, in_sem.at[n])]
    loads += [pltpu.make_async_copy(images.at[base + s], x_s.at[s], in_sem.at[s]) for s in range(n)]
    loads += [pltpu.make_async_copy(out_grad.at[pl.ds(base, n)], g_s, in_sem.at[n + 1])]
    for copy in loads:
        copy.start()

    smask = head_mask(HEADS * qry, qry, width)
    smask_low = smask.astype(BF16)
    tmask = head_mask(HEADS * ctx, ctx, width)
    tmask_low = tmask.astype(BF16)
    for e in range(emb):
        qs = spread(queries[e], smask_low)
        qs_s[e] = qs
        a_s[e] = (mm_bt(key_w[e], qs) * scale).astype(BF16)
        macc_s[e] = jnp.zeros((width, width), F32)
        vacc_s[e] = jnp.zeros((width, width), F32)
        mixacc_s[e] = jnp.zeros((width, width), F32)
        liftacc_s[e] = jnp.zeros(liftacc_s.shape[1:], F32)

    loads[0].wait()
    for s in range(n):
        e = emb_ref[base + s]
        lifted = mm(p_s[s].reshape(steps * ptok, -1), lift_w[e])
        act, dact = gelu_parts(lifted)
        act_low = act.astype(BF16)
        act_s[s] = act_low
        dact_s[s] = dact
        tok_s[s, :, qry:] = mm(act_low, mix_w[e]).astype(BF16).reshape(steps, ptok, width)

    view_of = lax.broadcasted_iota(jnp.int32, (keys, width), 0) // (keys // views)
    for s in range(n):
        e = emb_ref[base + s]
        bias = jnp.zeros((keys, width), F32)
        for v in range(views):
            lost = jnp.where(views_ref[base + s, v] > 0, 0.0, -1e30).astype(F32)
            bias = jnp.where(view_of == v, lost, bias)
        loads[1 + s].wait()
        for t in range(steps):
            x = x_s[s, t]
            xt_s[s, t] = x.T
            prob = softmax_rows(mm(x, a_s[e]), bias)
            prob_s[s, t] = prob
            prob_low = prob.astype(BF16)
            probb_s[s, t] = prob_low
            ut = mm(xt_s[s, t], prob_low).astype(BF16)
            ut_s[s, t] = ut
            satt_s[s, t] = fold(mm_at(ut, value_w[e]), smask).astype(BF16)
    image_tok = mm(satt_s[...].reshape(n * steps * qry, width), stem_proj[...])
    tok_s[:, :, :qry] = image_tok.astype(BF16).reshape(n, steps, qry, width)

    chunk = CORES * ctx
    spans = [pl.ds(i * chunk, chunk) for i in range(rows // chunk)]
    again_row = again[...].astype(F32).reshape(1, width)
    abias_row = abias[...].astype(F32).reshape(1, width)
    mgain_row = mgain[...].astype(F32).reshape(1, width)
    mbias_row = mbias[...].astype(F32).reshape(1, width)
    upb_row = up_b[...].astype(F32).reshape(1, ffw)
    downb_row = down_b[...].astype(F32).reshape(1, width)

    def tokens_of(i):
        return tok_s[CORES * i : CORES * (i + 1)].reshape(chunk, width).astype(F32)

    for i, span in enumerate(spans):
        hat, rstd = norm_parts(tokens_of(i))
        hat1_s[span] = hat
        rstd1_s[span] = jnp.broadcast_to(rstd, hat.shape)
        norm1 = (hat * again_row + abias_row).astype(BF16)
        norm1_s[span] = norm1
        qkv_s[span] = mm(norm1, qkv_w[...]).astype(BF16)

    key_step = lax.broadcasted_iota(jnp.int32, (ctx, 1), 0) // half_tok
    for s in range(n):
        mine = pl.ds(s * ctx, ctx)
        query, key, value = (qkv_s[mine, width * j : width * (j + 1)] for j in range(3))
        dead = jnp.where(key_step < steps_ref[base + s], 0.0, -1e30).astype(F32)
        prob = softmax_rows(mm_bt(key, spread(query, tmask_low)) * scale, dead)
        tprob_s[s] = prob
        att_s[mine] = fold(mm_at(prob.astype(BF16), value), tmask).astype(BF16)

    loads[n + 1].wait()
    row_step = lax.broadcasted_iota(jnp.int32, (ctx, 1), 0) // half_tok
    mgain_sum = jnp.zeros((1, width), F32)
    mbias_sum = jnp.zeros((1, width), F32)
    downb_sum = jnp.zeros((1, width), F32)
    upb_sum = jnp.zeros((1, ffw), F32)
    for i, span in enumerate(spans):
        middle = tokens_of(i) + mm(att_s[span], aproj[...])
        hat, rstd = norm_parts(middle)
        hat2_s[span] = hat
        rstd2_s[span] = jnp.broadcast_to(rstd, hat.shape)
        norm2 = (hat * mgain_row + mbias_row).astype(BF16)
        norm2_s[span] = norm2
        act, dact = gelu_parts(mm(norm2, up_w[...]) + upb_row)
        act_low = act.astype(BF16)
        up_s[span] = act_low
        live = jnp.concatenate(
            [
                jnp.where(row_step < steps_ref[base + CORES * i + j], 1.0, 0.0).astype(F32)
                for j in range(CORES)
            ],
            axis=0,
        )
        result = (middle + mm(act_low, down_w[...]) + downb_row) * live
        blk_s[CORES * i : CORES * (i + 1)] = result.astype(BF16).reshape(CORES, steps, half_tok, width)
        grad = g_s[CORES * i : CORES * (i + 1)].reshape(chunk, width).astype(F32) * live
        grad_low = grad.astype(BF16)
        glow_s[span] = grad_low
        downb_sum += jnp.sum(grad, axis=0, keepdims=True)
        grad_up = mm_bt(grad_low, down_w[...]).astype(BF16).astype(F32)
        grad_pre = (grad_up * dact).astype(BF16)
        gpre_s[span] = grad_pre
        upb_sum += jnp.sum(grad_pre.astype(F32), axis=0, keepdims=True)
        grad_norm2 = mm_bt(grad_pre, up_w[...]).astype(BF16).astype(F32)
        mgain_sum += jnp.sum(grad_norm2 * hat, axis=0, keepdims=True)
        mbias_sum += jnp.sum(grad_norm2, axis=0, keepdims=True)
        grad_mid = norm_grad(grad_norm2, mgain_row, hat, rstd) + grad
        gn2_s[span] = grad_mid
        grad_mid_low = grad_mid.astype(BF16)
        gmid_s[span] = grad_mid_low
        gatt_s[span] = mm_bt(grad_mid_low, aproj[...]).astype(BF16)
    put("aproj", 0, mm_at(att_s[...], gmid_s[...]))
    put("down", 0, mm_at(up_s[...], glow_s[...]))
    for j in range(ffw // width):
        cols = slice(width * j, width * (j + 1))
        put("up", width * j, mm_at(norm2_s[...], gpre_s[:, cols]))

    for s in range(n):
        mine = pl.ds(s * ctx, ctx)
        query, key, value = (qkv_s[mine, width * j : width * (j + 1)] for j in range(3))
        query_spread = spread(query, tmask_low)
        grad_spread = spread(gatt_s[mine], tmask_low)
        prob = tprob_s[s]
        grad_prob = mm_bt(value, grad_spread).astype(BF16).astype(F32)
        grad_raw = (softmax_rows_grad(prob, grad_prob) * scale).astype(BF16)
        grad_query = fold(mm_at(grad_raw, key), tmask)
        gqkv_s[mine, :width] = grad_query.astype(BF16)
        gqkv_s[mine, width : 2 * width] = mm(grad_raw, query_spread).astype(BF16)
        gqkv_s[mine, 2 * width :] = mm(prob.astype(BF16), grad_spread).astype(BF16)
    again_sum = jnp.zeros((1, width), F32)
    abias_sum = jnp.zeros((1, width), F32)
    for i, span in enumerate(spans):
        grad_norm1 = mm_bt(gqkv_s[span], qkv_w[...]).astype(BF16).astype(F32)
        hat = hat1_s[span]
        again_sum += jnp.sum(grad_norm1 * hat, axis=0, keepdims=True)
        abias_sum += jnp.sum(grad_norm1, axis=0, keepdims=True)
        grad_tok = norm_grad(grad_norm1, again_row, hat, rstd1_s[span]) + gn2_s[span]
        gtok_s[CORES * i : CORES * (i + 1)] = grad_tok.astype(BF16).reshape(CORES, steps, half_tok, width)
    for j in range(3):
        cols = slice(width * j, width * (j + 1))
        put("qkv", width * j, mm_at(norm1_s[...], gqkv_s[:, cols]))
    vectors = [again_sum, abias_sum, mgain_sum, mbias_sum, downb_sum]
    vectors += [upb_sum[:, width * j : width * (j + 1)] for j in range(ffw // width)]
    vectors += [jnp.zeros((16 - len(vectors), width), F32)]
    put("vectors", 0, jnp.concatenate(vectors, axis=0))

    for s in range(n):
        e = emb_ref[base + s]
        grad_prop = gtok_s[s, :, qry:].reshape(steps * ptok, width)
        mixacc_s[e] += mm_at(act_s[s], grad_prop)
        grad_act = mm_bt(grad_prop, mix_w[e]).astype(BF16).astype(F32)
        grad_lift = (grad_act * dact_s[s]).astype(BF16)
        liftacc_s[e] += mm_at(p_s[s].reshape(steps * ptok, -1), grad_lift)
        prp_s[s] = mm_bt(grad_lift, lift_w[e]).astype(BF16).reshape(steps, ptok, -1)

    grad_img = gtok_s[:, :, :qry].reshape(n * steps * qry, width)
    put("stem", 0, mm_at(satt_s[...].reshape(n * steps * qry, width), grad_img))
    gsatt_s[...] = mm_bt(grad_img, stem_proj[...]).astype(BF16).reshape(n, steps, qry, width)
    for s in range(n):
        e = emb_ref[base + s]
        for t in range(steps):
            grad_spread = spread(gsatt_s[s, t], smask_low)
            back = mm_bt(value_w[e], grad_spread).astype(BF16)
            prob = prob_s[s, t]
            grad_prob = mm(x_s[s, t], back).astype(BF16).astype(F32)
            grad_raw = softmax_rows_grad(prob, grad_prob).astype(BF16)
            macc_s[e] += mm(xt_s[s, t], grad_raw)
            vacc_s[e] += mm(ut_s[s, t], grad_spread)
            image = mm_bt(grad_raw, a_s[e]) + mm_bt(probb_s[s, t], back)
            img_s[s, t] = image.astype(BF16)
    for e in range(emb):
        moment = (macc_s[e] * scale).astype(BF16)
        put("keyw", width * e, mm(moment, qs_s[e]))
        put("queries", qry * e, fold(mm_at(moment, key_w[e]), smask))
        put("valuew", width * e, vacc_s[e])
        put("mixer", width * e, mixacc_s[e])
        put("lift", liftacc_s.shape[1] * e, liftacc_s[e])
    used = max(first + count for first, count in table.values())
    for at, lo, _, count in cuts(used, 2 * PIECES * piece - used, piece):
        pack_s[at // PIECES, at % PIECES, lo : lo + count] = jnp.zeros((count, width), BF16)

    other = 1 - sec
    mine = pl.ds(base, n)
    stores = (
        (pack_s.at[sec], keep),
        (pack_s.at[other], send),
        (blk_s.at[:, sec], block_out.at[mine]),
        (blk_s.at[:, other], block_send),
        (img_s.at[:, sec], image_out.at[mine, 0]),
        (img_s.at[:, other], image_send),
        (prp_s.at[:, sec], prop_out.at[mine, 0]),
        (prp_s.at[:, other], prop_send),
    )
    stores = [pltpu.make_async_copy(a, b, out_sem.at[i]) for i, (a, b) in enumerate(stores)]
    for copy in stores:
        copy.start()
    for copy in stores:
        copy.wait()


def compute(args, table, total):
    images, proprio, view_mask, embodiment, ctx_steps = args[:5]
    weights, out_grad = args[5:21], args[21]
    samples, steps, keys, width = images.shape
    ptok, feats = proprio.shape[2:]
    emb, qry = weights[0].shape[:2]
    ffw = weights[12].shape[1]
    n = samples // CORES
    half_tok = qry + ptok
    ctx = steps * half_tok
    rows = n * ctx
    piece = total // (CORES * PIECES)
    dims = (n, steps, keys, width, qry, ptok, emb, ffw, table, view_mask.shape[1])

    def low(*shape):
        return pltpu.VMEM(shape, BF16)

    def full(*shape):
        return pltpu.VMEM(shape, F32)

    scratch = [
        low(n, steps, keys, width),
        low(n, steps, ptok, feats),
        low(n, ctx, width),
        low(emb, HEADS * qry, width),
        low(emb, width, HEADS * qry),
        low(n, steps, half_tok, width),
        low(n, steps, width, keys),
        full(n, steps, keys, HEADS * qry),
        low(n, steps, keys, HEADS * qry),
        low(n, steps, width, HEADS * qry),
        low(n, steps, qry, width),
        low(n, steps * ptok, width),
        full(n, steps * ptok, width),
        full(rows, width),
        full(rows, width),
        low(rows, width),
        low(rows, 3 * width),
        full(n, ctx, HEADS * ctx),
        low(rows, width),
        full(rows, width),
        full(rows, width),
        low(rows, width),
        low(rows, ffw),
        full(rows, ffw),
        low(rows, width),
        low(rows, ffw),
        full(rows, width),
        low(rows, width),
        low(rows, width),
        low(rows, 3 * width),
        full(rows, width),
        low(n, steps, half_tok, width),
        low(n, steps, qry, width),
        low(n, steps, half_tok, width),
        low(n, steps, keys, width),
        low(n, steps, ptok, feats),
        full(emb, width, HEADS * qry),
        full(emb, width, width),
        full(emb, width, width),
        full(emb, feats, width),
        low(CORES, PIECES, piece, width),
        pltpu.SemaphoreType.DMA((n + 2,)),
        pltpu.SemaphoreType.DMA((8,)),
    ]
    shape = jax.ShapeDtypeStruct
    return pl.pallas_call(
        functools.partial(compute_kernel, dims),
        out_shape=(
            shape((PIECES, piece, width), BF16),
            shape((PIECES, piece, width), BF16),
            shape((samples, half_tok, width), BF16),
            shape((n, half_tok, width), BF16),
            shape((samples, 1, keys, width), BF16),
            shape((n, keys, width), BF16),
            shape((samples, 1, ptok, feats), BF16),
            shape((n, ptok, feats), BF16),
        ),
        in_specs=[SMEM] * 3 + [ANY] * 3 + [VMEM] * 16,
        out_specs=(ANY,) * 8,
        scratch_shapes=scratch,
        compiler_params=pltpu.CompilerParams(vmem_limit_bytes=56 * 2**20),
        name="stem_trunk",
    )(embodiment, ctx_steps, view_mask, images, proprio, out_grad, *weights)


def own_bits():
    dp, sec = lax.axis_index("dp"), lax.axis_index("section")
    low, high = dp % 2, (dp // 2) % 2
    return jnp.where(sec == 0, low, high), jnp.where(sec == 0, high, low)


def add_split_kernel(which, held, came, keep, send):
    bit = own_bits()[which]
    keep[...] = (held[bit].astype(F32) + came[bit].astype(F32)).astype(BF16)
    send[...] = (held[1 - bit].astype(F32) + came[1 - bit].astype(F32)).astype(BF16)


def add_split(which, held, came):
    held, came = (v.reshape((2, -1) + v.shape[-1:]) for v in (held, came))
    shape = jax.ShapeDtypeStruct(held.shape[1:], BF16)
    return pl.pallas_call(
        functools.partial(add_split_kernel, which),
        out_shape=(shape, shape),
        in_specs=[VMEM] * 2,
        out_specs=(VMEM,) * 2,
        name=f"add_split_{which}",
    )(held, came)


def swap_cores(value):
    return lax.ppermute(value, "section", [(0, 1), (1, 0)])


def swap_chips(value, bits):
    count = lax.axis_size("dp")
    pairs = [
        (s * count + i, s * count + (i ^ (1 << bits[s]))) for s in range(CORES) for i in range(count)
    ]
    return lax.ppermute(value, ("section", "dp"), pairs)


def join_kernel(blk_in, img_in, prp_in, blk_r, img_r, prp_r, blk, img, prp, sem):
    n = blk_r.shape[0]
    other = pl.ds((1 - lax.axis_index("section")) * n, n)
    copies = (
        pltpu.make_async_copy(blk_r, blk.at[other], sem.at[0]),
        pltpu.make_async_copy(img_r, img.at[other, 0], sem.at[1]),
        pltpu.make_async_copy(prp_r, prp.at[other, 0], sem.at[2]),
    )
    for copy in copies:
        copy.start()
    for copy in copies:
        copy.wait()


def join(own, came):
    return pl.pallas_call(
        join_kernel,
        out_shape=tuple(jax.ShapeDtypeStruct(v.shape, v.dtype) for v in own),
        in_specs=[ANY] * 6,
        out_specs=(ANY,) * 3,
        input_output_aliases={0: 0, 1: 1, 2: 2},
        scratch_shapes=[pltpu.SemaphoreType.DMA((3,))],
        name="join_outputs",
    )(*own, *came)


def unpack_kernel(table, *refs):
    pieces, outs, (pack, sem) = refs[:8], refs[8:-2], refs[-2:]
    sec = lax.axis_index("section")
    one, two = own_bits()
    copies = []
    for owner in range(CORES):
        first, second = (one, two) if owner == 0 else (two, one)
        start = (sec if owner == 0 else 1 - sec) * PIECES
        for j in range(PIECES):
            x = first if j < 2 else 1 - first
            y = second if j % 2 == 0 else 1 - second
            at = start + 2 * x + y
            i = owner * PIECES + j
            copies.append(pltpu.make_async_copy(pieces[i], pack.at[at], sem.at[i]))
    for copy in copies:
        copy.start()
    for copy in copies:
        copy.wait()
    piece = pack.shape[1]

    def get(name, row, count, store):
        for at, lo, done, size in cuts(table[name][0] + row, count, piece):
            store(done, size, pack[at, lo : lo + size].astype(F32))

    def flat(ref, name):
        def store(done, size, value):
            ref[done : done + size] = value

        get(name, 0, ref.shape[0], store)

    def stacked(ref, name):
        for e in range(ref.shape[0]):

            def store(done, size, value, e=e):
                ref[e, done : done + size] = value

            get(name, e * ref.shape[1], ref.shape[1], store)

    def blocks(ref, name):
        depth, width = ref.shape[0], pack.shape[2]
        for j in range(ref.shape[1] // width):

            def store(done, size, value, j=j):
                ref[done : done + size, width * j : width * (j + 1)] = value

            get(name, j * depth, depth, store)

    q, k, v, stem, lift, mix, again, abias, qkv, aproj, mgain, mbias, up, upb, down, downb = outs
    for ref, name in ((q, "queries"), (k, "keyw"), (v, "valuew"), (lift, "lift"), (mix, "mixer")):
        stacked(ref, name)
    for ref, name in ((stem, "stem"), (aproj, "aproj"), (down, "down")):
        flat(ref, name)
    for ref, name in ((qkv, "qkv"), (up, "up")):
        blocks(ref, name)
    at, lo, _, _ = next(cuts(table["vectors"][0], 16, piece))
    vectors = pack[at, lo : lo + 16].astype(F32)
    width = pack.shape[2]
    for i, ref in enumerate((again, abias, mgain, mbias, downb)):
        ref[...] = vectors[i]
    for j in range(upb.shape[0] // width):
        upb[width * j : width * (j + 1)] = vectors[5 + j]


def unpack(pieces, table, shapes):
    return pl.pallas_call(
        functools.partial(unpack_kernel, table),
        out_shape=tuple(jax.ShapeDtypeStruct(s, F32) for s in shapes),
        in_specs=[ANY] * 8,
        out_specs=(VMEM,) * len(shapes),
        scratch_shapes=[
            pltpu.VMEM((CORES * PIECES,) + pieces[0].shape, BF16),
            pltpu.SemaphoreType.DMA((8,)),
        ],
        compiler_params=pltpu.CompilerParams(vmem_limit_bytes=32 * 2**20),
        name="unpack",
    )(*pieces)


def sum_chips(held, came):
    levels = lax.axis_size("dp").bit_length() - 1
    first, second = (0, 1), (1, 0)
    keep, send = add_split(0, held, came)
    keep, send = add_split(1, keep, swap_chips(send, first))
    total = keep + swap_chips(send, second)
    for bits in zip(range(2, levels), reversed(range(2, levels))):
        total = total + swap_chips(total, bits)
    by_second = swap_chips(total, second)
    by_first = swap_chips(total, first)
    by_both = swap_chips(by_second, first)
    return total, by_second, by_first, by_both


def per_device(*args):
    weights = args[5:21]
    emb, qry, width = weights[0].shape
    table, total = layout(width, weights[12].shape[1], emb, qry, weights[4].shape[1])
    keep, send, blk, blk_s, img, img_s, prp, prp_s = compute(args, table, total)
    came = swap_cores(send)
    others = tuple(swap_cores(v) for v in (blk_s, img_s, prp_s))
    pieces = sum_chips(keep, came)
    pieces += tuple(swap_cores(v) for v in pieces)
    blk, img, prp = join((blk, img, prp), others)
    grads = unpack(pieces, table, [w.shape for w in weights])
    return (blk, img, prp) + tuple(grads)


def solution(mesh):
    sample = [P("dp")] * 5
    return jax.shard_map(
        per_device,
        mesh=mesh,
        in_specs=tuple(sample + [P()] * 16 + [P("dp")]),
        out_specs=(P("dp", "section"),) * 3 + (P(),) * 16,
        check_vma=False,
    )
```

time: 578 us -> 92.1 us (0.16); the launches traced: 567 us -> 91.6 us
  local copies, waits for them, and re-layouts: 195 us -> 8.01 us
  matrix products: 131 us -> 0 us
  waiting for transfers between devices: 93.4 us -> 18.5 us
  other arithmetic: 61.1 us -> 1 us
  Pallas kernels: 0 us -> 45.2 us
  blocking collectives: 43.4 us -> 0 us
  loops' own time: 16.2 us -> 0 us
  between operations: 15.1 us -> 0.76 us
  starting transfers between devices: 12.3 us -> 18.2 us
    dot_general x88 -> x0, matrix products: 131 us -> none  [the longest x4 19.1 us: stem_backward(): jnp.einsum('stqj,stqd->stjd', stem_prob.astype(jnp.bfloat16), grad_att, p...]
    psum x1 -> x0, waiting for transfers between devices: 93.4 us -> none  [per_device(): lax.psum((grads[0], grads[1], grads[2], grads[3], grads[4], grads[5], gra...]
    mul x52 -> x0, local copies, waits for them, and re-layouts: 55.2 us -> none  [the longest x48 52.4 us: spread_heads(): spread = rows[..., None, :, :] * table[:, None, :]]
    pallas_call x0 -> x5, Pallas kernels: none -> 45.2 us  [the longest x1 25.1 us: compute(): pl.pallas_call(functools.partial(compute_kernel, dims), out_shape=(shape(...]
    reshape x12 -> x0, local copies, waits for them, and re-layouts: 44.3 us -> none  [the longest x8 41.5 us: fold_heads(): rows.reshape(rows.shape[:-2] + (HEADS, rows.shape[-2] // HEADS, rows.shap...]
    psum x1 -> x0, blocking collectives: 43.4 us -> none  [per_device(): lax.psum((grads[0], grads[1], grads[2], grads[3], grads[4], grads[5], gra...]
    gather x32 -> x0, local copies, waits for them, and re-layouts: 22.7 us -> none  [the longest x4 5.06 us: stem_backward(): kv_rows = jnp.take(kv_weight, embod_mb, axis=0)]
    reduce_sum x8 -> x0, other arithmetic: 21 us -> none  [the longest x4 19.2 us: fold_heads(): return jnp.sum(grouped * table.astype(jnp.float32)[:, None, :], axis=-3)]
  transfers between devices with their start and end apart: 12 -> 15, of which waited for: 1 -> 8; matrix products, arithmetic and copies ran while one was open for 49% -> 2% of each run, Pallas kernels for 0% -> 15%
where the time goes in v1:
time: 92.1 us; the launch traced here: 91.6 us
  Pallas kernels  45.2 us (49%)
  waiting for transfers between devices  18.5 us (20%)
  starting transfers between devices  18.2 us (20%)
  local copies, waits for them, and re-layouts  8.01 us (9%)
  other arithmetic  1 us (1%)
    pallas_call x1, Pallas kernels, compute(): pl.pallas_call(functools.partial(compute_kernel, dims), out_shape=(shape(...  25.1 us
    ppermute x7, starting transfers between devices, swap_chips(): return lax.ppermute(value, ('section', 'dp'), pairs)  16.3 us
    ppermute x7, waiting for transfers between devices, swap_chips(): return lax.ppermute(value, ('section', 'dp'), pairs)  15.9 us
    pallas_call x1, Pallas kernels, join(): pl.pallas_call(join_kernel, out_shape=tuple((jax.ShapeDtypeStruct(v.shape...  13.5 us
    unnamed x19, local copies, waits for them, and re-layouts  8.01 us
    pallas_call x2, Pallas kernels, add_split(): pl.pallas_call(functools.partial(add_split_kernel, which), out_shape=(sha...  3.74 us
    pallas_call x1, Pallas kernels, unpack(): pl.pallas_call(functools.partial(unpack_kernel, table), out_shape=tuple((...  2.8 us
    ppermute x8, waiting for transfers between devices, swap_cores(): return lax.ppermute(value, 'section', [(0, 1), (1, 0)])  2.53 us
  transfers between devices with their start and end apart: 15, of which 8 were waited for; matrix products, arithmetic and copies ran while one was open for 2% of the time, Pallas kernels for 15%

profile of v1, /device:TPU:0, one launch (start us, length us, event | category | flops | bytes accessed | tf_op | source)
XLA Modules:
  0.0 91.6 jit_solution(16762829782592432249)
XLA Ops:
  0.7 1.4 %copy.44.views_ref = s32[16,3]{1,0:T(8,128)} copy(s32[16,3]{0,1:T(4,128)} %param.24) | data formatting | bytes 384 | tf_op args[2]
  2.0 2.5 %copy.45.images = bf16[16,2,147,128]{3,2,1,0:T(8,128)(2,1)} copy(bf16[16,2,147,128]{3,1,2,0:T(2,128)(2,1)} %param.22) | data formatting | bytes 2408448 | tf_op args[0]
  4.5 25.1 %stem_trunk.1 = (bf16[4,448,128]{2,1,0:T(8,128)(2,1)}, bf16[4,448,128]{2,1,0:T(8,128)(2,1)}, bf16[16,32,128]{2,1,0:T(8,128)(2,1)}, bf16[8,32,128]{2,1,0:T(8,128)...) custom-call(s32[16]{0:T(128)} %emb_ref.1, ...), custom_call_target="tpu_custom_call" | custom-call | tf_op jit(solution)/shard_map/stem_trunk/pallas_call | solution.py:477
  30.1 1.7 %collective-permute-done.3 = bf16[4,448,128]{2,1,0:T(8,128)(2,1)S(1)} collective-permute-done((bf16[4,448,128]{2,1,0:T(8,128)(2,1)}, bf16[4,448,128]{2,1,0:T(8,128)(2,1)S(1)}, u32[]{:S(2)}, u32[]{:S(2)}) %collective-permute-start.3) | collective-permute-done | bytes 458784 | tf_op jit(solution)/shard_map/ppermute | solution.py:522
  32.6 2.0 %add_split_0.1 = (bf16[896,128]{1,0:T(8,128)(2,1)}, bf16[896,128]{1,0:T(8,128)(2,1)}) custom-call(bf16[2,896,128]{2,1,0:T(8,128)(2,1)} %bitcast.4, bf16[2,896,128]{2,1,0:T(8,128)(2,1)} %bitcast.5), custom_call_target="tpu_custom_call" | custom-call | tf_op jit(solution)/shard_map/add_split_0/pallas_call | solution.py:512
  34.6 2.9 %collective-permute-start.4 = (bf16[896,128]{1,0:T(8,128)(2,1)}, bf16[896,128]{1,0:T(8,128)(2,1)S(1)}, u32[]{:S(2)}, u32[]{:S(2)}) collective-permute-start(bf16[896,128]{1,0:T(8,128)(2,1)} %get-tuple-element.62), channel_id=1, source_target_pairs={{0,1},{1,0},{2,3},{3,2},{4,5},{5,4},{6,7},{7,6},{8,9},{9,8},{10,11... | collective-permute-start | bytes 688136 | tf_op jit(solution)/shard_map/ppermute | solution.py:530
  37.4 4.2 %collective-permute-done.4 = bf16[896,128]{1,0:T(8,128)(2,1)S(1)} collective-permute-done((bf16[896,128]{1,0:T(8,128)(2,1)}, bf16[896,128]{1,0:T(8,128)(2,1)S(1)}, u32[]{:S(2)}, u32[]{:S(2)}) %collective-permute-start.4) | collective-permute-done | bytes 229408 | tf_op jit(solution)/shard_map/ppermute | solution.py:530
  42.3 1.8 %add_split_1.1 = (bf16[448,128]{1,0:T(8,128)(2,1)}, bf16[448,128]{1,0:T(8,128)(2,1)}) custom-call(bf16[2,448,128]{2,1,0:T(8,128)(2,1)} %bitcast.6, bf16[2,448,128]{2,1,0:T(8,128)(2,1)} %bitcast.7), custom_call_target="tpu_custom_call" | custom-call | tf_op jit(solution)/shard_map/add_split_1/pallas_call | solution.py:512
  44.1 2.1 %collective-permute-start.5 = (bf16[448,128]{1,0:T(8,128)(2,1)}, bf16[448,128]{1,0:T(8,128)(2,1)S(1)}, u32[]{:S(2)}, u32[]{:S(2)}) collective-permute-start(bf16[448,128]{1,0:T(8,128)(2,1)} %get-tuple-element.64), channel_id=1, source_target_pairs={{0,2},{1,3},{2,0},{3,1},{4,6},{5,7},{6,4},{7,5},{8,10},{9,11},{10,... | collective-permute-start | bytes 344072 | tf_op jit(solution)/shard_map/ppermute | solution.py:530
  46.1 3.0 %collective-permute-done.5 = bf16[448,128]{1,0:T(8,128)(2,1)S(1)} collective-permute-done((bf16[448,128]{1,0:T(8,128)(2,1)}, bf16[448,128]{1,0:T(8,128)(2,1)S(1)}, u32[]{:S(2)}, u32[]{:S(2)}) %collective-permute-start.5) | collective-permute-done | bytes 114720 | tf_op jit(solution)/shard_map/ppermute | solution.py:530
  49.1 0.9 %add.9 = bf16[448,128]{1,0:T(8,128)(2,1)S(1)} add(bf16[448,128]{1,0:T(8,128)(2,1)} %get-tuple-element.63, bf16[448,128]{1,0:T(8,128)(2,1)S(1)} %collective-permute-done.5) | non-fusion elementwise | flops 57344 | bytes 344064 | tf_op jit(solution)/shard_map/add | solution.py:642
  50.0 2.1 %collective-permute-start.6 = (bf16[448,128]{1,0:T(8,128)(2,1)S(1)}, bf16[448,128]{1,0:T(8,128)(2,1)S(1)}, u32[]{:S(2)}, u32[]{:S(2)}) collective-permute-start(bf16[448,128]{1,0:T(8,128)(2,1)S(1)} %add.9), channel_id=1, source_target_pairs={{0,4},{1,5},{2,6},{3,7},{4,0},{5,1},{6,2},{7,3},{8,12},{9,13},{10,... | collective-permute-start | bytes 344072 | tf_op jit(solution)/shard_map/ppermute | solution.py:530
  52.2 2.8 %collective-permute-done.6 = bf16[448,128]{1,0:T(8,128)(2,1)S(1)} collective-permute-done((bf16[448,128]{1,0:T(8,128)(2,1)S(1)}, bf16[448,128]{1,0:T(8,128)(2,1)S(1)}, u32[]{:S(2)}, u32[]{:S(2)}) %collective-permute-start.6) | collective-permute-done | bytes 114720 | tf_op jit(solution)/shard_map/ppermute | solution.py:530
  55.1 3.0 %collective-permute-start.7 = (bf16[448,128]{1,0:T(8,128)(2,1)S(1)}, bf16[448,128]{1,0:T(8,128)(2,1)S(1)}, u32[]{:S(2)}, u32[]{:S(2)}) collective-permute-start(bf16[448,128]{1,0:T(8,128)(2,1)S(1)} %add.10), channel_id=1, source_target_pairs={{0,8},{1,9},{2,10},{3,11},{4,12},{5,13},{6,14},{7,15},{8,0},{9,1},... | collective-permute-start | bytes 344072 | tf_op jit(solution)/shard_map/ppermute | solution.py:530
  58.1 2.8 %collective-permute-done.7 = bf16[448,128]{1,0:T(8,128)(2,1)S(1)} collective-permute-done((bf16[448,128]{1,0:T(8,128)(2,1)S(1)}, bf16[448,128]{1,0:T(8,128)(2,1)S(1)}, u32[]{:S(2)}, u32[]{:S(2)}) %collective-permute-start.7) | collective-permute-done | bytes 114720 | tf_op jit(solution)/shard_map/ppermute | solution.py:530
  60.9 3.3 %collective-permute-start.8 = (bf16[448,128]{1,0:T(8,128)(2,1)S(1)}, bf16[448,128]{1,0:T(8,128)(2,1)S(1)}, u32[]{:S(2)}, u32[]{:S(2)}) collective-permute-start(bf16[448,128]{1,0:T(8,128)(2,1)S(1)} %add.11.refs_0_), channel_id=1, source_target_pairs={{0,2},{1,3},{2,0},{3,1},{4,6},{5,7},{6,4},{7,5},{8,10},{9,11},{10,... | collective-permute-start | bytes 344072 | tf_op jit(solution)/shard_map/ppermute | solution.py:530
  64.2 1.5 %collective-permute-start.9 = (bf16[448,128]{1,0:T(8,128)(2,1)S(1)}, bf16[448,128]{1,0:T(8,128)(2,1)S(1)}, u32[]{:S(2)}, u32[]{:S(2)}) collective-permute-start(bf16[448,128]{1,0:T(8,128)(2,1)S(1)} %add.11.refs_0_), channel_id=1, source_target_pairs={{0,1},{1,0},{2,3},{3,2},{4,5},{5,4},{6,7},{7,6},{8,9},{9,8},{10,11... | collective-permute-start | bytes 344072 | tf_op jit(solution)/shard_map/ppermute | solution.py:530
  65.7 2.0 %collective-permute-done.8.refs_1_ = bf16[448,128]{1,0:T(8,128)(2,1)S(1)} collective-permute-done((bf16[448,128]{1,0:T(8,128)(2,1)S(1)}, bf16[448,128]{1,0:T(8,128)(2,1)S(1)}, u32[]{:S(2)}, u32[]{:S(2)}) %collective-permute-start.8) | collective-permute-done | bytes 114720 | tf_op jit(solution)/shard_map/ppermute | solution.py:530
  67.7 1.4 %collective-permute-start.10 = (bf16[448,128]{1,0:T(8,128)(2,1)S(1)}, bf16[448,128]{1,0:T(8,128)(2,1)S(1)}, u32[]{:S(2)}, u32[]{:S(2)}) collective-permute-start(bf16[448,128]{1,0:T(8,128)(2,1)S(1)} %collective-permute-done.8.refs_1_), channel_id=1, source_target_pairs={{0,1},{1,0},{2,3},{3,2},{4,5},{5,4},{6,7},{7,6},{8,9},{9,8},{10,11... | collective-permute-start | bytes 344072 | tf_op jit(solution)/shard_map/ppermute | solution.py:530
  69.7 0.9 collective-permute-done.2.prp_r
  71.4 1.1 %collective-permute-done.10.refs_3_ = bf16[448,128]{1,0:T(8,128)(2,1)S(1)} collective-permute-done((bf16[448,128]{1,0:T(8,128)(2,1)S(1)}, bf16[448,128]{1,0:T(8,128)(2,1)S(1)}, u32[]{:S(2)}, u32[]{:S(2)}) %collective-permute-start.10) | collective-permute-done | bytes 114720 | tf_op jit(solution)/shard_map/ppermute | solution.py:530
  73.2 13.5 %join_outputs.1 = (bf16[16,32,128]{2,1,0:T(8,128)(2,1)}, bf16[16,1,147,128]{3,2,1,0:T(8,128)(2,1)}, bf16[16,1,16,64]{3,2,1,0:T(8,128)(2,1)}) custom-call(bf16[16,32,128]{2,1,0:T(8,128)(2,1)} %get-tuple-element.50.blk_in, bf16[16,1,147,128]{3,2,1,0:T(8,128)(2,1)} %get-tuple-element.51.img_in, ...), custom_call_target="tpu_custom_call", output_to_operand_aliasing={{0}: (0, {}), {1}: (1, {}), {2}: (2, {})} | custom-call | tf_op jit(solution)/shard_map/join_outputs/pallas_call | solution.py:548
  86.8 2.0 %copy.46 = bf16[16,1,147,128]{3,0,2,1:T(8,128)(2,1)} copy(bf16[16,1,147,128]{3,2,1,0:T(8,128)(2,1)} %get-tuple-element.82) | data formatting | bytes 1204224
  88.8 2.8 %unpack.1 = (f32[4,16,128]{2,1,0:T(8,128)}, f32[4,128,128]{2,1,0:T(8,128)}, f32[4,128,128]{2,1,0:T(8,128)}, f32[128,128]{1,0:T(8,128)}, f32[4,64,128]{2,1,0:T(8,...) custom-call(bf16[448,128]{1,0:T(8,128)(2,1)S(1)} %add.11.refs_0_, ...), custom_call_target="tpu_custom_call" | custom-call | tf_op jit(solution)/shard_map/unpack/pallas_call | solution.py:623
  (33 shorter events, 4.2 us)
Async XLA Ops:
  29.6 34.6 %copy-start.5 = (bf16[8,147,128]{2,1,0:T(8,128)(2,1)S(1)}, bf16[8,147,128]{2,1,0:T(8,128)(2,1)}, u32[]{:S(2)}) copy-start(bf16[8,147,128]{2,1,0:T(8,128)(2,1)} %get-tuple-element.54) | copy-start | bytes 903172
  29.6 39.5 %copy-start.6 = (bf16[8,32,128]{2,1,0:T(8,128)(2,1)S(1)}, bf16[8,32,128]{2,1,0:T(8,128)(2,1)}, u32[]{:S(2)}) copy-start(bf16[8,32,128]{2,1,0:T(8,128)(2,1)} %get-tuple-element.53) | copy-start | bytes 196612
  29.6 39.5 %copy-start.7 = (bf16[8,16,64]{2,1,0:T(8,128)(2,1)S(1)}, bf16[8,16,64]{2,1,0:T(8,128)(2,1)}, u32[]{:S(2)}) copy-start(bf16[8,16,64]{2,1,0:T(8,128)(2,1)} %get-tuple-element.55) | copy-start | bytes 49156
  29.6 2.2 %collective-permute-start.3 = (bf16[4,448,128]{2,1,0:T(8,128)(2,1)}, bf16[4,448,128]{2,1,0:T(8,128)(2,1)S(1)}, u32[]{:S(2)}, u32[]{:S(2)}) collective-permute-start(bf16[4,448,128]{2,1,0:T(8,128)(2,1)} %get-tuple-element.60), channel_id=1, source_target_pairs={{0,16},{16,0},{1,17},{17,1},{2,18},{18,2},{3,19},{19,3},{4,20},{20... | collective-permute-start | bytes 1376264 | tf_op jit(solution)/shard_map/ppermute | solution.py:522
  31.8 0.8 copy-start
  34.6 7.1 %collective-permute-start.4 = (bf16[896,128]{1,0:T(8,128)(2,1)}, bf16[896,128]{1,0:T(8,128)(2,1)S(1)}, u32[]{:S(2)}, u32[]{:S(2)}) collective-permute-start(bf16[896,128]{1,0:T(8,128)(2,1)} %get-tuple-element.62), channel_id=1, source_target_pairs={{0,1},{1,0},{2,3},{3,2},{4,5},{5,4},{6,7},{7,6},{8,9},{9,8},{10,11... | collective-permute-start | bytes 688136 | tf_op jit(solution)/shard_map/ppermute | solution.py:530
  41.6 0.7 copy-start.2
  44.1 5.0 %collective-permute-start.5 = (bf16[448,128]{1,0:T(8,128)(2,1)}, bf16[448,128]{1,0:T(8,128)(2,1)S(1)}, u32[]{:S(2)}, u32[]{:S(2)}) collective-permute-start(bf16[448,128]{1,0:T(8,128)(2,1)} %get-tuple-element.64), channel_id=1, source_target_pairs={{0,2},{1,3},{2,0},{3,1},{4,6},{5,7},{6,4},{7,5},{8,10},{9,11},{10,... | collective-permute-start | bytes 344072 | tf_op jit(solution)/shard_map/ppermute | solution.py:530
  50.0 5.0 %collective-permute-start.6 = (bf16[448,128]{1,0:T(8,128)(2,1)S(1)}, bf16[448,128]{1,0:T(8,128)(2,1)S(1)}, u32[]{:S(2)}, u32[]{:S(2)}) collective-permute-start(bf16[448,128]{1,0:T(8,128)(2,1)S(1)} %add.9), channel_id=1, source_target_pairs={{0,4},{1,5},{2,6},{3,7},{4,0},{5,1},{6,2},{7,3},{8,12},{9,13},{10,... | collective-permute-start | bytes 344072 | tf_op jit(solution)/shard_map/ppermute | solution.py:530
  55.1 5.8 %collective-permute-start.7 = (bf16[448,128]{1,0:T(8,128)(2,1)S(1)}, bf16[448,128]{1,0:T(8,128)(2,1)S(1)}, u32[]{:S(2)}, u32[]{:S(2)}) collective-permute-start(bf16[448,128]{1,0:T(8,128)(2,1)S(1)} %add.10), channel_id=1, source_target_pairs={{0,8},{1,9},{2,10},{3,11},{4,12},{5,13},{6,14},{7,15},{8,0},{9,1},... | collective-permute-start | bytes 344072 | tf_op jit(solution)/shard_map/ppermute | solution.py:530
  60.9 6.8 %collective-permute-start.8 = (bf16[448,128]{1,0:T(8,128)(2,1)S(1)}, bf16[448,128]{1,0:T(8,128)(2,1)S(1)}, u32[]{:S(2)}, u32[]{:S(2)}) collective-permute-start(bf16[448,128]{1,0:T(8,128)(2,1)S(1)} %add.11.refs_0_), channel_id=1, source_target_pairs={{0,2},{1,3},{2,0},{3,1},{4,6},{5,7},{6,4},{7,5},{8,10},{9,11},{10,... | collective-permute-start | bytes 344072 | tf_op jit(solution)/shard_map/ppermute | solution.py:530
  64.2 8.3 %collective-permute-start.1 = (bf16[8,147,128]{2,1,0:T(8,128)(2,1)S(1)}, bf16[8,147,128]{2,1,0:T(8,128)(2,1)S(1)}, u32[]{:S(2)}, u32[]{:S(2)}) collective-permute-start(bf16[8,147,128]{2,1,0:T(8,128)(2,1)S(1)} %copy-done.5), channel_id=1, source_target_pairs={{0,16},{16,0},{1,17},{17,1},{2,18},{18,2},{3,19},{19,3},{4,20},{20... | collective-permute-start | bytes 903176 | tf_op jit(solution)/shard_map/ppermute | solution.py:522
  64.2 6.9 %collective-permute-start.9 = (bf16[448,128]{1,0:T(8,128)(2,1)S(1)}, bf16[448,128]{1,0:T(8,128)(2,1)S(1)}, u32[]{:S(2)}, u32[]{:S(2)}) collective-permute-start(bf16[448,128]{1,0:T(8,128)(2,1)S(1)} %add.11.refs_0_), channel_id=1, source_target_pairs={{0,1},{1,0},{2,3},{3,2},{4,5},{5,4},{6,7},{7,6},{8,9},{9,8},{10,11... | collective-permute-start | bytes 344072 | tf_op jit(solution)/shard_map/ppermute | solution.py:530
  67.7 4.8 %collective-permute-start.10 = (bf16[448,128]{1,0:T(8,128)(2,1)S(1)}, bf16[448,128]{1,0:T(8,128)(2,1)S(1)}, u32[]{:S(2)}, u32[]{:S(2)}) collective-permute-start(bf16[448,128]{1,0:T(8,128)(2,1)S(1)} %collective-permute-done.8.refs_1_), channel_id=1, source_target_pairs={{0,1},{1,0},{2,3},{3,2},{4,5},{5,4},{6,7},{7,6},{8,9},{9,8},{10,11... | collective-permute-start | bytes 344072 | tf_op jit(solution)/shard_map/ppermute | solution.py:530
  69.1 1.7 %collective-permute-start = (bf16[8,32,128]{2,1,0:T(8,128)(2,1)S(1)}, bf16[8,32,128]{2,1,0:T(8,128)(2,1)S(1)}, u32[]{:S(2)}, u32[]{:S(2)}) collective-permute-start(bf16[8,32,128]{2,1,0:T(8,128)(2,1)S(1)} %copy-done.6), channel_id=1, source_target_pairs={{0,16},{16,0},{1,17},{17,1},{2,18},{18,2},{3,19},{19,3},{4,20},{20... | collective-permute-start | bytes 196616 | tf_op jit(solution)/shard_map/ppermute | solution.py:522
  69.2 1.4 %collective-permute-start.2 = (bf16[8,16,64]{2,1,0:T(8,128)(2,1)S(1)}, bf16[8,16,64]{2,1,0:T(8,128)(2,1)S(1)}, u32[]{:S(2)}, u32[]{:S(2)}) collective-permute-start(bf16[8,16,64]{2,1,0:T(8,128)(2,1)S(1)} %copy-done.7), channel_id=1, source_target_pairs={{0,16},{16,0},{1,17},{17,1},{2,18},{18,2},{3,19},{19,3},{4,20},{20... | collective-permute-start | bytes 49160 | tf_op jit(solution)/shard_map/ppermute | solution.py:522
  70.5 2.0 %copy-start.4 = (bf16[8,16,64]{2,1,0:T(8,128)(2,1)}, bf16[8,16,64]{2,1,0:T(8,128)(2,1)S(1)}, u32[]{:S(2)}) copy-start(bf16[8,16,64]{2,1,0:T(8,128)(2,1)S(1)} %collective-permute-done.2.prp_r) | copy-start | bytes 49156
  70.5 18.2 %collective-permute-start.11 = (bf16[448,128]{1,0:T(8,128)(2,1)S(1)}, bf16[448,128]{1,0:T(8,128)(2,1)S(1)}, u32[]{:S(2)}, u32[]{:S(2)}) collective-permute-start(bf16[448,128]{1,0:T(8,128)(2,1)S(1)} %add.11.refs_0_), channel_id=1, source_target_pairs={{0,16},{16,0},{1,17},{17,1},{2,18},{18,2},{3,19},{19,3},{4,20},{20... | collective-permute-start | bytes 344072 | tf_op jit(solution)/shard_map/ppermute | solution.py:522
  70.9 1.6 %copy-start.3 = (bf16[8,32,128]{2,1,0:T(8,128)(2,1)}, bf16[8,32,128]{2,1,0:T(8,128)(2,1)S(1)}, u32[]{:S(2)}) copy-start(bf16[8,32,128]{2,1,0:T(8,128)(2,1)S(1)} %collective-permute-done.blk_r) | copy-start | bytes 196612
  70.9 17.9 %collective-permute-start.12 = (bf16[448,128]{1,0:T(8,128)(2,1)S(1)}, bf16[448,128]{1,0:T(8,128)(2,1)S(1)}, u32[]{:S(2)}, u32[]{:S(2)}) collective-permute-start(bf16[448,128]{1,0:T(8,128)(2,1)S(1)} %collective-permute-done.8.refs_1_), channel_id=1, source_target_pairs={{0,16},{16,0},{1,17},{17,1},{2,18},{18,2},{3,19},{19,3},{4,20},{20... | collective-permute-start | bytes 344072 | tf_op jit(solution)/shard_map/ppermute | solution.py:522
  71.0 17.7 %collective-permute-start.13 = (bf16[448,128]{1,0:T(8,128)(2,1)S(1)}, bf16[448,128]{1,0:T(8,128)(2,1)S(1)}, u32[]{:S(2)}, u32[]{:S(2)}) collective-permute-start(bf16[448,128]{1,0:T(8,128)(2,1)S(1)} %collective-permute-done.9.refs_2_), channel_id=1, source_target_pairs={{0,16},{16,0},{1,17},{17,1},{2,18},{18,2},{3,19},{19,3},{4,20},{20... | collective-permute-start | bytes 344072 | tf_op jit(solution)/shard_map/ppermute | solution.py:522
  72.5 16.3 %collective-permute-start.14 = (bf16[448,128]{1,0:T(8,128)(2,1)S(1)}, bf16[448,128]{1,0:T(8,128)(2,1)S(1)}, u32[]{:S(2)}, u32[]{:S(2)}) collective-permute-start(bf16[448,128]{1,0:T(8,128)(2,1)S(1)} %collective-permute-done.10.refs_3_), channel_id=1, source_target_pairs={{0,16},{16,0},{1,17},{17,1},{2,18},{18,2},{3,19},{19,3},{4,20},{20... | collective-permute-start | bytes 344072 | tf_op jit(solution)/shard_map/ppermute | solution.py:522
  72.5 0.7 copy-start.1

commit v2 on v1

--- a/solution.py
+++ b/solution.py
@@ -89,6 +89,26 @@
     scores = scores + bias
     expo = jnp.exp(scores - jnp.max(scores, axis=0, keepdims=True))
     return expo / jnp.sum(expo, axis=0, keepdims=True)
+
+
+def per_step(row, reduce):
+    part = reduce(row.reshape(-1, 8, row.shape[1]), axis=0)
+    pair = jnp.maximum if reduce is jnp.max else jnp.add
+    part = pair(part, pltpu.roll(part, 4, 0))
+    return pair(part, pltpu.roll(part, 2, 0))
+
+
+def softmax_lines(scores, bias):
+    tiles = (scores + bias).reshape(-1, 8, scores.shape[1])
+    expo = jnp.exp(tiles - per_step(scores + bias, jnp.max))
+    return (expo * (1.0 / per_step(expo.reshape(scores.shape), jnp.sum))).reshape(scores.shape)
+
+
+def softmax_lines_grad(probs, grad):
+    terms = probs * grad
+    total = per_step(terms, jnp.sum)
+    tiles = (-1, 8, probs.shape[1])
+    return (terms.reshape(tiles) - probs.reshape(tiles) * total).reshape(probs.shape)
 
 
 def softmax_rows_grad(probs, grad):
@@ -141,6 +161,7 @@
     image_send,
     prop_out,
     prop_send,
+    xin_s,
     x_s,
     p_s,
     g_s,
@@ -149,7 +170,8 @@
     tok_s,
     xt_s,
     prob_s,
-    probb_s,
+    mix_s,
+    ab_s,
     ut_s,
     satt_s,
     act_s,
@@ -164,14 +186,12 @@
     rstd2_s,
     norm2_s,
     up_s,
-    dup_s,
     glow_s,
     gpre_s,
     gn2_s,
     gmid_s,
     gatt_s,
     gqkv_s,
-    gn1_s,
     gtok_s,
     gsatt_s,
     blk_s,
@@ -193,15 +213,23 @@
     piece = pack_s.shape[2]
     sec = lax.axis_index("section")
     base = sec * n
+    lines = steps * keys
+    tall = x_s.shape[1]
 
     def put(name, row, value):
         first = table[name][0] + row
         for at, lo, done, count in cuts(first, value.shape[0], piece):
             pack_s[at // PIECES, at % PIECES, lo : lo + count] = value[done : done + count].astype(BF16)
 
-    loads = [pltpu.make_async_copy(proprio.at[pl.ds(base, n)], p_s, in_sem.at[n])]
-    loads += [pltpu.make_async_copy(images.at[base + s], x_s.at[s], in_sem.at[s]) for s in range(n)]
-    loads += [pltpu.make_async_copy(out_grad.at[pl.ds(base, n)], g_s, in_sem.at[n + 1])]
+    loads = [
+        pltpu.make_async_copy(proprio.at[pl.ds(base, n)], p_s, in_sem.at[0]),
+        pltpu.make_async_copy(
+            images.at[pl.ds(pl.multiple_of(sec * n * lines, 16), n * lines)],
+            xin_s.at[pl.ds(0, n * lines)],
+            in_sem.at[1],
+        ),
+        pltpu.make_async_copy(out_grad.at[pl.ds(base, n)], g_s, in_sem.at[2]),
+    ]
     for copy in loads:
         copy.start()
 
@@ -228,24 +256,34 @@
         dact_s[s] = dact
         tok_s[s, :, qry:] = mm(act_low, mix_w[e]).astype(BF16).reshape(steps, ptok, width)
 
-    view_of = lax.broadcasted_iota(jnp.int32, (keys, width), 0) // (keys // views)
+    loads[1].wait()
+    xin_s[n * lines :] = jnp.zeros((xin_s.shape[0] - n * lines, width), BF16)
+    edge = lines // 16 * 16
+    inside = lax.broadcasted_iota(jnp.int32, (tall - edge, width), 0) < lines - edge
+    for s in range(n):
+        x_s[s] = xin_s[lines * s : lines * s + tall]
+        last = x_s[s, edge:].astype(F32)
+        x_s[s, edge:] = jnp.where(inside, last, 0.0).astype(BF16)
+
+    row = lax.broadcasted_iota(jnp.int32, (tall, width), 0)
+    first_step = row % steps == 0
     for s in range(n):
         e = emb_ref[base + s]
-        bias = jnp.zeros((keys, width), F32)
-        for v in range(views):
-            lost = jnp.where(views_ref[base + s, v] > 0, 0.0, -1e30).astype(F32)
-            bias = jnp.where(view_of == v, lost, bias)
-        loads[1 + s].wait()
+        bias = jnp.full((tall, width), -1e30, F32)
+        for v in reversed(range(views)):
+            lost = jnp.where(views_ref[v, base + s] > 0, 0.0, -1e30).astype(F32)
+            bias = jnp.where(row < lines // views * (v + 1), lost, bias)
+        prob = softmax_lines(mm(x_s[s], a_s[e]), bias)
+        prob_s[s] = prob
+        mix_s[s, :, :width] = jnp.where(first_step, prob, 0.0).astype(BF16)
+        mix_s[s, :, width : 2 * width] = jnp.where(first_step, 0.0, prob).astype(BF16)
+        turned = x_s[s].T
+        xt_s[s] = turned
+        ut = mm(turned, mix_s[s, :, : 2 * width]).astype(BF16)
+        ut_s[s] = ut
+        values = mm(ut.T, value_w[e])
         for t in range(steps):
-            x = x_s[s, t]
-            xt_s[s, t] = x.T
-            prob = softmax_rows(mm(x, a_s[e]), bias)
-            prob_s[s, t] = prob
-            prob_low = prob.astype(BF16)
-            probb_s[s, t] = prob_low
-            ut = mm(xt_s[s, t], prob_low).astype(BF16)
-            ut_s[s, t] = ut
-            satt_s[s, t] = fold(mm_at(ut, value_w[e]), smask).astype(BF16)
+            satt_s[s, t] = fold(values[width * t : width * (t + 1)], smask).astype(BF16)
     image_tok = mm(satt_s[...].reshape(n * steps * qry, width), stem_proj[...])
     tok_s[:, :, :qry] = image_tok.astype(BF16).reshape(n, steps, qry, width)
 
@@ -278,7 +316,7 @@
         tprob_s[s] = prob
         att_s[mine] = fold(mm_at(prob.astype(BF16), value), tmask).astype(BF16)
 
-    loads[n + 1].wait()
+    loads[2].wait()
     row_step = lax.broadcasted_iota(jnp.int32, (ctx, 1), 0) // half_tok
     mgain_sum = jnp.zeros((1, width), F32)
     mbias_sum = jnp.zeros((1, width), F32)
@@ -368,16 +406,20 @@
     gsatt_s[...] = mm_bt(grad_img, stem_proj[...]).astype(BF16).reshape(n, steps, qry, width)
     for s in range(n):
         e = emb_ref[base + s]
-        for t in range(steps):
-            grad_spread = spread(gsatt_s[s, t], smask_low)
-            back = mm_bt(value_w[e], grad_spread).astype(BF16)
-            prob = prob_s[s, t]
-            grad_prob = mm(x_s[s, t], back).astype(BF16).astype(F32)
-            grad_raw = softmax_rows_grad(prob, grad_prob).astype(BF16)
-            macc_s[e] += mm(xt_s[s, t], grad_raw)
-            vacc_s[e] += mm(ut_s[s, t], grad_spread)
-            image = mm_bt(grad_raw, a_s[e]) + mm_bt(probb_s[s, t], back)
-            img_s[s, t] = image.astype(BF16)
+        grad_spread = jnp.concatenate([spread(gsatt_s[s, t], smask_low) for t in range(steps)], axis=0)
+        back = mm_bt(value_w[e], grad_spread).astype(BF16)
+        ab_s[s, :, : 2 * width] = back
+        ab_s[s, :, 2 * width :] = a_s[e]
+        both = mm(x_s[s], back)
+        grad_prob = jnp.where(first_step, both[:, :width], both[:, width:])
+        grad_raw = softmax_lines_grad(prob_s[s], grad_prob.astype(BF16).astype(F32)).astype(BF16)
+        mix_s[s, :, 2 * width :] = grad_raw
+        macc_s[e] += mm(xt_s[s], grad_raw)
+        vacc_s[e] += mm(ut_s[s], grad_spread)
+
+    for s in range(n):
+        img_s[pl.ds(s, tall, stride=n)] = mm_bt(mix_s[s], ab_s[s])
+
     for e in range(emb):
         moment = (macc_s[e] * scale).astype(BF16)
         put("keyw", width * e, mm(moment, qs_s[e]))
@@ -390,15 +432,15 @@
         pack_s[at // PIECES, at % PIECES, lo : lo + count] = jnp.zeros((count, width), BF16)
 
     other = 1 - sec
-    mine = pl.ds(base, n)
+    image = img_s.reshape(tall // steps, steps, n, width)
     stores = (
         (pack_s.at[sec], keep),
         (pack_s.at[other], send),
-        (blk_s.at[:, sec], block_out.at[mine]),
+        (blk_s.at[:, sec], block_out),
         (blk_s.at[:, other], block_send),
-        (img_s.at[:, sec], image_out.at[mine, 0]),
-        (img_s.at[:, other], image_send),
-        (prp_s.at[:, sec], prop_out.at[mine, 0]),
+        (image.at[pl.ds(0, keys), sec], image_out),
+        (image.at[pl.ds(0, keys), other], image_send),
+        (prp_s.at[:, sec], prop_out),
         (prp_s.at[:, other], prop_send),
     )
     stores = [pltpu.make_async_copy(a, b, out_sem.at[i]) for i, (a, b) in enumerate(stores)]
@@ -406,6 +448,10 @@
         copy.start()
     for copy in stores:
         copy.wait()
+
+
+def rows_of(images):
+    return images.transpose(0, 2, 1, 3).reshape(-1, images.shape[-1])
 
 
 def compute(args, table, total):
@@ -420,6 +466,8 @@
     ctx = steps * half_tok
     rows = n * ctx
     piece = total // (CORES * PIECES)
+    lines = steps * keys
+    tall = (lines + 15) // 16 * 16
     dims = (n, steps, keys, width, qry, ptok, emb, ffw, table, view_mask.shape[1])
 
     def low(*shape):
@@ -429,16 +477,18 @@
         return pltpu.VMEM(shape, F32)
 
     scratch = [
-        low(n, steps, keys, width),
+        low((n * lines + 31) // 16 * 16, width),
+        low(n, tall, width),
         low(n, steps, ptok, feats),
         low(n, ctx, width),
         low(emb, HEADS * qry, width),
         low(emb, width, HEADS * qry),
         low(n, steps, half_tok, width),
-        low(n, steps, width, keys),
-        full(n, steps, keys, HEADS * qry),
-        low(n, steps, keys, HEADS * qry),
-        low(n, steps, width, HEADS * qry),
+        low(n, width, tall),
+        full(n, tall, HEADS * qry),
+        low(n, tall, (steps + 1) * width),
+        low(n, width, (steps + 1) * width),
+        low(n, width, steps * width),
         low(n, steps, qry, width),
         low(n, steps * ptok, width),
         full(n, steps * ptok, width),
@@ -452,25 +502,23 @@
         full(rows, width),
         low(rows, width),
         low(rows, ffw),
-        full(rows, ffw),
         low(rows, width),
         low(rows, ffw),
         full(rows, width),
         low(rows, width),
         low(rows, width),
         low(rows, 3 * width),
-        full(rows, width),
         low(n, steps, half_tok, width),
         low(n, steps, qry, width),
         low(n, steps, half_tok, width),
-        low(n, steps, keys, width),
+        full(tall * n, width),
         low(n, steps, ptok, feats),
         full(emb, width, HEADS * qry),
         full(emb, width, width),
         full(emb, width, width),
         full(emb, feats, width),
         low(CORES, PIECES, piece, width),
-        pltpu.SemaphoreType.DMA((n + 2,)),
+        pltpu.SemaphoreType.DMA((3,)),
         pltpu.SemaphoreType.DMA((8,)),
     ]
     shape = jax.ShapeDtypeStruct
@@ -479,11 +527,11 @@
         out_shape=(
             shape((PIECES, piece, width), BF16),
             shape((PIECES, piece, width), BF16),
-            shape((samples, half_tok, width), BF16),
             shape((n, half_tok, width), BF16),
-            shape((samples, 1, keys, width), BF16),
-            shape((n, keys, width), BF16),
-            shape((samples, 1, ptok, feats), BF16),
+            shape((n, half_tok, width), BF16),
+            shape((keys, n, width), F32),
+            shape((keys, n, width), F32),
+            shape((n, ptok, feats), BF16),
             shape((n, ptok, feats), BF16),
         ),
         in_specs=[SMEM] * 3 + [ANY] * 3 + [VMEM] * 16,
@@ -491,7 +539,7 @@
         scratch_shapes=scratch,
         compiler_params=pltpu.CompilerParams(vmem_limit_bytes=56 * 2**20),
         name="stem_trunk",
-    )(embodiment, ctx_steps, view_mask, images, proprio, out_grad, *weights)
+    )(embodiment, ctx_steps, view_mask.T, rows_of(images), proprio, out_grad, *weights)
 
 
 def own_bits():
@@ -500,22 +548,10 @@
     return jnp.where(sec == 0, low, high), jnp.where(sec == 0, high, low)
 
 
-def add_split_kernel(which, held, came, keep, send):
-    bit = own_bits()[which]
-    keep[...] = (held[bit].astype(F32) + came[bit].astype(F32)).astype(BF16)
-    send[...] = (held[1 - bit].astype(F32) + came[1 - bit].astype(F32)).astype(BF16)
-
-
-def add_split(which, held, came):
-    held, came = (v.reshape((2, -1) + v.shape[-1:]) for v in (held, came))
-    shape = jax.ShapeDtypeStruct(held.shape[1:], BF16)
-    return pl.pallas_call(
-        functools.partial(add_split_kernel, which),
-        out_shape=(shape, shape),
-        in_specs=[VMEM] * 2,
-        out_specs=(VMEM,) * 2,
-        name=f"add_split_{which}",
-    )(held, came)
+def add_split(bit, held, came):
+    total = (held.astype(F32) + came.astype(F32)).astype(BF16)
+    low, high = total.reshape((2, -1, total.shape[-1]))
+    return jnp.where(bit == 0, low, high), jnp.where(bit == 0, high, low)
 
 
 def swap_cores(value):
@@ -530,30 +566,9 @@
     return lax.ppermute(value, ("section", "dp"), pairs)
 
 
-def join_kernel(blk_in, img_in, prp_in, blk_r, img_r, prp_r, blk, img, prp, sem):
-    n = blk_r.shape[0]
-    other = pl.ds((1 - lax.axis_index("section")) * n, n)
-    copies = (
-        pltpu.make_async_copy(blk_r, blk.at[other], sem.at[0]),
-        pltpu.make_async_copy(img_r, img.at[other, 0], sem.at[1]),
-        pltpu.make_async_copy(prp_r, prp.at[other, 0], sem.at[2]),
-    )
-    for copy in copies:
-        copy.start()
-    for copy in copies:
-        copy.wait()
-
-
-def join(own, came):
-    return pl.pallas_call(
-        join_kernel,
-        out_shape=tuple(jax.ShapeDtypeStruct(v.shape, v.dtype) for v in own),
-        in_specs=[ANY] * 6,
-        out_specs=(ANY,) * 3,
-        input_output_aliases={0: 0, 1: 1, 2: 2},
-        scratch_shapes=[pltpu.SemaphoreType.DMA((3,))],
-        name="join_outputs",
-    )(*own, *came)
+def join(own, came, axis):
+    first = lax.axis_index("section") == 0
+    return jnp.where(first, jnp.concatenate([own, came], axis), jnp.concatenate([came, own], axis))
 
 
 def unpack_kernel(table, *refs):
@@ -637,8 +652,9 @@
 def sum_chips(held, came):
     levels = lax.axis_size("dp").bit_length() - 1
     first, second = (0, 1), (1, 0)
-    keep, send = add_split(0, held, came)
-    keep, send = add_split(1, keep, swap_chips(send, first))
+    one, two = own_bits()
+    keep, send = add_split(one, held, came)
+    keep, send = add_split(two, keep, swap_chips(send, first))
     total = keep + swap_chips(send, second)
     for bits in zip(range(2, levels), reversed(range(2, levels))):
         total = total + swap_chips(total, bits)
@@ -654,10 +670,12 @@
     table, total = layout(width, weights[12].shape[1], emb, qry, weights[4].shape[1])
     keep, send, blk, blk_s, img, img_s, prp, prp_s = compute(args, table, total)
     came = swap_cores(send)
-    others = tuple(swap_cores(v) for v in (blk_s, img_s, prp_s))
+    blk_r, img_r, prp_r = (swap_cores(v) for v in (blk_s, img_s, prp_s))
     pieces = sum_chips(keep, came)
     pieces += tuple(swap_cores(v) for v in pieces)
-    blk, img, prp = join((blk, img, prp), others)
+    blk = join(blk, blk_r, 0)
+    prp = join(prp, prp_r, 0)[:, None]
+    img = join(img, img_r, 1).astype(BF16).transpose(1, 0, 2)[:, None]
     grads = unpack(pieces, table, [w.shape for w in weights])
     return (blk, img, prp) + tuple(grads)
 

time: 92.1 us -> 63.1 us (0.69)
  Pallas kernels: 45.2 us -> 23.5 us
  local copies, waits for them, and re-layouts: 8.01 us -> 0.03 us
  other arithmetic: 1 us -> 3.68 us
  waiting for transfers between devices: 18.5 us -> 16.7 us
    pallas_call x3 -> x0, Pallas kernels: 17.3 us -> none  [the longest x1 13.5 us: join(): pl.pallas_call(join_kernel, out_shape=tuple((jax.ShapeDtypeStruct(v.shape...]
    unnamed x19 -> x12, local copies, waits for them, and re-layouts: 8.01 us -> 0.03 us
    pallas_call x1, Pallas kernels: 25.1 us -> 20.8 us  [compute(): pl.pallas_call(functools.partial(compute_kernel, dims), out_shape=(shape(...]
    ppermute x7, waiting for transfers between devices: 15.9 us -> 14.7 us  [swap_chips(): return lax.ppermute(value, ('section', 'dp'), pairs)]
    convert_element_type x0 -> x2, other arithmetic: none -> 1.22 us  [add_split(): total = (held.astype(F32) + came.astype(F32)).astype(BF16)]
    broadcast_in_dim x0 -> x1, other arithmetic: none -> 0.97 us  [per_device(): img = join(img, img_r, 1).astype(BF16).transpose(1, 0, 2)[:, None]]
  transfers between devices with their start and end apart: 15 -> 15, of which waited for: 8 -> 8; matrix products, arithmetic and copies ran while one was open for 2% -> 4% of each run, Pallas kernels for 15% -> 0%
where the time goes in v2:
time: 63.1 us; the launch traced here: 62.9 us
  Pallas kernels  23.5 us (37%)
  starting transfers between devices  18.2 us (29%)
  waiting for transfers between devices  16.7 us (26%)
  other arithmetic  3.68 us (6%)
  between operations  0.8 us (1%)
    pallas_call x1, Pallas kernels, compute(): pl.pallas_call(functools.partial(compute_kernel, dims), out_shape=(shape(...  20.8 us
    ppermute x7, starting transfers between devices, swap_chips(): return lax.ppermute(value, ('section', 'dp'), pairs)  16.6 us
    ppermute x7, waiting for transfers between devices, swap_chips(): return lax.ppermute(value, ('section', 'dp'), pairs)  14.7 us
    pallas_call x1, Pallas kernels, unpack(): pl.pallas_call(functools.partial(unpack_kernel, table), out_shape=tuple((...  2.75 us
    ppermute x8, waiting for transfers between devices, swap_cores(): return lax.ppermute(value, 'section', [(0, 1), (1, 0)])  2 us
    ppermute x8, starting transfers between devices, swap_cores(): return lax.ppermute(value, 'section', [(0, 1), (1, 0)])  1.6 us
  transfers between devices with their start and end apart: 15, of which 8 were waited for; matrix products, arithmetic and copies ran while one was open for 4% of the time, Pallas kernels for 0%

profile of v2, /device:TPU:0, one launch (start us, length us, event | category | flops | bytes accessed | tf_op | source)
XLA Modules:
  0.0 62.9 jit_solution(2193937742204898743)
XLA Ops:
  0.7 20.8 %stem_trunk.1 = (bf16[4,448,128]{2,1,0:T(8,128)(2,1)}, bf16[4,448,128]{2,1,0:T(8,128)(2,1)}, bf16[8,32,128]{2,1,0:T(8,128)(2,1)}, bf16[8,32,128]{2,1,0:T(8,128)(...) custom-call(s32[16]{0:T(128)} %emb_ref.1, ...), custom_call_target="tpu_custom_call" | custom-call | tf_op jit(solution)/shard_map/stem_trunk/pallas_call | solution.py:525
  21.5 0.5 collective-permute-start.3
  22.0 1.7 %collective-permute-done.3 = bf16[4,448,128]{2,1,0:T(8,128)(2,1)S(1)} collective-permute-done((bf16[4,448,128]{2,1,0:T(8,128)(2,1)}, bf16[4,448,128]{2,1,0:T(8,128)(2,1)S(1)}, u32[]{:S(2)}, u32[]{:S(2)}) %collective-permute-start.3) | collective-permute-done | bytes 458784 | tf_op jit(solution)/shard_map/ppermute | solution.py:558
  23.6 1.1 %add_convert_fusion = bf16[4,448,128]{2,1,0:T(8,128)(2,1)S(1)} fusion(bf16[4,448,128]{2,1,0:T(8,128)(2,1)S(1)} %collective-permute-done.3, bf16[4,448,128]{2,1,0:T(8,128)(2,1)} %get-tuple-element.49), kind=kLoop, calls=%fused_computation.2 | loop fusion | flops 917504 | bytes 1376256 | tf_op jit(solution)/shard_map/convert_element_type | solution.py:552
  24.8 2.9 %collective-permute-start.4 = (bf16[896,128]{1,0:T(8,128)(2,1)S(1)}, bf16[896,128]{1,0:T(8,128)(2,1)S(1)}, u32[]{:S(2)}, u32[]{:S(2)}) collective-permute-start(bf16[896,128]{1,0:T(8,128)(2,1)S(1)} %bitcast.17), channel_id=1, source_target_pairs={{0,1},{1,0},{2,3},{3,2},{4,5},{5,4},{6,7},{7,6},{8,9},{9,8},{10,11... | collective-permute-start | bytes 688136 | tf_op jit(solution)/shard_map/ppermute | solution.py:566
  27.8 4.0 %collective-permute-done.4 = bf16[896,128]{1,0:T(8,128)(2,1)S(1)} collective-permute-done((bf16[896,128]{1,0:T(8,128)(2,1)S(1)}, bf16[896,128]{1,0:T(8,128)(2,1)S(1)}, u32[]{:S(2)}, u32[]{:S(2)}) %collective-permute-start.4) | collective-permute-done | bytes 229408 | tf_op jit(solution)/shard_map/ppermute | solution.py:566
  31.9 2.1 %collective-permute-start.5 = (bf16[448,128]{1,0:T(8,128)(2,1)S(1)}, bf16[448,128]{1,0:T(8,128)(2,1)S(1)}, u32[]{:S(2)}, u32[]{:S(2)}) collective-permute-start(bf16[448,128]{1,0:T(8,128)(2,1)S(1)} %broadcast_select_fusion.2), channel_id=1, source_target_pairs={{0,2},{1,3},{2,0},{3,1},{4,6},{5,7},{6,4},{7,5},{8,10},{9,11},{10,... | collective-permute-start | bytes 344072 | tf_op jit(solution)/shard_map/ppermute | solution.py:566
  34.0 2.8 %collective-permute-done.5 = bf16[448,128]{1,0:T(8,128)(2,1)S(1)} collective-permute-done((bf16[448,128]{1,0:T(8,128)(2,1)S(1)}, bf16[448,128]{1,0:T(8,128)(2,1)S(1)}, u32[]{:S(2)}, u32[]{:S(2)}) %collective-permute-start.5) | collective-permute-done | bytes 114720 | tf_op jit(solution)/shard_map/ppermute | solution.py:566
  36.8 2.1 %collective-permute-start.6 = (bf16[448,128]{1,0:T(8,128)(2,1)S(1)}, bf16[448,128]{1,0:T(8,128)(2,1)S(1)}, u32[]{:S(2)}, u32[]{:S(2)}) collective-permute-start(bf16[448,128]{1,0:T(8,128)(2,1)S(1)} %select_add_fusion), channel_id=1, source_target_pairs={{0,4},{1,5},{2,6},{3,7},{4,0},{5,1},{6,2},{7,3},{8,12},{9,13},{10,... | collective-permute-start | bytes 344072 | tf_op jit(solution)/shard_map/ppermute | solution.py:566
  39.0 2.8 %collective-permute-done.6 = bf16[448,128]{1,0:T(8,128)(2,1)S(1)} collective-permute-done((bf16[448,128]{1,0:T(8,128)(2,1)S(1)}, bf16[448,128]{1,0:T(8,128)(2,1)S(1)}, u32[]{:S(2)}, u32[]{:S(2)}) %collective-permute-start.6) | collective-permute-done | bytes 114720 | tf_op jit(solution)/shard_map/ppermute | solution.py:566
  41.8 3.0 %collective-permute-start.7 = (bf16[448,128]{1,0:T(8,128)(2,1)S(1)}, bf16[448,128]{1,0:T(8,128)(2,1)S(1)}, u32[]{:S(2)}, u32[]{:S(2)}) collective-permute-start(bf16[448,128]{1,0:T(8,128)(2,1)S(1)} %add.28), channel_id=1, source_target_pairs={{0,8},{1,9},{2,10},{3,11},{4,12},{5,13},{6,14},{7,15},{8,0},{9,1},... | collective-permute-start | bytes 344072 | tf_op jit(solution)/shard_map/ppermute | solution.py:566
  45.0 0.5 collective-permute-start.2
  45.5 2.2 %collective-permute-done.7 = bf16[448,128]{1,0:T(8,128)(2,1)S(1)} collective-permute-done((bf16[448,128]{1,0:T(8,128)(2,1)S(1)}, bf16[448,128]{1,0:T(8,128)(2,1)S(1)}, u32[]{:S(2)}, u32[]{:S(2)}) %collective-permute-start.7) | collective-permute-done | bytes 114720 | tf_op jit(solution)/shard_map/ppermute | solution.py:566
  47.7 3.3 %collective-permute-start.8 = (bf16[448,128]{1,0:T(8,128)(2,1)S(1)}, bf16[448,128]{1,0:T(8,128)(2,1)S(1)}, u32[]{:S(2)}, u32[]{:S(2)}) collective-permute-start(bf16[448,128]{1,0:T(8,128)(2,1)S(1)} %add.29.refs_0_), channel_id=1, source_target_pairs={{0,2},{1,3},{2,0},{3,1},{4,6},{5,7},{6,4},{7,5},{8,10},{9,11},{10,... | collective-permute-start | bytes 344072 | tf_op jit(solution)/shard_map/ppermute | solution.py:566
  51.0 0.6 %fusion.3 = bf16[16,1,16,64]{3,2,1,0:T(8,128)(2,1)} fusion(bf16[8,1,16,64]{3,2,0,1:T(8,128)(2,1)S(1)} %bitcast.19, bf16[8,1,16,64]{3,2,0,1:T(8,128)(2,1)S(1)} %bitcast.18, pred[]{:T(512)S(6)} %eq.9), kind=kLoop, calls=%fused_computation.12 | loop fusion | flops 49152 | bytes 65537
  51.6 1.5 %collective-permute-start.9 = (bf16[448,128]{1,0:T(8,128)(2,1)S(1)}, bf16[448,128]{1,0:T(8,128)(2,1)S(1)}, u32[]{:S(2)}, u32[]{:S(2)}) collective-permute-start(bf16[448,128]{1,0:T(8,128)(2,1)S(1)} %add.29.refs_0_), channel_id=1, source_target_pairs={{0,1},{1,0},{2,3},{3,2},{4,5},{5,4},{6,7},{7,6},{8,9},{9,8},{10,11... | collective-permute-start | bytes 344072 | tf_op jit(solution)/shard_map/ppermute | solution.py:566
  53.1 1.0 %collective-permute-done.8.refs_1_ = bf16[448,128]{1,0:T(8,128)(2,1)S(1)} collective-permute-done((bf16[448,128]{1,0:T(8,128)(2,1)S(1)}, bf16[448,128]{1,0:T(8,128)(2,1)S(1)}, u32[]{:S(2)}, u32[]{:S(2)}) %collective-permute-start.8) | collective-permute-done | bytes 114720 | tf_op jit(solution)/shard_map/ppermute | solution.py:566
  54.1 1.6 %collective-permute-start.10 = (bf16[448,128]{1,0:T(8,128)(2,1)S(1)}, bf16[448,128]{1,0:T(8,128)(2,1)S(1)}, u32[]{:S(2)}, u32[]{:S(2)}) collective-permute-start(bf16[448,128]{1,0:T(8,128)(2,1)S(1)} %collective-permute-done.8.refs_1_), channel_id=1, source_target_pairs={{0,1},{1,0},{2,3},{3,2},{4,5},{5,4},{6,7},{7,6},{8,9},{9,8},{10,11... | collective-permute-start | bytes 344072 | tf_op jit(solution)/shard_map/ppermute | solution.py:566
  55.7 0.7 %maximum_select_fusion.1 = bf16[16,32,128]{2,1,0:T(8,128)(2,1)} fusion(bf16[8,32,128]{2,1,0:T(8,128)(2,1)S(1)} %collective-permute-done, bf16[8,32,128]{2,1,0:T(8,128)(2,1)S(1)} %copy-done.2, pred[]{:T(512)S(6)} %eq.9), kind=kLoop, calls=%fused_computation.8 | loop fusion | flops 196608 | bytes 262145 | tf_op jit(solution)/shard_map/jit(_where)/select_n | solution.py:571
  56.4 0.5 collective-permute-start.12
  56.9 2.0 %collective-permute-done.10.refs_3_ = bf16[448,128]{1,0:T(8,128)(2,1)S(1)} collective-permute-done((bf16[448,128]{1,0:T(8,128)(2,1)S(1)}, bf16[448,128]{1,0:T(8,128)(2,1)S(1)}, u32[]{:S(2)}, u32[]{:S(2)}) %collective-permute-start.10) | collective-permute-done | bytes 114720 | tf_op jit(solution)/shard_map/ppermute | solution.py:566
  58.9 1.0 %fusion.1 = bf16[16,1,147,128]{3,0,2,1:T(8,128)(2,1)} fusion(f32[147,8,128]{2,1,0:T(8,128)S(1)} %copy-done.1, bf16[147,8,128]{2,1,0:T(8,128)(2,1)S(1)} %collective-permute-done.1, pred[]{:T(512)S(6)} %eq.9), kind=kLoop, calls=%fused_computation.3 | loop fusion | flops 2709504 | bytes 1505281 | tf_op jit(solution)/shard_map/broadcast_in_dim | solution.py:678
  59.9 0.3 collective-permute-done.14.refs_7_
  60.2 2.7 %unpack.1 = (f32[4,16,128]{2,1,0:T(8,128)}, f32[4,128,128]{2,1,0:T(8,128)}, f32[4,128,128]{2,1,0:T(8,128)}, f32[128,128]{1,0:T(8,128)}, f32[4,64,128]{2,1,0:T(8,...) custom-call(bf16[448,128]{1,0:T(8,128)(2,1)S(1)} %add.29.refs_0_, ...), custom_call_target="tpu_custom_call" | custom-call | tf_op jit(solution)/shard_map/unpack/pallas_call | solution.py:638
  (31 shorter events, 0.4 us)
Async XLA Ops:
  21.5 2.2 %collective-permute-start.3 = (bf16[4,448,128]{2,1,0:T(8,128)(2,1)}, bf16[4,448,128]{2,1,0:T(8,128)(2,1)S(1)}, u32[]{:S(2)}, u32[]{:S(2)}) collective-permute-start(bf16[4,448,128]{2,1,0:T(8,128)(2,1)} %get-tuple-element.50), channel_id=1, source_target_pairs={{0,16},{16,0},{1,17},{17,1},{2,18},{18,2},{3,19},{19,3},{4,20},{20... | collective-permute-start | bytes 1376264 | tf_op jit(solution)/shard_map/ppermute | solution.py:558
  24.8 20.1 %copy-start = (f32[147,8,128]{2,1,0:T(8,128)S(1)}, f32[147,8,128]{2,1,0:T(8,128)}, u32[]{:S(2)}) copy-start(f32[147,8,128]{2,1,0:T(8,128)} %get-tuple-element.46) | copy-start | bytes 1806340
  24.8 6.9 %collective-permute-start.4 = (bf16[896,128]{1,0:T(8,128)(2,1)S(1)}, bf16[896,128]{1,0:T(8,128)(2,1)S(1)}, u32[]{:S(2)}, u32[]{:S(2)}) collective-permute-start(bf16[896,128]{1,0:T(8,128)(2,1)S(1)} %bitcast.17), channel_id=1, source_target_pairs={{0,1},{1,0},{2,3},{3,2},{4,5},{5,4},{6,7},{7,6},{8,9},{9,8},{10,11... | collective-permute-start | bytes 688136 | tf_op jit(solution)/shard_map/ppermute | solution.py:566
  31.8 13.2 %copy-start.5 = (bf16[8,16,64]{2,1,0:T(8,128)(2,1)S(1)}, bf16[8,16,64]{2,1,0:T(8,128)(2,1)}, u32[]{:S(2)}) copy-start(bf16[8,16,64]{2,1,0:T(8,128)(2,1)} %get-tuple-element.48) | copy-start | bytes 49156
  31.8 19.1 %copy-start.4 = (bf16[8,32,128]{2,1,0:T(8,128)(2,1)S(1)}, bf16[8,32,128]{2,1,0:T(8,128)(2,1)}, u32[]{:S(2)}) copy-start(bf16[8,32,128]{2,1,0:T(8,128)(2,1)} %get-tuple-element.44) | copy-start | bytes 196612
  31.9 19.1 %copy-start.3 = (bf16[8,16,64]{2,1,0:T(8,128)(2,1)S(1)}, bf16[8,16,64]{2,1,0:T(8,128)(2,1)}, u32[]{:S(2)}) copy-start(bf16[8,16,64]{2,1,0:T(8,128)(2,1)} %get-tuple-element.47) | copy-start | bytes 49156
  31.9 23.8 %copy-start.2 = (bf16[8,32,128]{2,1,0:T(8,128)(2,1)S(1)}, bf16[8,32,128]{2,1,0:T(8,128)(2,1)}, u32[]{:S(2)}) copy-start(bf16[8,32,128]{2,1,0:T(8,128)(2,1)} %get-tuple-element.43) | copy-start | bytes 196612
  31.9 27.0 %copy-start.1 = (f32[147,8,128]{2,1,0:T(8,128)S(1)}, f32[147,8,128]{2,1,0:T(8,128)}, u32[]{:S(2)}) copy-start(f32[147,8,128]{2,1,0:T(8,128)} %get-tuple-element.45) | copy-start | bytes 1806340
  31.9 4.9 %collective-permute-start.5 = (bf16[448,128]{1,0:T(8,128)(2,1)S(1)}, bf16[448,128]{1,0:T(8,128)(2,1)S(1)}, u32[]{:S(2)}, u32[]{:S(2)}) collective-permute-start(bf16[448,128]{1,0:T(8,128)(2,1)S(1)} %broadcast_select_fusion.2), channel_id=1, source_target_pairs={{0,2},{1,3},{2,0},{3,1},{4,6},{5,7},{6,4},{7,5},{8,10},{9,11},{10,... | collective-permute-start | bytes 344072 | tf_op jit(solution)/shard_map/ppermute | solution.py:566
  36.8 5.0 %collective-permute-start.6 = (bf16[448,128]{1,0:T(8,128)(2,1)S(1)}, bf16[448,128]{1,0:T(8,128)(2,1)S(1)}, u32[]{:S(2)}, u32[]{:S(2)}) collective-permute-start(bf16[448,128]{1,0:T(8,128)(2,1)S(1)} %select_add_fusion), channel_id=1, source_target_pairs={{0,4},{1,5},{2,6},{3,7},{4,0},{5,1},{6,2},{7,3},{8,12},{9,13},{10,... | collective-permute-start | bytes 344072 | tf_op jit(solution)/shard_map/ppermute | solution.py:566
  41.8 5.8 %collective-permute-start.7 = (bf16[448,128]{1,0:T(8,128)(2,1)S(1)}, bf16[448,128]{1,0:T(8,128)(2,1)S(1)}, u32[]{:S(2)}, u32[]{:S(2)}) collective-permute-start(bf16[448,128]{1,0:T(8,128)(2,1)S(1)} %add.28), channel_id=1, source_target_pairs={{0,8},{1,9},{2,10},{3,11},{4,12},{5,13},{6,14},{7,15},{8,0},{9,1},... | collective-permute-start | bytes 344072 | tf_op jit(solution)/shard_map/ppermute | solution.py:566
  44.9 14.0 %collective-permute-start.1 = (bf16[147,8,128]{2,1,0:T(8,128)(2,1)S(1)}, bf16[147,8,128]{2,1,0:T(8,128)(2,1)S(1)}, u32[]{:S(2)}, u32[]{:S(2)}) collective-permute-start(bf16[147,8,128]{2,1,0:T(8,128)(2,1)S(1)} %convert.5), channel_id=1, source_target_pairs={{0,16},{16,0},{1,17},{17,1},{2,18},{18,2},{3,19},{19,3},{4,20},{20... | collective-permute-start | bytes 903176 | tf_op jit(solution)/shard_map/ppermute | solution.py:558
  45.0 6.0 %collective-permute-start.2 = (bf16[8,16,64]{2,1,0:T(8,128)(2,1)S(1)}, bf16[8,16,64]{2,1,0:T(8,128)(2,1)S(1)}, u32[]{:S(2)}, u32[]{:S(2)}) collective-permute-start(bf16[8,16,64]{2,1,0:T(8,128)(2,1)S(1)} %copy-done.5), channel_id=1, source_target_pairs={{0,16},{16,0},{1,17},{17,1},{2,18},{18,2},{3,19},{19,3},{4,20},{20... | collective-permute-start | bytes 49160 | tf_op jit(solution)/shard_map/ppermute | solution.py:558
  47.7 6.4 %collective-permute-start.8 = (bf16[448,128]{1,0:T(8,128)(2,1)S(1)}, bf16[448,128]{1,0:T(8,128)(2,1)S(1)}, u32[]{:S(2)}, u32[]{:S(2)}) collective-permute-start(bf16[448,128]{1,0:T(8,128)(2,1)S(1)} %add.29.refs_0_), channel_id=1, source_target_pairs={{0,2},{1,3},{2,0},{3,1},{4,6},{5,7},{6,4},{7,5},{8,10},{9,11},{10,... | collective-permute-start | bytes 344072 | tf_op jit(solution)/shard_map/ppermute | solution.py:566
  50.9 4.8 %collective-permute-start = (bf16[8,32,128]{2,1,0:T(8,128)(2,1)S(1)}, bf16[8,32,128]{2,1,0:T(8,128)(2,1)S(1)}, u32[]{:S(2)}, u32[]{:S(2)}) collective-permute-start(bf16[8,32,128]{2,1,0:T(8,128)(2,1)S(1)} %copy-done.4), channel_id=1, source_target_pairs={{0,16},{16,0},{1,17},{17,1},{2,18},{18,2},{3,19},{19,3},{4,20},{20... | collective-permute-start | bytes 196616 | tf_op jit(solution)/shard_map/ppermute | solution.py:558
  51.6 5.3 %collective-permute-start.9 = (bf16[448,128]{1,0:T(8,128)(2,1)S(1)}, bf16[448,128]{1,0:T(8,128)(2,1)S(1)}, u32[]{:S(2)}, u32[]{:S(2)}) collective-permute-start(bf16[448,128]{1,0:T(8,128)(2,1)S(1)} %add.29.refs_0_), channel_id=1, source_target_pairs={{0,1},{1,0},{2,3},{3,2},{4,5},{5,4},{6,7},{7,6},{8,9},{9,8},{10,11... | collective-permute-start | bytes 344072 | tf_op jit(solution)/shard_map/ppermute | solution.py:566
  54.1 4.8 %collective-permute-start.10 = (bf16[448,128]{1,0:T(8,128)(2,1)S(1)}, bf16[448,128]{1,0:T(8,128)(2,1)S(1)}, u32[]{:S(2)}, u32[]{:S(2)}) collective-permute-start(bf16[448,128]{1,0:T(8,128)(2,1)S(1)} %collective-permute-done.8.refs_1_), channel_id=1, source_target_pairs={{0,1},{1,0},{2,3},{3,2},{4,5},{5,4},{6,7},{7,6},{8,9},{9,8},{10,11... | collective-permute-start | bytes 344072 | tf_op jit(solution)/shard_map/ppermute | solution.py:566
  56.4 3.5 %collective-permute-start.11 = (bf16[448,128]{1,0:T(8,128)(2,1)S(1)}, bf16[448,128]{1,0:T(8,128)(2,1)S(1)}, u32[]{:S(2)}, u32[]{:S(2)}) collective-permute-start(bf16[448,128]{1,0:T(8,128)(2,1)S(1)} %add.29.refs_0_), channel_id=1, source_target_pairs={{0,16},{16,0},{1,17},{17,1},{2,18},{18,2},{3,19},{19,3},{4,20},{20... | collective-permute-start | bytes 344072 | tf_op jit(solution)/shard_map/ppermute | solution.py:558
  56.4 3.5 %collective-permute-start.12 = (bf16[448,128]{1,0:T(8,128)(2,1)S(1)}, bf16[448,128]{1,0:T(8,128)(2,1)S(1)}, u32[]{:S(2)}, u32[]{:S(2)}) collective-permute-start(bf16[448,128]{1,0:T(8,128)(2,1)S(1)} %collective-permute-done.8.refs_1_), channel_id=1, source_target_pairs={{0,16},{16,0},{1,17},{17,1},{2,18},{18,2},{3,19},{19,3},{4,20},{20... | collective-permute-start | bytes 344072 | tf_op jit(solution)/shard_map/ppermute | solution.py:558
  56.9 3.0 %collective-permute-start.13 = (bf16[448,128]{1,0:T(8,128)(2,1)S(1)}, bf16[448,128]{1,0:T(8,128)(2,1)S(1)}, u32[]{:S(2)}, u32[]{:S(2)}) collective-permute-start(bf16[448,128]{1,0:T(8,128)(2,1)S(1)} %collective-permute-done.9.refs_2_), channel_id=1, source_target_pairs={{0,16},{16,0},{1,17},{17,1},{2,18},{18,2},{3,19},{19,3},{4,20},{20... | collective-permute-start | bytes 344072 | tf_op jit(solution)/shard_map/ppermute | solution.py:558
  58.9 1.3 %collective-permute-start.14 = (bf16[448,128]{1,0:T(8,128)(2,1)S(1)}, bf16[448,128]{1,0:T(8,128)(2,1)S(1)}, u32[]{:S(2)}, u32[]{:S(2)}) collective-permute-start(bf16[448,128]{1,0:T(8,128)(2,1)S(1)} %collective-permute-done.10.refs_3_), channel_id=1, source_target_pairs={{0,16},{16,0},{1,17},{17,1},{2,18},{18,2},{3,19},{19,3},{4,20},{20... | collective-permute-start | bytes 344072 | tf_op jit(solution)/shard_map/ppermute | solution.py:558

commit v3 on v2

--- a/solution.py
+++ b/solution.py
@@ -12,7 +12,8 @@
 F32 = jnp.float32
 BF16 = jnp.bfloat16
 CORES = 2
-PIECES = 4
+CHAINS = 2
+PIECES = 2 * CHAINS
 EPS = 1e-05
 INV_SQRT2 = 1.0 / math.sqrt(2.0)
 INV_SQRT2PI = 1.0 / math.sqrt(2.0 * math.pi)
@@ -51,7 +52,7 @@
     for name, rows in counts:
         table[name] = (first, rows)
         first += rows
-    step = CORES * PIECES * 16
+    step = CORES * PIECES * 32
     return table, (first + step - 1) // step * step
 
 
@@ -85,8 +86,14 @@
     return values * cdf, cdf + values * pdf
 
 
-def softmax_rows(scores, bias):
-    scores = scores + bias
+def staged(count, *stages):
+    for step in range(count + len(stages) - 1):
+        for lag, stage in enumerate(stages):
+            if 0 <= step - lag < count:
+                stage(step - lag)
+
+
+def softmax_rows(scores):
     expo = jnp.exp(scores - jnp.max(scores, axis=0, keepdims=True))
     return expo / jnp.sum(expo, axis=0, keepdims=True)
 
@@ -98,9 +105,8 @@
     return pair(part, pltpu.roll(part, 2, 0))
 
 
-def softmax_lines(scores, bias):
-    tiles = (scores + bias).reshape(-1, 8, scores.shape[1])
-    expo = jnp.exp(tiles - per_step(scores + bias, jnp.max))
+def softmax_lines(scores):
+    expo = jnp.exp(scores.reshape(-1, 8, scores.shape[1]) - per_step(scores, jnp.max))
     return (expo * (1.0 / per_step(expo.reshape(scores.shape), jnp.sum))).reshape(scores.shape)
 
 
@@ -137,30 +143,42 @@
     images,
     proprio,
     out_grad,
+    queries_h,
+    key_h,
+    value_h,
+    stem_h,
+    lift_h,
+    mix_h,
+    again,
+    abias,
+    qkv_h,
+    aproj_h,
+    mgain,
+    mbias,
+    up_h,
+    up_b,
+    down_h,
+    down_b,
+    keep0,
+    keep1,
+    send0,
+    send1,
+    block_out,
+    block_send,
+    image_out,
+    image_send,
+    prop_out,
+    prop_send,
     queries,
     key_w,
     value_w,
     stem_proj,
     lift_w,
     mix_w,
-    again,
-    abias,
     qkv_w,
     aproj,
-    mgain,
-    mbias,
     up_w,
-    up_b,
     down_w,
-    down_b,
-    keep,
-    send,
-    block_out,
-    block_send,
-    image_out,
-    image_send,
-    prop_out,
-    prop_send,
     xin_s,
     x_s,
     p_s,
@@ -170,6 +188,7 @@
     tok_s,
     xt_s,
     prob_s,
+    sgrad_s,
     mix_s,
     ab_s,
     ut_s,
@@ -181,6 +200,8 @@
     norm1_s,
     qkv_s,
     tprob_s,
+    tlow_s,
+    gprob_s,
     att_s,
     hat2_s,
     rstd2_s,
@@ -215,6 +236,7 @@
     base = sec * n
     lines = steps * keys
     tall = x_s.shape[1]
+    embs = [emb_ref[base + s] for s in range(n)]
 
     def put(name, row, value):
         first = table[name][0] + row
@@ -222,13 +244,24 @@
             pack_s[at // PIECES, at % PIECES, lo : lo + count] = value[done : done + count].astype(BF16)
 
     loads = [
-        pltpu.make_async_copy(proprio.at[pl.ds(base, n)], p_s, in_sem.at[0]),
-        pltpu.make_async_copy(
-            images.at[pl.ds(pl.multiple_of(sec * n * lines, 16), n * lines)],
-            xin_s.at[pl.ds(0, n * lines)],
-            in_sem.at[1],
-        ),
-        pltpu.make_async_copy(out_grad.at[pl.ds(base, n)], g_s, in_sem.at[2]),
+        pltpu.make_async_copy(a, b, in_sem.at[i])
+        for i, (a, b) in enumerate(
+            (
+                (queries_h, queries),
+                (key_h, key_w),
+                (images.at[pl.ds(pl.multiple_of(sec * n * lines, 16), n * lines)], xin_s.at[pl.ds(0, n * lines)]),
+                (proprio.at[pl.ds(base, n)], p_s),
+                (lift_h, lift_w),
+                (mix_h, mix_w),
+                (value_h, value_w),
+                (stem_h, stem_proj),
+                (qkv_h, qkv_w),
+                (aproj_h, aproj),
+                (up_h, up_w),
+                (down_h, down_w),
+                (out_grad.at[pl.ds(base, n)], g_s),
+            )
+        )
     ]
     for copy in loads:
         copy.start()
@@ -238,17 +271,34 @@
     tmask = head_mask(HEADS * ctx, ctx, width)
     tmask_low = tmask.astype(BF16)
     for e in range(emb):
-        qs = spread(queries[e], smask_low)
-        qs_s[e] = qs
-        a_s[e] = (mm_bt(key_w[e], qs) * scale).astype(BF16)
         macc_s[e] = jnp.zeros((width, width), F32)
         vacc_s[e] = jnp.zeros((width, width), F32)
         mixacc_s[e] = jnp.zeros((width, width), F32)
         liftacc_s[e] = jnp.zeros(liftacc_s.shape[1:], F32)
-
+    used = max(first + count for first, count in table.values())
+    for at, lo, _, count in cuts(used, CORES * PIECES * piece - used, piece):
+        pack_s[at // PIECES, at % PIECES, lo : lo + count] = jnp.zeros((count, width), BF16)
+    xin_s[n * lines :] = jnp.zeros((xin_s.shape[0] - n * lines, width), BF16)
     loads[0].wait()
+    loads[1].wait()
+    for e in range(emb):
+        qs = spread(queries[e], smask_low)
+        qs_s[e] = qs
+        a_s[e] = (mm_bt(key_w[e], qs) * scale).astype(BF16)
+
+    loads[2].wait()
+    edge = lines // 16 * 16
+    inside = lax.broadcasted_iota(jnp.int32, (tall - edge, width), 0) < lines - edge
     for s in range(n):
-        e = emb_ref[base + s]
+        x_s[s] = xin_s[lines * s : lines * s + tall]
+        last = x_s[s, edge:].astype(F32)
+        x_s[s, edge:] = jnp.where(inside, last, 0.0).astype(BF16)
+
+    loads[3].wait()
+    loads[4].wait()
+    loads[5].wait()
+    loads[6].wait()
+    for s, e in enumerate(embs):
         lifted = mm(p_s[s].reshape(steps * ptok, -1), lift_w[e])
         act, dact = gelu_parts(lifted)
         act_low = act.astype(BF16)
@@ -256,37 +306,50 @@
         dact_s[s] = dact
         tok_s[s, :, qry:] = mm(act_low, mix_w[e]).astype(BF16).reshape(steps, ptok, width)
 
-    loads[1].wait()
-    xin_s[n * lines :] = jnp.zeros((xin_s.shape[0] - n * lines, width), BF16)
-    edge = lines // 16 * 16
-    inside = lax.broadcasted_iota(jnp.int32, (tall - edge, width), 0) < lines - edge
-    for s in range(n):
-        x_s[s] = xin_s[lines * s : lines * s + tall]
-        last = x_s[s, edge:].astype(F32)
-        x_s[s, edge:] = jnp.where(inside, last, 0.0).astype(BF16)
-
-    row = lax.broadcasted_iota(jnp.int32, (tall, width), 0)
-    first_step = row % steps == 0
-    for s in range(n):
-        e = emb_ref[base + s]
-        bias = jnp.full((tall, width), -1e30, F32)
-        for v in reversed(range(views)):
-            lost = jnp.where(views_ref[v, base + s] > 0, 0.0, -1e30).astype(F32)
-            bias = jnp.where(row < lines // views * (v + 1), lost, bias)
-        prob = softmax_lines(mm(x_s[s], a_s[e]), bias)
+    first_step = lax.broadcasted_iota(jnp.int32, (tall, width), 0) % steps == 0
+
+    def view_bias(s):
+        lost = [jnp.where(views_ref[v, base + s] > 0, 0.0, -1e30).astype(F32) for v in range(views)]
+        lost.append(jnp.float32(-1e30))
+        ends = [lines // views * (v + 1) for v in range(views)]
+        tiles, at = [], 0
+        while at < tall:
+            view = sum(at >= end for end in ends)
+            stop = min([end // 8 * 8 for end in ends if end // 8 * 8 > at] + [tall])
+            if view < views and ends[view] < at + 8:
+                row = lax.broadcasted_iota(jnp.int32, (8, width), 0)
+                tiles.append(jnp.where(row < ends[view] - at, lost[view], lost[view + 1]))
+                at += 8
+            else:
+                tiles.append(jnp.full((stop - at, width), lost[view], F32))
+                at = stop
+        return jnp.concatenate(tiles, axis=0)
+
+    def stem_scores(s):
+        prob_s[s] = mm(x_s[s], a_s[embs[s]]) + view_bias(s)
+
+    def stem_softmax(s):
+        prob = softmax_lines(prob_s[s])
         prob_s[s] = prob
         mix_s[s, :, :width] = jnp.where(first_step, prob, 0.0).astype(BF16)
         mix_s[s, :, width : 2 * width] = jnp.where(first_step, 0.0, prob).astype(BF16)
+
+    def stem_moments(s):
         turned = x_s[s].T
         xt_s[s] = turned
-        ut = mm(turned, mix_s[s, :, : 2 * width]).astype(BF16)
-        ut_s[s] = ut
-        values = mm(ut.T, value_w[e])
+        ut_s[s] = mm(turned, mix_s[s, :, : 2 * width]).astype(BF16)
+
+    def stem_values(s):
+        values = mm(ut_s[s].T, value_w[embs[s]])
         for t in range(steps):
             satt_s[s, t] = fold(values[width * t : width * (t + 1)], smask).astype(BF16)
+
+    staged(n, stem_scores, stem_softmax, stem_moments, stem_values)
+    loads[7].wait()
     image_tok = mm(satt_s[...].reshape(n * steps * qry, width), stem_proj[...])
     tok_s[:, :, :qry] = image_tok.astype(BF16).reshape(n, steps, qry, width)
 
+    loads[8].wait()
     chunk = CORES * ctx
     spans = [pl.ds(i * chunk, chunk) for i in range(rows // chunk)]
     again_row = again[...].astype(F32).reshape(1, width)
@@ -308,15 +371,28 @@
         qkv_s[span] = mm(norm1, qkv_w[...]).astype(BF16)
 
     key_step = lax.broadcasted_iota(jnp.int32, (ctx, 1), 0) // half_tok
-    for s in range(n):
+    def trunk_rows(s):
         mine = pl.ds(s * ctx, ctx)
-        query, key, value = (qkv_s[mine, width * j : width * (j + 1)] for j in range(3))
+        return (qkv_s[mine, width * j : width * (j + 1)] for j in range(3))
+
+    def trunk_scores(s):
+        query, key, _ = trunk_rows(s)
         dead = jnp.where(key_step < steps_ref[base + s], 0.0, -1e30).astype(F32)
-        prob = softmax_rows(mm_bt(key, spread(query, tmask_low)) * scale, dead)
+        tprob_s[s] = mm_bt(key, spread(query, tmask_low)) * scale + dead
+
+    def trunk_softmax(s):
+        prob = softmax_rows(tprob_s[s])
         tprob_s[s] = prob
-        att_s[mine] = fold(mm_at(prob.astype(BF16), value), tmask).astype(BF16)
-
-    loads[2].wait()
+        tlow_s[s] = prob.astype(BF16)
+
+    def trunk_values(s):
+        _, _, value = trunk_rows(s)
+        att_s[pl.ds(s * ctx, ctx)] = fold(mm_at(tlow_s[s], value), tmask).astype(BF16)
+
+    staged(n, trunk_scores, trunk_softmax, trunk_values)
+
+    for load in loads[9:]:
+        load.wait()
     row_step = lax.broadcasted_iota(jnp.int32, (ctx, 1), 0) // half_tok
     mgain_sum = jnp.zeros((1, width), F32)
     mbias_sum = jnp.zeros((1, width), F32)
@@ -363,18 +439,24 @@
         cols = slice(width * j, width * (j + 1))
         put("up", width * j, mm_at(norm2_s[...], gpre_s[:, cols]))
 
-    for s in range(n):
+    def trunk_back_probs(s):
+        _, _, value = trunk_rows(s)
+        grad_spread = spread(gatt_s[pl.ds(s * ctx, ctx)], tmask_low)
+        gprob_s[s] = mm_bt(value, grad_spread)
+        gqkv_s[pl.ds(s * ctx, ctx), 2 * width :] = mm(tlow_s[s], grad_spread).astype(BF16)
+
+    def trunk_back_softmax(s):
+        grad_prob = gprob_s[s].astype(BF16).astype(F32)
+        tlow_s[s] = (softmax_rows_grad(tprob_s[s], grad_prob) * scale).astype(BF16)
+
+    def trunk_back_rows(s):
+        query, key, _ = trunk_rows(s)
         mine = pl.ds(s * ctx, ctx)
-        query, key, value = (qkv_s[mine, width * j : width * (j + 1)] for j in range(3))
-        query_spread = spread(query, tmask_low)
-        grad_spread = spread(gatt_s[mine], tmask_low)
-        prob = tprob_s[s]
-        grad_prob = mm_bt(value, grad_spread).astype(BF16).astype(F32)
-        grad_raw = (softmax_rows_grad(prob, grad_prob) * scale).astype(BF16)
-        grad_query = fold(mm_at(grad_raw, key), tmask)
-        gqkv_s[mine, :width] = grad_query.astype(BF16)
-        gqkv_s[mine, width : 2 * width] = mm(grad_raw, query_spread).astype(BF16)
-        gqkv_s[mine, 2 * width :] = mm(prob.astype(BF16), grad_spread).astype(BF16)
+        gqkv_s[mine, :width] = fold(mm_at(tlow_s[s], key), tmask).astype(BF16)
+        gqkv_s[mine, width : 2 * width] = mm(tlow_s[s], spread(query, tmask_low)).astype(BF16)
+
+    staged(n, trunk_back_probs, trunk_back_softmax, trunk_back_rows)
+
     again_sum = jnp.zeros((1, width), F32)
     abias_sum = jnp.zeros((1, width), F32)
     for i, span in enumerate(spans):
@@ -392,8 +474,7 @@
     vectors += [jnp.zeros((16 - len(vectors), width), F32)]
     put("vectors", 0, jnp.concatenate(vectors, axis=0))
 
-    for s in range(n):
-        e = emb_ref[base + s]
+    for s, e in enumerate(embs):
         grad_prop = gtok_s[s, :, qry:].reshape(steps * ptok, width)
         mixacc_s[e] += mm_at(act_s[s], grad_prop)
         grad_act = mm_bt(grad_prop, mix_w[e]).astype(BF16).astype(F32)
@@ -404,21 +485,29 @@
     grad_img = gtok_s[:, :, :qry].reshape(n * steps * qry, width)
     put("stem", 0, mm_at(satt_s[...].reshape(n * steps * qry, width), grad_img))
     gsatt_s[...] = mm_bt(grad_img, stem_proj[...]).astype(BF16).reshape(n, steps, qry, width)
-    for s in range(n):
-        e = emb_ref[base + s]
-        grad_spread = jnp.concatenate([spread(gsatt_s[s, t], smask_low) for t in range(steps)], axis=0)
-        back = mm_bt(value_w[e], grad_spread).astype(BF16)
-        ab_s[s, :, : 2 * width] = back
-        ab_s[s, :, 2 * width :] = a_s[e]
-        both = mm(x_s[s], back)
-        grad_prob = jnp.where(first_step, both[:, :width], both[:, width:])
-        grad_raw = softmax_lines_grad(prob_s[s], grad_prob.astype(BF16).astype(F32)).astype(BF16)
-        mix_s[s, :, 2 * width :] = grad_raw
-        macc_s[e] += mm(xt_s[s], grad_raw)
-        vacc_s[e] += mm(ut_s[s], grad_spread)
-
-    for s in range(n):
+
+    def stem_back_values(s):
+        spreads = [spread(gsatt_s[s, t], smask_low) for t in range(steps)]
+        grad_spread = jnp.concatenate(spreads, axis=0)
+        ab_s[s, :, : 2 * width] = mm_bt(value_w[embs[s]], grad_spread).astype(BF16)
+        ab_s[s, :, 2 * width :] = a_s[embs[s]]
+        vacc_s[embs[s]] += mm(ut_s[s], grad_spread)
+
+    def stem_back_probs(s):
+        both = mm(x_s[s], ab_s[s, :, : 2 * width])
+        sgrad_s[s] = jnp.where(first_step, both[:, :width], both[:, width:])
+
+    def stem_back_softmax(s):
+        grad_prob = sgrad_s[s].astype(BF16).astype(F32)
+        mix_s[s, :, 2 * width :] = softmax_lines_grad(prob_s[s], grad_prob).astype(BF16)
+
+    def stem_back_moments(s):
+        macc_s[embs[s]] += mm(xt_s[s], mix_s[s, :, 2 * width :])
+
+    def image_gradient(s):
         img_s[pl.ds(s, tall, stride=n)] = mm_bt(mix_s[s], ab_s[s])
+
+    staged(n, stem_back_values, stem_back_probs, stem_back_softmax, stem_back_moments, image_gradient)
 
     for e in range(emb):
         moment = (macc_s[e] * scale).astype(BF16)
@@ -427,21 +516,20 @@
         put("valuew", width * e, vacc_s[e])
         put("mixer", width * e, mixacc_s[e])
         put("lift", liftacc_s.shape[1] * e, liftacc_s[e])
-    used = max(first + count for first, count in table.values())
-    for at, lo, _, count in cuts(used, 2 * PIECES * piece - used, piece):
-        pack_s[at // PIECES, at % PIECES, lo : lo + count] = jnp.zeros((count, width), BF16)
-
     other = 1 - sec
+    half = own_half()
     image = img_s.reshape(tall // steps, steps, n, width)
     stores = (
-        (pack_s.at[sec], keep),
-        (pack_s.at[other], send),
+        (image.at[pl.ds(0, keys), sec], image_out),
+        (image.at[pl.ds(0, keys), other], image_send),
         (blk_s.at[:, sec], block_out),
         (blk_s.at[:, other], block_send),
-        (image.at[pl.ds(0, keys), sec], image_out),
-        (image.at[pl.ds(0, keys), other], image_send),
         (prp_s.at[:, sec], prop_out),
         (prp_s.at[:, other], prop_send),
+        (pack_s.at[half, pl.ds(0, 2)], keep0),
+        (pack_s.at[half, pl.ds(2, 2)], keep1),
+        (pack_s.at[1 - half, pl.ds(0, 2)], send0),
+        (pack_s.at[1 - half, pl.ds(2, 2)], send1),
     )
     stores = [pltpu.make_async_copy(a, b, out_sem.at[i]) for i, (a, b) in enumerate(stores)]
     for copy in stores:
@@ -476,7 +564,9 @@
     def full(*shape):
         return pltpu.VMEM(shape, F32)
 
-    scratch = [
+    held = [0, 1, 2, 3, 4, 5, 8, 9, 12, 14]
+    scratch = [low(*weights[i].shape) for i in held]
+    scratch += [
         low((n * lines + 31) // 16 * 16, width),
         low(n, tall, width),
         low(n, steps, ptok, feats),
@@ -485,6 +575,7 @@
         low(emb, width, HEADS * qry),
         low(n, steps, half_tok, width),
         low(n, width, tall),
+        full(n, tall, HEADS * qry),
         full(n, tall, HEADS * qry),
         low(n, tall, (steps + 1) * width),
         low(n, width, (steps + 1) * width),
@@ -496,6 +587,8 @@
         full(rows, width),
         low(rows, width),
         low(rows, 3 * width),
+        full(n, ctx, HEADS * ctx),
+        low(n, ctx, HEADS * ctx),
         full(n, ctx, HEADS * ctx),
         low(rows, width),
         full(rows, width),
@@ -518,15 +611,17 @@
         full(emb, width, width),
         full(emb, feats, width),
         low(CORES, PIECES, piece, width),
-        pltpu.SemaphoreType.DMA((3,)),
-        pltpu.SemaphoreType.DMA((8,)),
+        pltpu.SemaphoreType.DMA((13,)),
+        pltpu.SemaphoreType.DMA((10,)),
     ]
     shape = jax.ShapeDtypeStruct
     return pl.pallas_call(
         functools.partial(compute_kernel, dims),
         out_shape=(
-            shape((PIECES, piece, width), BF16),
-            shape((PIECES, piece, width), BF16),
+            shape((2, piece, width), BF16),
+            shape((2, piece, width), BF16),
+            shape((2, piece, width), BF16),
+            shape((2, piece, width), BF16),
             shape((n, half_tok, width), BF16),
             shape((n, half_tok, width), BF16),
             shape((keys, n, width), F32),
@@ -534,24 +629,38 @@
             shape((n, ptok, feats), BF16),
             shape((n, ptok, feats), BF16),
         ),
-        in_specs=[SMEM] * 3 + [ANY] * 3 + [VMEM] * 16,
-        out_specs=(ANY,) * 8,
+        in_specs=[SMEM] * 3 + [ANY] * 3 + [ANY if i in held else VMEM for i in range(16)],
+        out_specs=(ANY,) * 10,
         scratch_shapes=scratch,
         compiler_params=pltpu.CompilerParams(vmem_limit_bytes=56 * 2**20),
         name="stem_trunk",
     )(embodiment, ctx_steps, view_mask.T, rows_of(images), proprio, out_grad, *weights)
 
 
-def own_bits():
-    dp, sec = lax.axis_index("dp"), lax.axis_index("section")
-    low, high = dp % 2, (dp // 2) % 2
-    return jnp.where(sec == 0, low, high), jnp.where(sec == 0, high, low)
-
-
-def add_split(bit, held, came):
-    total = (held.astype(F32) + came.astype(F32)).astype(BF16)
-    low, high = total.reshape((2, -1, total.shape[-1]))
-    return jnp.where(bit == 0, low, high), jnp.where(bit == 0, high, low)
+def parity(index, levels):
+    total = index & 1
+    for level in range(1, levels):
+        total = total ^ ((index >> level) & 1)
+    return total
+
+
+def own_half():
+    levels = lax.axis_size("dp").bit_length() - 1
+    return lax.axis_index("section") ^ parity(lax.axis_index("dp"), levels)
+
+
+def own_bits(half):
+    dp = lax.axis_index("dp")
+    low, high = dp & 1, (dp >> 1) & 1
+    return jnp.where(half == 0, low, high), jnp.where(half == 0, high, low)
+
+
+def select(bit, low, high):
+    return jnp.where(bit == 0, low, high)
+
+
+def add(held, came):
+    return (held.astype(F32) + came.astype(F32)).astype(BF16)
 
 
 def swap_cores(value):
@@ -560,9 +669,12 @@
 
 def swap_chips(value, bits):
     count = lax.axis_size("dp")
-    pairs = [
-        (s * count + i, s * count + (i ^ (1 << bits[s]))) for s in range(CORES) for i in range(count)
-    ]
+    levels = count.bit_length() - 1
+    pairs = []
+    for core in range(CORES):
+        for i in range(count):
+            bit = bits[core ^ parity(i, levels)]
+            pairs.append((core * count + i, (1 - core) * count + (i ^ (1 << bit))))
     return lax.ppermute(value, ("section", "dp"), pairs)
 
 
@@ -573,18 +685,14 @@
 
 def unpack_kernel(table, *refs):
     pieces, outs, (pack, sem) = refs[:8], refs[8:-2], refs[-2:]
-    sec = lax.axis_index("section")
-    one, two = own_bits()
+    own = own_half()
     copies = []
-    for owner in range(CORES):
-        first, second = (one, two) if owner == 0 else (two, one)
-        start = (sec if owner == 0 else 1 - sec) * PIECES
-        for j in range(PIECES):
-            x = first if j < 2 else 1 - first
-            y = second if j % 2 == 0 else 1 - second
-            at = start + 2 * x + y
-            i = owner * PIECES + j
-            copies.append(pltpu.make_async_copy(pieces[i], pack.at[at], sem.at[i]))
+    for i, ref in enumerate(pieces):
+        half = own if i < PIECES else 1 - own
+        first = own_bits(half)[0]
+        chain, far = i % CHAINS, i // CHAINS % 2
+        at = half * PIECES + chain * 2 + (first ^ far)
+        copies.append(pltpu.make_async_copy(ref, pack.at[at], sem.at[i]))
     for copy in copies:
         copy.start()
     for copy in copies:
@@ -652,24 +760,30 @@
 def sum_chips(held, came):
     levels = lax.axis_size("dp").bit_length() - 1
     first, second = (0, 1), (1, 0)
-    one, two = own_bits()
-    keep, send = add_split(one, held, came)
-    keep, send = add_split(two, keep, swap_chips(send, first))
-    total = keep + swap_chips(send, second)
+    one, two = own_bits(own_half())
+    totals = [add(a, b) for a, b in zip(held, came)]
+    for bit, bits in ((one, first), (two, second)):
+        split = [t.reshape((2, -1, t.shape[-1])) for t in totals]
+        sent = [swap_chips(select(bit, t[1], t[0]), bits) for t in split]
+        totals = [add(select(bit, t[0], t[1]), c) for t, c in zip(split, sent)]
     for bits in zip(range(2, levels), reversed(range(2, levels))):
-        total = total + swap_chips(total, bits)
-    by_second = swap_chips(total, second)
-    by_first = swap_chips(total, first)
-    by_both = swap_chips(by_second, first)
-    return total, by_second, by_first, by_both
+        sent = [swap_chips(t, bits) for t in totals]
+        totals = [add(t, c) for t, c in zip(totals, sent)]
+    sent = [swap_chips(t, second) for t in totals]
+    near = [
+        select(two, jnp.concatenate([t, c]), jnp.concatenate([c, t])) for t, c in zip(totals, sent)
+    ]
+    far = [swap_chips(t, first) for t in near]
+    return tuple(near) + tuple(far)
 
 
 def per_device(*args):
     weights = args[5:21]
     emb, qry, width = weights[0].shape
     table, total = layout(width, weights[12].shape[1], emb, qry, weights[4].shape[1])
-    keep, send, blk, blk_s, img, img_s, prp, prp_s = compute(args, table, total)
-    came = swap_cores(send)
+    *packed, blk, blk_s, img, img_s, prp, prp_s = compute(args, table, total)
+    keep, send = packed[:CHAINS], packed[CHAINS:]
+    came = [swap_cores(v) for v in send]
     blk_r, img_r, prp_r = (swap_cores(v) for v in (blk_s, img_s, prp_s))
     pieces = sum_chips(keep, came)
     pieces += tuple(swap_cores(v) for v in pieces)

time: 63.1 us -> 54.9 us (0.87)
  waiting for transfers between devices: 16.7 us -> 7.38 us
  Pallas kernels: 23.5 us -> 18.7 us
  starting transfers between devices: 18.2 us -> 22.9 us
  other arithmetic: 3.68 us -> 4.69 us
    ppermute x7 -> x12, waiting for transfers between devices: 14.7 us -> 7.03 us  [swap_chips(): return lax.ppermute(value, ('section', 'dp'), pairs)]
    pallas_call x1, Pallas kernels: 20.8 us -> 16 us  [compute(): pl.pallas_call(functools.partial(compute_kernel, dims), out_shape=(shape(...]
    ppermute x7 -> x12, starting transfers between devices: 16.6 us -> 20.8 us  [swap_chips(): return lax.ppermute(value, ('section', 'dp'), pairs)]
    unnamed x2, other arithmetic: 0.68 us -> 2.59 us
    ppermute x8 -> x9, waiting for transfers between devices: 2 us -> 0.35 us  [swap_cores(): return lax.ppermute(value, 'section', [(0, 1), (1, 0)])]
    convert_element_type x2 -> x10, other arithmetic: 1.22 us -> 0.35 us  [add(): return (held.astype(F32) + came.astype(F32)).astype(BF16)]
    ppermute x8 -> x9, starting transfers between devices: 1.6 us -> 2.12 us  [swap_cores(): return lax.ppermute(value, 'section', [(0, 1), (1, 0)])]
  transfers between devices with their start and end apart: 15 -> 21, of which waited for: 8 -> 9; matrix products, arithmetic and copies ran while one was open for 4% -> 9% of each run, Pallas kernels for 0% -> 0%
where the time goes in v3:
time: 54.9 us; the launch traced here: 54.6 us
  starting transfers between devices  22.9 us (42%)
  Pallas kernels  18.7 us (34%)
  waiting for transfers between devices  7.38 us (13%)
  other arithmetic  4.69 us (9%)
  between operations  0.82 us (1%)
    ppermute x12, starting transfers between devices, swap_chips(): return lax.ppermute(value, ('section', 'dp'), pairs)  20.8 us
    pallas_call x1, Pallas kernels, compute(): pl.pallas_call(functools.partial(compute_kernel, dims), out_shape=(shape(...  16 us
    ppermute x12, waiting for transfers between devices, swap_chips(): return lax.ppermute(value, ('section', 'dp'), pairs)  7.03 us
    pallas_call x1, Pallas kernels, unpack(): pl.pallas_call(functools.partial(unpack_kernel, table), out_shape=tuple((...  2.75 us
    unnamed x2, other arithmetic  2.59 us
    ppermute x9, starting transfers between devices, swap_cores(): return lax.ppermute(value, 'section', [(0, 1), (1, 0)])  2.12 us
  transfers between devices with their start and end apart: 21, of which 9 were waited for; matrix products, arithmetic and copies ran while one was open for 9% of the time, Pallas kernels for 0%

profile of v3, /device:TPU:0, one launch (start us, length us, event | category | flops | bytes accessed | tf_op | source)
XLA Modules:
  0.0 54.6 jit_solution(1090383968976371970)
XLA Ops:
  0.7 16.0 %stem_trunk.1 = (bf16[2,448,128]{2,1,0:T(8,128)(2,1)}, bf16[2,448,128]{2,1,0:T(8,128)(2,1)}, bf16[2,448,128]{2,1,0:T(8,128)(2,1)}, bf16[2,448,128]{2,1,0:T(8,128...) custom-call(s32[16]{0:T(128)} %emb_ref.1, ...), custom_call_target="tpu_custom_call" | custom-call | tf_op jit(solution)/shard_map/stem_trunk/pallas_call | solution.py:618
  16.7 0.5 collective-permute-start.3
  17.8 1.1 %convert.10 = bf16[147,8,128]{2,1,0:T(8,128)(2,1)S(1)} convert(f32[147,8,128]{2,1,0:T(8,128)} %get-tuple-element.48) | non-fusion elementwise | flops 150528 | bytes 903168
  19.4 1.5 %fusion.4 = bf16[16,1,16,64]{3,2,1,0:T(8,128)(2,1)} fusion(bf16[8,1,16,64]{3,2,0,1:T(8,128)(2,1)S(1)} %bitcast.24, bf16[8,1,16,64]{3,2,0,1:T(8,128)(2,1)} %bitcast.23, pred[]{:T(512)S(6)} %eq.8), kind=kLoop, calls=%fused_computation.21 | loop fusion | flops 49152 | bytes 65537
  21.0 2.7 %collective-permute-start.4 = (bf16[448,128]{1,0:T(8,128)(2,1)S(1)}, bf16[448,128]{1,0:T(8,128)(2,1)S(1)}, u32[]{:S(2)}, u32[]{:S(2)}) collective-permute-start(bf16[448,128]{1,0:T(8,128)(2,1)S(1)} %select_bitcast_fusion.1), channel_id=1, source_target_pairs={{0,17},{1,19},{2,16},{3,18},{4,22},{5,20},{6,23},{7,21},{8,26},{9,... | collective-permute-start | bytes 344072 | tf_op jit(solution)/shard_map/ppermute | solution.py:678
  23.8 2.3 %collective-permute-done.4 = bf16[448,128]{1,0:T(8,128)(2,1)S(1)} collective-permute-done((bf16[448,128]{1,0:T(8,128)(2,1)S(1)}, bf16[448,128]{1,0:T(8,128)(2,1)S(1)}, u32[]{:S(2)}, u32[]{:S(2)}) %collective-permute-start.4) | collective-permute-done | bytes 114720 | tf_op jit(solution)/shard_map/ppermute | solution.py:678
  26.2 2.1 %collective-permute-start.5 = (bf16[224,128]{1,0:T(8,128)(2,1)S(1)}, bf16[224,128]{1,0:T(8,128)(2,1)S(1)}, u32[]{:S(2)}, u32[]{:S(2)}) collective-permute-start(bf16[224,128]{1,0:T(8,128)(2,1)S(1)} %broadcast_select_fusion.1), channel_id=1, source_target_pairs={{0,18},{1,16},{2,19},{3,17},{4,21},{5,23},{6,20},{7,22},{8,25},{9,... | collective-permute-start | bytes 172040 | tf_op jit(solution)/shard_map/ppermute | solution.py:678
  28.4 0.9 %collective-permute-start.11 = (bf16[224,128]{1,0:T(8,128)(2,1)S(1)}, bf16[224,128]{1,0:T(8,128)(2,1)S(1)}, u32[]{:S(2)}, u32[]{:S(2)}) collective-permute-start(bf16[224,128]{1,0:T(8,128)(2,1)S(1)} %broadcast_select_fusion), channel_id=1, source_target_pairs={{0,18},{1,16},{2,19},{3,17},{4,21},{5,23},{6,20},{7,22},{8,25},{9,... | collective-permute-start | bytes 172040 | tf_op jit(solution)/shard_map/ppermute | solution.py:678
  29.4 0.8 %collective-permute-done.5 = bf16[224,128]{1,0:T(8,128)(2,1)S(1)} collective-permute-done((bf16[224,128]{1,0:T(8,128)(2,1)S(1)}, bf16[224,128]{1,0:T(8,128)(2,1)S(1)}, u32[]{:S(2)}, u32[]{:S(2)}) %collective-permute-start.5) | collective-permute-done | bytes 57376 | tf_op jit(solution)/shard_map/ppermute | solution.py:678
  30.2 1.9 %collective-permute-start.6 = (bf16[224,128]{1,0:T(8,128)(2,1)S(1)}, bf16[224,128]{1,0:T(8,128)(2,1)S(1)}, u32[]{:S(2)}, u32[]{:S(2)}) collective-permute-start(bf16[224,128]{1,0:T(8,128)(2,1)S(1)} %add_convert_fusion.7), channel_id=1, source_target_pairs={{0,20},{1,25},{2,26},{3,23},{4,28},{5,17},{6,18},{7,31},{8,16},{9,... | collective-permute-start | bytes 172040 | tf_op jit(solution)/shard_map/ppermute | solution.py:678
  32.1 1.3 %collective-permute-start.12 = (bf16[224,128]{1,0:T(8,128)(2,1)S(1)}, bf16[224,128]{1,0:T(8,128)(2,1)S(1)}, u32[]{:S(2)}, u32[]{:S(2)}) collective-permute-start(bf16[224,128]{1,0:T(8,128)(2,1)S(1)} %add_convert_fusion.4), channel_id=1, source_target_pairs={{0,20},{1,25},{2,26},{3,23},{4,28},{5,17},{6,18},{7,31},{8,16},{9,... | collective-permute-start | bytes 172040 | tf_op jit(solution)/shard_map/ppermute | solution.py:678
  33.5 0.8 %collective-permute-done.6 = bf16[224,128]{1,0:T(8,128)(2,1)S(1)} collective-permute-done((bf16[224,128]{1,0:T(8,128)(2,1)S(1)}, bf16[224,128]{1,0:T(8,128)(2,1)S(1)}, u32[]{:S(2)}, u32[]{:S(2)}) %collective-permute-start.6) | collective-permute-done | bytes 57376 | tf_op jit(solution)/shard_map/ppermute | solution.py:678
  34.2 2.9 %collective-permute-start.7 = (bf16[224,128]{1,0:T(8,128)(2,1)S(1)}, bf16[224,128]{1,0:T(8,128)(2,1)S(1)}, u32[]{:S(2)}, u32[]{:S(2)}) collective-permute-start(bf16[224,128]{1,0:T(8,128)(2,1)S(1)} %add_convert_fusion.6), channel_id=1, source_target_pairs={{0,24},{1,21},{2,22},{3,27},{4,16},{5,29},{6,30},{7,19},{8,28},{9,... | collective-permute-start | bytes 172040 | tf_op jit(solution)/shard_map/ppermute | solution.py:678
  37.1 1.3 %collective-permute-start.13 = (bf16[224,128]{1,0:T(8,128)(2,1)S(1)}, bf16[224,128]{1,0:T(8,128)(2,1)S(1)}, u32[]{:S(2)}, u32[]{:S(2)}) collective-permute-start(bf16[224,128]{1,0:T(8,128)(2,1)S(1)} %add_convert_fusion.3), channel_id=1, source_target_pairs={{0,24},{1,21},{2,22},{3,27},{4,16},{5,29},{6,30},{7,19},{8,28},{9,... | collective-permute-start | bytes 172040 | tf_op jit(solution)/shard_map/ppermute | solution.py:678
  38.4 1.0 %collective-permute-done.7 = bf16[224,128]{1,0:T(8,128)(2,1)S(1)} collective-permute-done((bf16[224,128]{1,0:T(8,128)(2,1)S(1)}, bf16[224,128]{1,0:T(8,128)(2,1)S(1)}, u32[]{:S(2)}, u32[]{:S(2)}) %collective-permute-start.7) | collective-permute-done | bytes 57376 | tf_op jit(solution)/shard_map/ppermute | solution.py:678
  39.4 2.1 %collective-permute-start.8 = (bf16[224,128]{1,0:T(8,128)(2,1)S(1)}, bf16[224,128]{1,0:T(8,128)(2,1)S(1)}, u32[]{:S(2)}, u32[]{:S(2)}) collective-permute-start(bf16[224,128]{1,0:T(8,128)(2,1)S(1)} %add_convert_fusion.5), channel_id=1, source_target_pairs={{0,18},{1,16},{2,19},{3,17},{4,21},{5,23},{6,20},{7,22},{8,25},{9,... | collective-permute-start | bytes 172040 | tf_op jit(solution)/shard_map/ppermute | solution.py:678
  42.0 1.0 %collective-permute-start.14 = (bf16[224,128]{1,0:T(8,128)(2,1)S(1)}, bf16[224,128]{1,0:T(8,128)(2,1)S(1)}, u32[]{:S(2)}, u32[]{:S(2)}) collective-permute-start(bf16[224,128]{1,0:T(8,128)(2,1)S(1)} %add_convert_fusion.2), channel_id=1, source_target_pairs={{0,18},{1,16},{2,19},{3,17},{4,21},{5,23},{6,20},{7,22},{8,25},{9,... | collective-permute-start | bytes 172040 | tf_op jit(solution)/shard_map/ppermute | solution.py:678
  43.5 2.1 %collective-permute-start.15 = (bf16[448,128]{1,0:T(8,128)(2,1)S(1)}, bf16[448,128]{1,0:T(8,128)(2,1)S(1)}, u32[]{:S(2)}, u32[]{:S(2)}) collective-permute-start(bf16[448,128]{1,0:T(8,128)(2,1)S(1)} %maximum_select_fusion.2.refs_0_), channel_id=1, source_target_pairs={{0,17},{1,19},{2,16},{3,18},{4,22},{5,20},{6,23},{7,21},{8,26},{9,... | collective-permute-start | bytes 344072 | tf_op jit(solution)/shard_map/ppermute | solution.py:678
  45.7 2.3 %collective-permute-start.16 = (bf16[448,128]{1,0:T(8,128)(2,1)S(1)}, bf16[448,128]{1,0:T(8,128)(2,1)S(1)}, u32[]{:S(2)}, u32[]{:S(2)}) collective-permute-start(bf16[448,128]{1,0:T(8,128)(2,1)S(1)} %maximum_select_fusion.3.refs_1_), channel_id=1, source_target_pairs={{0,17},{1,19},{2,16},{3,18},{4,22},{5,20},{6,23},{7,21},{8,26},{9,... | collective-permute-start | bytes 344072 | tf_op jit(solution)/shard_map/ppermute | solution.py:678
  48.0 0.7 %maximum_select_fusion.1 = bf16[16,32,128]{2,1,0:T(8,128)(2,1)} fusion(bf16[8,32,128]{2,1,0:T(8,128)(2,1)S(1)} %collective-permute-done, bf16[8,32,128]{2,1,0:T(8,128)(2,1)S(1)} %copy-done.3, pred[]{:T(512)S(6)} %eq.8), kind=kLoop, calls=%fused_computation.9 | loop fusion | flops 196608 | bytes 262145 | tf_op jit(solution)/shard_map/jit(_where)/select_n | solution.py:683
  48.7 0.5 collective-permute-start.18
  49.2 1.3 %collective-permute-done.16.refs_3_ = bf16[448,128]{1,0:T(8,128)(2,1)S(1)} collective-permute-done((bf16[448,128]{1,0:T(8,128)(2,1)S(1)}, bf16[448,128]{1,0:T(8,128)(2,1)S(1)}, u32[]{:S(2)}, u32[]{:S(2)}) %collective-permute-start.16) | collective-permute-done | bytes 114720 | tf_op jit(solution)/shard_map/ppermute | solution.py:678
  50.5 1.0 %fusion.1 = bf16[16,1,147,128]{3,0,2,1:T(8,128)(2,1)} fusion(f32[147,8,128]{2,1,0:T(8,128)S(1)} %copy-done, bf16[147,8,128]{2,1,0:T(8,128)(2,1)S(1)} %collective-permute-done.1, pred[]{:T(512)S(6)} %eq.8), kind=kLoop, calls=%fused_computation.2 | loop fusion | flops 2709504 | bytes 1505281 | tf_op jit(solution)/shard_map/broadcast_in_dim | solution.py:792
  51.8 2.7 %unpack.1 = (f32[4,16,128]{2,1,0:T(8,128)}, f32[4,128,128]{2,1,0:T(8,128)}, f32[4,128,128]{2,1,0:T(8,128)}, f32[128,128]{1,0:T(8,128)}, f32[4,64,128]{2,1,0:T(8,...) custom-call(bf16[448,128]{1,0:T(8,128)(2,1)S(1)} %maximum_select_fus, ...), custom_call_target="tpu_custom_call" | custom-call | tf_op jit(solution)/shard_map/unpack/pallas_call | solution.py:746
  (48 shorter events, 2.9 us)
Async XLA Ops:
  16.7 7.0 %copy-start.1 = (bf16[2,448,128]{2,1,0:T(8,128)(2,1)S(1)}, bf16[2,448,128]{2,1,0:T(8,128)(2,1)}, u32[]{:S(2)}) copy-start(bf16[2,448,128]{2,1,0:T(8,128)(2,1)} %get-tuple-element.53) | copy-start | bytes 688132
  16.7 4.2 %collective-permute-start.3 = (bf16[2,448,128]{2,1,0:T(8,128)(2,1)}, bf16[2,448,128]{2,1,0:T(8,128)(2,1)S(1)}, u32[]{:S(2)}, u32[]{:S(2)}) collective-permute-start(bf16[2,448,128]{2,1,0:T(8,128)(2,1)} %get-tuple-element.52), channel_id=1, source_target_pairs={{0,16},{16,0},{1,17},{17,1},{2,18},{18,2},{3,19},{19,3},{4,20},{20... | collective-permute-start | bytes 688136 | tf_op jit(solution)/shard_map/ppermute | solution.py:667
  17.2 2.2 %collective-permute-start.2 = (bf16[8,16,64]{2,1,0:T(8,128)(2,1)}, bf16[8,16,64]{2,1,0:T(8,128)(2,1)S(1)}, u32[]{:S(2)}, u32[]{:S(2)}) collective-permute-start(bf16[8,16,64]{2,1,0:T(8,128)(2,1)} %get-tuple-element.50), channel_id=1, source_target_pairs={{0,16},{16,0},{1,17},{17,1},{2,18},{18,2},{3,19},{19,3},{4,20},{20... | collective-permute-start | bytes 49160 | tf_op jit(solution)/shard_map/ppermute | solution.py:667
  17.3 30.8 %collective-permute-start = (bf16[8,32,128]{2,1,0:T(8,128)(2,1)}, bf16[8,32,128]{2,1,0:T(8,128)(2,1)S(1)}, u32[]{:S(2)}, u32[]{:S(2)}) collective-permute-start(bf16[8,32,128]{2,1,0:T(8,128)(2,1)} %get-tuple-element.46), channel_id=1, source_target_pairs={{0,16},{16,0},{1,17},{17,1},{2,18},{18,2},{3,19},{19,3},{4,20},{20... | collective-permute-start | bytes 196616 | tf_op jit(solution)/shard_map/ppermute | solution.py:667
  17.7 5.9 %collective-permute-start.9 = (bf16[2,448,128]{2,1,0:T(8,128)(2,1)}, bf16[2,448,128]{2,1,0:T(8,128)(2,1)S(1)}, u32[]{:S(2)}, u32[]{:S(2)}) collective-permute-start(bf16[2,448,128]{2,1,0:T(8,128)(2,1)} %get-tuple-element.54), channel_id=1, source_target_pairs={{0,16},{16,0},{1,17},{17,1},{2,18},{18,2},{3,19},{19,3},{4,20},{20... | collective-permute-start | bytes 688136 | tf_op jit(solution)/shard_map/ppermute | solution.py:667
  18.9 31.6 %collective-permute-start.1 = (bf16[147,8,128]{2,1,0:T(8,128)(2,1)S(1)}, bf16[147,8,128]{2,1,0:T(8,128)(2,1)S(1)}, u32[]{:S(2)}, u32[]{:S(2)}) collective-permute-start(bf16[147,8,128]{2,1,0:T(8,128)(2,1)S(1)} %convert.10), channel_id=1, source_target_pairs={{0,16},{16,0},{1,17},{17,1},{2,18},{18,2},{3,19},{19,3},{4,20},{20... | collective-permute-start | bytes 903176 | tf_op jit(solution)/shard_map/ppermute | solution.py:667
  21.0 5.1 %collective-permute-start.4 = (bf16[448,128]{1,0:T(8,128)(2,1)S(1)}, bf16[448,128]{1,0:T(8,128)(2,1)S(1)}, u32[]{:S(2)}, u32[]{:S(2)}) collective-permute-start(bf16[448,128]{1,0:T(8,128)(2,1)S(1)} %select_bitcast_fusion.1), channel_id=1, source_target_pairs={{0,17},{1,19},{2,16},{3,18},{4,22},{5,20},{6,23},{7,21},{8,26},{9,... | collective-permute-start | bytes 344072 | tf_op jit(solution)/shard_map/ppermute | solution.py:678
  23.7 4.6 %collective-permute-start.10 = (bf16[448,128]{1,0:T(8,128)(2,1)S(1)}, bf16[448,128]{1,0:T(8,128)(2,1)S(1)}, u32[]{:S(2)}, u32[]{:S(2)}) collective-permute-start(bf16[448,128]{1,0:T(8,128)(2,1)S(1)} %select_bitcast_fusion), channel_id=1, source_target_pairs={{0,17},{1,19},{2,16},{3,18},{4,22},{5,20},{6,23},{7,21},{8,26},{9,... | collective-permute-start | bytes 344072 | tf_op jit(solution)/shard_map/ppermute | solution.py:678
  26.2 21.9 %copy-start.3 = (bf16[8,32,128]{2,1,0:T(8,128)(2,1)S(1)}, bf16[8,32,128]{2,1,0:T(8,128)(2,1)}, u32[]{:S(2)}) copy-start(bf16[8,32,128]{2,1,0:T(8,128)(2,1)} %get-tuple-element.45) | copy-start | bytes 196612
  26.2 24.3 %copy-start = (f32[147,8,128]{2,1,0:T(8,128)S(1)}, f32[147,8,128]{2,1,0:T(8,128)}, u32[]{:S(2)}) copy-start(f32[147,8,128]{2,1,0:T(8,128)} %get-tuple-element.47) | copy-start | bytes 1806340
  26.2 4.0 %collective-permute-start.5 = (bf16[224,128]{1,0:T(8,128)(2,1)S(1)}, bf16[224,128]{1,0:T(8,128)(2,1)S(1)}, u32[]{:S(2)}, u32[]{:S(2)}) collective-permute-start(bf16[224,128]{1,0:T(8,128)(2,1)S(1)} %broadcast_select_fusion.1), channel_id=1, source_target_pairs={{0,18},{1,16},{2,19},{3,17},{4,21},{5,23},{6,20},{7,22},{8,25},{9,... | collective-permute-start | bytes 172040 | tf_op jit(solution)/shard_map/ppermute | solution.py:678
  28.4 3.7 %collective-permute-start.11 = (bf16[224,128]{1,0:T(8,128)(2,1)S(1)}, bf16[224,128]{1,0:T(8,128)(2,1)S(1)}, u32[]{:S(2)}, u32[]{:S(2)}) collective-permute-start(bf16[224,128]{1,0:T(8,128)(2,1)S(1)} %broadcast_select_fusion), channel_id=1, source_target_pairs={{0,18},{1,16},{2,19},{3,17},{4,21},{5,23},{6,20},{7,22},{8,25},{9,... | collective-permute-start | bytes 172040 | tf_op jit(solution)/shard_map/ppermute | solution.py:678
  30.2 4.0 %collective-permute-start.6 = (bf16[224,128]{1,0:T(8,128)(2,1)S(1)}, bf16[224,128]{1,0:T(8,128)(2,1)S(1)}, u32[]{:S(2)}, u32[]{:S(2)}) collective-permute-start(bf16[224,128]{1,0:T(8,128)(2,1)S(1)} %add_convert_fusion.7), channel_id=1, source_target_pairs={{0,20},{1,25},{2,26},{3,23},{4,28},{5,17},{6,18},{7,31},{8,16},{9,... | collective-permute-start | bytes 172040 | tf_op jit(solution)/shard_map/ppermute | solution.py:678
  32.1 5.0 %collective-permute-start.12 = (bf16[224,128]{1,0:T(8,128)(2,1)S(1)}, bf16[224,128]{1,0:T(8,128)(2,1)S(1)}, u32[]{:S(2)}, u32[]{:S(2)}) collective-permute-start(bf16[224,128]{1,0:T(8,128)(2,1)S(1)} %add_convert_fusion.4), channel_id=1, source_target_pairs={{0,20},{1,25},{2,26},{3,23},{4,28},{5,17},{6,18},{7,31},{8,16},{9,... | collective-permute-start | bytes 172040 | tf_op jit(solution)/shard_map/ppermute | solution.py:678
  34.2 5.2 %collective-permute-start.7 = (bf16[224,128]{1,0:T(8,128)(2,1)S(1)}, bf16[224,128]{1,0:T(8,128)(2,1)S(1)}, u32[]{:S(2)}, u32[]{:S(2)}) collective-permute-start(bf16[224,128]{1,0:T(8,128)(2,1)S(1)} %add_convert_fusion.6), channel_id=1, source_target_pairs={{0,24},{1,21},{2,22},{3,27},{4,16},{5,29},{6,30},{7,19},{8,28},{9,... | collective-permute-start | bytes 172040 | tf_op jit(solution)/shard_map/ppermute | solution.py:678
  37.1 4.9 %collective-permute-start.13 = (bf16[224,128]{1,0:T(8,128)(2,1)S(1)}, bf16[224,128]{1,0:T(8,128)(2,1)S(1)}, u32[]{:S(2)}, u32[]{:S(2)}) collective-permute-start(bf16[224,128]{1,0:T(8,128)(2,1)S(1)} %add_convert_fusion.3), channel_id=1, source_target_pairs={{0,24},{1,21},{2,22},{3,27},{4,16},{5,29},{6,30},{7,19},{8,28},{9,... | collective-permute-start | bytes 172040 | tf_op jit(solution)/shard_map/ppermute | solution.py:678
  39.4 4.0 %collective-permute-start.8 = (bf16[224,128]{1,0:T(8,128)(2,1)S(1)}, bf16[224,128]{1,0:T(8,128)(2,1)S(1)}, u32[]{:S(2)}, u32[]{:S(2)}) collective-permute-start(bf16[224,128]{1,0:T(8,128)(2,1)S(1)} %add_convert_fusion.5), channel_id=1, source_target_pairs={{0,18},{1,16},{2,19},{3,17},{4,21},{5,23},{6,20},{7,22},{8,25},{9,... | collective-permute-start | bytes 172040 | tf_op jit(solution)/shard_map/ppermute | solution.py:678
  42.0 3.7 %collective-permute-start.14 = (bf16[224,128]{1,0:T(8,128)(2,1)S(1)}, bf16[224,128]{1,0:T(8,128)(2,1)S(1)}, u32[]{:S(2)}, u32[]{:S(2)}) collective-permute-start(bf16[224,128]{1,0:T(8,128)(2,1)S(1)} %add_convert_fusion.2), channel_id=1, source_target_pairs={{0,18},{1,16},{2,19},{3,17},{4,21},{5,23},{6,20},{7,22},{8,25},{9,... | collective-permute-start | bytes 172040 | tf_op jit(solution)/shard_map/ppermute | solution.py:678
  43.5 5.8 %collective-permute-start.15 = (bf16[448,128]{1,0:T(8,128)(2,1)S(1)}, bf16[448,128]{1,0:T(8,128)(2,1)S(1)}, u32[]{:S(2)}, u32[]{:S(2)}) collective-permute-start(bf16[448,128]{1,0:T(8,128)(2,1)S(1)} %maximum_select_fusion.2.refs_0_), channel_id=1, source_target_pairs={{0,17},{1,19},{2,16},{3,18},{4,22},{5,20},{6,23},{7,21},{8,26},{9,... | collective-permute-start | bytes 344072 | tf_op jit(solution)/shard_map/ppermute | solution.py:678
  45.7 4.8 %collective-permute-start.16 = (bf16[448,128]{1,0:T(8,128)(2,1)S(1)}, bf16[448,128]{1,0:T(8,128)(2,1)S(1)}, u32[]{:S(2)}, u32[]{:S(2)}) collective-permute-start(bf16[448,128]{1,0:T(8,128)(2,1)S(1)} %maximum_select_fusion.3.refs_1_), channel_id=1, source_target_pairs={{0,17},{1,19},{2,16},{3,18},{4,22},{5,20},{6,23},{7,21},{8,26},{9,... | collective-permute-start | bytes 344072 | tf_op jit(solution)/shard_map/ppermute | solution.py:678
  48.7 2.8 %collective-permute-start.17 = (bf16[448,128]{1,0:T(8,128)(2,1)S(1)}, bf16[448,128]{1,0:T(8,128)(2,1)S(1)}, u32[]{:S(2)}, u32[]{:S(2)}) collective-permute-start(bf16[448,128]{1,0:T(8,128)(2,1)S(1)} %maximum_select_fusion.2.refs_0_), channel_id=1, source_target_pairs={{0,16},{16,0},{1,17},{17,1},{2,18},{18,2},{3,19},{19,3},{4,20},{20... | collective-permute-start | bytes 344072 | tf_op jit(solution)/shard_map/ppermute | solution.py:667
  48.7 2.8 %collective-permute-start.18 = (bf16[448,128]{1,0:T(8,128)(2,1)S(1)}, bf16[448,128]{1,0:T(8,128)(2,1)S(1)}, u32[]{:S(2)}, u32[]{:S(2)}) collective-permute-start(bf16[448,128]{1,0:T(8,128)(2,1)S(1)} %maximum_select_fusion.3.refs_1_), channel_id=1, source_target_pairs={{0,16},{16,0},{1,17},{17,1},{2,18},{18,2},{3,19},{19,3},{4,20},{20... | collective-permute-start | bytes 344072 | tf_op jit(solution)/shard_map/ppermute | solution.py:667
  49.2 2.3 %collective-permute-start.19 = (bf16[448,128]{1,0:T(8,128)(2,1)S(1)}, bf16[448,128]{1,0:T(8,128)(2,1)S(1)}, u32[]{:S(2)}, u32[]{:S(2)}) collective-permute-start(bf16[448,128]{1,0:T(8,128)(2,1)S(1)} %collective-permute-done.15.refs_2_), channel_id=1, source_target_pairs={{0,16},{16,0},{1,17},{17,1},{2,18},{18,2},{3,19},{19,3},{4,20},{20... | collective-permute-start | bytes 344072 | tf_op jit(solution)/shard_map/ppermute | solution.py:667
  50.5 1.3 %collective-permute-start.20 = (bf16[448,128]{1,0:T(8,128)(2,1)S(1)}, bf16[448,128]{1,0:T(8,128)(2,1)S(1)}, u32[]{:S(2)}, u32[]{:S(2)}) collective-permute-start(bf16[448,128]{1,0:T(8,128)(2,1)S(1)} %collective-permute-done.16.refs_3_), channel_id=1, source_target_pairs={{0,16},{16,0},{1,17},{17,1},{2,18},{18,2},{3,19},{19,3},{4,20},{20... | collective-permute-start | bytes 344072 | tf_op jit(solution)/shard_map/ppermute | solution.py:667
  (1 other events, 4.2 us)

commit v4 on v3

--- a/solution.py
+++ b/solution.py
@@ -137,9 +137,9 @@
 
 def compute_kernel(
     dims,
-    emb_ref,
-    steps_ref,
-    views_ref,
+    emb_h,
+    steps_h,
+    views_h,
     images,
     proprio,
     out_grad,
@@ -149,16 +149,16 @@
     stem_h,
     lift_h,
     mix_h,
-    again,
-    abias,
+    again_h,
+    abias_h,
     qkv_h,
     aproj_h,
-    mgain,
-    mbias,
+    mgain_h,
+    mbias_h,
     up_h,
-    up_b,
+    up_bh,
     down_h,
-    down_b,
+    down_bh,
     keep0,
     keep1,
     send0,
@@ -169,16 +169,25 @@
     image_send,
     prop_out,
     prop_send,
+    emb_ref,
+    steps_ref,
+    views_ref,
     queries,
     key_w,
     value_w,
     stem_proj,
     lift_w,
     mix_w,
+    again,
+    abias,
     qkv_w,
     aproj,
+    mgain,
+    mbias,
     up_w,
+    up_b,
     down_w,
+    down_b,
     xin_s,
     x_s,
     p_s,
@@ -203,6 +212,8 @@
     tlow_s,
     gprob_s,
     att_s,
+    mid_s,
+    pre_s,
     hat2_s,
     rstd2_s,
     norm2_s,
@@ -220,11 +231,8 @@
     prp_s,
     macc_s,
     vacc_s,
-    mixacc_s,
-    liftacc_s,
     pack_s,
     in_sem,
-    out_sem,
 ):
     n, steps, keys, width, qry, ptok, emb, ffw, table, views = dims
     half_tok = qry + ptok
@@ -236,35 +244,44 @@
     base = sec * n
     lines = steps * keys
     tall = x_s.shape[1]
-    embs = [emb_ref[base + s] for s in range(n)]
-
     def put(name, row, value):
         first = table[name][0] + row
         for at, lo, done, count in cuts(first, value.shape[0], piece):
             pack_s[at // PIECES, at % PIECES, lo : lo + count] = value[done : done + count].astype(BF16)
 
-    loads = [
-        pltpu.make_async_copy(a, b, in_sem.at[i])
-        for i, (a, b) in enumerate(
-            (
-                (queries_h, queries),
-                (key_h, key_w),
-                (images.at[pl.ds(pl.multiple_of(sec * n * lines, 16), n * lines)], xin_s.at[pl.ds(0, n * lines)]),
-                (proprio.at[pl.ds(base, n)], p_s),
-                (lift_h, lift_w),
-                (mix_h, mix_w),
-                (value_h, value_w),
-                (stem_h, stem_proj),
-                (qkv_h, qkv_w),
-                (aproj_h, aproj),
-                (up_h, up_w),
-                (down_h, down_w),
-                (out_grad.at[pl.ds(base, n)], g_s),
-            )
-        )
-    ]
+    sources = (
+        (emb_h, emb_ref),
+        (queries_h, queries),
+        (key_h, key_w),
+        (images.at[pl.ds(pl.multiple_of(sec * n * lines, 16), n * lines)], xin_s.at[pl.ds(0, n * lines)]),
+        (views_h, views_ref),
+        (value_h, value_w),
+        (proprio.at[pl.ds(base, n)], p_s),
+        (lift_h, lift_w),
+        (mix_h, mix_w),
+        (stem_h, stem_proj),
+        (again_h, again),
+        (abias_h, abias),
+        (qkv_h, qkv_w),
+        (steps_h, steps_ref),
+        (aproj_h, aproj),
+        (mgain_h, mgain),
+        (mbias_h, mbias),
+        (up_h, up_w),
+        (up_bh, up_b),
+        (down_h, down_w),
+        (down_bh, down_b),
+        (out_grad.at[pl.ds(base, n)], g_s),
+    )
+    loads = [pltpu.make_async_copy(a, b, in_sem.at[i]) for i, (a, b) in enumerate(sources)]
     for copy in loads:
         copy.start()
+    waited = [0]
+
+    def ready(count):
+        for copy in loads[waited[0] : count]:
+            copy.wait()
+        waited[0] = max(waited[0], count)
 
     smask = head_mask(HEADS * qry, qry, width)
     smask_low = smask.astype(BF16)
@@ -273,38 +290,24 @@
     for e in range(emb):
         macc_s[e] = jnp.zeros((width, width), F32)
         vacc_s[e] = jnp.zeros((width, width), F32)
-        mixacc_s[e] = jnp.zeros((width, width), F32)
-        liftacc_s[e] = jnp.zeros(liftacc_s.shape[1:], F32)
     used = max(first + count for first, count in table.values())
     for at, lo, _, count in cuts(used, CORES * PIECES * piece - used, piece):
         pack_s[at // PIECES, at % PIECES, lo : lo + count] = jnp.zeros((count, width), BF16)
     xin_s[n * lines :] = jnp.zeros((xin_s.shape[0] - n * lines, width), BF16)
-    loads[0].wait()
-    loads[1].wait()
+    ready(3)
+    embs = [emb_ref[base + s] for s in range(n)]
     for e in range(emb):
         qs = spread(queries[e], smask_low)
         qs_s[e] = qs
         a_s[e] = (mm_bt(key_w[e], qs) * scale).astype(BF16)
 
-    loads[2].wait()
+    ready(4)
     edge = lines // 16 * 16
     inside = lax.broadcasted_iota(jnp.int32, (tall - edge, width), 0) < lines - edge
     for s in range(n):
         x_s[s] = xin_s[lines * s : lines * s + tall]
         last = x_s[s, edge:].astype(F32)
         x_s[s, edge:] = jnp.where(inside, last, 0.0).astype(BF16)
-
-    loads[3].wait()
-    loads[4].wait()
-    loads[5].wait()
-    loads[6].wait()
-    for s, e in enumerate(embs):
-        lifted = mm(p_s[s].reshape(steps * ptok, -1), lift_w[e])
-        act, dact = gelu_parts(lifted)
-        act_low = act.astype(BF16)
-        act_s[s] = act_low
-        dact_s[s] = dact
-        tok_s[s, :, qry:] = mm(act_low, mix_w[e]).astype(BF16).reshape(steps, ptok, width)
 
     first_step = lax.broadcasted_iota(jnp.int32, (tall, width), 0) % steps == 0
 
@@ -344,12 +347,35 @@
         for t in range(steps):
             satt_s[s, t] = fold(values[width * t : width * (t + 1)], smask).astype(BF16)
 
+    ready(6)
     staged(n, stem_scores, stem_softmax, stem_moments, stem_values)
-    loads[7].wait()
+    ready(9)
+    emb_rows = jnp.concatenate([jnp.full((steps * ptok, width), e) for e in embs], axis=0)
+    lift_cat = jnp.concatenate([lift_w[e] for e in range(emb)], axis=1)
+    mix_cat = jnp.concatenate([mix_w[e] for e in range(emb)], axis=1)
+
+    def own_columns(values):
+        result = values[:, :width]
+        for e in range(1, emb):
+            result = jnp.where(emb_rows == e, values[:, width * e : width * (e + 1)], result)
+        return result
+
+    def spread_columns(values):
+        parts = [jnp.where(emb_rows == e, values, 0.0).astype(BF16) for e in range(emb)]
+        return jnp.concatenate(parts, axis=1)
+
+    prop_rows = p_s[...].reshape(n * steps * ptok, -1)
+    act, dact = gelu_parts(own_columns(mm(prop_rows, lift_cat)))
+    act_s[...] = act.astype(BF16)
+    dact_s[...] = dact
+    prop_tok = own_columns(mm(act_s[...], mix_cat)).astype(BF16)
+    tok_s[:, :, qry:] = prop_tok.reshape(n, steps, ptok, width)
+
+    ready(10)
     image_tok = mm(satt_s[...].reshape(n * steps * qry, width), stem_proj[...])
     tok_s[:, :, :qry] = image_tok.astype(BF16).reshape(n, steps, qry, width)
 
-    loads[8].wait()
+    ready(len(loads))
     chunk = CORES * ctx
     spans = [pl.ds(i * chunk, chunk) for i in range(rows // chunk)]
     again_row = again[...].astype(F32).reshape(1, width)
@@ -391,53 +417,71 @@
 
     staged(n, trunk_scores, trunk_softmax, trunk_values)
 
-    for load in loads[9:]:
-        load.wait()
     row_step = lax.broadcasted_iota(jnp.int32, (ctx, 1), 0) // half_tok
-    mgain_sum = jnp.zeros((1, width), F32)
-    mbias_sum = jnp.zeros((1, width), F32)
-    downb_sum = jnp.zeros((1, width), F32)
-    upb_sum = jnp.zeros((1, ffw), F32)
-    for i, span in enumerate(spans):
+    sums = {name: jnp.zeros((1, width), F32) for name in ("mgain", "mbias", "downb")}
+    sums["upb"] = jnp.zeros((1, ffw), F32)
+
+    def total(name, values):
+        sums[name] += jnp.sum(values, axis=0, keepdims=True)
+
+    def live_rows(i):
+        parts = [row_step < steps_ref[base + CORES * i + j] for j in range(CORES)]
+        return jnp.concatenate([jnp.where(part, 1.0, 0.0).astype(F32) for part in parts], axis=0)
+
+    def mlp_in(i):
+        span = spans[i]
         middle = tokens_of(i) + mm(att_s[span], aproj[...])
+        mid_s[span] = middle
         hat, rstd = norm_parts(middle)
         hat2_s[span] = hat
         rstd2_s[span] = jnp.broadcast_to(rstd, hat.shape)
         norm2 = (hat * mgain_row + mbias_row).astype(BF16)
         norm2_s[span] = norm2
-        act, dact = gelu_parts(mm(norm2, up_w[...]) + upb_row)
-        act_low = act.astype(BF16)
-        up_s[span] = act_low
-        live = jnp.concatenate(
-            [
-                jnp.where(row_step < steps_ref[base + CORES * i + j], 1.0, 0.0).astype(F32)
-                for j in range(CORES)
-            ],
-            axis=0,
-        )
-        result = (middle + mm(act_low, down_w[...]) + downb_row) * live
-        blk_s[CORES * i : CORES * (i + 1)] = result.astype(BF16).reshape(CORES, steps, half_tok, width)
-        grad = g_s[CORES * i : CORES * (i + 1)].reshape(chunk, width).astype(F32) * live
+        pre_s[span] = mm(norm2, up_w[...]) + upb_row
+
+    def mlp_gelu(i):
+        span = spans[i]
+        act, dact = gelu_parts(pre_s[span])
+        up_s[span] = act.astype(BF16)
+        pre_s[span] = dact
+
+    def mlp_back(i):
+        span = spans[i]
+        grad = g_s[CORES * i : CORES * (i + 1)].reshape(chunk, width).astype(F32) * live_rows(i)
         grad_low = grad.astype(BF16)
         glow_s[span] = grad_low
-        downb_sum += jnp.sum(grad, axis=0, keepdims=True)
+        total("downb", grad)
         grad_up = mm_bt(grad_low, down_w[...]).astype(BF16).astype(F32)
-        grad_pre = (grad_up * dact).astype(BF16)
+        grad_pre = (grad_up * pre_s[span]).astype(BF16)
         gpre_s[span] = grad_pre
-        upb_sum += jnp.sum(grad_pre.astype(F32), axis=0, keepdims=True)
-        grad_norm2 = mm_bt(grad_pre, up_w[...]).astype(BF16).astype(F32)
-        mgain_sum += jnp.sum(grad_norm2 * hat, axis=0, keepdims=True)
-        mbias_sum += jnp.sum(grad_norm2, axis=0, keepdims=True)
-        grad_mid = norm_grad(grad_norm2, mgain_row, hat, rstd) + grad
+        total("upb", grad_pre.astype(F32))
+
+    def mlp_norm_back(i):
+        span = spans[i]
+        grad_norm2 = mm_bt(gpre_s[span], up_w[...]).astype(BF16).astype(F32)
+        hat = hat2_s[span]
+        total("mgain", grad_norm2 * hat)
+        total("mbias", grad_norm2)
+        grad_mid = norm_grad(grad_norm2, mgain_row, hat, rstd2_s[span]) + glow_s[span].astype(F32)
         gn2_s[span] = grad_mid
         grad_mid_low = grad_mid.astype(BF16)
         gmid_s[span] = grad_mid_low
         gatt_s[span] = mm_bt(grad_mid_low, aproj[...]).astype(BF16)
+
+    def mlp_out(i):
+        span = spans[i]
+        result = (mid_s[span] + mm(up_s[span], down_w[...]) + downb_row) * live_rows(i)
+        blk_s[CORES * i : CORES * (i + 1)] = result.astype(BF16).reshape(CORES, steps, half_tok, width)
+
+    staged(len(spans), mlp_in, mlp_gelu, mlp_back, mlp_norm_back, mlp_out)
+
     put("aproj", 0, mm_at(att_s[...], gmid_s[...]))
-    put("down", 0, mm_at(up_s[...], glow_s[...]))
+    down = mm_at(glow_s[...], up_s[...]).astype(BF16)
+    up = mm_at(norm2_s[...], gpre_s[...])
     for j in range(ffw // width):
         cols = slice(width * j, width * (j + 1))
-        put("up", width * j, mm_at(norm2_s[...], gpre_s[:, cols]))
+        put("down", width * j, down[:, cols].T)
+        put("up", width * j, up[:, cols])
 
     def trunk_back_probs(s):
         _, _, value = trunk_rows(s)
@@ -466,21 +510,23 @@
         abias_sum += jnp.sum(grad_norm1, axis=0, keepdims=True)
         grad_tok = norm_grad(grad_norm1, again_row, hat, rstd1_s[span]) + gn2_s[span]
         gtok_s[CORES * i : CORES * (i + 1)] = grad_tok.astype(BF16).reshape(CORES, steps, half_tok, width)
+    qkv = mm_at(norm1_s[...], gqkv_s[...])
     for j in range(3):
-        cols = slice(width * j, width * (j + 1))
-        put("qkv", width * j, mm_at(norm1_s[...], gqkv_s[:, cols]))
-    vectors = [again_sum, abias_sum, mgain_sum, mbias_sum, downb_sum]
-    vectors += [upb_sum[:, width * j : width * (j + 1)] for j in range(ffw // width)]
+        put("qkv", width * j, qkv[:, width * j : width * (j + 1)])
+    vectors = [again_sum, abias_sum, sums["mgain"], sums["mbias"], sums["downb"]]
+    vectors += [sums["upb"][:, width * j : width * (j + 1)] for j in range(ffw // width)]
     vectors += [jnp.zeros((16 - len(vectors), width), F32)]
     put("vectors", 0, jnp.concatenate(vectors, axis=0))
 
-    for s, e in enumerate(embs):
-        grad_prop = gtok_s[s, :, qry:].reshape(steps * ptok, width)
-        mixacc_s[e] += mm_at(act_s[s], grad_prop)
-        grad_act = mm_bt(grad_prop, mix_w[e]).astype(BF16).astype(F32)
-        grad_lift = (grad_act * dact_s[s]).astype(BF16)
-        liftacc_s[e] += mm_at(p_s[s].reshape(steps * ptok, -1), grad_lift)
-        prp_s[s] = mm_bt(grad_lift, lift_w[e]).astype(BF16).reshape(steps, ptok, -1)
+    grad_prop = spread_columns(gtok_s[:, :, qry:].reshape(n * steps * ptok, width).astype(F32))
+    mixer = mm_at(act_s[...], grad_prop)
+    grad_act = mm_bt(grad_prop, mix_cat).astype(BF16).astype(F32)
+    grad_lift = spread_columns((grad_act * dact_s[...]).astype(BF16).astype(F32))
+    lift = mm_at(prop_rows, grad_lift)
+    for e in range(emb):
+        put("mixer", width * e, mixer[:, width * e : width * (e + 1)])
+        put("lift", lift.shape[0] * e, lift[:, width * e : width * (e + 1)])
+    prp_s[...] = mm_bt(grad_lift, lift_cat).astype(BF16).reshape(n, steps, ptok, -1)
 
     grad_img = gtok_s[:, :, :qry].reshape(n * steps * qry, width)
     put("stem", 0, mm_at(satt_s[...].reshape(n * steps * qry, width), grad_img))
@@ -514,28 +560,17 @@
         put("keyw", width * e, mm(moment, qs_s[e]))
         put("queries", qry * e, fold(mm_at(moment, key_w[e]), smask))
         put("valuew", width * e, vacc_s[e])
-        put("mixer", width * e, mixacc_s[e])
-        put("lift", liftacc_s.shape[1] * e, liftacc_s[e])
     other = 1 - sec
     half = own_half()
     image = img_s.reshape(tall // steps, steps, n, width)
-    stores = (
-        (image.at[pl.ds(0, keys), sec], image_out),
-        (image.at[pl.ds(0, keys), other], image_send),
-        (blk_s.at[:, sec], block_out),
-        (blk_s.at[:, other], block_send),
-        (prp_s.at[:, sec], prop_out),
-        (prp_s.at[:, other], prop_send),
-        (pack_s.at[half, pl.ds(0, 2)], keep0),
-        (pack_s.at[half, pl.ds(2, 2)], keep1),
-        (pack_s.at[1 - half, pl.ds(0, 2)], send0),
-        (pack_s.at[1 - half, pl.ds(2, 2)], send1),
-    )
-    stores = [pltpu.make_async_copy(a, b, out_sem.at[i]) for i, (a, b) in enumerate(stores)]
-    for copy in stores:
-        copy.start()
-    for copy in stores:
-        copy.wait()
+    for ref, at in ((image_out, sec), (image_send, other)):
+        ref[...] = image[:keys, at]
+    for ref, at in ((block_out, sec), (block_send, other)):
+        ref[...] = blk_s[:, at]
+    for ref, at in ((prop_out, sec), (prop_send, other)):
+        ref[...] = prp_s[:, at]
+    for ref, at, chain in ((keep0, half, 0), (keep1, half, 1), (send0, 1 - half, 0), (send1, 1 - half, 1)):
+        ref[...] = pack_s[at, 2 * chain : 2 * chain + 2]
 
 
 def rows_of(images):
@@ -564,8 +599,9 @@
     def full(*shape):
         return pltpu.VMEM(shape, F32)
 
-    held = [0, 1, 2, 3, 4, 5, 8, 9, 12, 14]
-    scratch = [low(*weights[i].shape) for i in held]
+    small = (embodiment, ctx_steps, view_mask.T)
+    scratch = [pltpu.SMEM(v.shape, v.dtype) for v in small]
+    scratch += [low(*w.shape) for w in weights]
     scratch += [
         low((n * lines + 31) // 16 * 16, width),
         low(n, tall, width),
@@ -581,8 +617,8 @@
         low(n, width, (steps + 1) * width),
         low(n, width, steps * width),
         low(n, steps, qry, width),
-        low(n, steps * ptok, width),
-        full(n, steps * ptok, width),
+        low(n * steps * ptok, width),
+        full(n * steps * ptok, width),
         full(rows, width),
         full(rows, width),
         low(rows, width),
@@ -591,6 +627,8 @@
         low(n, ctx, HEADS * ctx),
         full(n, ctx, HEADS * ctx),
         low(rows, width),
+        full(rows, width),
+        full(rows, ffw),
         full(rows, width),
         full(rows, width),
         low(rows, width),
@@ -608,33 +646,30 @@
         low(n, steps, ptok, feats),
         full(emb, width, HEADS * qry),
         full(emb, width, width),
-        full(emb, width, width),
-        full(emb, feats, width),
         low(CORES, PIECES, piece, width),
-        pltpu.SemaphoreType.DMA((13,)),
-        pltpu.SemaphoreType.DMA((10,)),
+        pltpu.SemaphoreType.DMA((22,)),
     ]
-    shape = jax.ShapeDtypeStruct
+    inputs = (*small, rows_of(images), proprio, out_grad, *weights)
     return pl.pallas_call(
         functools.partial(compute_kernel, dims),
         out_shape=(
-            shape((2, piece, width), BF16),
-            shape((2, piece, width), BF16),
-            shape((2, piece, width), BF16),
-            shape((2, piece, width), BF16),
-            shape((n, half_tok, width), BF16),
-            shape((n, half_tok, width), BF16),
-            shape((keys, n, width), F32),
-            shape((keys, n, width), F32),
-            shape((n, ptok, feats), BF16),
-            shape((n, ptok, feats), BF16),
+            low(2, piece, width),
+            low(2, piece, width),
+            low(2, piece, width),
+            low(2, piece, width),
+            low(n, half_tok, width),
+            low(n, half_tok, width),
+            full(keys, n, width),
+            full(keys, n, width),
+            low(n, ptok, feats),
+            low(n, ptok, feats),
         ),
-        in_specs=[SMEM] * 3 + [ANY] * 3 + [ANY if i in held else VMEM for i in range(16)],
-        out_specs=(ANY,) * 10,
+        in_specs=[ANY] * 22,
+        out_specs=(VMEM,) * 10,
         scratch_shapes=scratch,
-        compiler_params=pltpu.CompilerParams(vmem_limit_bytes=56 * 2**20),
+        compiler_params=pltpu.CompilerParams(vmem_limit_bytes=40 * 2**20),
         name="stem_trunk",
-    )(embodiment, ctx_steps, view_mask.T, rows_of(images), proprio, out_grad, *weights)
+    )(*(pltpu.with_memory_space_constraint(v, pltpu.HBM) for v in inputs))
 
 
 def parity(index, levels):

time: 54.9 us -> 48.2 us (0.88)
  Pallas kernels: 18.7 us -> 14.6 us
  other arithmetic: 4.69 us -> 2.79 us
  starting transfers between devices: 22.9 us -> 22 us
    pallas_call x1, Pallas kernels: 16 us -> 11.8 us  [compute(): pl.pallas_call(functools.partial(compute_kernel, dims), out_shape=(low(2,...]
    unnamed x2, other arithmetic: 2.59 us -> 0.68 us
    ppermute x12, starting transfers between devices: 20.8 us -> 19.7 us  [swap_chips(): return lax.ppermute(value, ('section', 'dp'), pairs)]
  transfers between devices with their start and end apart: 21 -> 21, of which waited for: 9 -> 10; matrix products, arithmetic and copies ran while one was open for 9% -> 6% of each run, Pallas kernels for 0% -> 0%
where the time goes in v4:
time: 48.2 us; the launch traced here: 48 us
  starting transfers between devices  22 us (46%)
  Pallas kernels  14.6 us (30%)
  waiting for transfers between devices  7.83 us (16%)
  other arithmetic  2.79 us (6%)
  between operations  0.78 us (2%)
    ppermute x12, starting transfers between devices, swap_chips(): return lax.ppermute(value, ('section', 'dp'), pairs)  19.7 us
    pallas_call x1, Pallas kernels, compute(): pl.pallas_call(functools.partial(compute_kernel, dims), out_shape=(low(2,...  11.8 us
    ppermute x12, waiting for transfers between devices, swap_chips(): return lax.ppermute(value, ('section', 'dp'), pairs)  7.51 us
    pallas_call x1, Pallas kernels, unpack(): pl.pallas_call(functools.partial(unpack_kernel, table), out_shape=tuple((...  2.75 us
    ppermute x9, starting transfers between devices, swap_cores(): return lax.ppermute(value, 'section', [(0, 1), (1, 0)])  2.37 us
    broadcast_in_dim x1, other arithmetic, per_device(): img = join(img, img_r, 1).astype(BF16).transpose(1, 0, 2)[:, None]  0.98 us
  transfers between devices with their start and end apart: 21, of which 10 were waited for; matrix products, arithmetic and copies ran while one was open for 6% of the time, Pallas kernels for 0%

profile of v4, /device:TPU:0, one launch (start us, length us, event | category | flops | bytes accessed | tf_op | source)
XLA Modules:
  0.0 48.0 jit_solution(11888116736424955868)
XLA Ops:
  0.7 11.8 %stem_trunk.1 = (bf16[2,448,128]{2,1,0:T(8,128)(2,1)S(1)}, bf16[2,448,128]{2,1,0:T(8,128)(2,1)S(1)}, bf16[2,448,128]{2,1,0:T(8,128)(2,1)S(1)}, bf16[2,448,128]{2...) custom-call(s32[16]{0:T(128)} %emb_h.1, ...), custom_call_target="tpu_custom_call" | custom-call | tf_op jit(solution)/shard_map/stem_trunk/pallas_call | solution.py:653
  12.5 0.5 %collective-permute-start.3 = (bf16[2,448,128]{2,1,0:T(8,128)(2,1)S(1)}, bf16[2,448,128]{2,1,0:T(8,128)(2,1)S(1)}, u32[]{:S(2)}, u32[]{:S(2)}) collective-permute-start(bf16[2,448,128]{2,1,0:T(8,128)(2,1)S(1)} %get-tuple-element.52), channel_id=1, source_target_pairs={{0,16},{16,0},{1,17},{17,1},{2,18},{18,2},{3,19},{19,3},{4,20},{20... | collective-permute-start | bytes 688136 | tf_op jit(solution)/shard_map/ppermute | solution.py:702
  13.6 0.5 %collective-permute-start.1 = (bf16[147,8,128]{2,1,0:T(8,128)(2,1)S(1)}, bf16[147,8,128]{2,1,0:T(8,128)(2,1)S(1)}, u32[]{:S(2)}, u32[]{:S(2)}) collective-permute-start(bf16[147,8,128]{2,1,0:T(8,128)(2,1)S(1)} %convert.10), channel_id=1, source_target_pairs={{0,16},{16,0},{1,17},{17,1},{2,18},{18,2},{3,19},{19,3},{4,20},{20... | collective-permute-start | bytes 903176 | tf_op jit(solution)/shard_map/ppermute | solution.py:702
  14.2 0.6 %fusion.4 = bf16[16,1,16,64]{3,2,1,0:T(8,128)(2,1)} fusion(bf16[8,1,16,64]{3,2,0,1:T(8,128)(2,1)S(1)} %bitcast.24, bf16[8,1,16,64]{3,2,0,1:T(8,128)(2,1)S(1)} %bitcast.22, pred[]{:T(512)S(6)} %eq.8), kind=kLoop, calls=%fused_computation.21 | loop fusion | flops 49152 | bytes 65537
  15.0 2.7 %collective-permute-start.4 = (bf16[448,128]{1,0:T(8,128)(2,1)S(1)}, bf16[448,128]{1,0:T(8,128)(2,1)S(1)}, u32[]{:S(2)}, u32[]{:S(2)}) collective-permute-start(bf16[448,128]{1,0:T(8,128)(2,1)S(1)} %select_bitcast_fusion.1), channel_id=1, source_target_pairs={{0,17},{1,19},{2,16},{3,18},{4,22},{5,20},{6,23},{7,21},{8,26},{9,... | collective-permute-start | bytes 344072 | tf_op jit(solution)/shard_map/ppermute | solution.py:713
  17.8 2.3 %collective-permute-done.4 = bf16[448,128]{1,0:T(8,128)(2,1)S(1)} collective-permute-done((bf16[448,128]{1,0:T(8,128)(2,1)S(1)}, bf16[448,128]{1,0:T(8,128)(2,1)S(1)}, u32[]{:S(2)}, u32[]{:S(2)}) %collective-permute-start.4) | collective-permute-done | bytes 114720 | tf_op jit(solution)/shard_map/ppermute | solution.py:713
  20.2 2.1 %collective-permute-start.5 = (bf16[224,128]{1,0:T(8,128)(2,1)S(1)}, bf16[224,128]{1,0:T(8,128)(2,1)S(1)}, u32[]{:S(2)}, u32[]{:S(2)}) collective-permute-start(bf16[224,128]{1,0:T(8,128)(2,1)S(1)} %broadcast_select_fusion.1), channel_id=1, source_target_pairs={{0,18},{1,16},{2,19},{3,17},{4,21},{5,23},{6,20},{7,22},{8,25},{9,... | collective-permute-start | bytes 172040 | tf_op jit(solution)/shard_map/ppermute | solution.py:713
  22.4 1.2 %collective-permute-start.11 = (bf16[224,128]{1,0:T(8,128)(2,1)S(1)}, bf16[224,128]{1,0:T(8,128)(2,1)S(1)}, u32[]{:S(2)}, u32[]{:S(2)}) collective-permute-start(bf16[224,128]{1,0:T(8,128)(2,1)S(1)} %broadcast_select_fusion), channel_id=1, source_target_pairs={{0,18},{1,16},{2,19},{3,17},{4,21},{5,23},{6,20},{7,22},{8,25},{9,... | collective-permute-start | bytes 172040 | tf_op jit(solution)/shard_map/ppermute | solution.py:713
  23.6 0.6 %collective-permute-done.5 = bf16[224,128]{1,0:T(8,128)(2,1)S(1)} collective-permute-done((bf16[224,128]{1,0:T(8,128)(2,1)S(1)}, bf16[224,128]{1,0:T(8,128)(2,1)S(1)}, u32[]{:S(2)}, u32[]{:S(2)}) %collective-permute-start.5) | collective-permute-done | bytes 57376 | tf_op jit(solution)/shard_map/ppermute | solution.py:713
  24.2 1.9 %collective-permute-start.6 = (bf16[224,128]{1,0:T(8,128)(2,1)S(1)}, bf16[224,128]{1,0:T(8,128)(2,1)S(1)}, u32[]{:S(2)}, u32[]{:S(2)}) collective-permute-start(bf16[224,128]{1,0:T(8,128)(2,1)S(1)} %add_convert_fusion.7), channel_id=1, source_target_pairs={{0,20},{1,25},{2,26},{3,23},{4,28},{5,17},{6,18},{7,31},{8,16},{9,... | collective-permute-start | bytes 172040 | tf_op jit(solution)/shard_map/ppermute | solution.py:713
  26.1 1.3 %collective-permute-start.12 = (bf16[224,128]{1,0:T(8,128)(2,1)S(1)}, bf16[224,128]{1,0:T(8,128)(2,1)S(1)}, u32[]{:S(2)}, u32[]{:S(2)}) collective-permute-start(bf16[224,128]{1,0:T(8,128)(2,1)S(1)} %add_convert_fusion.4), channel_id=1, source_target_pairs={{0,20},{1,25},{2,26},{3,23},{4,28},{5,17},{6,18},{7,31},{8,16},{9,... | collective-permute-start | bytes 172040 | tf_op jit(solution)/shard_map/ppermute | solution.py:713
  27.4 0.7 %collective-permute-done.6 = bf16[224,128]{1,0:T(8,128)(2,1)S(1)} collective-permute-done((bf16[224,128]{1,0:T(8,128)(2,1)S(1)}, bf16[224,128]{1,0:T(8,128)(2,1)S(1)}, u32[]{:S(2)}, u32[]{:S(2)}) %collective-permute-start.6) | collective-permute-done | bytes 57376 | tf_op jit(solution)/shard_map/ppermute | solution.py:713
  28.1 2.9 %collective-permute-start.7 = (bf16[224,128]{1,0:T(8,128)(2,1)S(1)}, bf16[224,128]{1,0:T(8,128)(2,1)S(1)}, u32[]{:S(2)}, u32[]{:S(2)}) collective-permute-start(bf16[224,128]{1,0:T(8,128)(2,1)S(1)} %add_convert_fusion.6), channel_id=1, source_target_pairs={{0,24},{1,21},{2,22},{3,27},{4,16},{5,29},{6,30},{7,19},{8,28},{9,... | collective-permute-start | bytes 172040 | tf_op jit(solution)/shard_map/ppermute | solution.py:713
  31.1 1.3 %collective-permute-start.13 = (bf16[224,128]{1,0:T(8,128)(2,1)S(1)}, bf16[224,128]{1,0:T(8,128)(2,1)S(1)}, u32[]{:S(2)}, u32[]{:S(2)}) collective-permute-start(bf16[224,128]{1,0:T(8,128)(2,1)S(1)} %add_convert_fusion.3), channel_id=1, source_target_pairs={{0,24},{1,21},{2,22},{3,27},{4,16},{5,29},{6,30},{7,19},{8,28},{9,... | collective-permute-start | bytes 172040 | tf_op jit(solution)/shard_map/ppermute | solution.py:713
  32.4 1.0 %collective-permute-done.7 = bf16[224,128]{1,0:T(8,128)(2,1)S(1)} collective-permute-done((bf16[224,128]{1,0:T(8,128)(2,1)S(1)}, bf16[224,128]{1,0:T(8,128)(2,1)S(1)}, u32[]{:S(2)}, u32[]{:S(2)}) %collective-permute-start.7) | collective-permute-done | bytes 57376 | tf_op jit(solution)/shard_map/ppermute | solution.py:713
  33.4 2.1 %collective-permute-start.8 = (bf16[224,128]{1,0:T(8,128)(2,1)S(1)}, bf16[224,128]{1,0:T(8,128)(2,1)S(1)}, u32[]{:S(2)}, u32[]{:S(2)}) collective-permute-start(bf16[224,128]{1,0:T(8,128)(2,1)S(1)} %add_convert_fusion.5), channel_id=1, source_target_pairs={{0,18},{1,16},{2,19},{3,17},{4,21},{5,23},{6,20},{7,22},{8,25},{9,... | collective-permute-start | bytes 172040 | tf_op jit(solution)/shard_map/ppermute | solution.py:713
  36.0 1.1 %collective-permute-start.14 = (bf16[224,128]{1,0:T(8,128)(2,1)S(1)}, bf16[224,128]{1,0:T(8,128)(2,1)S(1)}, u32[]{:S(2)}, u32[]{:S(2)}) collective-permute-start(bf16[224,128]{1,0:T(8,128)(2,1)S(1)} %add_convert_fusion.2), channel_id=1, source_target_pairs={{0,18},{1,16},{2,19},{3,17},{4,21},{5,23},{6,20},{7,22},{8,25},{9,... | collective-permute-start | bytes 172040 | tf_op jit(solution)/shard_map/ppermute | solution.py:713
  37.4 1.8 %collective-permute-start.15 = (bf16[448,128]{1,0:T(8,128)(2,1)S(1)}, bf16[448,128]{1,0:T(8,128)(2,1)S(1)}, u32[]{:S(2)}, u32[]{:S(2)}) collective-permute-start(bf16[448,128]{1,0:T(8,128)(2,1)S(1)} %maximum_select_fusion.2.refs_0_), channel_id=1, source_target_pairs={{0,17},{1,19},{2,16},{3,18},{4,22},{5,20},{6,23},{7,21},{8,26},{9,... | collective-permute-start | bytes 344072 | tf_op jit(solution)/shard_map/ppermute | solution.py:713
  39.2 0.4 collective-permute-done.14
  39.7 1.2 %collective-permute-start.16 = (bf16[448,128]{1,0:T(8,128)(2,1)S(1)}, bf16[448,128]{1,0:T(8,128)(2,1)S(1)}, u32[]{:S(2)}, u32[]{:S(2)}) collective-permute-start(bf16[448,128]{1,0:T(8,128)(2,1)S(1)} %maximum_select_fusion.3.refs_1_), channel_id=1, source_target_pairs={{0,17},{1,19},{2,16},{3,18},{4,22},{5,20},{6,23},{7,21},{8,26},{9,... | collective-permute-start | bytes 344072 | tf_op jit(solution)/shard_map/ppermute | solution.py:713
  40.9 0.7 %maximum_select_fusion.1 = bf16[16,32,128]{2,1,0:T(8,128)(2,1)} fusion(bf16[8,32,128]{2,1,0:T(8,128)(2,1)S(1)} %collective-permute-done, bf16[8,32,128]{2,1,0:T(8,128)(2,1)S(1)} %get-tuple-element.45, pred[]{:T(512)S(6)} %eq.8), kind=kLoop, calls=%fused_computation.9 | loop fusion | flops 196608 | bytes 262145 | tf_op jit(solution)/shard_map/jit(_where)/select_n | solution.py:718
  42.2 1.7 %collective-permute-done.16.refs_3_ = bf16[448,128]{1,0:T(8,128)(2,1)S(1)} collective-permute-done((bf16[448,128]{1,0:T(8,128)(2,1)S(1)}, bf16[448,128]{1,0:T(8,128)(2,1)S(1)}, u32[]{:S(2)}, u32[]{:S(2)}) %collective-permute-start.16) | collective-permute-done | bytes 114720 | tf_op jit(solution)/shard_map/ppermute | solution.py:713
  44.1 1.0 %fusion.1 = bf16[16,1,147,128]{3,0,2,1:T(8,128)(2,1)} fusion(f32[147,8,128]{2,1,0:T(8,128)S(1)} %get-tuple-element.47, bf16[147,8,128]{2,1,0:T(8,128)(2,1)S(1)} %collective-permute-done.1, pred[]{:T(512)S(6)} %eq.8), kind=kLoop, calls=%fused_computation.2 | loop fusion | flops 2709504 | bytes 1505281 | tf_op jit(solution)/shard_map/broadcast_in_dim | solution.py:827
  45.3 2.7 %unpack.1 = (f32[4,16,128]{2,1,0:T(8,128)}, f32[4,128,128]{2,1,0:T(8,128)}, f32[4,128,128]{2,1,0:T(8,128)}, f32[128,128]{1,0:T(8,128)}, f32[4,64,128]{2,1,0:T(8,...) custom-call(bf16[448,128]{1,0:T(8,128)(2,1)S(1)} %maximum_select_fus, ...), custom_call_target="tpu_custom_call" | custom-call | tf_op jit(solution)/shard_map/unpack/pallas_call | solution.py:781
  (40 shorter events, 3.0 us)
Async XLA Ops:
  12.5 2.4 %collective-permute-start.3 = (bf16[2,448,128]{2,1,0:T(8,128)(2,1)S(1)}, bf16[2,448,128]{2,1,0:T(8,128)(2,1)S(1)}, u32[]{:S(2)}, u32[]{:S(2)}) collective-permute-start(bf16[2,448,128]{2,1,0:T(8,128)(2,1)S(1)} %get-tuple-element.52), channel_id=1, source_target_pairs={{0,16},{16,0},{1,17},{17,1},{2,18},{18,2},{3,19},{19,3},{4,20},{20... | collective-permute-start | bytes 688136 | tf_op jit(solution)/shard_map/ppermute | solution.py:702
  13.0 1.2 %collective-permute-start.2 = (bf16[8,16,64]{2,1,0:T(8,128)(2,1)S(1)}, bf16[8,16,64]{2,1,0:T(8,128)(2,1)S(1)}, u32[]{:S(2)}, u32[]{:S(2)}) collective-permute-start(bf16[8,16,64]{2,1,0:T(8,128)(2,1)S(1)} %get-tuple-element.50), channel_id=1, source_target_pairs={{0,16},{16,0},{1,17},{17,1},{2,18},{18,2},{3,19},{19,3},{4,20},{20... | collective-permute-start | bytes 49160 | tf_op jit(solution)/shard_map/ppermute | solution.py:702
  13.1 27.8 %collective-permute-start = (bf16[8,32,128]{2,1,0:T(8,128)(2,1)S(1)}, bf16[8,32,128]{2,1,0:T(8,128)(2,1)S(1)}, u32[]{:S(2)}, u32[]{:S(2)}) collective-permute-start(bf16[8,32,128]{2,1,0:T(8,128)(2,1)S(1)} %get-tuple-element.46), channel_id=1, source_target_pairs={{0,16},{16,0},{1,17},{17,1},{2,18},{18,2},{3,19},{19,3},{4,20},{20... | collective-permute-start | bytes 196616 | tf_op jit(solution)/shard_map/ppermute | solution.py:702
  13.5 4.1 %collective-permute-start.9 = (bf16[2,448,128]{2,1,0:T(8,128)(2,1)S(1)}, bf16[2,448,128]{2,1,0:T(8,128)(2,1)S(1)}, u32[]{:S(2)}, u32[]{:S(2)}) collective-permute-start(bf16[2,448,128]{2,1,0:T(8,128)(2,1)S(1)} %get-tuple-element.54), channel_id=1, source_target_pairs={{0,16},{16,0},{1,17},{17,1},{2,18},{18,2},{3,19},{19,3},{4,20},{20... | collective-permute-start | bytes 688136 | tf_op jit(solution)/shard_map/ppermute | solution.py:702
  13.6 30.4 %collective-permute-start.1 = (bf16[147,8,128]{2,1,0:T(8,128)(2,1)S(1)}, bf16[147,8,128]{2,1,0:T(8,128)(2,1)S(1)}, u32[]{:S(2)}, u32[]{:S(2)}) collective-permute-start(bf16[147,8,128]{2,1,0:T(8,128)(2,1)S(1)} %convert.10), channel_id=1, source_target_pairs={{0,16},{16,0},{1,17},{17,1},{2,18},{18,2},{3,19},{19,3},{4,20},{20... | collective-permute-start | bytes 903176 | tf_op jit(solution)/shard_map/ppermute | solution.py:702
  15.0 5.1 %collective-permute-start.4 = (bf16[448,128]{1,0:T(8,128)(2,1)S(1)}, bf16[448,128]{1,0:T(8,128)(2,1)S(1)}, u32[]{:S(2)}, u32[]{:S(2)}) collective-permute-start(bf16[448,128]{1,0:T(8,128)(2,1)S(1)} %select_bitcast_fusion.1), channel_id=1, source_target_pairs={{0,17},{1,19},{2,16},{3,18},{4,22},{5,20},{6,23},{7,21},{8,26},{9,... | collective-permute-start | bytes 344072 | tf_op jit(solution)/shard_map/ppermute | solution.py:713
  17.7 4.6 %collective-permute-start.10 = (bf16[448,128]{1,0:T(8,128)(2,1)S(1)}, bf16[448,128]{1,0:T(8,128)(2,1)S(1)}, u32[]{:S(2)}, u32[]{:S(2)}) collective-permute-start(bf16[448,128]{1,0:T(8,128)(2,1)S(1)} %select_bitcast_fusion), channel_id=1, source_target_pairs={{0,17},{1,19},{2,16},{3,18},{4,22},{5,20},{6,23},{7,21},{8,26},{9,... | collective-permute-start | bytes 344072 | tf_op jit(solution)/shard_map/ppermute | solution.py:713
  20.2 4.0 %collective-permute-start.5 = (bf16[224,128]{1,0:T(8,128)(2,1)S(1)}, bf16[224,128]{1,0:T(8,128)(2,1)S(1)}, u32[]{:S(2)}, u32[]{:S(2)}) collective-permute-start(bf16[224,128]{1,0:T(8,128)(2,1)S(1)} %broadcast_select_fusion.1), channel_id=1, source_target_pairs={{0,18},{1,16},{2,19},{3,17},{4,21},{5,23},{6,20},{7,22},{8,25},{9,... | collective-permute-start | bytes 172040 | tf_op jit(solution)/shard_map/ppermute | solution.py:713
  22.4 3.7 %collective-permute-start.11 = (bf16[224,128]{1,0:T(8,128)(2,1)S(1)}, bf16[224,128]{1,0:T(8,128)(2,1)S(1)}, u32[]{:S(2)}, u32[]{:S(2)}) collective-permute-start(bf16[224,128]{1,0:T(8,128)(2,1)S(1)} %broadcast_select_fusion), channel_id=1, source_target_pairs={{0,18},{1,16},{2,19},{3,17},{4,21},{5,23},{6,20},{7,22},{8,25},{9,... | collective-permute-start | bytes 172040 | tf_op jit(solution)/shard_map/ppermute | solution.py:713
  24.2 3.9 %collective-permute-start.6 = (bf16[224,128]{1,0:T(8,128)(2,1)S(1)}, bf16[224,128]{1,0:T(8,128)(2,1)S(1)}, u32[]{:S(2)}, u32[]{:S(2)}) collective-permute-start(bf16[224,128]{1,0:T(8,128)(2,1)S(1)} %add_convert_fusion.7), channel_id=1, source_target_pairs={{0,20},{1,25},{2,26},{3,23},{4,28},{5,17},{6,18},{7,31},{8,16},{9,... | collective-permute-start | bytes 172040 | tf_op jit(solution)/shard_map/ppermute | solution.py:713
  26.1 5.0 %collective-permute-start.12 = (bf16[224,128]{1,0:T(8,128)(2,1)S(1)}, bf16[224,128]{1,0:T(8,128)(2,1)S(1)}, u32[]{:S(2)}, u32[]{:S(2)}) collective-permute-start(bf16[224,128]{1,0:T(8,128)(2,1)S(1)} %add_convert_fusion.4), channel_id=1, source_target_pairs={{0,20},{1,25},{2,26},{3,23},{4,28},{5,17},{6,18},{7,31},{8,16},{9,... | collective-permute-start | bytes 172040 | tf_op jit(solution)/shard_map/ppermute | solution.py:713
  28.1 5.3 %collective-permute-start.7 = (bf16[224,128]{1,0:T(8,128)(2,1)S(1)}, bf16[224,128]{1,0:T(8,128)(2,1)S(1)}, u32[]{:S(2)}, u32[]{:S(2)}) collective-permute-start(bf16[224,128]{1,0:T(8,128)(2,1)S(1)} %add_convert_fusion.6), channel_id=1, source_target_pairs={{0,24},{1,21},{2,22},{3,27},{4,16},{5,29},{6,30},{7,19},{8,28},{9,... | collective-permute-start | bytes 172040 | tf_op jit(solution)/shard_map/ppermute | solution.py:713
  31.1 4.8 %collective-permute-start.13 = (bf16[224,128]{1,0:T(8,128)(2,1)S(1)}, bf16[224,128]{1,0:T(8,128)(2,1)S(1)}, u32[]{:S(2)}, u32[]{:S(2)}) collective-permute-start(bf16[224,128]{1,0:T(8,128)(2,1)S(1)} %add_convert_fusion.3), channel_id=1, source_target_pairs={{0,24},{1,21},{2,22},{3,27},{4,16},{5,29},{6,30},{7,19},{8,28},{9,... | collective-permute-start | bytes 172040 | tf_op jit(solution)/shard_map/ppermute | solution.py:713
  33.4 3.9 %collective-permute-start.8 = (bf16[224,128]{1,0:T(8,128)(2,1)S(1)}, bf16[224,128]{1,0:T(8,128)(2,1)S(1)}, u32[]{:S(2)}, u32[]{:S(2)}) collective-permute-start(bf16[224,128]{1,0:T(8,128)(2,1)S(1)} %add_convert_fusion.5), channel_id=1, source_target_pairs={{0,18},{1,16},{2,19},{3,17},{4,21},{5,23},{6,20},{7,22},{8,25},{9,... | collective-permute-start | bytes 172040 | tf_op jit(solution)/shard_map/ppermute | solution.py:713
  36.0 3.7 %collective-permute-start.14 = (bf16[224,128]{1,0:T(8,128)(2,1)S(1)}, bf16[224,128]{1,0:T(8,128)(2,1)S(1)}, u32[]{:S(2)}, u32[]{:S(2)}) collective-permute-start(bf16[224,128]{1,0:T(8,128)(2,1)S(1)} %add_convert_fusion.2), channel_id=1, source_target_pairs={{0,18},{1,16},{2,19},{3,17},{4,21},{5,23},{6,20},{7,22},{8,25},{9,... | collective-permute-start | bytes 172040 | tf_op jit(solution)/shard_map/ppermute | solution.py:713
  37.4 4.7 %collective-permute-start.15 = (bf16[448,128]{1,0:T(8,128)(2,1)S(1)}, bf16[448,128]{1,0:T(8,128)(2,1)S(1)}, u32[]{:S(2)}, u32[]{:S(2)}) collective-permute-start(bf16[448,128]{1,0:T(8,128)(2,1)S(1)} %maximum_select_fusion.2.refs_0_), channel_id=1, source_target_pairs={{0,17},{1,19},{2,16},{3,18},{4,22},{5,20},{6,23},{7,21},{8,26},{9,... | collective-permute-start | bytes 344072 | tf_op jit(solution)/shard_map/ppermute | solution.py:713
  39.7 4.3 %collective-permute-start.16 = (bf16[448,128]{1,0:T(8,128)(2,1)S(1)}, bf16[448,128]{1,0:T(8,128)(2,1)S(1)}, u32[]{:S(2)}, u32[]{:S(2)}) collective-permute-start(bf16[448,128]{1,0:T(8,128)(2,1)S(1)} %maximum_select_fusion.3.refs_1_), channel_id=1, source_target_pairs={{0,17},{1,19},{2,16},{3,18},{4,22},{5,20},{6,23},{7,21},{8,26},{9,... | collective-permute-start | bytes 344072 | tf_op jit(solution)/shard_map/ppermute | solution.py:713
  41.6 3.5 %collective-permute-start.17 = (bf16[448,128]{1,0:T(8,128)(2,1)S(1)}, bf16[448,128]{1,0:T(8,128)(2,1)S(1)}, u32[]{:S(2)}, u32[]{:S(2)}) collective-permute-start(bf16[448,128]{1,0:T(8,128)(2,1)S(1)} %maximum_select_fusion.2.refs_0_), channel_id=1, source_target_pairs={{0,16},{16,0},{1,17},{17,1},{2,18},{18,2},{3,19},{19,3},{4,20},{20... | collective-permute-start | bytes 344072 | tf_op jit(solution)/shard_map/ppermute | solution.py:702
  41.7 3.3 %collective-permute-start.18 = (bf16[448,128]{1,0:T(8,128)(2,1)S(1)}, bf16[448,128]{1,0:T(8,128)(2,1)S(1)}, u32[]{:S(2)}, u32[]{:S(2)}) collective-permute-start(bf16[448,128]{1,0:T(8,128)(2,1)S(1)} %maximum_select_fusion.3.refs_1_), channel_id=1, source_target_pairs={{0,16},{16,0},{1,17},{17,1},{2,18},{18,2},{3,19},{19,3},{4,20},{20... | collective-permute-start | bytes 344072 | tf_op jit(solution)/shard_map/ppermute | solution.py:702
  42.1 3.0 %collective-permute-start.19 = (bf16[448,128]{1,0:T(8,128)(2,1)S(1)}, bf16[448,128]{1,0:T(8,128)(2,1)S(1)}, u32[]{:S(2)}, u32[]{:S(2)}) collective-permute-start(bf16[448,128]{1,0:T(8,128)(2,1)S(1)} %collective-permute-done.15.refs_2_), channel_id=1, source_target_pairs={{0,16},{16,0},{1,17},{17,1},{2,18},{18,2},{3,19},{19,3},{4,20},{20... | collective-permute-start | bytes 344072 | tf_op jit(solution)/shard_map/ppermute | solution.py:702
  43.9 1.3 %collective-permute-start.20 = (bf16[448,128]{1,0:T(8,128)(2,1)S(1)}, bf16[448,128]{1,0:T(8,128)(2,1)S(1)}, u32[]{:S(2)}, u32[]{:S(2)}) collective-permute-start(bf16[448,128]{1,0:T(8,128)(2,1)S(1)} %collective-permute-done.16.refs_3_), channel_id=1, source_target_pairs={{0,16},{16,0},{1,17},{17,1},{2,18},{18,2},{3,19},{19,3},{4,20},{20... | collective-permute-start | bytes 344072 | tf_op jit(solution)/shard_map/ppermute | solution.py:702

commit v5 on v4

--- a/solution.py
+++ b/solution.py
@@ -163,12 +163,8 @@
     keep1,
     send0,
     send1,
-    block_out,
-    block_send,
-    image_out,
-    image_send,
-    prop_out,
-    prop_send,
+    extra_keep,
+    extra_send,
     emb_ref,
     steps_ref,
     views_ref,
@@ -376,7 +372,8 @@
     tok_s[:, :, :qry] = image_tok.astype(BF16).reshape(n, steps, qry, width)
 
     ready(len(loads))
-    chunk = CORES * ctx
+    group = n
+    chunk = group * ctx
     spans = [pl.ds(i * chunk, chunk) for i in range(rows // chunk)]
     again_row = again[...].astype(F32).reshape(1, width)
     abias_row = abias[...].astype(F32).reshape(1, width)
@@ -386,7 +383,7 @@
     downb_row = down_b[...].astype(F32).reshape(1, width)
 
     def tokens_of(i):
-        return tok_s[CORES * i : CORES * (i + 1)].reshape(chunk, width).astype(F32)
+        return tok_s[group * i : group * (i + 1)].reshape(chunk, width).astype(F32)
 
     for i, span in enumerate(spans):
         hat, rstd = norm_parts(tokens_of(i))
@@ -425,7 +422,7 @@
         sums[name] += jnp.sum(values, axis=0, keepdims=True)
 
     def live_rows(i):
-        parts = [row_step < steps_ref[base + CORES * i + j] for j in range(CORES)]
+        parts = [row_step < steps_ref[base + group * i + j] for j in range(group)]
         return jnp.concatenate([jnp.where(part, 1.0, 0.0).astype(F32) for part in parts], axis=0)
 
     def mlp_in(i):
@@ -447,7 +444,7 @@
 
     def mlp_back(i):
         span = spans[i]
-        grad = g_s[CORES * i : CORES * (i + 1)].reshape(chunk, width).astype(F32) * live_rows(i)
+        grad = g_s[group * i : group * (i + 1)].reshape(chunk, width).astype(F32) * live_rows(i)
         grad_low = grad.astype(BF16)
         glow_s[span] = grad_low
         total("downb", grad)
@@ -471,7 +468,7 @@
     def mlp_out(i):
         span = spans[i]
         result = (mid_s[span] + mm(up_s[span], down_w[...]) + downb_row) * live_rows(i)
-        blk_s[CORES * i : CORES * (i + 1)] = result.astype(BF16).reshape(CORES, steps, half_tok, width)
+        blk_s[group * i : group * (i + 1)] = result.astype(BF16).reshape(group, steps, half_tok, width)
 
     staged(len(spans), mlp_in, mlp_gelu, mlp_back, mlp_norm_back, mlp_out)
 
@@ -509,7 +506,7 @@
         again_sum += jnp.sum(grad_norm1 * hat, axis=0, keepdims=True)
         abias_sum += jnp.sum(grad_norm1, axis=0, keepdims=True)
         grad_tok = norm_grad(grad_norm1, again_row, hat, rstd1_s[span]) + gn2_s[span]
-        gtok_s[CORES * i : CORES * (i + 1)] = grad_tok.astype(BF16).reshape(CORES, steps, half_tok, width)
+        gtok_s[group * i : group * (i + 1)] = grad_tok.astype(BF16).reshape(group, steps, half_tok, width)
     qkv = mm_at(norm1_s[...], gqkv_s[...])
     for j in range(3):
         put("qkv", width * j, qkv[:, width * j : width * (j + 1)])
@@ -563,12 +560,12 @@
     other = 1 - sec
     half = own_half()
     image = img_s.reshape(tall // steps, steps, n, width)
-    for ref, at in ((image_out, sec), (image_send, other)):
-        ref[...] = image[:keys, at]
-    for ref, at in ((block_out, sec), (block_send, other)):
-        ref[...] = blk_s[:, at]
-    for ref, at in ((prop_out, sec), (prop_send, other)):
-        ref[...] = prp_s[:, at]
+    first, second = keys * n, keys * n + n * half_tok
+    for ref, at in ((extra_keep, sec), (extra_send, other)):
+        ref[:first] = image[:keys, at].reshape(first, width).astype(BF16)
+        ref[first:second] = blk_s[:, at].reshape(second - first, width)
+        ref[second:, : prp_s.shape[3]] = prp_s[:, at].reshape(n * ptok, -1)
+        ref[second:, prp_s.shape[3] :] = jnp.zeros((n * ptok, width - prp_s.shape[3]), BF16)
     for ref, at, chain in ((keep0, half, 0), (keep1, half, 1), (send0, 1 - half, 0), (send1, 1 - half, 1)):
         ref[...] = pack_s[at, 2 * chain : 2 * chain + 2]
 
@@ -657,15 +654,11 @@
             low(2, piece, width),
             low(2, piece, width),
             low(2, piece, width),
-            low(n, half_tok, width),
-            low(n, half_tok, width),
-            full(keys, n, width),
-            full(keys, n, width),
-            low(n, ptok, feats),
-            low(n, ptok, feats),
+            low(keys * n + n * half_tok + n * ptok, width),
+            low(keys * n + n * half_tok + n * ptok, width),
         ),
         in_specs=[ANY] * 22,
-        out_specs=(VMEM,) * 10,
+        out_specs=(VMEM,) * 6,
         scratch_shapes=scratch,
         compiler_params=pltpu.CompilerParams(vmem_limit_bytes=40 * 2**20),
         name="stem_trunk",
@@ -713,120 +706,104 @@
     return lax.ppermute(value, ("section", "dp"), pairs)
 
 
-def join(own, came, axis):
-    first = lax.axis_index("section") == 0
-    return jnp.where(first, jnp.concatenate([own, came], axis), jnp.concatenate([came, own], axis))
-
-
-def unpack_kernel(table, *refs):
-    pieces, outs, (pack, sem) = refs[:8], refs[8:-2], refs[-2:]
-    own = own_half()
+def finish_kernel(table, pack, blk, img, prp, *refs):
+    count = len(refs) // 2 - 2
+    outs, held, sem = refs[: count + 3], refs[count + 3 : -1], refs[-1]
     copies = []
-    for i, ref in enumerate(pieces):
-        half = own if i < PIECES else 1 - own
-        first = own_bits(half)[0]
-        chain, far = i % CHAINS, i // CHAINS % 2
-        at = half * PIECES + chain * 2 + (first ^ far)
-        copies.append(pltpu.make_async_copy(ref, pack.at[at], sem.at[i]))
-    for copy in copies:
+
+    def send(source, target):
+        copy = pltpu.make_async_copy(source, target, sem.at[len(copies)])
         copy.start()
+        copies.append(copy)
+
+    for source, target in zip((blk, img, prp), outs):
+        send(source, target)
+    names = ("queries", "keyw", "valuew", "stem", "lift", "mixer", "again", "abias", "qkv", "aproj")
+    names += ("mgain", "mbias", "up", "upb", "down", "downb")
+    vectors = pack[pl.ds(table["vectors"][0], 16)].astype(F32)
+    width = pack.shape[1]
+    rows = {"again": 0, "abias": 1, "mgain": 2, "mbias": 3, "downb": 4}
+    order = sorted(range(count), key=lambda i: table.get(names[i], (1 << 30,))[0])
+    for i in order:
+        name, ref = names[i], held[i]
+        if name in rows:
+            ref[...] = vectors[rows[name]]
+        elif name == "upb":
+            for j in range(ref.shape[0] // width):
+                ref[width * j : width * (j + 1)] = vectors[5 + j]
+        else:
+            first, total = table[name]
+            wide = ref.shape[-1] // width
+            for j in range(wide):
+                part = pack[first + total // wide * j : first + total // wide * (j + 1)].astype(F32)
+                if ref.ndim == 3:
+                    ref[...] = part.reshape(ref.shape)
+                else:
+                    ref[:, width * j : width * (j + 1)] = part
+        send(ref, outs[3 + i])
     for copy in copies:
         copy.wait()
-    piece = pack.shape[1]
-
-    def get(name, row, count, store):
-        for at, lo, done, size in cuts(table[name][0] + row, count, piece):
-            store(done, size, pack[at, lo : lo + size].astype(F32))
-
-    def flat(ref, name):
-        def store(done, size, value):
-            ref[done : done + size] = value
-
-        get(name, 0, ref.shape[0], store)
-
-    def stacked(ref, name):
-        for e in range(ref.shape[0]):
-
-            def store(done, size, value, e=e):
-                ref[e, done : done + size] = value
-
-            get(name, e * ref.shape[1], ref.shape[1], store)
-
-    def blocks(ref, name):
-        depth, width = ref.shape[0], pack.shape[2]
-        for j in range(ref.shape[1] // width):
-
-            def store(done, size, value, j=j):
-                ref[done : done + size, width * j : width * (j + 1)] = value
-
-            get(name, j * depth, depth, store)
-
-    q, k, v, stem, lift, mix, again, abias, qkv, aproj, mgain, mbias, up, upb, down, downb = outs
-    for ref, name in ((q, "queries"), (k, "keyw"), (v, "valuew"), (lift, "lift"), (mix, "mixer")):
-        stacked(ref, name)
-    for ref, name in ((stem, "stem"), (aproj, "aproj"), (down, "down")):
-        flat(ref, name)
-    for ref, name in ((qkv, "qkv"), (up, "up")):
-        blocks(ref, name)
-    at, lo, _, _ = next(cuts(table["vectors"][0], 16, piece))
-    vectors = pack[at, lo : lo + 16].astype(F32)
-    width = pack.shape[2]
-    for i, ref in enumerate((again, abias, mgain, mbias, downb)):
-        ref[...] = vectors[i]
-    for j in range(upb.shape[0] // width):
-        upb[width * j : width * (j + 1)] = vectors[5 + j]
-
-
-def unpack(pieces, table, shapes):
+
+
+def finish(table, pack, blk, img, prp, shapes):
+    inputs = (pack, blk, img, prp)
     return pl.pallas_call(
-        functools.partial(unpack_kernel, table),
-        out_shape=tuple(jax.ShapeDtypeStruct(s, F32) for s in shapes),
-        in_specs=[ANY] * 8,
-        out_specs=(VMEM,) * len(shapes),
-        scratch_shapes=[
-            pltpu.VMEM((CORES * PIECES,) + pieces[0].shape, BF16),
-            pltpu.SemaphoreType.DMA((8,)),
-        ],
-        compiler_params=pltpu.CompilerParams(vmem_limit_bytes=32 * 2**20),
-        name="unpack",
-    )(*pieces)
-
-
-def sum_chips(held, came):
+        functools.partial(finish_kernel, table),
+        out_shape=tuple(jax.ShapeDtypeStruct(v.shape, BF16) for v in inputs[1:])
+        + tuple(jax.ShapeDtypeStruct(v, F32) for v in shapes),
+        in_specs=[VMEM] * 4,
+        out_specs=(ANY,) * (3 + len(shapes)),
+        scratch_shapes=[pltpu.VMEM(v, F32) for v in shapes]
+        + [pltpu.SemaphoreType.DMA((3 + len(shapes),))],
+        compiler_params=pltpu.CompilerParams(vmem_limit_bytes=24 * 2**20),
+        name="finish",
+    )(*(pltpu.with_memory_space_constraint(v, pltpu.VMEM) for v in inputs))
+
+
+def sum_chips(held, came, extra):
     levels = lax.axis_size("dp").bit_length() - 1
     first, second = (0, 1), (1, 0)
-    one, two = own_bits(own_half())
+    half = own_half()
+    one, two = own_bits(half)
     totals = [add(a, b) for a, b in zip(held, came)]
+    *totals[1:], extra = lax.optimization_barrier((*totals[1:], extra))
     for bit, bits in ((one, first), (two, second)):
         split = [t.reshape((2, -1, t.shape[-1])) for t in totals]
         sent = [swap_chips(select(bit, t[1], t[0]), bits) for t in split]
         totals = [add(select(bit, t[0], t[1]), c) for t, c in zip(split, sent)]
+    extra = swap_cores(extra)
     for bits in zip(range(2, levels), reversed(range(2, levels))):
         sent = [swap_chips(t, bits) for t in totals]
         totals = [add(t, c) for t, c in zip(totals, sent)]
     sent = [swap_chips(t, second) for t in totals]
-    near = [
-        select(two, jnp.concatenate([t, c]), jnp.concatenate([c, t])) for t, c in zip(totals, sent)
-    ]
+    near = [either(two, t, c) for t, c in zip(totals, sent)]
     far = [swap_chips(t, first) for t in near]
-    return tuple(near) + tuple(far)
+    own = [either(one, *v) for v in zip(near, far)]
+    bit = own_bits(1 - half)[0]
+    other = [either(bit, *v) for v in zip(*([swap_cores(t) for t in v] for v in (near, far)))]
+    return either(half, jnp.concatenate(own), jnp.concatenate(other)), extra
+
+
+def either(bit, mine, came, axis=0):
+    return select(bit, jnp.concatenate([mine, came], axis), jnp.concatenate([came, mine], axis))
 
 
 def per_device(*args):
-    weights = args[5:21]
+    images, proprio, weights = args[0], args[1], args[5:21]
     emb, qry, width = weights[0].shape
+    n, keys = images.shape[0] // CORES, images.shape[2]
+    ptok, feats = proprio.shape[2:]
     table, total = layout(width, weights[12].shape[1], emb, qry, weights[4].shape[1])
-    *packed, blk, blk_s, img, img_s, prp, prp_s = compute(args, table, total)
+    *packed, extra, extra_sent = compute(args, table, total)
     keep, send = packed[:CHAINS], packed[CHAINS:]
-    came = [swap_cores(v) for v in send]
-    blk_r, img_r, prp_r = (swap_cores(v) for v in (blk_s, img_s, prp_s))
-    pieces = sum_chips(keep, came)
-    pieces += tuple(swap_cores(v) for v in pieces)
-    blk = join(blk, blk_r, 0)
-    prp = join(prp, prp_r, 0)[:, None]
-    img = join(img, img_r, 1).astype(BF16).transpose(1, 0, 2)[:, None]
-    grads = unpack(pieces, table, [w.shape for w in weights])
-    return (blk, img, prp) + tuple(grads)
+    pack, came = sum_chips(keep, [swap_cores(v) for v in send], extra_sent)
+    sec = lax.axis_index("section")
+    first, second = keys * n, keys * n + n * (qry + ptok)
+    img = either(sec, *(v[:first].reshape(keys, n, width) for v in (extra, came)), 1)
+    blk = either(sec, *(v[first:second].reshape(n, -1, width) for v in (extra, came)))
+    prp = either(sec, *(v[second:, :feats].reshape(n, ptok, feats) for v in (extra, came)))
+    blk, img, prp, *grads = finish(table, pack, blk, img, prp, [w.shape for w in weights])
+    return (blk, img.transpose(1, 0, 2)[:, None], prp[:, None]) + tuple(grads)
 
 
 def solution(mesh):

time: 48.2 us -> 46.3 us (0.961)
  waiting for transfers between devices: 7.83 us -> 9.87 us
  Pallas kernels: 14.6 us -> 13 us
  other arithmetic: 2.79 us -> 1.22 us
  starting transfers between devices: 22 us -> 21.2 us
    ppermute x9 -> x7, waiting for transfers between devices: 0.32 us -> 1.77 us  [swap_cores(): return lax.ppermute(value, 'section', [(0, 1), (1, 0)])]
    pallas_call x1, Pallas kernels: 2.75 us -> 1.66 us  [finish(): pl.pallas_call(functools.partial(finish_kernel, table), out_shape=tuple((...]
    broadcast_in_dim x1 -> x0, other arithmetic: 0.98 us -> none  [per_device(): img = join(img, img_r, 1).astype(BF16).transpose(1, 0, 2)[:, None]]
    select_n x6 -> x14, other arithmetic: 0.11 us -> 0.87 us  [select(): return jnp.where(bit == 0, low, high)]
    unnamed x2 -> x0, other arithmetic: 0.68 us -> none
    select_n x1 -> x0, other arithmetic: 0.67 us -> none  [join(): jnp.where(first, jnp.concatenate([own, came], axis), jnp.concatenate([cam...]
    ppermute x12, starting transfers between devices: 19.7 us -> 19 us  [swap_chips(): return lax.ppermute(value, ('section', 'dp'), pairs)]
    ppermute x12, waiting for transfers between devices: 7.51 us -> 8.09 us  [swap_chips(): return lax.ppermute(value, ('section', 'dp'), pairs)]
  transfers between devices with their start and end apart: 21 -> 19, of which waited for: 10 -> 11; matrix products, arithmetic and copies ran while one was open for 6% -> 2% of each run, Pallas kernels for 0% -> 0%
where the time goes in v5:
time: 46.3 us; the launch traced here: 46.1 us
  starting transfers between devices  21.2 us (46%)
  Pallas kernels  13 us (28%)
  waiting for transfers between devices  9.87 us (21%)
  other arithmetic  1.22 us (3%)
  between operations  0.88 us (2%)
    ppermute x12, starting transfers between devices, swap_chips(): return lax.ppermute(value, ('section', 'dp'), pairs)  19 us
    pallas_call x1, Pallas kernels, compute(): pl.pallas_call(functools.partial(compute_kernel, dims), out_shape=(low(2,...  11.3 us
    ppermute x12, waiting for transfers between devices, swap_chips(): return lax.ppermute(value, ('section', 'dp'), pairs)  8.09 us
    ppermute x7, starting transfers between devices, swap_cores(): return lax.ppermute(value, 'section', [(0, 1), (1, 0)])  2.11 us
    ppermute x7, waiting for transfers between devices, swap_cores(): return lax.ppermute(value, 'section', [(0, 1), (1, 0)])  1.77 us
    pallas_call x1, Pallas kernels, finish(): pl.pallas_call(functools.partial(finish_kernel, table), out_shape=tuple((...  1.66 us
  transfers between devices with their start and end apart: 19, of which 11 were waited for; matrix products, arithmetic and copies ran while one was open for 2% of the time, Pallas kernels for 0%

profile of v5, /device:TPU:0, one launch (start us, length us, event | category | flops | bytes accessed | tf_op | source)
XLA Modules:
  0.0 46.1 jit_solution(18073464543672151951)
XLA Ops:
  0.7 11.3 %stem_trunk.1 = (bf16[2,448,128]{2,1,0:T(8,128)(2,1)S(1)}, bf16[2,448,128]{2,1,0:T(8,128)(2,1)S(1)}, bf16[2,448,128]{2,1,0:T(8,128)(2,1)S(1)}, bf16[2,448,128]{2...) custom-call(s32[16]{0:T(128)} %emb_h.1, s32[16]{0:T(128)} %steps_h.1, ...), custom_call_target="tpu_custom_call" | custom-call | tf_op jit(solution)/shard_map/stem_trunk/pallas_call | solution.py:650
  12.0 0.5 %collective-permute-start = (bf16[2,448,128]{2,1,0:T(8,128)(2,1)S(1)}, bf16[2,448,128]{2,1,0:T(8,128)(2,1)S(1)}, u32[]{:S(2)}, u32[]{:S(2)}) collective-permute-start(bf16[2,448,128]{2,1,0:T(8,128)(2,1)S(1)} %get-tuple-element.47), channel_id=1, source_target_pairs={{0,16},{16,0},{1,17},{17,1},{2,18},{18,2},{3,19},{19,3},{4,20},{20... | collective-permute-start | bytes 688136 | tf_op jit(solution)/shard_map/ppermute | solution.py:695
  12.6 1.0 %collective-permute-done = bf16[2,448,128]{2,1,0:T(8,128)(2,1)S(1)} collective-permute-done((bf16[2,448,128]{2,1,0:T(8,128)(2,1)S(1)}, bf16[2,448,128]{2,1,0:T(8,128)(2,1)S(1)}, u32[]{:S(2)}, u32[]{:S(2)}) %collective-permute-start) | collective-permute-done | bytes 229408 | tf_op jit(solution)/shard_map/ppermute | solution.py:695
  13.7 2.7 %collective-permute-start.1 = (bf16[448,128]{1,0:T(8,128)(2,1)S(1)}, bf16[448,128]{1,0:T(8,128)(2,1)S(1)}, u32[]{:S(2)}, u32[]{:S(2)}) collective-permute-start(bf16[448,128]{1,0:T(8,128)(2,1)S(1)} %select_bitcast_fusion.1), channel_id=1, source_target_pairs={{0,17},{1,19},{2,16},{3,18},{4,22},{5,20},{6,23},{7,21},{8,26},{9,... | collective-permute-start | bytes 344072 | tf_op jit(solution)/shard_map/ppermute | solution.py:706
  17.1 1.7 %collective-permute-done.1 = bf16[448,128]{1,0:T(8,128)(2,1)S(1)} collective-permute-done((bf16[448,128]{1,0:T(8,128)(2,1)S(1)}, bf16[448,128]{1,0:T(8,128)(2,1)S(1)}, u32[]{:S(2)}, u32[]{:S(2)}) %collective-permute-start.1) | collective-permute-done | bytes 114720 | tf_op jit(solution)/shard_map/ppermute | solution.py:706
  18.9 2.1 %collective-permute-start.2 = (bf16[224,128]{1,0:T(8,128)(2,1)S(1)}, bf16[224,128]{1,0:T(8,128)(2,1)S(1)}, u32[]{:S(2)}, u32[]{:S(2)}) collective-permute-start(bf16[224,128]{1,0:T(8,128)(2,1)S(1)} %broadcast_select_fusion.1), channel_id=1, source_target_pairs={{0,18},{1,16},{2,19},{3,17},{4,21},{5,23},{6,20},{7,22},{8,25},{9,... | collective-permute-start | bytes 172040 | tf_op jit(solution)/shard_map/ppermute | solution.py:706
  21.1 1.2 %collective-permute-start.9 = (bf16[224,128]{1,0:T(8,128)(2,1)S(1)}, bf16[224,128]{1,0:T(8,128)(2,1)S(1)}, u32[]{:S(2)}, u32[]{:S(2)}) collective-permute-start(bf16[224,128]{1,0:T(8,128)(2,1)S(1)} %broadcast_select_fusion), channel_id=1, source_target_pairs={{0,18},{1,16},{2,19},{3,17},{4,21},{5,23},{6,20},{7,22},{8,25},{9,... | collective-permute-start | bytes 172040 | tf_op jit(solution)/shard_map/ppermute | solution.py:706
  22.4 0.5 %collective-permute-done.2 = bf16[224,128]{1,0:T(8,128)(2,1)S(1)} collective-permute-done((bf16[224,128]{1,0:T(8,128)(2,1)S(1)}, bf16[224,128]{1,0:T(8,128)(2,1)S(1)}, u32[]{:S(2)}, u32[]{:S(2)}) %collective-permute-start.2) | collective-permute-done | bytes 57376 | tf_op jit(solution)/shard_map/ppermute | solution.py:706
  22.9 1.9 %collective-permute-start.3 = (bf16[224,128]{1,0:T(8,128)(2,1)S(1)}, bf16[224,128]{1,0:T(8,128)(2,1)S(1)}, u32[]{:S(2)}, u32[]{:S(2)}) collective-permute-start(bf16[224,128]{1,0:T(8,128)(2,1)S(1)} %add_convert_fusion.7), channel_id=1, source_target_pairs={{0,20},{1,25},{2,26},{3,23},{4,28},{5,17},{6,18},{7,31},{8,16},{9,... | collective-permute-start | bytes 172040 | tf_op jit(solution)/shard_map/ppermute | solution.py:706
  24.8 1.3 %collective-permute-start.10 = (bf16[224,128]{1,0:T(8,128)(2,1)S(1)}, bf16[224,128]{1,0:T(8,128)(2,1)S(1)}, u32[]{:S(2)}, u32[]{:S(2)}) collective-permute-start(bf16[224,128]{1,0:T(8,128)(2,1)S(1)} %add_convert_fusion.4), channel_id=1, source_target_pairs={{0,20},{1,25},{2,26},{3,23},{4,28},{5,17},{6,18},{7,31},{8,16},{9,... | collective-permute-start | bytes 172040 | tf_op jit(solution)/shard_map/ppermute | solution.py:706
  26.1 0.6 %collective-permute-done.3 = bf16[224,128]{1,0:T(8,128)(2,1)S(1)} collective-permute-done((bf16[224,128]{1,0:T(8,128)(2,1)S(1)}, bf16[224,128]{1,0:T(8,128)(2,1)S(1)}, u32[]{:S(2)}, u32[]{:S(2)}) %collective-permute-start.3) | collective-permute-done | bytes 57376 | tf_op jit(solution)/shard_map/ppermute | solution.py:706
  26.8 3.0 %collective-permute-start.4 = (bf16[224,128]{1,0:T(8,128)(2,1)S(1)}, bf16[224,128]{1,0:T(8,128)(2,1)S(1)}, u32[]{:S(2)}, u32[]{:S(2)}) collective-permute-start(bf16[224,128]{1,0:T(8,128)(2,1)S(1)} %add_convert_fusion.6), channel_id=1, source_target_pairs={{0,24},{1,21},{2,22},{3,27},{4,16},{5,29},{6,30},{7,19},{8,28},{9,... | collective-permute-start | bytes 172040 | tf_op jit(solution)/shard_map/ppermute | solution.py:706
  29.8 1.3 %collective-permute-start.11 = (bf16[224,128]{1,0:T(8,128)(2,1)S(1)}, bf16[224,128]{1,0:T(8,128)(2,1)S(1)}, u32[]{:S(2)}, u32[]{:S(2)}) collective-permute-start(bf16[224,128]{1,0:T(8,128)(2,1)S(1)} %add_convert_fusion.3), channel_id=1, source_target_pairs={{0,24},{1,21},{2,22},{3,27},{4,16},{5,29},{6,30},{7,19},{8,28},{9,... | collective-permute-start | bytes 172040 | tf_op jit(solution)/shard_map/ppermute | solution.py:706
  31.2 1.0 %collective-permute-done.4 = bf16[224,128]{1,0:T(8,128)(2,1)S(1)} collective-permute-done((bf16[224,128]{1,0:T(8,128)(2,1)S(1)}, bf16[224,128]{1,0:T(8,128)(2,1)S(1)}, u32[]{:S(2)}, u32[]{:S(2)}) %collective-permute-start.4) | collective-permute-done | bytes 57376 | tf_op jit(solution)/shard_map/ppermute | solution.py:706
  32.2 2.1 %collective-permute-start.5 = (bf16[224,128]{1,0:T(8,128)(2,1)S(1)}, bf16[224,128]{1,0:T(8,128)(2,1)S(1)}, u32[]{:S(2)}, u32[]{:S(2)}) collective-permute-start(bf16[224,128]{1,0:T(8,128)(2,1)S(1)} %add_convert_fusion.5), channel_id=1, source_target_pairs={{0,18},{1,16},{2,19},{3,17},{4,21},{5,23},{6,20},{7,22},{8,25},{9,... | collective-permute-start | bytes 172040 | tf_op jit(solution)/shard_map/ppermute | solution.py:706
  34.3 0.4 collective-permute-done.11
  34.7 1.0 %collective-permute-start.12 = (bf16[224,128]{1,0:T(8,128)(2,1)S(1)}, bf16[224,128]{1,0:T(8,128)(2,1)S(1)}, u32[]{:S(2)}, u32[]{:S(2)}) collective-permute-start(bf16[224,128]{1,0:T(8,128)(2,1)S(1)} %add_convert_fusion.2), channel_id=1, source_target_pairs={{0,18},{1,16},{2,19},{3,17},{4,21},{5,23},{6,20},{7,22},{8,25},{9,... | collective-permute-start | bytes 172040 | tf_op jit(solution)/shard_map/ppermute | solution.py:706
  36.3 1.2 %collective-permute-start.6 = (bf16[448,128]{1,0:T(8,128)(2,1)S(1)}, bf16[448,128]{1,0:T(8,128)(2,1)S(1)}, u32[]{:S(2)}, u32[]{:S(2)}) collective-permute-start(bf16[448,128]{1,0:T(8,128)(2,1)S(1)} %maximum_select_fusion.7), channel_id=1, source_target_pairs={{0,17},{1,19},{2,16},{3,18},{4,22},{5,20},{6,23},{7,21},{8,26},{9,... | collective-permute-start | bytes 344072 | tf_op jit(solution)/shard_map/ppermute | solution.py:706
  37.5 0.9 %collective-permute-done.12 = bf16[224,128]{1,0:T(8,128)(2,1)S(1)} collective-permute-done((bf16[224,128]{1,0:T(8,128)(2,1)S(1)}, bf16[224,128]{1,0:T(8,128)(2,1)S(1)}, u32[]{:S(2)}, u32[]{:S(2)}) %collective-permute-start.12) | collective-permute-done | bytes 57376 | tf_op jit(solution)/shard_map/ppermute | solution.py:706
  38.6 0.9 %collective-permute-start.13 = (bf16[448,128]{1,0:T(8,128)(2,1)S(1)}, bf16[448,128]{1,0:T(8,128)(2,1)S(1)}, u32[]{:S(2)}, u32[]{:S(2)}) collective-permute-start(bf16[448,128]{1,0:T(8,128)(2,1)S(1)} %maximum_select_fusion.8), channel_id=1, source_target_pairs={{0,17},{1,19},{2,16},{3,18},{4,22},{5,20},{6,23},{7,21},{8,26},{9,... | collective-permute-start | bytes 344072 | tf_op jit(solution)/shard_map/ppermute | solution.py:706
  39.8 0.7 %collective-permute-done.6 = bf16[448,128]{1,0:T(8,128)(2,1)S(1)} collective-permute-done((bf16[448,128]{1,0:T(8,128)(2,1)S(1)}, bf16[448,128]{1,0:T(8,128)(2,1)S(1)}, u32[]{:S(2)}, u32[]{:S(2)}) %collective-permute-start.6) | collective-permute-done | bytes 114720 | tf_op jit(solution)/shard_map/ppermute | solution.py:706
  41.0 1.8 %collective-permute-done.13 = bf16[448,128]{1,0:T(8,128)(2,1)S(1)} collective-permute-done((bf16[448,128]{1,0:T(8,128)(2,1)S(1)}, bf16[448,128]{1,0:T(8,128)(2,1)S(1)}, u32[]{:S(2)}, u32[]{:S(2)}) %collective-permute-start.13) | collective-permute-done | bytes 114720 | tf_op jit(solution)/shard_map/ppermute | solution.py:706
  43.4 0.8 %collective-permute-done.17 = bf16[448,128]{1,0:T(8,128)(2,1)S(1)} collective-permute-done((bf16[448,128]{1,0:T(8,128)(2,1)S(1)}, bf16[448,128]{1,0:T(8,128)(2,1)S(1)}, u32[]{:S(2)}, u32[]{:S(2)}) %collective-permute-start.17) | collective-permute-done | bytes 114720 | tf_op jit(solution)/shard_map/ppermute | solution.py:695
  44.5 1.7 %finish.1 = (bf16[16,32,128]{2,1,0:T(8,128)(2,1)}, bf16[147,16,128]{2,1,0:T(8,128)(2,1)}, bf16[16,16,64]{2,1,0:T(8,128)(2,1)}, f32[4,16,128]{2,1,0:T(8,128)}, f3...) custom-call(bf16[3584,128]{1,0:T(8,128)(2,1)S(1)} %maximum_select_fu, ...), custom_call_target="tpu_custom_call" | custom-call | tf_op jit(solution)/shard_map/finish/pallas_call | solution.py:750
  (46 shorter events, 3.6 us)
Async XLA Ops:
  12.0 1.6 %collective-permute-start = (bf16[2,448,128]{2,1,0:T(8,128)(2,1)S(1)}, bf16[2,448,128]{2,1,0:T(8,128)(2,1)S(1)}, u32[]{:S(2)}, u32[]{:S(2)}) collective-permute-start(bf16[2,448,128]{2,1,0:T(8,128)(2,1)S(1)} %get-tuple-element.47), channel_id=1, source_target_pairs={{0,16},{16,0},{1,17},{17,1},{2,18},{18,2},{3,19},{19,3},{4,20},{20... | collective-permute-start | bytes 688136 | tf_op jit(solution)/shard_map/ppermute | solution.py:695
  12.5 3.9 %collective-permute-start.7 = (bf16[2,448,128]{2,1,0:T(8,128)(2,1)S(1)}, bf16[2,448,128]{2,1,0:T(8,128)(2,1)S(1)}, u32[]{:S(2)}, u32[]{:S(2)}) collective-permute-start(bf16[2,448,128]{2,1,0:T(8,128)(2,1)S(1)} %get-tuple-element.49), channel_id=1, source_target_pairs={{0,16},{16,0},{1,17},{17,1},{2,18},{18,2},{3,19},{19,3},{4,20},{20... | collective-permute-start | bytes 688136 | tf_op jit(solution)/shard_map/ppermute | solution.py:695
  13.7 5.1 %collective-permute-start.1 = (bf16[448,128]{1,0:T(8,128)(2,1)S(1)}, bf16[448,128]{1,0:T(8,128)(2,1)S(1)}, u32[]{:S(2)}, u32[]{:S(2)}) collective-permute-start(bf16[448,128]{1,0:T(8,128)(2,1)S(1)} %select_bitcast_fusion.1), channel_id=1, source_target_pairs={{0,17},{1,19},{2,16},{3,18},{4,22},{5,20},{6,23},{7,21},{8,26},{9,... | collective-permute-start | bytes 344072 | tf_op jit(solution)/shard_map/ppermute | solution.py:706
  16.5 4.6 %collective-permute-start.8 = (bf16[448,128]{1,0:T(8,128)(2,1)S(1)}, bf16[448,128]{1,0:T(8,128)(2,1)S(1)}, u32[]{:S(2)}, u32[]{:S(2)}) collective-permute-start(bf16[448,128]{1,0:T(8,128)(2,1)S(1)} %select_bitcast_fusion), channel_id=1, source_target_pairs={{0,17},{1,19},{2,16},{3,18},{4,22},{5,20},{6,23},{7,21},{8,26},{9,... | collective-permute-start | bytes 344072 | tf_op jit(solution)/shard_map/ppermute | solution.py:706
  16.7 22.8 %collective-permute-start.18 = (bf16[1560,128]{1,0:T(8,128)(2,1)S(1)}, bf16[1560,128]{1,0:T(8,128)(2,1)S(1)}, u32[]{:S(2)}, u32[]{:S(2)}) collective-permute-start(bf16[1560,128]{1,0:T(8,128)(2,1)S(1)} %get-tuple-element.53), channel_id=1, source_target_pairs={{0,16},{16,0},{1,17},{17,1},{2,18},{18,2},{3,19},{19,3},{4,20},{20... | collective-permute-start | bytes 1198088 | tf_op jit(solution)/shard_map/ppermute | solution.py:695
  18.9 4.0 %collective-permute-start.2 = (bf16[224,128]{1,0:T(8,128)(2,1)S(1)}, bf16[224,128]{1,0:T(8,128)(2,1)S(1)}, u32[]{:S(2)}, u32[]{:S(2)}) collective-permute-start(bf16[224,128]{1,0:T(8,128)(2,1)S(1)} %broadcast_select_fusion.1), channel_id=1, source_target_pairs={{0,18},{1,16},{2,19},{3,17},{4,21},{5,23},{6,20},{7,22},{8,25},{9,... | collective-permute-start | bytes 172040 | tf_op jit(solution)/shard_map/ppermute | solution.py:706
  21.1 3.7 %collective-permute-start.9 = (bf16[224,128]{1,0:T(8,128)(2,1)S(1)}, bf16[224,128]{1,0:T(8,128)(2,1)S(1)}, u32[]{:S(2)}, u32[]{:S(2)}) collective-permute-start(bf16[224,128]{1,0:T(8,128)(2,1)S(1)} %broadcast_select_fusion), channel_id=1, source_target_pairs={{0,18},{1,16},{2,19},{3,17},{4,21},{5,23},{6,20},{7,22},{8,25},{9,... | collective-permute-start | bytes 172040 | tf_op jit(solution)/shard_map/ppermute | solution.py:706
  22.9 3.8 %collective-permute-start.3 = (bf16[224,128]{1,0:T(8,128)(2,1)S(1)}, bf16[224,128]{1,0:T(8,128)(2,1)S(1)}, u32[]{:S(2)}, u32[]{:S(2)}) collective-permute-start(bf16[224,128]{1,0:T(8,128)(2,1)S(1)} %add_convert_fusion.7), channel_id=1, source_target_pairs={{0,20},{1,25},{2,26},{3,23},{4,28},{5,17},{6,18},{7,31},{8,16},{9,... | collective-permute-start | bytes 172040 | tf_op jit(solution)/shard_map/ppermute | solution.py:706
  24.8 5.0 %collective-permute-start.10 = (bf16[224,128]{1,0:T(8,128)(2,1)S(1)}, bf16[224,128]{1,0:T(8,128)(2,1)S(1)}, u32[]{:S(2)}, u32[]{:S(2)}) collective-permute-start(bf16[224,128]{1,0:T(8,128)(2,1)S(1)} %add_convert_fusion.4), channel_id=1, source_target_pairs={{0,20},{1,25},{2,26},{3,23},{4,28},{5,17},{6,18},{7,31},{8,16},{9,... | collective-permute-start | bytes 172040 | tf_op jit(solution)/shard_map/ppermute | solution.py:706
  26.8 5.3 %collective-permute-start.4 = (bf16[224,128]{1,0:T(8,128)(2,1)S(1)}, bf16[224,128]{1,0:T(8,128)(2,1)S(1)}, u32[]{:S(2)}, u32[]{:S(2)}) collective-permute-start(bf16[224,128]{1,0:T(8,128)(2,1)S(1)} %add_convert_fusion.6), channel_id=1, source_target_pairs={{0,24},{1,21},{2,22},{3,27},{4,16},{5,29},{6,30},{7,19},{8,28},{9,... | collective-permute-start | bytes 172040 | tf_op jit(solution)/shard_map/ppermute | solution.py:706
  29.8 4.9 %collective-permute-start.11 = (bf16[224,128]{1,0:T(8,128)(2,1)S(1)}, bf16[224,128]{1,0:T(8,128)(2,1)S(1)}, u32[]{:S(2)}, u32[]{:S(2)}) collective-permute-start(bf16[224,128]{1,0:T(8,128)(2,1)S(1)} %add_convert_fusion.3), channel_id=1, source_target_pairs={{0,24},{1,21},{2,22},{3,27},{4,16},{5,29},{6,30},{7,19},{8,28},{9,... | collective-permute-start | bytes 172040 | tf_op jit(solution)/shard_map/ppermute | solution.py:706
  32.2 4.0 %collective-permute-start.5 = (bf16[224,128]{1,0:T(8,128)(2,1)S(1)}, bf16[224,128]{1,0:T(8,128)(2,1)S(1)}, u32[]{:S(2)}, u32[]{:S(2)}) collective-permute-start(bf16[224,128]{1,0:T(8,128)(2,1)S(1)} %add_convert_fusion.5), channel_id=1, source_target_pairs={{0,18},{1,16},{2,19},{3,17},{4,21},{5,23},{6,20},{7,22},{8,25},{9,... | collective-permute-start | bytes 172040 | tf_op jit(solution)/shard_map/ppermute | solution.py:706
  34.7 3.7 %collective-permute-start.12 = (bf16[224,128]{1,0:T(8,128)(2,1)S(1)}, bf16[224,128]{1,0:T(8,128)(2,1)S(1)}, u32[]{:S(2)}, u32[]{:S(2)}) collective-permute-start(bf16[224,128]{1,0:T(8,128)(2,1)S(1)} %add_convert_fusion.2), channel_id=1, source_target_pairs={{0,18},{1,16},{2,19},{3,17},{4,21},{5,23},{6,20},{7,22},{8,25},{9,... | collective-permute-start | bytes 172040 | tf_op jit(solution)/shard_map/ppermute | solution.py:706
  36.1 7.1 %collective-permute-start.14 = (bf16[448,128]{1,0:T(8,128)(2,1)S(1)}, bf16[448,128]{1,0:T(8,128)(2,1)S(1)}, u32[]{:S(2)}, u32[]{:S(2)}) collective-permute-start(bf16[448,128]{1,0:T(8,128)(2,1)S(1)} %maximum_select_fusion.7), channel_id=1, source_target_pairs={{0,16},{16,0},{1,17},{17,1},{2,18},{18,2},{3,19},{19,3},{4,20},{20... | collective-permute-start | bytes 344072 | tf_op jit(solution)/shard_map/ppermute | solution.py:695
  36.3 4.2 %collective-permute-start.6 = (bf16[448,128]{1,0:T(8,128)(2,1)S(1)}, bf16[448,128]{1,0:T(8,128)(2,1)S(1)}, u32[]{:S(2)}, u32[]{:S(2)}) collective-permute-start(bf16[448,128]{1,0:T(8,128)(2,1)S(1)} %maximum_select_fusion.7), channel_id=1, source_target_pairs={{0,17},{1,19},{2,16},{3,18},{4,22},{5,20},{6,23},{7,21},{8,26},{9,... | collective-permute-start | bytes 344072 | tf_op jit(solution)/shard_map/ppermute | solution.py:706
  38.4 5.0 %collective-permute-start.16 = (bf16[448,128]{1,0:T(8,128)(2,1)S(1)}, bf16[448,128]{1,0:T(8,128)(2,1)S(1)}, u32[]{:S(2)}, u32[]{:S(2)}) collective-permute-start(bf16[448,128]{1,0:T(8,128)(2,1)S(1)} %maximum_select_fusion.8), channel_id=1, source_target_pairs={{0,16},{16,0},{1,17},{17,1},{2,18},{18,2},{3,19},{19,3},{4,20},{20... | collective-permute-start | bytes 344072 | tf_op jit(solution)/shard_map/ppermute | solution.py:695
  38.6 4.2 %collective-permute-start.13 = (bf16[448,128]{1,0:T(8,128)(2,1)S(1)}, bf16[448,128]{1,0:T(8,128)(2,1)S(1)}, u32[]{:S(2)}, u32[]{:S(2)}) collective-permute-start(bf16[448,128]{1,0:T(8,128)(2,1)S(1)} %maximum_select_fusion.8), channel_id=1, source_target_pairs={{0,17},{1,19},{2,16},{3,18},{4,22},{5,20},{6,23},{7,21},{8,26},{9,... | collective-permute-start | bytes 344072 | tf_op jit(solution)/shard_map/ppermute | solution.py:706
  40.5 2.8 %collective-permute-start.15 = (bf16[448,128]{1,0:T(8,128)(2,1)S(1)}, bf16[448,128]{1,0:T(8,128)(2,1)S(1)}, u32[]{:S(2)}, u32[]{:S(2)}) collective-permute-start(bf16[448,128]{1,0:T(8,128)(2,1)S(1)} %collective-permute-done.6), channel_id=1, source_target_pairs={{0,16},{16,0},{1,17},{17,1},{2,18},{18,2},{3,19},{19,3},{4,20},{20... | collective-permute-start | bytes 344072 | tf_op jit(solution)/shard_map/ppermute | solution.py:695
  42.8 1.4 %collective-permute-start.17 = (bf16[448,128]{1,0:T(8,128)(2,1)S(1)}, bf16[448,128]{1,0:T(8,128)(2,1)S(1)}, u32[]{:S(2)}, u32[]{:S(2)}) collective-permute-start(bf16[448,128]{1,0:T(8,128)(2,1)S(1)} %collective-permute-done.13), channel_id=1, source_target_pairs={{0,16},{16,0},{1,17},{17,1},{2,18},{18,2},{3,19},{19,3},{4,20},{20... | collective-permute-start | bytes 344072 | tf_op jit(solution)/shard_map/ppermute | solution.py:695

commit v6 on v5

--- a/solution.py
+++ b/solution.py
@@ -15,6 +15,7 @@
 CHAINS = 2
 PIECES = 2 * CHAINS
 EPS = 1e-05
+LAG = 4
 INV_SQRT2 = 1.0 / math.sqrt(2.0)
 INV_SQRT2PI = 1.0 / math.sqrt(2.0 * math.pi)
 ANY = pl.BlockSpec(memory_space=pl.ANY)
@@ -87,15 +88,15 @@
 
 
 def staged(count, *stages):
-    for step in range(count + len(stages) - 1):
+    for step in range(count + LAG * (len(stages) - 1)):
         for lag, stage in enumerate(stages):
-            if 0 <= step - lag < count:
-                stage(step - lag)
+            if 0 <= step - LAG * lag < count:
+                stage(step - LAG * lag)
 
 
 def softmax_rows(scores):
     expo = jnp.exp(scores - jnp.max(scores, axis=0, keepdims=True))
-    return expo / jnp.sum(expo, axis=0, keepdims=True)
+    return expo * (1.0 / jnp.sum(expo, axis=0, keepdims=True))
 
 
 def per_step(row, reduce):
@@ -122,16 +123,24 @@
     return terms - probs * jnp.sum(terms, axis=0, keepdims=True)
 
 
+def row_mean(values):
+    width = values.shape[1]
+    high = values.astype(BF16)
+    low = (values - high.astype(F32)).astype(BF16)
+    ones = jnp.full((2 * width, width), 1.0 / width, BF16)
+    return mm(jnp.concatenate([high, low], axis=1), ones)
+
+
 def norm_parts(values):
-    center = values - jnp.mean(values, axis=-1, keepdims=True)
-    rstd = lax.rsqrt(jnp.mean(center * center, axis=-1, keepdims=True) + EPS)
+    center = values - row_mean(values)
+    rstd = lax.rsqrt(row_mean(center * center) + EPS)
     return center * rstd, rstd
 
 
 def norm_grad(grad, gain, hat, rstd):
     scaled = grad * gain
-    first = jnp.mean(scaled, axis=-1, keepdims=True)
-    second = jnp.mean(scaled * hat, axis=-1, keepdims=True)
+    first = row_mean(scaled)
+    second = row_mean(scaled * hat)
     return rstd * (scaled - first - hat * second)
 
 
@@ -305,6 +314,28 @@
         last = x_s[s, edge:].astype(F32)
         x_s[s, edge:] = jnp.where(inside, last, 0.0).astype(BF16)
 
+    ready(9)
+    emb_rows = jnp.concatenate([jnp.full((steps * ptok, width), e) for e in embs], axis=0)
+    lift_cat = jnp.concatenate([lift_w[e] for e in range(emb)], axis=1)
+    mix_cat = jnp.concatenate([mix_w[e] for e in range(emb)], axis=1)
+
+    def own_columns(values):
+        result = values[:, :width]
+        for e in range(1, emb):
+            result = jnp.where(emb_rows == e, values[:, width * e : width * (e + 1)], result)
+        return result
+
+    def spread_columns(values):
+        parts = [jnp.where(emb_rows == e, values, 0.0).astype(BF16) for e in range(emb)]
+        return jnp.concatenate(parts, axis=1)
+
+    prop_rows = p_s[...].reshape(n * steps * ptok, -1)
+    act, dact = gelu_parts(own_columns(mm(prop_rows, lift_cat)))
+    act_s[...] = act.astype(BF16)
+    dact_s[...] = dact
+    prop_tok = own_columns(mm(act_s[...], mix_cat)).astype(BF16)
+    tok_s[:, :, qry:] = prop_tok.reshape(n, steps, ptok, width)
+
     first_step = lax.broadcasted_iota(jnp.int32, (tall, width), 0) % steps == 0
 
     def view_bias(s):
@@ -345,28 +376,6 @@
 
     ready(6)
     staged(n, stem_scores, stem_softmax, stem_moments, stem_values)
-    ready(9)
-    emb_rows = jnp.concatenate([jnp.full((steps * ptok, width), e) for e in embs], axis=0)
-    lift_cat = jnp.concatenate([lift_w[e] for e in range(emb)], axis=1)
-    mix_cat = jnp.concatenate([mix_w[e] for e in range(emb)], axis=1)
-
-    def own_columns(values):
-        result = values[:, :width]
-        for e in range(1, emb):
-            result = jnp.where(emb_rows == e, values[:, width * e : width * (e + 1)], result)
-        return result
-
-    def spread_columns(values):
-        parts = [jnp.where(emb_rows == e, values, 0.0).astype(BF16) for e in range(emb)]
-        return jnp.concatenate(parts, axis=1)
-
-    prop_rows = p_s[...].reshape(n * steps * ptok, -1)
-    act, dact = gelu_parts(own_columns(mm(prop_rows, lift_cat)))
-    act_s[...] = act.astype(BF16)
-    dact_s[...] = dact
-    prop_tok = own_columns(mm(act_s[...], mix_cat)).astype(BF16)
-    tok_s[:, :, qry:] = prop_tok.reshape(n, steps, ptok, width)
-
     ready(10)
     image_tok = mm(satt_s[...].reshape(n * steps * qry, width), stem_proj[...])
     tok_s[:, :, :qry] = image_tok.astype(BF16).reshape(n, steps, qry, width)
@@ -587,7 +596,7 @@
     rows = n * ctx
     piece = total // (CORES * PIECES)
     lines = steps * keys
-    tall = (lines + 15) // 16 * 16
+    tall = (lines + 31) // 32 * 32
     dims = (n, steps, keys, width, qry, ptok, emb, ffw, table, view_mask.shape[1])
 
     def low(*shape):
@@ -600,7 +609,7 @@
     scratch = [pltpu.SMEM(v.shape, v.dtype) for v in small]
     scratch += [low(*w.shape) for w in weights]
     scratch += [
-        low((n * lines + 31) // 16 * 16, width),
+        low(((n - 1) * lines + tall + 15) // 16 * 16, width),
         low(n, tall, width),
         low(n, steps, ptok, feats),
         low(n, ctx, width),
@@ -706,26 +715,44 @@
     return lax.ppermute(value, ("section", "dp"), pairs)
 
 
-def finish_kernel(table, pack, blk, img, prp, *refs):
-    count = len(refs) // 2 - 2
-    outs, held, sem = refs[: count + 3], refs[count + 3 : -1], refs[-1]
-    copies = []
-
-    def send(source, target):
-        copy = pltpu.make_async_copy(source, target, sem.at[len(copies)])
+def send_kernel(count, *refs):
+    sem = refs[-1]
+    copies = [pltpu.make_async_copy(refs[i], refs[count + i], sem.at[i]) for i in range(count)]
+    for copy in copies:
         copy.start()
-        copies.append(copy)
-
-    for source, target in zip((blk, img, prp), outs):
-        send(source, target)
+    for copy in copies:
+        copy.wait()
+
+
+def send_out(*values):
+    return pl.pallas_call(
+        functools.partial(send_kernel, len(values)),
+        out_shape=tuple(jax.ShapeDtypeStruct(v.shape, v.dtype) for v in values),
+        in_specs=[VMEM] * len(values),
+        out_specs=(ANY,) * len(values),
+        scratch_shapes=[pltpu.SemaphoreType.DMA((len(values),))],
+        compiler_params=pltpu.CompilerParams(vmem_limit_bytes=8 * 2**20),
+        name="send_out",
+    )(*(pltpu.with_memory_space_constraint(v, pltpu.VMEM) for v in values))
+
+
+def finish_kernel(table, *refs):
+    pieces, refs = refs[: CORES * PIECES], refs[CORES * PIECES :]
+    count = len(refs) // 2 - 1
+    outs, held, (pack, sem) = refs[:count], refs[count : 2 * count], refs[2 * count :]
+    size, width = pieces[0].shape
+    own = own_half()
+    for i, ref in enumerate(pieces):
+        half = own if i < PIECES else 1 - own
+        chain, far = i % CHAINS, i // CHAINS % 2
+        at = half * PIECES + chain * 2 + (own_bits(half)[0] ^ far)
+        pack[pl.ds(pl.multiple_of(at * size, size), size)] = ref[...]
     names = ("queries", "keyw", "valuew", "stem", "lift", "mixer", "again", "abias", "qkv", "aproj")
     names += ("mgain", "mbias", "up", "upb", "down", "downb")
     vectors = pack[pl.ds(table["vectors"][0], 16)].astype(F32)
-    width = pack.shape[1]
     rows = {"again": 0, "abias": 1, "mgain": 2, "mbias": 3, "downb": 4}
-    order = sorted(range(count), key=lambda i: table.get(names[i], (1 << 30,))[0])
-    for i in order:
-        name, ref = names[i], held[i]
+    copies = []
+    for i, (name, out, ref) in enumerate(zip(names, outs, held)):
         if name in rows:
             ref[...] = vectors[rows[name]]
         elif name == "upb":
@@ -740,24 +767,24 @@
                     ref[...] = part.reshape(ref.shape)
                 else:
                     ref[:, width * j : width * (j + 1)] = part
-        send(ref, outs[3 + i])
+        copies.append(pltpu.make_async_copy(ref, out, sem.at[i]))
+        copies[-1].start()
     for copy in copies:
         copy.wait()
 
 
-def finish(table, pack, blk, img, prp, shapes):
-    inputs = (pack, blk, img, prp)
+def finish(table, pieces, shapes):
+    total = len(pieces) * pieces[0].shape[0]
     return pl.pallas_call(
         functools.partial(finish_kernel, table),
-        out_shape=tuple(jax.ShapeDtypeStruct(v.shape, BF16) for v in inputs[1:])
-        + tuple(jax.ShapeDtypeStruct(v, F32) for v in shapes),
-        in_specs=[VMEM] * 4,
-        out_specs=(ANY,) * (3 + len(shapes)),
+        out_shape=tuple(jax.ShapeDtypeStruct(v, F32) for v in shapes),
+        in_specs=[VMEM] * len(pieces),
+        out_specs=(ANY,) * len(shapes),
         scratch_shapes=[pltpu.VMEM(v, F32) for v in shapes]
-        + [pltpu.SemaphoreType.DMA((3 + len(shapes),))],
+        + [pltpu.VMEM((total, pieces[0].shape[1]), BF16), pltpu.SemaphoreType.DMA((len(shapes),))],
         compiler_params=pltpu.CompilerParams(vmem_limit_bytes=24 * 2**20),
         name="finish",
-    )(*(pltpu.with_memory_space_constraint(v, pltpu.VMEM) for v in inputs))
+    )(*(pltpu.with_memory_space_constraint(v, pltpu.VMEM) for v in pieces))
 
 
 def sum_chips(held, came, extra):
@@ -778,10 +805,7 @@
     sent = [swap_chips(t, second) for t in totals]
     near = [either(two, t, c) for t, c in zip(totals, sent)]
     far = [swap_chips(t, first) for t in near]
-    own = [either(one, *v) for v in zip(near, far)]
-    bit = own_bits(1 - half)[0]
-    other = [either(bit, *v) for v in zip(*([swap_cores(t) for t in v] for v in (near, far)))]
-    return either(half, jnp.concatenate(own), jnp.concatenate(other)), extra
+    return near + far + [swap_cores(t) for t in near + far], extra
 
 
 def either(bit, mine, came, axis=0):
@@ -796,13 +820,14 @@
     table, total = layout(width, weights[12].shape[1], emb, qry, weights[4].shape[1])
     *packed, extra, extra_sent = compute(args, table, total)
     keep, send = packed[:CHAINS], packed[CHAINS:]
-    pack, came = sum_chips(keep, [swap_cores(v) for v in send], extra_sent)
+    pieces, came = sum_chips(keep, [swap_cores(v) for v in send], extra_sent)
     sec = lax.axis_index("section")
     first, second = keys * n, keys * n + n * (qry + ptok)
     img = either(sec, *(v[:first].reshape(keys, n, width) for v in (extra, came)), 1)
     blk = either(sec, *(v[first:second].reshape(n, -1, width) for v in (extra, came)))
     prp = either(sec, *(v[second:, :feats].reshape(n, ptok, feats) for v in (extra, came)))
-    blk, img, prp, *grads = finish(table, pack, blk, img, prp, [w.shape for w in weights])
+    blk, img, prp = send_out(blk, img, prp)
+    grads = finish(table, pieces, [w.shape for w in weights])
     return (blk, img.transpose(1, 0, 2)[:, None], prp[:, None]) + tuple(grads)
 
 

time: 46.3 us -> 45.1 us (0.974)
  waiting for transfers between devices: 9.87 us -> 9.28 us
  other arithmetic: 1.22 us -> 0.71 us
    pallas_call x0 -> x1, Pallas kernels: none -> 0.9 us  [send_out(): pl.pallas_call(functools.partial(send_kernel, len(values)), out_shape=tup...]
    pallas_call x1, Pallas kernels: 11.3 us -> 10.5 us  [compute(): pl.pallas_call(functools.partial(compute_kernel, dims), out_shape=(low(2,...]
    ppermute x7, waiting for transfers between devices: 1.77 us -> 1 us  [swap_cores(): return lax.ppermute(value, 'section', [(0, 1), (1, 0)])]
    select_n x14 -> x9, other arithmetic: 0.87 us -> 0.35 us  [select(): return jnp.where(bit == 0, low, high)]
  transfers between devices with their start and end apart: 19 -> 19, of which waited for: 11 -> 10; matrix products, arithmetic and copies ran while one was open for 2% -> 2% of each run, Pallas kernels for 0% -> 2%
where the time goes in v6:
time: 45.1 us; the launch traced here: 44.9 us
  starting transfers between devices  21.1 us (47%)
  Pallas kernels  12.9 us (29%)
  waiting for transfers between devices  9.28 us (21%)
  between operations  0.87 us (2%)
  other arithmetic  0.71 us (2%)
    ppermute x12, starting transfers between devices, swap_chips(): return lax.ppermute(value, ('section', 'dp'), pairs)  19 us
    pallas_call x1, Pallas kernels, compute(): pl.pallas_call(functools.partial(compute_kernel, dims), out_shape=(low(2,...  10.5 us
    ppermute x12, waiting for transfers between devices, swap_chips(): return lax.ppermute(value, ('section', 'dp'), pairs)  8.28 us
    ppermute x7, starting transfers between devices, swap_cores(): return lax.ppermute(value, 'section', [(0, 1), (1, 0)])  2.1 us
    pallas_call x1, Pallas kernels, finish(): pl.pallas_call(functools.partial(finish_kernel, table), out_shape=tuple((...  1.47 us
    ppermute x7, waiting for transfers between devices, swap_cores(): return lax.ppermute(value, 'section', [(0, 1), (1, 0)])  1 us
  transfers between devices with their start and end apart: 19, of which 10 were waited for; matrix products, arithmetic and copies ran while one was open for 2% of the time, Pallas kernels for 2%

profile of v6, /device:TPU:0, one launch (start us, length us, event | category | flops | bytes accessed | tf_op | source)
XLA Modules:
  0.0 44.9 jit_solution(7160494282882113434)
XLA Ops:
  0.7 10.5 %stem_trunk.1 = (bf16[2,448,128]{2,1,0:T(8,128)(2,1)S(1)}, bf16[2,448,128]{2,1,0:T(8,128)(2,1)S(1)}, bf16[2,448,128]{2,1,0:T(8,128)(2,1)S(1)}, bf16[2,448,128]{2...) custom-call(s32[16]{0:T(128)} %emb_h.1, s32[16]{0:T(128)} %steps_h.1, ...), custom_call_target="tpu_custom_call" | custom-call | tf_op jit(solution)/shard_map/stem_trunk/pallas_call | solution.py:659
  11.2 0.5 %collective-permute-start = (bf16[2,448,128]{2,1,0:T(8,128)(2,1)S(1)}, bf16[2,448,128]{2,1,0:T(8,128)(2,1)S(1)}, u32[]{:S(2)}, u32[]{:S(2)}) collective-permute-start(bf16[2,448,128]{2,1,0:T(8,128)(2,1)S(1)} %get-tuple-element.48), channel_id=1, source_target_pairs={{0,16},{16,0},{1,17},{17,1},{2,18},{18,2},{3,19},{19,3},{4,20},{20... | collective-permute-start | bytes 688136 | tf_op jit(solution)/shard_map/ppermute | solution.py:704
  11.8 1.0 %collective-permute-done = bf16[2,448,128]{2,1,0:T(8,128)(2,1)S(1)} collective-permute-done((bf16[2,448,128]{2,1,0:T(8,128)(2,1)S(1)}, bf16[2,448,128]{2,1,0:T(8,128)(2,1)S(1)}, u32[]{:S(2)}, u32[]{:S(2)}) %collective-permute-start) | collective-permute-done | bytes 229408 | tf_op jit(solution)/shard_map/ppermute | solution.py:704
  12.9 2.7 %collective-permute-start.8 = (bf16[448,128]{1,0:T(8,128)(2,1)S(1)}, bf16[448,128]{1,0:T(8,128)(2,1)S(1)}, u32[]{:S(2)}, u32[]{:S(2)}) collective-permute-start(bf16[448,128]{1,0:T(8,128)(2,1)S(1)} %select_bitcast_fusion), channel_id=1, source_target_pairs={{0,17},{1,19},{2,16},{3,18},{4,22},{5,20},{6,23},{7,21},{8,26},{9,... | collective-permute-start | bytes 344072 | tf_op jit(solution)/shard_map/ppermute | solution.py:715
  16.3 1.7 %collective-permute-done.8 = bf16[448,128]{1,0:T(8,128)(2,1)S(1)} collective-permute-done((bf16[448,128]{1,0:T(8,128)(2,1)S(1)}, bf16[448,128]{1,0:T(8,128)(2,1)S(1)}, u32[]{:S(2)}, u32[]{:S(2)}) %collective-permute-start.8) | collective-permute-done | bytes 114720 | tf_op jit(solution)/shard_map/ppermute | solution.py:715
  18.1 2.1 %collective-permute-start.9 = (bf16[224,128]{1,0:T(8,128)(2,1)S(1)}, bf16[224,128]{1,0:T(8,128)(2,1)S(1)}, u32[]{:S(2)}, u32[]{:S(2)}) collective-permute-start(bf16[224,128]{1,0:T(8,128)(2,1)S(1)} %broadcast_select_fusion), channel_id=1, source_target_pairs={{0,18},{1,16},{2,19},{3,17},{4,21},{5,23},{6,20},{7,22},{8,25},{9,... | collective-permute-start | bytes 172040 | tf_op jit(solution)/shard_map/ppermute | solution.py:715
  20.3 1.3 %collective-permute-start.4 = (bf16[224,128]{1,0:T(8,128)(2,1)S(1)}, bf16[224,128]{1,0:T(8,128)(2,1)S(1)}, u32[]{:S(2)}, u32[]{:S(2)}) collective-permute-start(bf16[224,128]{1,0:T(8,128)(2,1)S(1)} %broadcast_select_fusion.1), channel_id=1, source_target_pairs={{0,18},{1,16},{2,19},{3,17},{4,21},{5,23},{6,20},{7,22},{8,25},{9,... | collective-permute-start | bytes 172040 | tf_op jit(solution)/shard_map/ppermute | solution.py:715
  21.6 0.5 %collective-permute-done.9 = bf16[224,128]{1,0:T(8,128)(2,1)S(1)} collective-permute-done((bf16[224,128]{1,0:T(8,128)(2,1)S(1)}, bf16[224,128]{1,0:T(8,128)(2,1)S(1)}, u32[]{:S(2)}, u32[]{:S(2)}) %collective-permute-start.9) | collective-permute-done | bytes 57376 | tf_op jit(solution)/shard_map/ppermute | solution.py:715
  22.1 1.9 %collective-permute-start.10 = (bf16[224,128]{1,0:T(8,128)(2,1)S(1)}, bf16[224,128]{1,0:T(8,128)(2,1)S(1)}, u32[]{:S(2)}, u32[]{:S(2)}) collective-permute-start(bf16[224,128]{1,0:T(8,128)(2,1)S(1)} %add_convert_fusion.4), channel_id=1, source_target_pairs={{0,20},{1,25},{2,26},{3,23},{4,28},{5,17},{6,18},{7,31},{8,16},{9,... | collective-permute-start | bytes 172040 | tf_op jit(solution)/shard_map/ppermute | solution.py:715
  24.1 1.3 %collective-permute-start.5 = (bf16[224,128]{1,0:T(8,128)(2,1)S(1)}, bf16[224,128]{1,0:T(8,128)(2,1)S(1)}, u32[]{:S(2)}, u32[]{:S(2)}) collective-permute-start(bf16[224,128]{1,0:T(8,128)(2,1)S(1)} %add_convert_fusion.7), channel_id=1, source_target_pairs={{0,20},{1,25},{2,26},{3,23},{4,28},{5,17},{6,18},{7,31},{8,16},{9,... | collective-permute-start | bytes 172040 | tf_op jit(solution)/shard_map/ppermute | solution.py:715
  25.4 0.7 %collective-permute-done.10 = bf16[224,128]{1,0:T(8,128)(2,1)S(1)} collective-permute-done((bf16[224,128]{1,0:T(8,128)(2,1)S(1)}, bf16[224,128]{1,0:T(8,128)(2,1)S(1)}, u32[]{:S(2)}, u32[]{:S(2)}) %collective-permute-start.10) | collective-permute-done | bytes 57376 | tf_op jit(solution)/shard_map/ppermute | solution.py:715
  26.0 3.0 %collective-permute-start.11 = (bf16[224,128]{1,0:T(8,128)(2,1)S(1)}, bf16[224,128]{1,0:T(8,128)(2,1)S(1)}, u32[]{:S(2)}, u32[]{:S(2)}) collective-permute-start(bf16[224,128]{1,0:T(8,128)(2,1)S(1)} %add_convert_fusion.3), channel_id=1, source_target_pairs={{0,24},{1,21},{2,22},{3,27},{4,16},{5,29},{6,30},{7,19},{8,28},{9,... | collective-permute-start | bytes 172040 | tf_op jit(solution)/shard_map/ppermute | solution.py:715
  29.0 1.3 %collective-permute-start.6 = (bf16[224,128]{1,0:T(8,128)(2,1)S(1)}, bf16[224,128]{1,0:T(8,128)(2,1)S(1)}, u32[]{:S(2)}, u32[]{:S(2)}) collective-permute-start(bf16[224,128]{1,0:T(8,128)(2,1)S(1)} %add_convert_fusion.6), channel_id=1, source_target_pairs={{0,24},{1,21},{2,22},{3,27},{4,16},{5,29},{6,30},{7,19},{8,28},{9,... | collective-permute-start | bytes 172040 | tf_op jit(solution)/shard_map/ppermute | solution.py:715
  30.4 1.0 %collective-permute-done.11 = bf16[224,128]{1,0:T(8,128)(2,1)S(1)} collective-permute-done((bf16[224,128]{1,0:T(8,128)(2,1)S(1)}, bf16[224,128]{1,0:T(8,128)(2,1)S(1)}, u32[]{:S(2)}, u32[]{:S(2)}) %collective-permute-start.11) | collective-permute-done | bytes 57376 | tf_op jit(solution)/shard_map/ppermute | solution.py:715
  31.4 2.1 %collective-permute-start.12 = (bf16[224,128]{1,0:T(8,128)(2,1)S(1)}, bf16[224,128]{1,0:T(8,128)(2,1)S(1)}, u32[]{:S(2)}, u32[]{:S(2)}) collective-permute-start(bf16[224,128]{1,0:T(8,128)(2,1)S(1)} %add_convert_fusion.2), channel_id=1, source_target_pairs={{0,18},{1,16},{2,19},{3,17},{4,21},{5,23},{6,20},{7,22},{8,25},{9,... | collective-permute-start | bytes 172040 | tf_op jit(solution)/shard_map/ppermute | solution.py:715
  33.5 0.5 %collective-permute-done.6 = bf16[224,128]{1,0:T(8,128)(2,1)S(1)} collective-permute-done((bf16[224,128]{1,0:T(8,128)(2,1)S(1)}, bf16[224,128]{1,0:T(8,128)(2,1)S(1)}, u32[]{:S(2)}, u32[]{:S(2)}) %collective-permute-start.6) | collective-permute-done | bytes 57376 | tf_op jit(solution)/shard_map/ppermute | solution.py:715
  33.9 1.0 %collective-permute-start.7 = (bf16[224,128]{1,0:T(8,128)(2,1)S(1)}, bf16[224,128]{1,0:T(8,128)(2,1)S(1)}, u32[]{:S(2)}, u32[]{:S(2)}) collective-permute-start(bf16[224,128]{1,0:T(8,128)(2,1)S(1)} %add_convert_fusion.5), channel_id=1, source_target_pairs={{0,18},{1,16},{2,19},{3,17},{4,21},{5,23},{6,20},{7,22},{8,25},{9,... | collective-permute-start | bytes 172040 | tf_op jit(solution)/shard_map/ppermute | solution.py:715
  35.5 1.2 %collective-permute-start.14 = (bf16[448,128]{1,0:T(8,128)(2,1)S(1)}, bf16[448,128]{1,0:T(8,128)(2,1)S(1)}, u32[]{:S(2)}, u32[]{:S(2)}) collective-permute-start(bf16[448,128]{1,0:T(8,128)(2,1)S(1)} %maximum_select_fusion.3.refs_1_), channel_id=1, source_target_pairs={{0,17},{1,19},{2,16},{3,18},{4,22},{5,20},{6,23},{7,21},{8,26},{9,... | collective-permute-start | bytes 344072 | tf_op jit(solution)/shard_map/ppermute | solution.py:715
  36.7 0.9 %collective-permute-done.7 = bf16[224,128]{1,0:T(8,128)(2,1)S(1)} collective-permute-done((bf16[224,128]{1,0:T(8,128)(2,1)S(1)}, bf16[224,128]{1,0:T(8,128)(2,1)S(1)}, u32[]{:S(2)}, u32[]{:S(2)}) %collective-permute-start.7) | collective-permute-done | bytes 57376 | tf_op jit(solution)/shard_map/ppermute | solution.py:715
  37.8 0.9 %collective-permute-start.13 = (bf16[448,128]{1,0:T(8,128)(2,1)S(1)}, bf16[448,128]{1,0:T(8,128)(2,1)S(1)}, u32[]{:S(2)}, u32[]{:S(2)}) collective-permute-start(bf16[448,128]{1,0:T(8,128)(2,1)S(1)} %maximum_select_fusion.2.refs_0_), channel_id=1, source_target_pairs={{0,17},{1,19},{2,16},{3,18},{4,22},{5,20},{6,23},{7,21},{8,26},{9,... | collective-permute-start | bytes 344072 | tf_op jit(solution)/shard_map/ppermute | solution.py:715
  39.0 0.8 %collective-permute-done.14.refs_3_ = bf16[448,128]{1,0:T(8,128)(2,1)S(1)} collective-permute-done((bf16[448,128]{1,0:T(8,128)(2,1)S(1)}, bf16[448,128]{1,0:T(8,128)(2,1)S(1)}, u32[]{:S(2)}, u32[]{:S(2)}) %collective-permute-start.14) | collective-permute-done | bytes 114720 | tf_op jit(solution)/shard_map/ppermute | solution.py:715
  40.2 1.9 %collective-permute-done.13.refs_2_ = bf16[448,128]{1,0:T(8,128)(2,1)S(1)} collective-permute-done((bf16[448,128]{1,0:T(8,128)(2,1)S(1)}, bf16[448,128]{1,0:T(8,128)(2,1)S(1)}, u32[]{:S(2)}, u32[]{:S(2)}) %collective-permute-start.13) | collective-permute-done | bytes 114720 | tf_op jit(solution)/shard_map/ppermute | solution.py:715
  42.5 0.9 %send_out.1 = (bf16[16,32,128]{2,1,0:T(8,128)(2,1)}, bf16[147,16,128]{2,1,0:T(8,128)(2,1)}, bf16[16,16,64]{2,1,0:T(8,128)(2,1)}) custom-call(bf16[16,32,128]{2,1,0:T(8,128)(2,1)S(1)} %maximum_select_fusion.1.refs_0_, bf16[147,16,128]{2,1,0:T(8,128)(2,1)S(1)} %maximum_select_fusion.refs_1_, bf16[16,16,64]{2,1,0:T(8,128)(2,1)S(1)} %maximum_select_fusion.4.refs_2_), custom_call_target="tpu_custom_call" | custom-call | tf_op jit(solution)/shard_map/send_out/pallas_call | solution.py:728
  43.4 1.5 %finish.1 = (f32[4,16,128]{2,1,0:T(8,128)}, f32[4,128,128]{2,1,0:T(8,128)}, f32[4,128,128]{2,1,0:T(8,128)}, f32[128,128]{1,0:T(8,128)}, f32[4,64,128]{2,1,0:T(8,...) custom-call(bf16[448,128]{1,0:T(8,128)(2,1)S(1)} %maximum_select_fus, ...), custom_call_target="tpu_custom_call" | custom-call | tf_op jit(solution)/shard_map/finish/pallas_call | solution.py:778
  (42 shorter events, 3.0 us)
Async XLA Ops:
  11.2 1.6 %collective-permute-start = (bf16[2,448,128]{2,1,0:T(8,128)(2,1)S(1)}, bf16[2,448,128]{2,1,0:T(8,128)(2,1)S(1)}, u32[]{:S(2)}, u32[]{:S(2)}) collective-permute-start(bf16[2,448,128]{2,1,0:T(8,128)(2,1)S(1)} %get-tuple-element.48), channel_id=1, source_target_pairs={{0,16},{16,0},{1,17},{17,1},{2,18},{18,2},{3,19},{19,3},{4,20},{20... | collective-permute-start | bytes 688136 | tf_op jit(solution)/shard_map/ppermute | solution.py:704
  11.7 3.9 %collective-permute-start.2 = (bf16[2,448,128]{2,1,0:T(8,128)(2,1)S(1)}, bf16[2,448,128]{2,1,0:T(8,128)(2,1)S(1)}, u32[]{:S(2)}, u32[]{:S(2)}) collective-permute-start(bf16[2,448,128]{2,1,0:T(8,128)(2,1)S(1)} %get-tuple-element.55), channel_id=1, source_target_pairs={{0,16},{16,0},{1,17},{17,1},{2,18},{18,2},{3,19},{19,3},{4,20},{20... | collective-permute-start | bytes 688136 | tf_op jit(solution)/shard_map/ppermute | solution.py:704
  12.9 5.1 %collective-permute-start.8 = (bf16[448,128]{1,0:T(8,128)(2,1)S(1)}, bf16[448,128]{1,0:T(8,128)(2,1)S(1)}, u32[]{:S(2)}, u32[]{:S(2)}) collective-permute-start(bf16[448,128]{1,0:T(8,128)(2,1)S(1)} %select_bitcast_fusion), channel_id=1, source_target_pairs={{0,17},{1,19},{2,16},{3,18},{4,22},{5,20},{6,23},{7,21},{8,26},{9,... | collective-permute-start | bytes 344072 | tf_op jit(solution)/shard_map/ppermute | solution.py:715
  15.7 4.6 %collective-permute-start.3 = (bf16[448,128]{1,0:T(8,128)(2,1)S(1)}, bf16[448,128]{1,0:T(8,128)(2,1)S(1)}, u32[]{:S(2)}, u32[]{:S(2)}) collective-permute-start(bf16[448,128]{1,0:T(8,128)(2,1)S(1)} %select_bitcast_fusion.1), channel_id=1, source_target_pairs={{0,17},{1,19},{2,16},{3,18},{4,22},{5,20},{6,23},{7,21},{8,26},{9,... | collective-permute-start | bytes 344072 | tf_op jit(solution)/shard_map/ppermute | solution.py:715
  15.9 22.8 %collective-permute-start.1 = (bf16[1560,128]{1,0:T(8,128)(2,1)S(1)}, bf16[1560,128]{1,0:T(8,128)(2,1)S(1)}, u32[]{:S(2)}, u32[]{:S(2)}) collective-permute-start(bf16[1560,128]{1,0:T(8,128)(2,1)S(1)} %get-tuple-element.50), channel_id=1, source_target_pairs={{0,16},{16,0},{1,17},{17,1},{2,18},{18,2},{3,19},{19,3},{4,20},{20... | collective-permute-start | bytes 1198088 | tf_op jit(solution)/shard_map/ppermute | solution.py:704
  18.1 4.0 %collective-permute-start.9 = (bf16[224,128]{1,0:T(8,128)(2,1)S(1)}, bf16[224,128]{1,0:T(8,128)(2,1)S(1)}, u32[]{:S(2)}, u32[]{:S(2)}) collective-permute-start(bf16[224,128]{1,0:T(8,128)(2,1)S(1)} %broadcast_select_fusion), channel_id=1, source_target_pairs={{0,18},{1,16},{2,19},{3,17},{4,21},{5,23},{6,20},{7,22},{8,25},{9,... | collective-permute-start | bytes 172040 | tf_op jit(solution)/shard_map/ppermute | solution.py:715
  20.3 3.7 %collective-permute-start.4 = (bf16[224,128]{1,0:T(8,128)(2,1)S(1)}, bf16[224,128]{1,0:T(8,128)(2,1)S(1)}, u32[]{:S(2)}, u32[]{:S(2)}) collective-permute-start(bf16[224,128]{1,0:T(8,128)(2,1)S(1)} %broadcast_select_fusion.1), channel_id=1, source_target_pairs={{0,18},{1,16},{2,19},{3,17},{4,21},{5,23},{6,20},{7,22},{8,25},{9,... | collective-permute-start | bytes 172040 | tf_op jit(solution)/shard_map/ppermute | solution.py:715
  22.1 3.9 %collective-permute-start.10 = (bf16[224,128]{1,0:T(8,128)(2,1)S(1)}, bf16[224,128]{1,0:T(8,128)(2,1)S(1)}, u32[]{:S(2)}, u32[]{:S(2)}) collective-permute-start(bf16[224,128]{1,0:T(8,128)(2,1)S(1)} %add_convert_fusion.4), channel_id=1, source_target_pairs={{0,20},{1,25},{2,26},{3,23},{4,28},{5,17},{6,18},{7,31},{8,16},{9,... | collective-permute-start | bytes 172040 | tf_op jit(solution)/shard_map/ppermute | solution.py:715
  24.1 5.0 %collective-permute-start.5 = (bf16[224,128]{1,0:T(8,128)(2,1)S(1)}, bf16[224,128]{1,0:T(8,128)(2,1)S(1)}, u32[]{:S(2)}, u32[]{:S(2)}) collective-permute-start(bf16[224,128]{1,0:T(8,128)(2,1)S(1)} %add_convert_fusion.7), channel_id=1, source_target_pairs={{0,20},{1,25},{2,26},{3,23},{4,28},{5,17},{6,18},{7,31},{8,16},{9,... | collective-permute-start | bytes 172040 | tf_op jit(solution)/shard_map/ppermute | solution.py:715
  26.0 5.3 %collective-permute-start.11 = (bf16[224,128]{1,0:T(8,128)(2,1)S(1)}, bf16[224,128]{1,0:T(8,128)(2,1)S(1)}, u32[]{:S(2)}, u32[]{:S(2)}) collective-permute-start(bf16[224,128]{1,0:T(8,128)(2,1)S(1)} %add_convert_fusion.3), channel_id=1, source_target_pairs={{0,24},{1,21},{2,22},{3,27},{4,16},{5,29},{6,30},{7,19},{8,28},{9,... | collective-permute-start | bytes 172040 | tf_op jit(solution)/shard_map/ppermute | solution.py:715
  29.0 4.9 %collective-permute-start.6 = (bf16[224,128]{1,0:T(8,128)(2,1)S(1)}, bf16[224,128]{1,0:T(8,128)(2,1)S(1)}, u32[]{:S(2)}, u32[]{:S(2)}) collective-permute-start(bf16[224,128]{1,0:T(8,128)(2,1)S(1)} %add_convert_fusion.6), channel_id=1, source_target_pairs={{0,24},{1,21},{2,22},{3,27},{4,16},{5,29},{6,30},{7,19},{8,28},{9,... | collective-permute-start | bytes 172040 | tf_op jit(solution)/shard_map/ppermute | solution.py:715
  31.4 3.9 %collective-permute-start.12 = (bf16[224,128]{1,0:T(8,128)(2,1)S(1)}, bf16[224,128]{1,0:T(8,128)(2,1)S(1)}, u32[]{:S(2)}, u32[]{:S(2)}) collective-permute-start(bf16[224,128]{1,0:T(8,128)(2,1)S(1)} %add_convert_fusion.2), channel_id=1, source_target_pairs={{0,18},{1,16},{2,19},{3,17},{4,21},{5,23},{6,20},{7,22},{8,25},{9,... | collective-permute-start | bytes 172040 | tf_op jit(solution)/shard_map/ppermute | solution.py:715
  33.9 3.7 %collective-permute-start.7 = (bf16[224,128]{1,0:T(8,128)(2,1)S(1)}, bf16[224,128]{1,0:T(8,128)(2,1)S(1)}, u32[]{:S(2)}, u32[]{:S(2)}) collective-permute-start(bf16[224,128]{1,0:T(8,128)(2,1)S(1)} %add_convert_fusion.5), channel_id=1, source_target_pairs={{0,18},{1,16},{2,19},{3,17},{4,21},{5,23},{6,20},{7,22},{8,25},{9,... | collective-permute-start | bytes 172040 | tf_op jit(solution)/shard_map/ppermute | solution.py:715
  35.4 8.0 %collective-permute-start.16 = (bf16[448,128]{1,0:T(8,128)(2,1)S(1)}, bf16[448,128]{1,0:T(8,128)(2,1)S(1)}, u32[]{:S(2)}, u32[]{:S(2)}) collective-permute-start(bf16[448,128]{1,0:T(8,128)(2,1)S(1)} %maximum_select_fusion.3.refs_1_), channel_id=1, source_target_pairs={{0,16},{16,0},{1,17},{17,1},{2,18},{18,2},{3,19},{19,3},{4,20},{20... | collective-permute-start | bytes 344072 | tf_op jit(solution)/shard_map/ppermute | solution.py:704
  35.5 4.2 %collective-permute-start.14 = (bf16[448,128]{1,0:T(8,128)(2,1)S(1)}, bf16[448,128]{1,0:T(8,128)(2,1)S(1)}, u32[]{:S(2)}, u32[]{:S(2)}) collective-permute-start(bf16[448,128]{1,0:T(8,128)(2,1)S(1)} %maximum_select_fusion.3.refs_1_), channel_id=1, source_target_pairs={{0,17},{1,19},{2,16},{3,18},{4,22},{5,20},{6,23},{7,21},{8,26},{9,... | collective-permute-start | bytes 344072 | tf_op jit(solution)/shard_map/ppermute | solution.py:715
  37.6 5.8 %collective-permute-start.15 = (bf16[448,128]{1,0:T(8,128)(2,1)S(1)}, bf16[448,128]{1,0:T(8,128)(2,1)S(1)}, u32[]{:S(2)}, u32[]{:S(2)}) collective-permute-start(bf16[448,128]{1,0:T(8,128)(2,1)S(1)} %maximum_select_fusion.2.refs_0_), channel_id=1, source_target_pairs={{0,16},{16,0},{1,17},{17,1},{2,18},{18,2},{3,19},{19,3},{4,20},{20... | collective-permute-start | bytes 344072 | tf_op jit(solution)/shard_map/ppermute | solution.py:704
  37.8 4.2 %collective-permute-start.13 = (bf16[448,128]{1,0:T(8,128)(2,1)S(1)}, bf16[448,128]{1,0:T(8,128)(2,1)S(1)}, u32[]{:S(2)}, u32[]{:S(2)}) collective-permute-start(bf16[448,128]{1,0:T(8,128)(2,1)S(1)} %maximum_select_fusion.2.refs_0_), channel_id=1, source_target_pairs={{0,17},{1,19},{2,16},{3,18},{4,22},{5,20},{6,23},{7,21},{8,26},{9,... | collective-permute-start | bytes 344072 | tf_op jit(solution)/shard_map/ppermute | solution.py:715
  39.8 3.7 %collective-permute-start.18 = (bf16[448,128]{1,0:T(8,128)(2,1)S(1)}, bf16[448,128]{1,0:T(8,128)(2,1)S(1)}, u32[]{:S(2)}, u32[]{:S(2)}) collective-permute-start(bf16[448,128]{1,0:T(8,128)(2,1)S(1)} %collective-permute-done.14.refs_3_), channel_id=1, source_target_pairs={{0,16},{16,0},{1,17},{17,1},{2,18},{18,2},{3,19},{19,3},{4,20},{20... | collective-permute-start | bytes 344072 | tf_op jit(solution)/shard_map/ppermute | solution.py:704
  42.0 1.4 %collective-permute-start.17 = (bf16[448,128]{1,0:T(8,128)(2,1)S(1)}, bf16[448,128]{1,0:T(8,128)(2,1)S(1)}, u32[]{:S(2)}, u32[]{:S(2)}) collective-permute-start(bf16[448,128]{1,0:T(8,128)(2,1)S(1)} %collective-permute-done.13.refs_2_), channel_id=1, source_target_pairs={{0,16},{16,0},{1,17},{17,1},{2,18},{18,2},{3,19},{19,3},{4,20},{20... | collective-permute-start | bytes 344072 | tf_op jit(solution)/shard_map/ppermute | solution.py:704

commit v7 on v6

--- a/solution.py
+++ b/solution.py
@@ -15,7 +15,7 @@
 CHAINS = 2
 PIECES = 2 * CHAINS
 EPS = 1e-05
-LAG = 4
+LAG = 8
 INV_SQRT2 = 1.0 / math.sqrt(2.0)
 INV_SQRT2PI = 1.0 / math.sqrt(2.0 * math.pi)
 ANY = pl.BlockSpec(memory_space=pl.ANY)
@@ -245,6 +245,7 @@
     rows = n * ctx
     scale = 1.0 / math.sqrt(width // HEADS)
     piece = pack_s.shape[2]
+    scale_low = jnp.asarray(scale, BF16)
     sec = lax.axis_index("section")
     base = sec * n
     lines = steps * keys
@@ -338,6 +339,8 @@
 
     first_step = lax.broadcasted_iota(jnp.int32, (tall, width), 0) % steps == 0
 
+    first_low = jnp.where(first_step, 1.0, 0.0).astype(BF16)
+
     def view_bias(s):
         lost = [jnp.where(views_ref[v, base + s] > 0, 0.0, -1e30).astype(F32) for v in range(views)]
         lost.append(jnp.float32(-1e30))
@@ -361,8 +364,10 @@
     def stem_softmax(s):
         prob = softmax_lines(prob_s[s])
         prob_s[s] = prob
-        mix_s[s, :, :width] = jnp.where(first_step, prob, 0.0).astype(BF16)
-        mix_s[s, :, width : 2 * width] = jnp.where(first_step, 0.0, prob).astype(BF16)
+        prob_low = prob.astype(BF16)
+        even = prob_low * first_low
+        mix_s[s, :, :width] = even
+        mix_s[s, :, width : 2 * width] = prob_low - even
 
     def stem_moments(s):
         turned = x_s[s].T
@@ -410,7 +415,7 @@
     def trunk_scores(s):
         query, key, _ = trunk_rows(s)
         dead = jnp.where(key_step < steps_ref[base + s], 0.0, -1e30).astype(F32)
-        tprob_s[s] = mm_bt(key, spread(query, tmask_low)) * scale + dead
+        tprob_s[s] = mm_bt(key, spread(query * scale_low, tmask_low)) + dead
 
     def trunk_softmax(s):
         prob = softmax_rows(tprob_s[s])
@@ -481,29 +486,21 @@
 
     staged(len(spans), mlp_in, mlp_gelu, mlp_back, mlp_norm_back, mlp_out)
 
-    put("aproj", 0, mm_at(att_s[...], gmid_s[...]))
-    down = mm_at(glow_s[...], up_s[...]).astype(BF16)
-    up = mm_at(norm2_s[...], gpre_s[...])
-    for j in range(ffw // width):
-        cols = slice(width * j, width * (j + 1))
-        put("down", width * j, down[:, cols].T)
-        put("up", width * j, up[:, cols])
-
     def trunk_back_probs(s):
         _, _, value = trunk_rows(s)
         grad_spread = spread(gatt_s[pl.ds(s * ctx, ctx)], tmask_low)
-        gprob_s[s] = mm_bt(value, grad_spread)
+        gprob_s[s] = mm_bt(value, grad_spread).astype(BF16)
         gqkv_s[pl.ds(s * ctx, ctx), 2 * width :] = mm(tlow_s[s], grad_spread).astype(BF16)
 
     def trunk_back_softmax(s):
-        grad_prob = gprob_s[s].astype(BF16).astype(F32)
-        tlow_s[s] = (softmax_rows_grad(tprob_s[s], grad_prob) * scale).astype(BF16)
+        grad_prob = gprob_s[s].astype(F32)
+        tlow_s[s] = softmax_rows_grad(tprob_s[s], grad_prob).astype(BF16)
 
     def trunk_back_rows(s):
         query, key, _ = trunk_rows(s)
         mine = pl.ds(s * ctx, ctx)
-        gqkv_s[mine, :width] = fold(mm_at(tlow_s[s], key), tmask).astype(BF16)
-        gqkv_s[mine, width : 2 * width] = mm(tlow_s[s], spread(query, tmask_low)).astype(BF16)
+        gqkv_s[mine, :width] = (fold(mm_at(tlow_s[s], key), tmask) * scale).astype(BF16)
+        gqkv_s[mine, width : 2 * width] = (mm(tlow_s[s], spread(query, tmask_low)) * scale).astype(BF16)
 
     staged(n, trunk_back_probs, trunk_back_softmax, trunk_back_rows)
 
@@ -524,6 +521,14 @@
     vectors += [jnp.zeros((16 - len(vectors), width), F32)]
     put("vectors", 0, jnp.concatenate(vectors, axis=0))
 
+    put("aproj", 0, mm_at(att_s[...], gmid_s[...]))
+    down = mm_at(glow_s[...], up_s[...]).astype(BF16)
+    up = mm_at(norm2_s[...], gpre_s[...])
+    for j in range(ffw // width):
+        cols = slice(width * j, width * (j + 1))
+        put("down", width * j, down[:, cols].T)
+        put("up", width * j, up[:, cols])
+
     grad_prop = spread_columns(gtok_s[:, :, qry:].reshape(n * steps * ptok, width).astype(F32))
     mixer = mm_at(act_s[...], grad_prop)
     grad_act = mm_bt(grad_prop, mix_cat).astype(BF16).astype(F32)
@@ -547,10 +552,10 @@
 
     def stem_back_probs(s):
         both = mm(x_s[s], ab_s[s, :, : 2 * width])
-        sgrad_s[s] = jnp.where(first_step, both[:, :width], both[:, width:])
+        sgrad_s[s] = jnp.where(first_step, both[:, :width], both[:, width:]).astype(BF16)
 
     def stem_back_softmax(s):
-        grad_prob = sgrad_s[s].astype(BF16).astype(F32)
+        grad_prob = sgrad_s[s].astype(F32)
         mix_s[s, :, 2 * width :] = softmax_lines_grad(prob_s[s], grad_prob).astype(BF16)
 
     def stem_back_moments(s):
@@ -618,7 +623,7 @@
         low(n, steps, half_tok, width),
         low(n, width, tall),
         full(n, tall, HEADS * qry),
-        full(n, tall, HEADS * qry),
+        low(n, tall, HEADS * qry),
         low(n, tall, (steps + 1) * width),
         low(n, width, (steps + 1) * width),
         low(n, width, steps * width),
@@ -631,7 +636,7 @@
         low(rows, 3 * width),
         full(n, ctx, HEADS * ctx),
         low(n, ctx, HEADS * ctx),
-        full(n, ctx, HEADS * ctx),
+        low(n, ctx, HEADS * ctx),
         low(rows, width),
         full(rows, width),
         full(rows, ffw),

time: 45.1 us -> 44.6 us (0.989)
  Pallas kernels: 12.9 us -> 12.4 us
where the time goes in v7:
time: 44.6 us; the launch traced here: 44.5 us
  starting transfers between devices  21.1 us (47%)
  Pallas kernels  12.4 us (28%)
  waiting for transfers between devices  9.25 us (21%)
  between operations  0.87 us (2%)
  other arithmetic  0.71 us (2%)
    ppermute x12, starting transfers between devices, swap_chips(): return lax.ppermute(value, ('section', 'dp'), pairs)  19 us
    pallas_call x1, Pallas kernels, compute(): pl.pallas_call(functools.partial(compute_kernel, dims), out_shape=(low(2,...  10.1 us
    ppermute x12, waiting for transfers between devices, swap_chips(): return lax.ppermute(value, ('section', 'dp'), pairs)  8.26 us
    ppermute x7, starting transfers between devices, swap_cores(): return lax.ppermute(value, 'section', [(0, 1), (1, 0)])  2.1 us
    pallas_call x1, Pallas kernels, finish(): pl.pallas_call(functools.partial(finish_kernel, table), out_shape=tuple((...  1.47 us
    ppermute x7, waiting for transfers between devices, swap_cores(): return lax.ppermute(value, 'section', [(0, 1), (1, 0)])  1 us
    pallas_call x1, Pallas kernels, send_out(): pl.pallas_call(functools.partial(send_kernel, len(values)), out_shape=tup...  0.9 us
  transfers between devices with their start and end apart: 19, of which 10 were waited for; matrix products, arithmetic and copies ran while one was open for 2% of the time, Pallas kernels for 2%

profile of v7, /device:TPU:0, one launch (start us, length us, event | category | flops | bytes accessed | tf_op | source)
XLA Modules:
  0.0 44.5 jit_solution(7319338470030713962)
XLA Ops:
  0.7 10.1 %stem_trunk.1 = (bf16[2,448,128]{2,1,0:T(8,128)(2,1)S(1)}, bf16[2,448,128]{2,1,0:T(8,128)(2,1)S(1)}, bf16[2,448,128]{2,1,0:T(8,128)(2,1)S(1)}, bf16[2,448,128]{2...) custom-call(s32[16]{0:T(128)} %emb_h.1, s32[16]{0:T(128)} %steps_h.1, ...), custom_call_target="tpu_custom_call" | custom-call | tf_op jit(solution)/shard_map/stem_trunk/pallas_call | solution.py:664
  10.7 0.5 %collective-permute-start = (bf16[2,448,128]{2,1,0:T(8,128)(2,1)S(1)}, bf16[2,448,128]{2,1,0:T(8,128)(2,1)S(1)}, u32[]{:S(2)}, u32[]{:S(2)}) collective-permute-start(bf16[2,448,128]{2,1,0:T(8,128)(2,1)S(1)} %get-tuple-element.48), channel_id=1, source_target_pairs={{0,16},{16,0},{1,17},{17,1},{2,18},{18,2},{3,19},{19,3},{4,20},{20... | collective-permute-start | bytes 688136 | tf_op jit(solution)/shard_map/ppermute | solution.py:709
  11.4 1.0 %collective-permute-done = bf16[2,448,128]{2,1,0:T(8,128)(2,1)S(1)} collective-permute-done((bf16[2,448,128]{2,1,0:T(8,128)(2,1)S(1)}, bf16[2,448,128]{2,1,0:T(8,128)(2,1)S(1)}, u32[]{:S(2)}, u32[]{:S(2)}) %collective-permute-start) | collective-permute-done | bytes 229408 | tf_op jit(solution)/shard_map/ppermute | solution.py:709
  12.5 2.7 %collective-permute-start.8 = (bf16[448,128]{1,0:T(8,128)(2,1)S(1)}, bf16[448,128]{1,0:T(8,128)(2,1)S(1)}, u32[]{:S(2)}, u32[]{:S(2)}) collective-permute-start(bf16[448,128]{1,0:T(8,128)(2,1)S(1)} %select_bitcast_fusion), channel_id=1, source_target_pairs={{0,17},{1,19},{2,16},{3,18},{4,22},{5,20},{6,23},{7,21},{8,26},{9,... | collective-permute-start | bytes 344072 | tf_op jit(solution)/shard_map/ppermute | solution.py:720
  15.9 1.7 %collective-permute-done.8 = bf16[448,128]{1,0:T(8,128)(2,1)S(1)} collective-permute-done((bf16[448,128]{1,0:T(8,128)(2,1)S(1)}, bf16[448,128]{1,0:T(8,128)(2,1)S(1)}, u32[]{:S(2)}, u32[]{:S(2)}) %collective-permute-start.8) | collective-permute-done | bytes 114720 | tf_op jit(solution)/shard_map/ppermute | solution.py:720
  17.7 2.1 %collective-permute-start.9 = (bf16[224,128]{1,0:T(8,128)(2,1)S(1)}, bf16[224,128]{1,0:T(8,128)(2,1)S(1)}, u32[]{:S(2)}, u32[]{:S(2)}) collective-permute-start(bf16[224,128]{1,0:T(8,128)(2,1)S(1)} %broadcast_select_fusion), channel_id=1, source_target_pairs={{0,18},{1,16},{2,19},{3,17},{4,21},{5,23},{6,20},{7,22},{8,25},{9,... | collective-permute-start | bytes 172040 | tf_op jit(solution)/shard_map/ppermute | solution.py:720
  19.9 1.3 %collective-permute-start.4 = (bf16[224,128]{1,0:T(8,128)(2,1)S(1)}, bf16[224,128]{1,0:T(8,128)(2,1)S(1)}, u32[]{:S(2)}, u32[]{:S(2)}) collective-permute-start(bf16[224,128]{1,0:T(8,128)(2,1)S(1)} %broadcast_select_fusion.1), channel_id=1, source_target_pairs={{0,18},{1,16},{2,19},{3,17},{4,21},{5,23},{6,20},{7,22},{8,25},{9,... | collective-permute-start | bytes 172040 | tf_op jit(solution)/shard_map/ppermute | solution.py:720
  21.1 0.5 %collective-permute-done.9 = bf16[224,128]{1,0:T(8,128)(2,1)S(1)} collective-permute-done((bf16[224,128]{1,0:T(8,128)(2,1)S(1)}, bf16[224,128]{1,0:T(8,128)(2,1)S(1)}, u32[]{:S(2)}, u32[]{:S(2)}) %collective-permute-start.9) | collective-permute-done | bytes 57376 | tf_op jit(solution)/shard_map/ppermute | solution.py:720
  21.7 1.9 %collective-permute-start.10 = (bf16[224,128]{1,0:T(8,128)(2,1)S(1)}, bf16[224,128]{1,0:T(8,128)(2,1)S(1)}, u32[]{:S(2)}, u32[]{:S(2)}) collective-permute-start(bf16[224,128]{1,0:T(8,128)(2,1)S(1)} %add_convert_fusion.4), channel_id=1, source_target_pairs={{0,20},{1,25},{2,26},{3,23},{4,28},{5,17},{6,18},{7,31},{8,16},{9,... | collective-permute-start | bytes 172040 | tf_op jit(solution)/shard_map/ppermute | solution.py:720
  23.6 1.3 %collective-permute-start.5 = (bf16[224,128]{1,0:T(8,128)(2,1)S(1)}, bf16[224,128]{1,0:T(8,128)(2,1)S(1)}, u32[]{:S(2)}, u32[]{:S(2)}) collective-permute-start(bf16[224,128]{1,0:T(8,128)(2,1)S(1)} %add_convert_fusion.7), channel_id=1, source_target_pairs={{0,20},{1,25},{2,26},{3,23},{4,28},{5,17},{6,18},{7,31},{8,16},{9,... | collective-permute-start | bytes 172040 | tf_op jit(solution)/shard_map/ppermute | solution.py:720
  24.9 0.6 %collective-permute-done.10 = bf16[224,128]{1,0:T(8,128)(2,1)S(1)} collective-permute-done((bf16[224,128]{1,0:T(8,128)(2,1)S(1)}, bf16[224,128]{1,0:T(8,128)(2,1)S(1)}, u32[]{:S(2)}, u32[]{:S(2)}) %collective-permute-start.10) | collective-permute-done | bytes 57376 | tf_op jit(solution)/shard_map/ppermute | solution.py:720
  25.6 3.0 %collective-permute-start.11 = (bf16[224,128]{1,0:T(8,128)(2,1)S(1)}, bf16[224,128]{1,0:T(8,128)(2,1)S(1)}, u32[]{:S(2)}, u32[]{:S(2)}) collective-permute-start(bf16[224,128]{1,0:T(8,128)(2,1)S(1)} %add_convert_fusion.3), channel_id=1, source_target_pairs={{0,24},{1,21},{2,22},{3,27},{4,16},{5,29},{6,30},{7,19},{8,28},{9,... | collective-permute-start | bytes 172040 | tf_op jit(solution)/shard_map/ppermute | solution.py:720
  28.6 1.3 %collective-permute-start.6 = (bf16[224,128]{1,0:T(8,128)(2,1)S(1)}, bf16[224,128]{1,0:T(8,128)(2,1)S(1)}, u32[]{:S(2)}, u32[]{:S(2)}) collective-permute-start(bf16[224,128]{1,0:T(8,128)(2,1)S(1)} %add_convert_fusion.6), channel_id=1, source_target_pairs={{0,24},{1,21},{2,22},{3,27},{4,16},{5,29},{6,30},{7,19},{8,28},{9,... | collective-permute-start | bytes 172040 | tf_op jit(solution)/shard_map/ppermute | solution.py:720
  29.9 1.0 %collective-permute-done.11 = bf16[224,128]{1,0:T(8,128)(2,1)S(1)} collective-permute-done((bf16[224,128]{1,0:T(8,128)(2,1)S(1)}, bf16[224,128]{1,0:T(8,128)(2,1)S(1)}, u32[]{:S(2)}, u32[]{:S(2)}) %collective-permute-start.11) | collective-permute-done | bytes 57376 | tf_op jit(solution)/shard_map/ppermute | solution.py:720
  30.9 2.1 %collective-permute-start.12 = (bf16[224,128]{1,0:T(8,128)(2,1)S(1)}, bf16[224,128]{1,0:T(8,128)(2,1)S(1)}, u32[]{:S(2)}, u32[]{:S(2)}) collective-permute-start(bf16[224,128]{1,0:T(8,128)(2,1)S(1)} %add_convert_fusion.2), channel_id=1, source_target_pairs={{0,18},{1,16},{2,19},{3,17},{4,21},{5,23},{6,20},{7,22},{8,25},{9,... | collective-permute-start | bytes 172040 | tf_op jit(solution)/shard_map/ppermute | solution.py:720
  33.0 0.4 collective-permute-done.6
  33.5 1.0 %collective-permute-start.7 = (bf16[224,128]{1,0:T(8,128)(2,1)S(1)}, bf16[224,128]{1,0:T(8,128)(2,1)S(1)}, u32[]{:S(2)}, u32[]{:S(2)}) collective-permute-start(bf16[224,128]{1,0:T(8,128)(2,1)S(1)} %add_convert_fusion.5), channel_id=1, source_target_pairs={{0,18},{1,16},{2,19},{3,17},{4,21},{5,23},{6,20},{7,22},{8,25},{9,... | collective-permute-start | bytes 172040 | tf_op jit(solution)/shard_map/ppermute | solution.py:720
  35.1 1.2 %collective-permute-start.14 = (bf16[448,128]{1,0:T(8,128)(2,1)S(1)}, bf16[448,128]{1,0:T(8,128)(2,1)S(1)}, u32[]{:S(2)}, u32[]{:S(2)}) collective-permute-start(bf16[448,128]{1,0:T(8,128)(2,1)S(1)} %maximum_select_fusion.3.refs_1_), channel_id=1, source_target_pairs={{0,17},{1,19},{2,16},{3,18},{4,22},{5,20},{6,23},{7,21},{8,26},{9,... | collective-permute-start | bytes 344072 | tf_op jit(solution)/shard_map/ppermute | solution.py:720
  36.3 0.9 %collective-permute-done.7 = bf16[224,128]{1,0:T(8,128)(2,1)S(1)} collective-permute-done((bf16[224,128]{1,0:T(8,128)(2,1)S(1)}, bf16[224,128]{1,0:T(8,128)(2,1)S(1)}, u32[]{:S(2)}, u32[]{:S(2)}) %collective-permute-start.7) | collective-permute-done | bytes 57376 | tf_op jit(solution)/shard_map/ppermute | solution.py:720
  37.4 0.9 %collective-permute-start.13 = (bf16[448,128]{1,0:T(8,128)(2,1)S(1)}, bf16[448,128]{1,0:T(8,128)(2,1)S(1)}, u32[]{:S(2)}, u32[]{:S(2)}) collective-permute-start(bf16[448,128]{1,0:T(8,128)(2,1)S(1)} %maximum_select_fusion.2.refs_0_), channel_id=1, source_target_pairs={{0,17},{1,19},{2,16},{3,18},{4,22},{5,20},{6,23},{7,21},{8,26},{9,... | collective-permute-start | bytes 344072 | tf_op jit(solution)/shard_map/ppermute | solution.py:720
  38.5 0.8 %collective-permute-done.14.refs_3_ = bf16[448,128]{1,0:T(8,128)(2,1)S(1)} collective-permute-done((bf16[448,128]{1,0:T(8,128)(2,1)S(1)}, bf16[448,128]{1,0:T(8,128)(2,1)S(1)}, u32[]{:S(2)}, u32[]{:S(2)}) %collective-permute-start.14) | collective-permute-done | bytes 114720 | tf_op jit(solution)/shard_map/ppermute | solution.py:720
  39.7 1.9 %collective-permute-done.13.refs_2_ = bf16[448,128]{1,0:T(8,128)(2,1)S(1)} collective-permute-done((bf16[448,128]{1,0:T(8,128)(2,1)S(1)}, bf16[448,128]{1,0:T(8,128)(2,1)S(1)}, u32[]{:S(2)}, u32[]{:S(2)}) %collective-permute-start.13) | collective-permute-done | bytes 114720 | tf_op jit(solution)/shard_map/ppermute | solution.py:720
  42.0 0.9 %send_out.1 = (bf16[16,32,128]{2,1,0:T(8,128)(2,1)}, bf16[147,16,128]{2,1,0:T(8,128)(2,1)}, bf16[16,16,64]{2,1,0:T(8,128)(2,1)}) custom-call(bf16[16,32,128]{2,1,0:T(8,128)(2,1)S(1)} %maximum_select_fusion.1.refs_0_, bf16[147,16,128]{2,1,0:T(8,128)(2,1)S(1)} %maximum_select_fusion.refs_1_, bf16[16,16,64]{2,1,0:T(8,128)(2,1)S(1)} %maximum_select_fusion.4.refs_2_), custom_call_target="tpu_custom_call" | custom-call | tf_op jit(solution)/shard_map/send_out/pallas_call | solution.py:733
  43.0 1.5 %finish.1 = (f32[4,16,128]{2,1,0:T(8,128)}, f32[4,128,128]{2,1,0:T(8,128)}, f32[4,128,128]{2,1,0:T(8,128)}, f32[128,128]{1,0:T(8,128)}, f32[4,64,128]{2,1,0:T(8,...) custom-call(bf16[448,128]{1,0:T(8,128)(2,1)S(1)} %maximum_select_fus, ...), custom_call_target="tpu_custom_call" | custom-call | tf_op jit(solution)/shard_map/finish/pallas_call | solution.py:783
  (42 shorter events, 3.0 us)
Async XLA Ops:
  10.7 1.6 %collective-permute-start = (bf16[2,448,128]{2,1,0:T(8,128)(2,1)S(1)}, bf16[2,448,128]{2,1,0:T(8,128)(2,1)S(1)}, u32[]{:S(2)}, u32[]{:S(2)}) collective-permute-start(bf16[2,448,128]{2,1,0:T(8,128)(2,1)S(1)} %get-tuple-element.48), channel_id=1, source_target_pairs={{0,16},{16,0},{1,17},{17,1},{2,18},{18,2},{3,19},{19,3},{4,20},{20... | collective-permute-start | bytes 688136 | tf_op jit(solution)/shard_map/ppermute | solution.py:709
  11.2 3.9 %collective-permute-start.2 = (bf16[2,448,128]{2,1,0:T(8,128)(2,1)S(1)}, bf16[2,448,128]{2,1,0:T(8,128)(2,1)S(1)}, u32[]{:S(2)}, u32[]{:S(2)}) collective-permute-start(bf16[2,448,128]{2,1,0:T(8,128)(2,1)S(1)} %get-tuple-element.55), channel_id=1, source_target_pairs={{0,16},{16,0},{1,17},{17,1},{2,18},{18,2},{3,19},{19,3},{4,20},{20... | collective-permute-start | bytes 688136 | tf_op jit(solution)/shard_map/ppermute | solution.py:709
  12.5 5.1 %collective-permute-start.8 = (bf16[448,128]{1,0:T(8,128)(2,1)S(1)}, bf16[448,128]{1,0:T(8,128)(2,1)S(1)}, u32[]{:S(2)}, u32[]{:S(2)}) collective-permute-start(bf16[448,128]{1,0:T(8,128)(2,1)S(1)} %select_bitcast_fusion), channel_id=1, source_target_pairs={{0,17},{1,19},{2,16},{3,18},{4,22},{5,20},{6,23},{7,21},{8,26},{9,... | collective-permute-start | bytes 344072 | tf_op jit(solution)/shard_map/ppermute | solution.py:720
  15.2 4.6 %collective-permute-start.3 = (bf16[448,128]{1,0:T(8,128)(2,1)S(1)}, bf16[448,128]{1,0:T(8,128)(2,1)S(1)}, u32[]{:S(2)}, u32[]{:S(2)}) collective-permute-start(bf16[448,128]{1,0:T(8,128)(2,1)S(1)} %select_bitcast_fusion.1), channel_id=1, source_target_pairs={{0,17},{1,19},{2,16},{3,18},{4,22},{5,20},{6,23},{7,21},{8,26},{9,... | collective-permute-start | bytes 344072 | tf_op jit(solution)/shard_map/ppermute | solution.py:720
  15.5 22.8 %collective-permute-start.1 = (bf16[1560,128]{1,0:T(8,128)(2,1)S(1)}, bf16[1560,128]{1,0:T(8,128)(2,1)S(1)}, u32[]{:S(2)}, u32[]{:S(2)}) collective-permute-start(bf16[1560,128]{1,0:T(8,128)(2,1)S(1)} %get-tuple-element.50), channel_id=1, source_target_pairs={{0,16},{16,0},{1,17},{17,1},{2,18},{18,2},{3,19},{19,3},{4,20},{20... | collective-permute-start | bytes 1198088 | tf_op jit(solution)/shard_map/ppermute | solution.py:709
  17.7 4.0 %collective-permute-start.9 = (bf16[224,128]{1,0:T(8,128)(2,1)S(1)}, bf16[224,128]{1,0:T(8,128)(2,1)S(1)}, u32[]{:S(2)}, u32[]{:S(2)}) collective-permute-start(bf16[224,128]{1,0:T(8,128)(2,1)S(1)} %broadcast_select_fusion), channel_id=1, source_target_pairs={{0,18},{1,16},{2,19},{3,17},{4,21},{5,23},{6,20},{7,22},{8,25},{9,... | collective-permute-start | bytes 172040 | tf_op jit(solution)/shard_map/ppermute | solution.py:720
  19.9 3.7 %collective-permute-start.4 = (bf16[224,128]{1,0:T(8,128)(2,1)S(1)}, bf16[224,128]{1,0:T(8,128)(2,1)S(1)}, u32[]{:S(2)}, u32[]{:S(2)}) collective-permute-start(bf16[224,128]{1,0:T(8,128)(2,1)S(1)} %broadcast_select_fusion.1), channel_id=1, source_target_pairs={{0,18},{1,16},{2,19},{3,17},{4,21},{5,23},{6,20},{7,22},{8,25},{9,... | collective-permute-start | bytes 172040 | tf_op jit(solution)/shard_map/ppermute | solution.py:720
  21.7 3.9 %collective-permute-start.10 = (bf16[224,128]{1,0:T(8,128)(2,1)S(1)}, bf16[224,128]{1,0:T(8,128)(2,1)S(1)}, u32[]{:S(2)}, u32[]{:S(2)}) collective-permute-start(bf16[224,128]{1,0:T(8,128)(2,1)S(1)} %add_convert_fusion.4), channel_id=1, source_target_pairs={{0,20},{1,25},{2,26},{3,23},{4,28},{5,17},{6,18},{7,31},{8,16},{9,... | collective-permute-start | bytes 172040 | tf_op jit(solution)/shard_map/ppermute | solution.py:720
  23.6 5.0 %collective-permute-start.5 = (bf16[224,128]{1,0:T(8,128)(2,1)S(1)}, bf16[224,128]{1,0:T(8,128)(2,1)S(1)}, u32[]{:S(2)}, u32[]{:S(2)}) collective-permute-start(bf16[224,128]{1,0:T(8,128)(2,1)S(1)} %add_convert_fusion.7), channel_id=1, source_target_pairs={{0,20},{1,25},{2,26},{3,23},{4,28},{5,17},{6,18},{7,31},{8,16},{9,... | collective-permute-start | bytes 172040 | tf_op jit(solution)/shard_map/ppermute | solution.py:720
  25.6 5.3 %collective-permute-start.11 = (bf16[224,128]{1,0:T(8,128)(2,1)S(1)}, bf16[224,128]{1,0:T(8,128)(2,1)S(1)}, u32[]{:S(2)}, u32[]{:S(2)}) collective-permute-start(bf16[224,128]{1,0:T(8,128)(2,1)S(1)} %add_convert_fusion.3), channel_id=1, source_target_pairs={{0,24},{1,21},{2,22},{3,27},{4,16},{5,29},{6,30},{7,19},{8,28},{9,... | collective-permute-start | bytes 172040 | tf_op jit(solution)/shard_map/ppermute | solution.py:720
  28.6 4.9 %collective-permute-start.6 = (bf16[224,128]{1,0:T(8,128)(2,1)S(1)}, bf16[224,128]{1,0:T(8,128)(2,1)S(1)}, u32[]{:S(2)}, u32[]{:S(2)}) collective-permute-start(bf16[224,128]{1,0:T(8,128)(2,1)S(1)} %add_convert_fusion.6), channel_id=1, source_target_pairs={{0,24},{1,21},{2,22},{3,27},{4,16},{5,29},{6,30},{7,19},{8,28},{9,... | collective-permute-start | bytes 172040 | tf_op jit(solution)/shard_map/ppermute | solution.py:720
  30.9 3.9 %collective-permute-start.12 = (bf16[224,128]{1,0:T(8,128)(2,1)S(1)}, bf16[224,128]{1,0:T(8,128)(2,1)S(1)}, u32[]{:S(2)}, u32[]{:S(2)}) collective-permute-start(bf16[224,128]{1,0:T(8,128)(2,1)S(1)} %add_convert_fusion.2), channel_id=1, source_target_pairs={{0,18},{1,16},{2,19},{3,17},{4,21},{5,23},{6,20},{7,22},{8,25},{9,... | collective-permute-start | bytes 172040 | tf_op jit(solution)/shard_map/ppermute | solution.py:720
  33.5 3.7 %collective-permute-start.7 = (bf16[224,128]{1,0:T(8,128)(2,1)S(1)}, bf16[224,128]{1,0:T(8,128)(2,1)S(1)}, u32[]{:S(2)}, u32[]{:S(2)}) collective-permute-start(bf16[224,128]{1,0:T(8,128)(2,1)S(1)} %add_convert_fusion.5), channel_id=1, source_target_pairs={{0,18},{1,16},{2,19},{3,17},{4,21},{5,23},{6,20},{7,22},{8,25},{9,... | collective-permute-start | bytes 172040 | tf_op jit(solution)/shard_map/ppermute | solution.py:720
  34.9 8.0 %collective-permute-start.16 = (bf16[448,128]{1,0:T(8,128)(2,1)S(1)}, bf16[448,128]{1,0:T(8,128)(2,1)S(1)}, u32[]{:S(2)}, u32[]{:S(2)}) collective-permute-start(bf16[448,128]{1,0:T(8,128)(2,1)S(1)} %maximum_select_fusion.3.refs_1_), channel_id=1, source_target_pairs={{0,16},{16,0},{1,17},{17,1},{2,18},{18,2},{3,19},{19,3},{4,20},{20... | collective-permute-start | bytes 344072 | tf_op jit(solution)/shard_map/ppermute | solution.py:709
  35.1 4.2 %collective-permute-start.14 = (bf16[448,128]{1,0:T(8,128)(2,1)S(1)}, bf16[448,128]{1,0:T(8,128)(2,1)S(1)}, u32[]{:S(2)}, u32[]{:S(2)}) collective-permute-start(bf16[448,128]{1,0:T(8,128)(2,1)S(1)} %maximum_select_fusion.3.refs_1_), channel_id=1, source_target_pairs={{0,17},{1,19},{2,16},{3,18},{4,22},{5,20},{6,23},{7,21},{8,26},{9,... | collective-permute-start | bytes 344072 | tf_op jit(solution)/shard_map/ppermute | solution.py:720
  37.2 5.8 %collective-permute-start.15 = (bf16[448,128]{1,0:T(8,128)(2,1)S(1)}, bf16[448,128]{1,0:T(8,128)(2,1)S(1)}, u32[]{:S(2)}, u32[]{:S(2)}) collective-permute-start(bf16[448,128]{1,0:T(8,128)(2,1)S(1)} %maximum_select_fusion.2.refs_0_), channel_id=1, source_target_pairs={{0,16},{16,0},{1,17},{17,1},{2,18},{18,2},{3,19},{19,3},{4,20},{20... | collective-permute-start | bytes 344072 | tf_op jit(solution)/shard_map/ppermute | solution.py:709
  37.4 4.2 %collective-permute-start.13 = (bf16[448,128]{1,0:T(8,128)(2,1)S(1)}, bf16[448,128]{1,0:T(8,128)(2,1)S(1)}, u32[]{:S(2)}, u32[]{:S(2)}) collective-permute-start(bf16[448,128]{1,0:T(8,128)(2,1)S(1)} %maximum_select_fusion.2.refs_0_), channel_id=1, source_target_pairs={{0,17},{1,19},{2,16},{3,18},{4,22},{5,20},{6,23},{7,21},{8,26},{9,... | collective-permute-start | bytes 344072 | tf_op jit(solution)/shard_map/ppermute | solution.py:720
  39.3 3.7 %collective-permute-start.18 = (bf16[448,128]{1,0:T(8,128)(2,1)S(1)}, bf16[448,128]{1,0:T(8,128)(2,1)S(1)}, u32[]{:S(2)}, u32[]{:S(2)}) collective-permute-start(bf16[448,128]{1,0:T(8,128)(2,1)S(1)} %collective-permute-done.14.refs_3_), channel_id=1, source_target_pairs={{0,16},{16,0},{1,17},{17,1},{2,18},{18,2},{3,19},{19,3},{4,20},{20... | collective-permute-start | bytes 344072 | tf_op jit(solution)/shard_map/ppermute | solution.py:709
  41.6 1.4 %collective-permute-start.17 = (bf16[448,128]{1,0:T(8,128)(2,1)S(1)}, bf16[448,128]{1,0:T(8,128)(2,1)S(1)}, u32[]{:S(2)}, u32[]{:S(2)}) collective-permute-start(bf16[448,128]{1,0:T(8,128)(2,1)S(1)} %collective-permute-done.13.refs_2_), channel_id=1, source_target_pairs={{0,16},{16,0},{1,17},{17,1},{2,18},{18,2},{3,19},{19,3},{4,20},{20... | collective-permute-start | bytes 344072 | tf_op jit(solution)/shard_map/ppermute | solution.py:709

commit v8 on v7

--- a/solution.py
+++ b/solution.py
@@ -198,7 +198,9 @@
     p_s,
     g_s,
     qs_s,
+    qst_s,
     a_s,
+    keys_s,
     tok_s,
     xt_s,
     prob_s,
@@ -305,6 +307,7 @@
     for e in range(emb):
         qs = spread(queries[e], smask_low)
         qs_s[e] = qs
+        qst_s[e] = (qs * scale_low).T
         a_s[e] = (mm_bt(key_w[e], qs) * scale).astype(BF16)
 
     ready(4)
@@ -358,8 +361,11 @@
                 at = stop
         return jnp.concatenate(tiles, axis=0)
 
+    def stem_keys(s):
+        keys_s[s] = mm(x_s[s], key_w[embs[s]]).astype(BF16)
+
     def stem_scores(s):
-        prob_s[s] = mm(x_s[s], a_s[embs[s]]) + view_bias(s)
+        prob_s[s] = mm(keys_s[s], qst_s[embs[s]]) + view_bias(s)
 
     def stem_softmax(s):
         prob = softmax_lines(prob_s[s])
@@ -380,7 +386,7 @@
             satt_s[s, t] = fold(values[width * t : width * (t + 1)], smask).astype(BF16)
 
     ready(6)
-    staged(n, stem_scores, stem_softmax, stem_moments, stem_values)
+    staged(n, stem_keys, stem_scores, stem_softmax, stem_moments, stem_values)
     ready(10)
     image_tok = mm(satt_s[...].reshape(n * steps * qry, width), stem_proj[...])
     tok_s[:, :, :qry] = image_tok.astype(BF16).reshape(n, steps, qry, width)
@@ -620,6 +626,8 @@
         low(n, ctx, width),
         low(emb, HEADS * qry, width),
         low(emb, width, HEADS * qry),
+        low(emb, width, HEADS * qry),
+        low(n, tall, width),
         low(n, steps, half_tok, width),
         low(n, width, tall),
         full(n, tall, HEADS * qry),

time: 44.6 us -> 44.8 us (level)
  no operation moved by 1% of the time
where the time goes in v8:
time: 44.8 us; the launch traced here: 44.6 us
  starting transfers between devices  21.1 us (47%)
  Pallas kernels  12.6 us (28%)
  waiting for transfers between devices  9.26 us (21%)
  between operations  0.87 us (2%)
  other arithmetic  0.71 us (2%)
    ppermute x12, starting transfers between devices, swap_chips(): return lax.ppermute(value, ('section', 'dp'), pairs)  19 us
    pallas_call x1, Pallas kernels, compute(): pl.pallas_call(functools.partial(compute_kernel, dims), out_shape=(low(2,...  10.2 us
    ppermute x12, waiting for transfers between devices, swap_chips(): return lax.ppermute(value, ('section', 'dp'), pairs)  8.26 us
    ppermute x7, starting transfers between devices, swap_cores(): return lax.ppermute(value, 'section', [(0, 1), (1, 0)])  2.1 us
    pallas_call x1, Pallas kernels, finish(): pl.pallas_call(functools.partial(finish_kernel, table), out_shape=tuple((...  1.47 us
    ppermute x7, waiting for transfers between devices, swap_cores(): return lax.ppermute(value, 'section', [(0, 1), (1, 0)])  1 us
    pallas_call x1, Pallas kernels, send_out(): pl.pallas_call(functools.partial(send_kernel, len(values)), out_shape=tup...  0.9 us
  transfers between devices with their start and end apart: 19, of which 10 were waited for; matrix products, arithmetic and copies ran while one was open for 2% of the time, Pallas kernels for 2%

profile of v8, /device:TPU:0, one launch (start us, length us, event | category | flops | bytes accessed | tf_op | source)
XLA Modules:
  0.0 44.6 jit_solution(15918387609230161423)
XLA Ops:
  0.7 10.2 %stem_trunk.1 = (bf16[2,448,128]{2,1,0:T(8,128)(2,1)S(1)}, bf16[2,448,128]{2,1,0:T(8,128)(2,1)S(1)}, bf16[2,448,128]{2,1,0:T(8,128)(2,1)S(1)}, bf16[2,448,128]{2...) custom-call(s32[16]{0:T(128)} %emb_h.1, s32[16]{0:T(128)} %steps_h.1, ...), custom_call_target="tpu_custom_call" | custom-call | tf_op jit(solution)/shard_map/stem_trunk/pallas_call | solution.py:672
  10.9 0.5 %collective-permute-start = (bf16[2,448,128]{2,1,0:T(8,128)(2,1)S(1)}, bf16[2,448,128]{2,1,0:T(8,128)(2,1)S(1)}, u32[]{:S(2)}, u32[]{:S(2)}) collective-permute-start(bf16[2,448,128]{2,1,0:T(8,128)(2,1)S(1)} %get-tuple-element.48), channel_id=1, source_target_pairs={{0,16},{16,0},{1,17},{17,1},{2,18},{18,2},{3,19},{19,3},{4,20},{20... | collective-permute-start | bytes 688136 | tf_op jit(solution)/shard_map/ppermute | solution.py:717
  11.6 1.0 %collective-permute-done = bf16[2,448,128]{2,1,0:T(8,128)(2,1)S(1)} collective-permute-done((bf16[2,448,128]{2,1,0:T(8,128)(2,1)S(1)}, bf16[2,448,128]{2,1,0:T(8,128)(2,1)S(1)}, u32[]{:S(2)}, u32[]{:S(2)}) %collective-permute-start) | collective-permute-done | bytes 229408 | tf_op jit(solution)/shard_map/ppermute | solution.py:717
  12.6 2.7 %collective-permute-start.8 = (bf16[448,128]{1,0:T(8,128)(2,1)S(1)}, bf16[448,128]{1,0:T(8,128)(2,1)S(1)}, u32[]{:S(2)}, u32[]{:S(2)}) collective-permute-start(bf16[448,128]{1,0:T(8,128)(2,1)S(1)} %select_bitcast_fusion), channel_id=1, source_target_pairs={{0,17},{1,19},{2,16},{3,18},{4,22},{5,20},{6,23},{7,21},{8,26},{9,... | collective-permute-start | bytes 344072 | tf_op jit(solution)/shard_map/ppermute | solution.py:728
  16.0 1.7 %collective-permute-done.8 = bf16[448,128]{1,0:T(8,128)(2,1)S(1)} collective-permute-done((bf16[448,128]{1,0:T(8,128)(2,1)S(1)}, bf16[448,128]{1,0:T(8,128)(2,1)S(1)}, u32[]{:S(2)}, u32[]{:S(2)}) %collective-permute-start.8) | collective-permute-done | bytes 114720 | tf_op jit(solution)/shard_map/ppermute | solution.py:728
  17.8 2.1 %collective-permute-start.9 = (bf16[224,128]{1,0:T(8,128)(2,1)S(1)}, bf16[224,128]{1,0:T(8,128)(2,1)S(1)}, u32[]{:S(2)}, u32[]{:S(2)}) collective-permute-start(bf16[224,128]{1,0:T(8,128)(2,1)S(1)} %broadcast_select_fusion), channel_id=1, source_target_pairs={{0,18},{1,16},{2,19},{3,17},{4,21},{5,23},{6,20},{7,22},{8,25},{9,... | collective-permute-start | bytes 172040 | tf_op jit(solution)/shard_map/ppermute | solution.py:728
  20.0 1.3 %collective-permute-start.4 = (bf16[224,128]{1,0:T(8,128)(2,1)S(1)}, bf16[224,128]{1,0:T(8,128)(2,1)S(1)}, u32[]{:S(2)}, u32[]{:S(2)}) collective-permute-start(bf16[224,128]{1,0:T(8,128)(2,1)S(1)} %broadcast_select_fusion.1), channel_id=1, source_target_pairs={{0,18},{1,16},{2,19},{3,17},{4,21},{5,23},{6,20},{7,22},{8,25},{9,... | collective-permute-start | bytes 172040 | tf_op jit(solution)/shard_map/ppermute | solution.py:728
  21.3 0.5 %collective-permute-done.9 = bf16[224,128]{1,0:T(8,128)(2,1)S(1)} collective-permute-done((bf16[224,128]{1,0:T(8,128)(2,1)S(1)}, bf16[224,128]{1,0:T(8,128)(2,1)S(1)}, u32[]{:S(2)}, u32[]{:S(2)}) %collective-permute-start.9) | collective-permute-done | bytes 57376 | tf_op jit(solution)/shard_map/ppermute | solution.py:728
  21.9 1.9 %collective-permute-start.10 = (bf16[224,128]{1,0:T(8,128)(2,1)S(1)}, bf16[224,128]{1,0:T(8,128)(2,1)S(1)}, u32[]{:S(2)}, u32[]{:S(2)}) collective-permute-start(bf16[224,128]{1,0:T(8,128)(2,1)S(1)} %add_convert_fusion.4), channel_id=1, source_target_pairs={{0,20},{1,25},{2,26},{3,23},{4,28},{5,17},{6,18},{7,31},{8,16},{9,... | collective-permute-start | bytes 172040 | tf_op jit(solution)/shard_map/ppermute | solution.py:728
  23.8 1.3 %collective-permute-start.5 = (bf16[224,128]{1,0:T(8,128)(2,1)S(1)}, bf16[224,128]{1,0:T(8,128)(2,1)S(1)}, u32[]{:S(2)}, u32[]{:S(2)}) collective-permute-start(bf16[224,128]{1,0:T(8,128)(2,1)S(1)} %add_convert_fusion.7), channel_id=1, source_target_pairs={{0,20},{1,25},{2,26},{3,23},{4,28},{5,17},{6,18},{7,31},{8,16},{9,... | collective-permute-start | bytes 172040 | tf_op jit(solution)/shard_map/ppermute | solution.py:728
  25.1 0.6 %collective-permute-done.10 = bf16[224,128]{1,0:T(8,128)(2,1)S(1)} collective-permute-done((bf16[224,128]{1,0:T(8,128)(2,1)S(1)}, bf16[224,128]{1,0:T(8,128)(2,1)S(1)}, u32[]{:S(2)}, u32[]{:S(2)}) %collective-permute-start.10) | collective-permute-done | bytes 57376 | tf_op jit(solution)/shard_map/ppermute | solution.py:728
  25.7 3.0 %collective-permute-start.11 = (bf16[224,128]{1,0:T(8,128)(2,1)S(1)}, bf16[224,128]{1,0:T(8,128)(2,1)S(1)}, u32[]{:S(2)}, u32[]{:S(2)}) collective-permute-start(bf16[224,128]{1,0:T(8,128)(2,1)S(1)} %add_convert_fusion.3), channel_id=1, source_target_pairs={{0,24},{1,21},{2,22},{3,27},{4,16},{5,29},{6,30},{7,19},{8,28},{9,... | collective-permute-start | bytes 172040 | tf_op jit(solution)/shard_map/ppermute | solution.py:728
  28.8 1.3 %collective-permute-start.6 = (bf16[224,128]{1,0:T(8,128)(2,1)S(1)}, bf16[224,128]{1,0:T(8,128)(2,1)S(1)}, u32[]{:S(2)}, u32[]{:S(2)}) collective-permute-start(bf16[224,128]{1,0:T(8,128)(2,1)S(1)} %add_convert_fusion.6), channel_id=1, source_target_pairs={{0,24},{1,21},{2,22},{3,27},{4,16},{5,29},{6,30},{7,19},{8,28},{9,... | collective-permute-start | bytes 172040 | tf_op jit(solution)/shard_map/ppermute | solution.py:728
  30.1 1.0 %collective-permute-done.11 = bf16[224,128]{1,0:T(8,128)(2,1)S(1)} collective-permute-done((bf16[224,128]{1,0:T(8,128)(2,1)S(1)}, bf16[224,128]{1,0:T(8,128)(2,1)S(1)}, u32[]{:S(2)}, u32[]{:S(2)}) %collective-permute-start.11) | collective-permute-done | bytes 57376 | tf_op jit(solution)/shard_map/ppermute | solution.py:728
  31.1 2.1 %collective-permute-start.12 = (bf16[224,128]{1,0:T(8,128)(2,1)S(1)}, bf16[224,128]{1,0:T(8,128)(2,1)S(1)}, u32[]{:S(2)}, u32[]{:S(2)}) collective-permute-start(bf16[224,128]{1,0:T(8,128)(2,1)S(1)} %add_convert_fusion.2), channel_id=1, source_target_pairs={{0,18},{1,16},{2,19},{3,17},{4,21},{5,23},{6,20},{7,22},{8,25},{9,... | collective-permute-start | bytes 172040 | tf_op jit(solution)/shard_map/ppermute | solution.py:728
  33.2 0.4 collective-permute-done.6
  33.6 1.0 %collective-permute-start.7 = (bf16[224,128]{1,0:T(8,128)(2,1)S(1)}, bf16[224,128]{1,0:T(8,128)(2,1)S(1)}, u32[]{:S(2)}, u32[]{:S(2)}) collective-permute-start(bf16[224,128]{1,0:T(8,128)(2,1)S(1)} %add_convert_fusion.5), channel_id=1, source_target_pairs={{0,18},{1,16},{2,19},{3,17},{4,21},{5,23},{6,20},{7,22},{8,25},{9,... | collective-permute-start | bytes 172040 | tf_op jit(solution)/shard_map/ppermute | solution.py:728
  35.3 1.2 %collective-permute-start.14 = (bf16[448,128]{1,0:T(8,128)(2,1)S(1)}, bf16[448,128]{1,0:T(8,128)(2,1)S(1)}, u32[]{:S(2)}, u32[]{:S(2)}) collective-permute-start(bf16[448,128]{1,0:T(8,128)(2,1)S(1)} %maximum_select_fusion.3.refs_1_), channel_id=1, source_target_pairs={{0,17},{1,19},{2,16},{3,18},{4,22},{5,20},{6,23},{7,21},{8,26},{9,... | collective-permute-start | bytes 344072 | tf_op jit(solution)/shard_map/ppermute | solution.py:728
  36.4 0.9 %collective-permute-done.7 = bf16[224,128]{1,0:T(8,128)(2,1)S(1)} collective-permute-done((bf16[224,128]{1,0:T(8,128)(2,1)S(1)}, bf16[224,128]{1,0:T(8,128)(2,1)S(1)}, u32[]{:S(2)}, u32[]{:S(2)}) %collective-permute-start.7) | collective-permute-done | bytes 57376 | tf_op jit(solution)/shard_map/ppermute | solution.py:728
  37.5 0.9 %collective-permute-start.13 = (bf16[448,128]{1,0:T(8,128)(2,1)S(1)}, bf16[448,128]{1,0:T(8,128)(2,1)S(1)}, u32[]{:S(2)}, u32[]{:S(2)}) collective-permute-start(bf16[448,128]{1,0:T(8,128)(2,1)S(1)} %maximum_select_fusion.2.refs_0_), channel_id=1, source_target_pairs={{0,17},{1,19},{2,16},{3,18},{4,22},{5,20},{6,23},{7,21},{8,26},{9,... | collective-permute-start | bytes 344072 | tf_op jit(solution)/shard_map/ppermute | solution.py:728
  38.7 0.8 %collective-permute-done.14.refs_3_ = bf16[448,128]{1,0:T(8,128)(2,1)S(1)} collective-permute-done((bf16[448,128]{1,0:T(8,128)(2,1)S(1)}, bf16[448,128]{1,0:T(8,128)(2,1)S(1)}, u32[]{:S(2)}, u32[]{:S(2)}) %collective-permute-start.14) | collective-permute-done | bytes 114720 | tf_op jit(solution)/shard_map/ppermute | solution.py:728
  39.9 1.9 %collective-permute-done.13.refs_2_ = bf16[448,128]{1,0:T(8,128)(2,1)S(1)} collective-permute-done((bf16[448,128]{1,0:T(8,128)(2,1)S(1)}, bf16[448,128]{1,0:T(8,128)(2,1)S(1)}, u32[]{:S(2)}, u32[]{:S(2)}) %collective-permute-start.13) | collective-permute-done | bytes 114720 | tf_op jit(solution)/shard_map/ppermute | solution.py:728
  42.2 0.9 %send_out.1 = (bf16[16,32,128]{2,1,0:T(8,128)(2,1)}, bf16[147,16,128]{2,1,0:T(8,128)(2,1)}, bf16[16,16,64]{2,1,0:T(8,128)(2,1)}) custom-call(bf16[16,32,128]{2,1,0:T(8,128)(2,1)S(1)} %maximum_select_fusion.1.refs_0_, bf16[147,16,128]{2,1,0:T(8,128)(2,1)S(1)} %maximum_select_fusion.refs_1_, bf16[16,16,64]{2,1,0:T(8,128)(2,1)S(1)} %maximum_select_fusion.4.refs_2_), custom_call_target="tpu_custom_call" | custom-call | tf_op jit(solution)/shard_map/send_out/pallas_call | solution.py:741
  43.2 1.5 %finish.1 = (f32[4,16,128]{2,1,0:T(8,128)}, f32[4,128,128]{2,1,0:T(8,128)}, f32[4,128,128]{2,1,0:T(8,128)}, f32[128,128]{1,0:T(8,128)}, f32[4,64,128]{2,1,0:T(8,...) custom-call(bf16[448,128]{1,0:T(8,128)(2,1)S(1)} %maximum_select_fus, ...), custom_call_target="tpu_custom_call" | custom-call | tf_op jit(solution)/shard_map/finish/pallas_call | solution.py:791
  (42 shorter events, 3.0 us)
Async XLA Ops:
  10.9 1.6 %collective-permute-start = (bf16[2,448,128]{2,1,0:T(8,128)(2,1)S(1)}, bf16[2,448,128]{2,1,0:T(8,128)(2,1)S(1)}, u32[]{:S(2)}, u32[]{:S(2)}) collective-permute-start(bf16[2,448,128]{2,1,0:T(8,128)(2,1)S(1)} %get-tuple-element.48), channel_id=1, source_target_pairs={{0,16},{16,0},{1,17},{17,1},{2,18},{18,2},{3,19},{19,3},{4,20},{20... | collective-permute-start | bytes 688136 | tf_op jit(solution)/shard_map/ppermute | solution.py:717
  11.4 3.9 %collective-permute-start.2 = (bf16[2,448,128]{2,1,0:T(8,128)(2,1)S(1)}, bf16[2,448,128]{2,1,0:T(8,128)(2,1)S(1)}, u32[]{:S(2)}, u32[]{:S(2)}) collective-permute-start(bf16[2,448,128]{2,1,0:T(8,128)(2,1)S(1)} %get-tuple-element.55), channel_id=1, source_target_pairs={{0,16},{16,0},{1,17},{17,1},{2,18},{18,2},{3,19},{19,3},{4,20},{20... | collective-permute-start | bytes 688136 | tf_op jit(solution)/shard_map/ppermute | solution.py:717
  12.6 5.1 %collective-permute-start.8 = (bf16[448,128]{1,0:T(8,128)(2,1)S(1)}, bf16[448,128]{1,0:T(8,128)(2,1)S(1)}, u32[]{:S(2)}, u32[]{:S(2)}) collective-permute-start(bf16[448,128]{1,0:T(8,128)(2,1)S(1)} %select_bitcast_fusion), channel_id=1, source_target_pairs={{0,17},{1,19},{2,16},{3,18},{4,22},{5,20},{6,23},{7,21},{8,26},{9,... | collective-permute-start | bytes 344072 | tf_op jit(solution)/shard_map/ppermute | solution.py:728
  15.4 4.6 %collective-permute-start.3 = (bf16[448,128]{1,0:T(8,128)(2,1)S(1)}, bf16[448,128]{1,0:T(8,128)(2,1)S(1)}, u32[]{:S(2)}, u32[]{:S(2)}) collective-permute-start(bf16[448,128]{1,0:T(8,128)(2,1)S(1)} %select_bitcast_fusion.1), channel_id=1, source_target_pairs={{0,17},{1,19},{2,16},{3,18},{4,22},{5,20},{6,23},{7,21},{8,26},{9,... | collective-permute-start | bytes 344072 | tf_op jit(solution)/shard_map/ppermute | solution.py:728
  15.7 22.8 %collective-permute-start.1 = (bf16[1560,128]{1,0:T(8,128)(2,1)S(1)}, bf16[1560,128]{1,0:T(8,128)(2,1)S(1)}, u32[]{:S(2)}, u32[]{:S(2)}) collective-permute-start(bf16[1560,128]{1,0:T(8,128)(2,1)S(1)} %get-tuple-element.50), channel_id=1, source_target_pairs={{0,16},{16,0},{1,17},{17,1},{2,18},{18,2},{3,19},{19,3},{4,20},{20... | collective-permute-start | bytes 1198088 | tf_op jit(solution)/shard_map/ppermute | solution.py:717
  17.8 4.0 %collective-permute-start.9 = (bf16[224,128]{1,0:T(8,128)(2,1)S(1)}, bf16[224,128]{1,0:T(8,128)(2,1)S(1)}, u32[]{:S(2)}, u32[]{:S(2)}) collective-permute-start(bf16[224,128]{1,0:T(8,128)(2,1)S(1)} %broadcast_select_fusion), channel_id=1, source_target_pairs={{0,18},{1,16},{2,19},{3,17},{4,21},{5,23},{6,20},{7,22},{8,25},{9,... | collective-permute-start | bytes 172040 | tf_op jit(solution)/shard_map/ppermute | solution.py:728
  20.0 3.7 %collective-permute-start.4 = (bf16[224,128]{1,0:T(8,128)(2,1)S(1)}, bf16[224,128]{1,0:T(8,128)(2,1)S(1)}, u32[]{:S(2)}, u32[]{:S(2)}) collective-permute-start(bf16[224,128]{1,0:T(8,128)(2,1)S(1)} %broadcast_select_fusion.1), channel_id=1, source_target_pairs={{0,18},{1,16},{2,19},{3,17},{4,21},{5,23},{6,20},{7,22},{8,25},{9,... | collective-permute-start | bytes 172040 | tf_op jit(solution)/shard_map/ppermute | solution.py:728
  21.9 3.8 %collective-permute-start.10 = (bf16[224,128]{1,0:T(8,128)(2,1)S(1)}, bf16[224,128]{1,0:T(8,128)(2,1)S(1)}, u32[]{:S(2)}, u32[]{:S(2)}) collective-permute-start(bf16[224,128]{1,0:T(8,128)(2,1)S(1)} %add_convert_fusion.4), channel_id=1, source_target_pairs={{0,20},{1,25},{2,26},{3,23},{4,28},{5,17},{6,18},{7,31},{8,16},{9,... | collective-permute-start | bytes 172040 | tf_op jit(solution)/shard_map/ppermute | solution.py:728
  23.8 5.0 %collective-permute-start.5 = (bf16[224,128]{1,0:T(8,128)(2,1)S(1)}, bf16[224,128]{1,0:T(8,128)(2,1)S(1)}, u32[]{:S(2)}, u32[]{:S(2)}) collective-permute-start(bf16[224,128]{1,0:T(8,128)(2,1)S(1)} %add_convert_fusion.7), channel_id=1, source_target_pairs={{0,20},{1,25},{2,26},{3,23},{4,28},{5,17},{6,18},{7,31},{8,16},{9,... | collective-permute-start | bytes 172040 | tf_op jit(solution)/shard_map/ppermute | solution.py:728
  25.7 5.3 %collective-permute-start.11 = (bf16[224,128]{1,0:T(8,128)(2,1)S(1)}, bf16[224,128]{1,0:T(8,128)(2,1)S(1)}, u32[]{:S(2)}, u32[]{:S(2)}) collective-permute-start(bf16[224,128]{1,0:T(8,128)(2,1)S(1)} %add_convert_fusion.3), channel_id=1, source_target_pairs={{0,24},{1,21},{2,22},{3,27},{4,16},{5,29},{6,30},{7,19},{8,28},{9,... | collective-permute-start | bytes 172040 | tf_op jit(solution)/shard_map/ppermute | solution.py:728
  28.8 4.9 %collective-permute-start.6 = (bf16[224,128]{1,0:T(8,128)(2,1)S(1)}, bf16[224,128]{1,0:T(8,128)(2,1)S(1)}, u32[]{:S(2)}, u32[]{:S(2)}) collective-permute-start(bf16[224,128]{1,0:T(8,128)(2,1)S(1)} %add_convert_fusion.6), channel_id=1, source_target_pairs={{0,24},{1,21},{2,22},{3,27},{4,16},{5,29},{6,30},{7,19},{8,28},{9,... | collective-permute-start | bytes 172040 | tf_op jit(solution)/shard_map/ppermute | solution.py:728
  31.1 3.9 %collective-permute-start.12 = (bf16[224,128]{1,0:T(8,128)(2,1)S(1)}, bf16[224,128]{1,0:T(8,128)(2,1)S(1)}, u32[]{:S(2)}, u32[]{:S(2)}) collective-permute-start(bf16[224,128]{1,0:T(8,128)(2,1)S(1)} %add_convert_fusion.2), channel_id=1, source_target_pairs={{0,18},{1,16},{2,19},{3,17},{4,21},{5,23},{6,20},{7,22},{8,25},{9,... | collective-permute-start | bytes 172040 | tf_op jit(solution)/shard_map/ppermute | solution.py:728
  33.6 3.7 %collective-permute-start.7 = (bf16[224,128]{1,0:T(8,128)(2,1)S(1)}, bf16[224,128]{1,0:T(8,128)(2,1)S(1)}, u32[]{:S(2)}, u32[]{:S(2)}) collective-permute-start(bf16[224,128]{1,0:T(8,128)(2,1)S(1)} %add_convert_fusion.5), channel_id=1, source_target_pairs={{0,18},{1,16},{2,19},{3,17},{4,21},{5,23},{6,20},{7,22},{8,25},{9,... | collective-permute-start | bytes 172040 | tf_op jit(solution)/shard_map/ppermute | solution.py:728
  35.1 8.0 %collective-permute-start.16 = (bf16[448,128]{1,0:T(8,128)(2,1)S(1)}, bf16[448,128]{1,0:T(8,128)(2,1)S(1)}, u32[]{:S(2)}, u32[]{:S(2)}) collective-permute-start(bf16[448,128]{1,0:T(8,128)(2,1)S(1)} %maximum_select_fusion.3.refs_1_), channel_id=1, source_target_pairs={{0,16},{16,0},{1,17},{17,1},{2,18},{18,2},{3,19},{19,3},{4,20},{20... | collective-permute-start | bytes 344072 | tf_op jit(solution)/shard_map/ppermute | solution.py:717
  35.3 4.2 %collective-permute-start.14 = (bf16[448,128]{1,0:T(8,128)(2,1)S(1)}, bf16[448,128]{1,0:T(8,128)(2,1)S(1)}, u32[]{:S(2)}, u32[]{:S(2)}) collective-permute-start(bf16[448,128]{1,0:T(8,128)(2,1)S(1)} %maximum_select_fusion.3.refs_1_), channel_id=1, source_target_pairs={{0,17},{1,19},{2,16},{3,18},{4,22},{5,20},{6,23},{7,21},{8,26},{9,... | collective-permute-start | bytes 344072 | tf_op jit(solution)/shard_map/ppermute | solution.py:728
  37.4 5.8 %collective-permute-start.15 = (bf16[448,128]{1,0:T(8,128)(2,1)S(1)}, bf16[448,128]{1,0:T(8,128)(2,1)S(1)}, u32[]{:S(2)}, u32[]{:S(2)}) collective-permute-start(bf16[448,128]{1,0:T(8,128)(2,1)S(1)} %maximum_select_fusion.2.refs_0_), channel_id=1, source_target_pairs={{0,16},{16,0},{1,17},{17,1},{2,18},{18,2},{3,19},{19,3},{4,20},{20... | collective-permute-start | bytes 344072 | tf_op jit(solution)/shard_map/ppermute | solution.py:717
  37.5 4.2 %collective-permute-start.13 = (bf16[448,128]{1,0:T(8,128)(2,1)S(1)}, bf16[448,128]{1,0:T(8,128)(2,1)S(1)}, u32[]{:S(2)}, u32[]{:S(2)}) collective-permute-start(bf16[448,128]{1,0:T(8,128)(2,1)S(1)} %maximum_select_fusion.2.refs_0_), channel_id=1, source_target_pairs={{0,17},{1,19},{2,16},{3,18},{4,22},{5,20},{6,23},{7,21},{8,26},{9,... | collective-permute-start | bytes 344072 | tf_op jit(solution)/shard_map/ppermute | solution.py:728
  39.5 3.7 %collective-permute-start.18 = (bf16[448,128]{1,0:T(8,128)(2,1)S(1)}, bf16[448,128]{1,0:T(8,128)(2,1)S(1)}, u32[]{:S(2)}, u32[]{:S(2)}) collective-permute-start(bf16[448,128]{1,0:T(8,128)(2,1)S(1)} %collective-permute-done.14.refs_3_), channel_id=1, source_target_pairs={{0,16},{16,0},{1,17},{17,1},{2,18},{18,2},{3,19},{19,3},{4,20},{20... | collective-permute-start | bytes 344072 | tf_op jit(solution)/shard_map/ppermute | solution.py:717
  41.8 1.4 %collective-permute-start.17 = (bf16[448,128]{1,0:T(8,128)(2,1)S(1)}, bf16[448,128]{1,0:T(8,128)(2,1)S(1)}, u32[]{:S(2)}, u32[]{:S(2)}) collective-permute-start(bf16[448,128]{1,0:T(8,128)(2,1)S(1)} %collective-permute-done.13.refs_2_), channel_id=1, source_target_pairs={{0,16},{16,0},{1,17},{17,1},{2,18},{18,2},{3,19},{19,3},{4,20},{20... | collective-permute-start | bytes 344072 | tf_op jit(solution)/shard_map/ppermute | solution.py:717

commit v9 on v8

--- a/solution.py
+++ b/solution.py
@@ -201,6 +201,7 @@
     qst_s,
     a_s,
     keys_s,
+    vals_s,
     tok_s,
     xt_s,
     prob_s,
@@ -380,13 +381,16 @@
         xt_s[s] = turned
         ut_s[s] = mm(turned, mix_s[s, :, : 2 * width]).astype(BF16)
 
+    def stem_turned(s):
+        vals_s[s] = mm(x_s[s], value_w[embs[s]]).astype(BF16).T
+
     def stem_values(s):
-        values = mm(ut_s[s].T, value_w[embs[s]])
+        mixed = mm(vals_s[s], mix_s[s, :, : 2 * width]).astype(BF16).T.astype(F32)
         for t in range(steps):
-            satt_s[s, t] = fold(values[width * t : width * (t + 1)], smask).astype(BF16)
+            satt_s[s, t] = fold(mixed[width * t : width * (t + 1)], smask).astype(BF16)
 
     ready(6)
-    staged(n, stem_keys, stem_scores, stem_softmax, stem_moments, stem_values)
+    staged(n, stem_keys, stem_scores, stem_turned, stem_softmax, stem_values, stem_moments)
     ready(10)
     image_tok = mm(satt_s[...].reshape(n * steps * qry, width), stem_proj[...])
     tok_s[:, :, :qry] = image_tok.astype(BF16).reshape(n, steps, qry, width)
@@ -628,6 +632,7 @@
         low(emb, width, HEADS * qry),
         low(emb, width, HEADS * qry),
         low(n, tall, width),
+        low(n, width, tall),
         low(n, steps, half_tok, width),
         low(n, width, tall),
         full(n, tall, HEADS * qry),

time: 44.8 us -> 45 us (level)
  no operation moved by 1% of the time
where the time goes in v9:
time: 45 us; the launch traced here: 44.8 us
  starting transfers between devices  21.1 us (47%)
  Pallas kernels  12.8 us (28%)
  waiting for transfers between devices  9.26 us (21%)
  between operations  0.87 us (2%)
  other arithmetic  0.71 us (2%)
    ppermute x12, starting transfers between devices, swap_chips(): return lax.ppermute(value, ('section', 'dp'), pairs)  19 us
    pallas_call x1, Pallas kernels, compute(): pl.pallas_call(functools.partial(compute_kernel, dims), out_shape=(low(2,...  10.4 us
    ppermute x12, waiting for transfers between devices, swap_chips(): return lax.ppermute(value, ('section', 'dp'), pairs)  8.26 us
    ppermute x7, starting transfers between devices, swap_cores(): return lax.ppermute(value, 'section', [(0, 1), (1, 0)])  2.1 us
    pallas_call x1, Pallas kernels, finish(): pl.pallas_call(functools.partial(finish_kernel, table), out_shape=tuple((...  1.47 us
    ppermute x7, waiting for transfers between devices, swap_cores(): return lax.ppermute(value, 'section', [(0, 1), (1, 0)])  1 us
  transfers between devices with their start and end apart: 19, of which 10 were waited for; matrix products, arithmetic and copies ran while one was open for 2% of the time, Pallas kernels for 2%

profile of v9, /device:TPU:0, one launch (start us, length us, event | category | flops | bytes accessed | tf_op | source)
XLA Modules:
  0.0 44.8 jit_solution(14053741051611247455)
XLA Ops:
  0.7 10.4 %stem_trunk.1 = (bf16[2,448,128]{2,1,0:T(8,128)(2,1)S(1)}, bf16[2,448,128]{2,1,0:T(8,128)(2,1)S(1)}, bf16[2,448,128]{2,1,0:T(8,128)(2,1)S(1)}, bf16[2,448,128]{2...) custom-call(s32[16]{0:T(128)} %emb_h.1, s32[16]{0:T(128)} %steps_h.1, ...), custom_call_target="tpu_custom_call" | custom-call | tf_op jit(solution)/shard_map/stem_trunk/pallas_call | solution.py:677
  11.1 0.5 %collective-permute-start = (bf16[2,448,128]{2,1,0:T(8,128)(2,1)S(1)}, bf16[2,448,128]{2,1,0:T(8,128)(2,1)S(1)}, u32[]{:S(2)}, u32[]{:S(2)}) collective-permute-start(bf16[2,448,128]{2,1,0:T(8,128)(2,1)S(1)} %get-tuple-element.48), channel_id=1, source_target_pairs={{0,16},{16,0},{1,17},{17,1},{2,18},{18,2},{3,19},{19,3},{4,20},{20... | collective-permute-start | bytes 688136 | tf_op jit(solution)/shard_map/ppermute | solution.py:722
  11.7 1.0 %collective-permute-done = bf16[2,448,128]{2,1,0:T(8,128)(2,1)S(1)} collective-permute-done((bf16[2,448,128]{2,1,0:T(8,128)(2,1)S(1)}, bf16[2,448,128]{2,1,0:T(8,128)(2,1)S(1)}, u32[]{:S(2)}, u32[]{:S(2)}) %collective-permute-start) | collective-permute-done | bytes 229408 | tf_op jit(solution)/shard_map/ppermute | solution.py:722
  12.8 2.7 %collective-permute-start.8 = (bf16[448,128]{1,0:T(8,128)(2,1)S(1)}, bf16[448,128]{1,0:T(8,128)(2,1)S(1)}, u32[]{:S(2)}, u32[]{:S(2)}) collective-permute-start(bf16[448,128]{1,0:T(8,128)(2,1)S(1)} %select_bitcast_fusion), channel_id=1, source_target_pairs={{0,17},{1,19},{2,16},{3,18},{4,22},{5,20},{6,23},{7,21},{8,26},{9,... | collective-permute-start | bytes 344072 | tf_op jit(solution)/shard_map/ppermute | solution.py:733
  16.2 1.7 %collective-permute-done.8 = bf16[448,128]{1,0:T(8,128)(2,1)S(1)} collective-permute-done((bf16[448,128]{1,0:T(8,128)(2,1)S(1)}, bf16[448,128]{1,0:T(8,128)(2,1)S(1)}, u32[]{:S(2)}, u32[]{:S(2)}) %collective-permute-start.8) | collective-permute-done | bytes 114720 | tf_op jit(solution)/shard_map/ppermute | solution.py:733
  18.0 2.1 %collective-permute-start.9 = (bf16[224,128]{1,0:T(8,128)(2,1)S(1)}, bf16[224,128]{1,0:T(8,128)(2,1)S(1)}, u32[]{:S(2)}, u32[]{:S(2)}) collective-permute-start(bf16[224,128]{1,0:T(8,128)(2,1)S(1)} %broadcast_select_fusion), channel_id=1, source_target_pairs={{0,18},{1,16},{2,19},{3,17},{4,21},{5,23},{6,20},{7,22},{8,25},{9,... | collective-permute-start | bytes 172040 | tf_op jit(solution)/shard_map/ppermute | solution.py:733
  20.2 1.3 %collective-permute-start.4 = (bf16[224,128]{1,0:T(8,128)(2,1)S(1)}, bf16[224,128]{1,0:T(8,128)(2,1)S(1)}, u32[]{:S(2)}, u32[]{:S(2)}) collective-permute-start(bf16[224,128]{1,0:T(8,128)(2,1)S(1)} %broadcast_select_fusion.1), channel_id=1, source_target_pairs={{0,18},{1,16},{2,19},{3,17},{4,21},{5,23},{6,20},{7,22},{8,25},{9,... | collective-permute-start | bytes 172040 | tf_op jit(solution)/shard_map/ppermute | solution.py:733
  21.5 0.5 %collective-permute-done.9 = bf16[224,128]{1,0:T(8,128)(2,1)S(1)} collective-permute-done((bf16[224,128]{1,0:T(8,128)(2,1)S(1)}, bf16[224,128]{1,0:T(8,128)(2,1)S(1)}, u32[]{:S(2)}, u32[]{:S(2)}) %collective-permute-start.9) | collective-permute-done | bytes 57376 | tf_op jit(solution)/shard_map/ppermute | solution.py:733
  22.1 1.9 %collective-permute-start.10 = (bf16[224,128]{1,0:T(8,128)(2,1)S(1)}, bf16[224,128]{1,0:T(8,128)(2,1)S(1)}, u32[]{:S(2)}, u32[]{:S(2)}) collective-permute-start(bf16[224,128]{1,0:T(8,128)(2,1)S(1)} %add_convert_fusion.4), channel_id=1, source_target_pairs={{0,20},{1,25},{2,26},{3,23},{4,28},{5,17},{6,18},{7,31},{8,16},{9,... | collective-permute-start | bytes 172040 | tf_op jit(solution)/shard_map/ppermute | solution.py:733
  24.0 1.3 %collective-permute-start.5 = (bf16[224,128]{1,0:T(8,128)(2,1)S(1)}, bf16[224,128]{1,0:T(8,128)(2,1)S(1)}, u32[]{:S(2)}, u32[]{:S(2)}) collective-permute-start(bf16[224,128]{1,0:T(8,128)(2,1)S(1)} %add_convert_fusion.7), channel_id=1, source_target_pairs={{0,20},{1,25},{2,26},{3,23},{4,28},{5,17},{6,18},{7,31},{8,16},{9,... | collective-permute-start | bytes 172040 | tf_op jit(solution)/shard_map/ppermute | solution.py:733
  25.3 0.6 %collective-permute-done.10 = bf16[224,128]{1,0:T(8,128)(2,1)S(1)} collective-permute-done((bf16[224,128]{1,0:T(8,128)(2,1)S(1)}, bf16[224,128]{1,0:T(8,128)(2,1)S(1)}, u32[]{:S(2)}, u32[]{:S(2)}) %collective-permute-start.10) | collective-permute-done | bytes 57376 | tf_op jit(solution)/shard_map/ppermute | solution.py:733
  25.9 3.0 %collective-permute-start.11 = (bf16[224,128]{1,0:T(8,128)(2,1)S(1)}, bf16[224,128]{1,0:T(8,128)(2,1)S(1)}, u32[]{:S(2)}, u32[]{:S(2)}) collective-permute-start(bf16[224,128]{1,0:T(8,128)(2,1)S(1)} %add_convert_fusion.3), channel_id=1, source_target_pairs={{0,24},{1,21},{2,22},{3,27},{4,16},{5,29},{6,30},{7,19},{8,28},{9,... | collective-permute-start | bytes 172040 | tf_op jit(solution)/shard_map/ppermute | solution.py:733
  29.0 1.3 %collective-permute-start.6 = (bf16[224,128]{1,0:T(8,128)(2,1)S(1)}, bf16[224,128]{1,0:T(8,128)(2,1)S(1)}, u32[]{:S(2)}, u32[]{:S(2)}) collective-permute-start(bf16[224,128]{1,0:T(8,128)(2,1)S(1)} %add_convert_fusion.6), channel_id=1, source_target_pairs={{0,24},{1,21},{2,22},{3,27},{4,16},{5,29},{6,30},{7,19},{8,28},{9,... | collective-permute-start | bytes 172040 | tf_op jit(solution)/shard_map/ppermute | solution.py:733
  30.3 1.0 %collective-permute-done.11 = bf16[224,128]{1,0:T(8,128)(2,1)S(1)} collective-permute-done((bf16[224,128]{1,0:T(8,128)(2,1)S(1)}, bf16[224,128]{1,0:T(8,128)(2,1)S(1)}, u32[]{:S(2)}, u32[]{:S(2)}) %collective-permute-start.11) | collective-permute-done | bytes 57376 | tf_op jit(solution)/shard_map/ppermute | solution.py:733
  31.3 2.1 %collective-permute-start.12 = (bf16[224,128]{1,0:T(8,128)(2,1)S(1)}, bf16[224,128]{1,0:T(8,128)(2,1)S(1)}, u32[]{:S(2)}, u32[]{:S(2)}) collective-permute-start(bf16[224,128]{1,0:T(8,128)(2,1)S(1)} %add_convert_fusion.2), channel_id=1, source_target_pairs={{0,18},{1,16},{2,19},{3,17},{4,21},{5,23},{6,20},{7,22},{8,25},{9,... | collective-permute-start | bytes 172040 | tf_op jit(solution)/shard_map/ppermute | solution.py:733
  33.4 0.4 collective-permute-done.6
  33.8 1.0 %collective-permute-start.7 = (bf16[224,128]{1,0:T(8,128)(2,1)S(1)}, bf16[224,128]{1,0:T(8,128)(2,1)S(1)}, u32[]{:S(2)}, u32[]{:S(2)}) collective-permute-start(bf16[224,128]{1,0:T(8,128)(2,1)S(1)} %add_convert_fusion.5), channel_id=1, source_target_pairs={{0,18},{1,16},{2,19},{3,17},{4,21},{5,23},{6,20},{7,22},{8,25},{9,... | collective-permute-start | bytes 172040 | tf_op jit(solution)/shard_map/ppermute | solution.py:733
  35.4 1.2 %collective-permute-start.14 = (bf16[448,128]{1,0:T(8,128)(2,1)S(1)}, bf16[448,128]{1,0:T(8,128)(2,1)S(1)}, u32[]{:S(2)}, u32[]{:S(2)}) collective-permute-start(bf16[448,128]{1,0:T(8,128)(2,1)S(1)} %maximum_select_fusion.3.refs_1_), channel_id=1, source_target_pairs={{0,17},{1,19},{2,16},{3,18},{4,22},{5,20},{6,23},{7,21},{8,26},{9,... | collective-permute-start | bytes 344072 | tf_op jit(solution)/shard_map/ppermute | solution.py:733
  36.6 0.9 %collective-permute-done.7 = bf16[224,128]{1,0:T(8,128)(2,1)S(1)} collective-permute-done((bf16[224,128]{1,0:T(8,128)(2,1)S(1)}, bf16[224,128]{1,0:T(8,128)(2,1)S(1)}, u32[]{:S(2)}, u32[]{:S(2)}) %collective-permute-start.7) | collective-permute-done | bytes 57376 | tf_op jit(solution)/shard_map/ppermute | solution.py:733
  37.7 0.9 %collective-permute-start.13 = (bf16[448,128]{1,0:T(8,128)(2,1)S(1)}, bf16[448,128]{1,0:T(8,128)(2,1)S(1)}, u32[]{:S(2)}, u32[]{:S(2)}) collective-permute-start(bf16[448,128]{1,0:T(8,128)(2,1)S(1)} %maximum_select_fusion.2.refs_0_), channel_id=1, source_target_pairs={{0,17},{1,19},{2,16},{3,18},{4,22},{5,20},{6,23},{7,21},{8,26},{9,... | collective-permute-start | bytes 344072 | tf_op jit(solution)/shard_map/ppermute | solution.py:733
  38.9 0.8 %collective-permute-done.14.refs_3_ = bf16[448,128]{1,0:T(8,128)(2,1)S(1)} collective-permute-done((bf16[448,128]{1,0:T(8,128)(2,1)S(1)}, bf16[448,128]{1,0:T(8,128)(2,1)S(1)}, u32[]{:S(2)}, u32[]{:S(2)}) %collective-permute-start.14) | collective-permute-done | bytes 114720 | tf_op jit(solution)/shard_map/ppermute | solution.py:733
  40.1 1.9 %collective-permute-done.13.refs_2_ = bf16[448,128]{1,0:T(8,128)(2,1)S(1)} collective-permute-done((bf16[448,128]{1,0:T(8,128)(2,1)S(1)}, bf16[448,128]{1,0:T(8,128)(2,1)S(1)}, u32[]{:S(2)}, u32[]{:S(2)}) %collective-permute-start.13) | collective-permute-done | bytes 114720 | tf_op jit(solution)/shard_map/ppermute | solution.py:733
  42.4 0.9 %send_out.1 = (bf16[16,32,128]{2,1,0:T(8,128)(2,1)}, bf16[147,16,128]{2,1,0:T(8,128)(2,1)}, bf16[16,16,64]{2,1,0:T(8,128)(2,1)}) custom-call(bf16[16,32,128]{2,1,0:T(8,128)(2,1)S(1)} %maximum_select_fusion.1.refs_0_, bf16[147,16,128]{2,1,0:T(8,128)(2,1)S(1)} %maximum_select_fusion.refs_1_, bf16[16,16,64]{2,1,0:T(8,128)(2,1)S(1)} %maximum_select_fusion.4.refs_2_), custom_call_target="tpu_custom_call" | custom-call | tf_op jit(solution)/shard_map/send_out/pallas_call | solution.py:746
  43.3 1.5 %finish.1 = (f32[4,16,128]{2,1,0:T(8,128)}, f32[4,128,128]{2,1,0:T(8,128)}, f32[4,128,128]{2,1,0:T(8,128)}, f32[128,128]{1,0:T(8,128)}, f32[4,64,128]{2,1,0:T(8,...) custom-call(bf16[448,128]{1,0:T(8,128)(2,1)S(1)} %maximum_select_fus, ...), custom_call_target="tpu_custom_call" | custom-call | tf_op jit(solution)/shard_map/finish/pallas_call | solution.py:796
  (42 shorter events, 3.0 us)
Async XLA Ops:
  11.1 1.6 %collective-permute-start = (bf16[2,448,128]{2,1,0:T(8,128)(2,1)S(1)}, bf16[2,448,128]{2,1,0:T(8,128)(2,1)S(1)}, u32[]{:S(2)}, u32[]{:S(2)}) collective-permute-start(bf16[2,448,128]{2,1,0:T(8,128)(2,1)S(1)} %get-tuple-element.48), channel_id=1, source_target_pairs={{0,16},{16,0},{1,17},{17,1},{2,18},{18,2},{3,19},{19,3},{4,20},{20... | collective-permute-start | bytes 688136 | tf_op jit(solution)/shard_map/ppermute | solution.py:722
  11.6 3.9 %collective-permute-start.2 = (bf16[2,448,128]{2,1,0:T(8,128)(2,1)S(1)}, bf16[2,448,128]{2,1,0:T(8,128)(2,1)S(1)}, u32[]{:S(2)}, u32[]{:S(2)}) collective-permute-start(bf16[2,448,128]{2,1,0:T(8,128)(2,1)S(1)} %get-tuple-element.55), channel_id=1, source_target_pairs={{0,16},{16,0},{1,17},{17,1},{2,18},{18,2},{3,19},{19,3},{4,20},{20... | collective-permute-start | bytes 688136 | tf_op jit(solution)/shard_map/ppermute | solution.py:722
  12.8 5.1 %collective-permute-start.8 = (bf16[448,128]{1,0:T(8,128)(2,1)S(1)}, bf16[448,128]{1,0:T(8,128)(2,1)S(1)}, u32[]{:S(2)}, u32[]{:S(2)}) collective-permute-start(bf16[448,128]{1,0:T(8,128)(2,1)S(1)} %select_bitcast_fusion), channel_id=1, source_target_pairs={{0,17},{1,19},{2,16},{3,18},{4,22},{5,20},{6,23},{7,21},{8,26},{9,... | collective-permute-start | bytes 344072 | tf_op jit(solution)/shard_map/ppermute | solution.py:733
  15.6 4.6 %collective-permute-start.3 = (bf16[448,128]{1,0:T(8,128)(2,1)S(1)}, bf16[448,128]{1,0:T(8,128)(2,1)S(1)}, u32[]{:S(2)}, u32[]{:S(2)}) collective-permute-start(bf16[448,128]{1,0:T(8,128)(2,1)S(1)} %select_bitcast_fusion.1), channel_id=1, source_target_pairs={{0,17},{1,19},{2,16},{3,18},{4,22},{5,20},{6,23},{7,21},{8,26},{9,... | collective-permute-start | bytes 344072 | tf_op jit(solution)/shard_map/ppermute | solution.py:733
  15.9 22.8 %collective-permute-start.1 = (bf16[1560,128]{1,0:T(8,128)(2,1)S(1)}, bf16[1560,128]{1,0:T(8,128)(2,1)S(1)}, u32[]{:S(2)}, u32[]{:S(2)}) collective-permute-start(bf16[1560,128]{1,0:T(8,128)(2,1)S(1)} %get-tuple-element.50), channel_id=1, source_target_pairs={{0,16},{16,0},{1,17},{17,1},{2,18},{18,2},{3,19},{19,3},{4,20},{20... | collective-permute-start | bytes 1198088 | tf_op jit(solution)/shard_map/ppermute | solution.py:722
  18.0 4.0 %collective-permute-start.9 = (bf16[224,128]{1,0:T(8,128)(2,1)S(1)}, bf16[224,128]{1,0:T(8,128)(2,1)S(1)}, u32[]{:S(2)}, u32[]{:S(2)}) collective-permute-start(bf16[224,128]{1,0:T(8,128)(2,1)S(1)} %broadcast_select_fusion), channel_id=1, source_target_pairs={{0,18},{1,16},{2,19},{3,17},{4,21},{5,23},{6,20},{7,22},{8,25},{9,... | collective-permute-start | bytes 172040 | tf_op jit(solution)/shard_map/ppermute | solution.py:733
  20.2 3.7 %collective-permute-start.4 = (bf16[224,128]{1,0:T(8,128)(2,1)S(1)}, bf16[224,128]{1,0:T(8,128)(2,1)S(1)}, u32[]{:S(2)}, u32[]{:S(2)}) collective-permute-start(bf16[224,128]{1,0:T(8,128)(2,1)S(1)} %broadcast_select_fusion.1), channel_id=1, source_target_pairs={{0,18},{1,16},{2,19},{3,17},{4,21},{5,23},{6,20},{7,22},{8,25},{9,... | collective-permute-start | bytes 172040 | tf_op jit(solution)/shard_map/ppermute | solution.py:733
  22.1 3.9 %collective-permute-start.10 = (bf16[224,128]{1,0:T(8,128)(2,1)S(1)}, bf16[224,128]{1,0:T(8,128)(2,1)S(1)}, u32[]{:S(2)}, u32[]{:S(2)}) collective-permute-start(bf16[224,128]{1,0:T(8,128)(2,1)S(1)} %add_convert_fusion.4), channel_id=1, source_target_pairs={{0,20},{1,25},{2,26},{3,23},{4,28},{5,17},{6,18},{7,31},{8,16},{9,... | collective-permute-start | bytes 172040 | tf_op jit(solution)/shard_map/ppermute | solution.py:733
  24.0 5.0 %collective-permute-start.5 = (bf16[224,128]{1,0:T(8,128)(2,1)S(1)}, bf16[224,128]{1,0:T(8,128)(2,1)S(1)}, u32[]{:S(2)}, u32[]{:S(2)}) collective-permute-start(bf16[224,128]{1,0:T(8,128)(2,1)S(1)} %add_convert_fusion.7), channel_id=1, source_target_pairs={{0,20},{1,25},{2,26},{3,23},{4,28},{5,17},{6,18},{7,31},{8,16},{9,... | collective-permute-start | bytes 172040 | tf_op jit(solution)/shard_map/ppermute | solution.py:733
  25.9 5.3 %collective-permute-start.11 = (bf16[224,128]{1,0:T(8,128)(2,1)S(1)}, bf16[224,128]{1,0:T(8,128)(2,1)S(1)}, u32[]{:S(2)}, u32[]{:S(2)}) collective-permute-start(bf16[224,128]{1,0:T(8,128)(2,1)S(1)} %add_convert_fusion.3), channel_id=1, source_target_pairs={{0,24},{1,21},{2,22},{3,27},{4,16},{5,29},{6,30},{7,19},{8,28},{9,... | collective-permute-start | bytes 172040 | tf_op jit(solution)/shard_map/ppermute | solution.py:733
  29.0 4.9 %collective-permute-start.6 = (bf16[224,128]{1,0:T(8,128)(2,1)S(1)}, bf16[224,128]{1,0:T(8,128)(2,1)S(1)}, u32[]{:S(2)}, u32[]{:S(2)}) collective-permute-start(bf16[224,128]{1,0:T(8,128)(2,1)S(1)} %add_convert_fusion.6), channel_id=1, source_target_pairs={{0,24},{1,21},{2,22},{3,27},{4,16},{5,29},{6,30},{7,19},{8,28},{9,... | collective-permute-start | bytes 172040 | tf_op jit(solution)/shard_map/ppermute | solution.py:733
  31.3 3.9 %collective-permute-start.12 = (bf16[224,128]{1,0:T(8,128)(2,1)S(1)}, bf16[224,128]{1,0:T(8,128)(2,1)S(1)}, u32[]{:S(2)}, u32[]{:S(2)}) collective-permute-start(bf16[224,128]{1,0:T(8,128)(2,1)S(1)} %add_convert_fusion.2), channel_id=1, source_target_pairs={{0,18},{1,16},{2,19},{3,17},{4,21},{5,23},{6,20},{7,22},{8,25},{9,... | collective-permute-start | bytes 172040 | tf_op jit(solution)/shard_map/ppermute | solution.py:733
  33.8 3.7 %collective-permute-start.7 = (bf16[224,128]{1,0:T(8,128)(2,1)S(1)}, bf16[224,128]{1,0:T(8,128)(2,1)S(1)}, u32[]{:S(2)}, u32[]{:S(2)}) collective-permute-start(bf16[224,128]{1,0:T(8,128)(2,1)S(1)} %add_convert_fusion.5), channel_id=1, source_target_pairs={{0,18},{1,16},{2,19},{3,17},{4,21},{5,23},{6,20},{7,22},{8,25},{9,... | collective-permute-start | bytes 172040 | tf_op jit(solution)/shard_map/ppermute | solution.py:733
  35.3 8.0 %collective-permute-start.16 = (bf16[448,128]{1,0:T(8,128)(2,1)S(1)}, bf16[448,128]{1,0:T(8,128)(2,1)S(1)}, u32[]{:S(2)}, u32[]{:S(2)}) collective-permute-start(bf16[448,128]{1,0:T(8,128)(2,1)S(1)} %maximum_select_fusion.3.refs_1_), channel_id=1, source_target_pairs={{0,16},{16,0},{1,17},{17,1},{2,18},{18,2},{3,19},{19,3},{4,20},{20... | collective-permute-start | bytes 344072 | tf_op jit(solution)/shard_map/ppermute | solution.py:722
  35.4 4.2 %collective-permute-start.14 = (bf16[448,128]{1,0:T(8,128)(2,1)S(1)}, bf16[448,128]{1,0:T(8,128)(2,1)S(1)}, u32[]{:S(2)}, u32[]{:S(2)}) collective-permute-start(bf16[448,128]{1,0:T(8,128)(2,1)S(1)} %maximum_select_fusion.3.refs_1_), channel_id=1, source_target_pairs={{0,17},{1,19},{2,16},{3,18},{4,22},{5,20},{6,23},{7,21},{8,26},{9,... | collective-permute-start | bytes 344072 | tf_op jit(solution)/shard_map/ppermute | solution.py:733
  37.5 5.8 %collective-permute-start.15 = (bf16[448,128]{1,0:T(8,128)(2,1)S(1)}, bf16[448,128]{1,0:T(8,128)(2,1)S(1)}, u32[]{:S(2)}, u32[]{:S(2)}) collective-permute-start(bf16[448,128]{1,0:T(8,128)(2,1)S(1)} %maximum_select_fusion.2.refs_0_), channel_id=1, source_target_pairs={{0,16},{16,0},{1,17},{17,1},{2,18},{18,2},{3,19},{19,3},{4,20},{20... | collective-permute-start | bytes 344072 | tf_op jit(solution)/shard_map/ppermute | solution.py:722
  37.7 4.2 %collective-permute-start.13 = (bf16[448,128]{1,0:T(8,128)(2,1)S(1)}, bf16[448,128]{1,0:T(8,128)(2,1)S(1)}, u32[]{:S(2)}, u32[]{:S(2)}) collective-permute-start(bf16[448,128]{1,0:T(8,128)(2,1)S(1)} %maximum_select_fusion.2.refs_0_), channel_id=1, source_target_pairs={{0,17},{1,19},{2,16},{3,18},{4,22},{5,20},{6,23},{7,21},{8,26},{9,... | collective-permute-start | bytes 344072 | tf_op jit(solution)/shard_map/ppermute | solution.py:733
  39.7 3.7 %collective-permute-start.18 = (bf16[448,128]{1,0:T(8,128)(2,1)S(1)}, bf16[448,128]{1,0:T(8,128)(2,1)S(1)}, u32[]{:S(2)}, u32[]{:S(2)}) collective-permute-start(bf16[448,128]{1,0:T(8,128)(2,1)S(1)} %collective-permute-done.14.refs_3_), channel_id=1, source_target_pairs={{0,16},{16,0},{1,17},{17,1},{2,18},{18,2},{3,19},{19,3},{4,20},{20... | collective-permute-start | bytes 344072 | tf_op jit(solution)/shard_map/ppermute | solution.py:722
  41.9 1.4 %collective-permute-start.17 = (bf16[448,128]{1,0:T(8,128)(2,1)S(1)}, bf16[448,128]{1,0:T(8,128)(2,1)S(1)}, u32[]{:S(2)}, u32[]{:S(2)}) collective-permute-start(bf16[448,128]{1,0:T(8,128)(2,1)S(1)} %collective-permute-done.13.refs_2_), channel_id=1, source_target_pairs={{0,16},{16,0},{1,17},{17,1},{2,18},{18,2},{3,19},{19,3},{4,20},{20... | collective-permute-start | bytes 344072 | tf_op jit(solution)/shard_map/ppermute | solution.py:722
